TPU v7x, 32 devices: a whole 2x2x4 slice. The times are simulated.
32 devices in a mesh: expert: 8 (over z, x), shard: 4 (over y, core).
Axes of the slice: x: 2, y: 2, z: 4, core: 2. Of those that a mesh axis runs over, the one named last changes fastest.
Arguments:
- tokens: int32 [8192], replicated, may hold values from 0 to 50303
- prefix: int32 [32], P(('expert', 'shard')), may hold values from 1 to 256
- routes: int32 [8192, 4], P(('expert', 'shard')), may hold values from 0 to 7, all different within a row; in each aligned block of 256 rows (0 to 255, 256 to 511, ...) at most 144 rows name the same one
- picked: int32 [256], P(('expert', 'shard')), may hold values from 0 to 255, as said below
- loss_ids: int32 [256, 65], replicated, may hold values from 0 to 50303, as said below
- teacher_logits: float32 [256, 64], replicated, may hold values from -8 to 8
- embedding: float32 [50304, 1024], P(None, ('expert', 'shard')), may hold values from -6 to 6
- embedding_mean: float32 [50304, 1024], P(None, ('expert', 'shard')), may hold values from -4.5776367e-05 to 4.5776367e-05
- embedding_square: float32 [50304, 1024], P(None, ('expert', 'shard')), may hold values from 9.313226e-10 to 9.313226e-08
- attention: float32 [2, 1024, 4096], P(None, ('expert', 'shard'))
- attention_mean: float32 [2, 1024, 4096], P(None, ('expert', 'shard')), may hold values from -0.01171875 to 0.01171875
- attention_square: float32 [2, 1024, 4096], P(None, ('expert', 'shard')), may hold values from 2.3841858e-07 to 2.3841858e-05
- router: float32 [2, 1024, 8], P(None, ('expert', 'shard')), may hold values from -0.375 to 0.375
- router_mean: float32 [2, 1024, 8], P(None, ('expert', 'shard')), may hold values from -0.01171875 to 0.01171875
- router_square: float32 [2, 1024, 8], P(None, ('expert', 'shard')), may hold values from 3.8146973e-06 to 0.00038146973
- norm_gains: float32 [9, 1024], P(None, ('expert', 'shard')), may hold values from 0.5 to 1.5
- gains_mean: float32 [9, 1024], P(None, ('expert', 'shard')), may hold values from -0.01171875 to 0.01171875
- gains_square: float32 [9, 1024], P(None, ('expert', 'shard')), may hold values from 3.8146973e-06 to 0.00038146973
- expert_up: float32 [8, 2, 1024, 1024], P('expert', None, 'shard'), may hold values from -0.1875 to 0.1875
- upward_mean: float32 [8, 2, 1024, 1024], P('expert', None, 'shard'), may hold values from -0.0014648438 to 0.0014648438
- upward_square: float32 [8, 2, 1024, 1024], P('expert', None, 'shard'), may hold values from 2.9802322e-08 to 2.9802322e-06
- expert_down: float32 [8, 2, 512, 1024], P('expert', None, None, 'shard'), may hold values from -2 to 2
- downward_mean: float32 [8, 2, 512, 1024], P('expert', None, None, 'shard'), may hold values from -9.1552734e-05 to 9.1552734e-05
- downward_square: float32 [8, 2, 512, 1024], P('expert', None, None, 'shard'), may hold values from 2.3283064e-10 to 2.3283064e-08
- output_table: float32 [50304, 1024], P(('expert', 'shard')), may hold values from -0.375 to 0.375
- table_mean: float32 [50304, 1024], P(('expert', 'shard')), may hold values from -1.4909351e-05 to 1.4909351e-05
- table_square: float32 [50304, 1024], P(('expert', 'shard')), may hold values from 6.1746875e-12 to 6.1746874e-10
Outputs:
- loss_value: float32 [], replicated
- embedding_mean_next: float32 [50304, 1024], P(None, ('expert', 'shard'))
- embedding_square_next: float32 [50304, 1024], P(None, ('expert', 'shard'))
- embedding_update: float32 [50304, 1024], P(None, ('expert', 'shard'))
- attention_mean_next: float32 [2, 1024, 4096], P(None, ('expert', 'shard'))
- attention_square_next: float32 [2, 1024, 4096], P(None, ('expert', 'shard'))
- attention_update: float32 [2, 1024, 4096], P(None, ('expert', 'shard'))
- router_mean_next: float32 [2, 1024, 8], P(None, ('expert', 'shard'))
- router_square_next: float32 [2, 1024, 8], P(None, ('expert', 'shard'))
- router_update: float32 [2, 1024, 8], P(None, ('expert', 'shard'))
- gains_mean_next: float32 [9, 1024], P(None, ('expert', 'shard'))
- gains_square_next: float32 [9, 1024], P(None, ('expert', 'shard'))
- gains_update: float32 [9, 1024], P(None, ('expert', 'shard'))
- upward_mean_next: float32 [8, 2, 1024, 1024], P('expert', None, 'shard')
- upward_square_next: float32 [8, 2, 1024, 1024], P('expert', None, 'shard')
- upward_update: float32 [8, 2, 1024, 1024], P('expert', None, 'shard')
- downward_mean_next: float32 [8, 2, 512, 1024], P('expert', None, None, 'shard')
- downward_square_next: float32 [8, 2, 512, 1024], P('expert', None, None, 'shard')
- downward_update: float32 [8, 2, 512, 1024], P('expert', None, None, 'shard')
- table_mean_next: float32 [50304, 1024], P(('expert', 'shard'))
- table_square_next: float32 [50304, 1024], P(('expert', 'shard'))
- table_update: float32 [50304, 1024], P(('expert', 'shard'))
Inputs may be any that keep to these rules, and one draw needn't show every extreme that they name: `routes`: each row names 4 different experts. Within the 256 rows of one sequence no expert is named more than 144 times, a bound that some block reaches. `picked`: the 8 entries of one sequence are distinct positions of that sequence. `loss_ids`: column 0 holds a position's target token, columns 1 to 64 the teacher's 64 distinct candidate tokens.
All inputs are finite; a program needn't handle non-finite values.
Results may differ from a plain program's by a relative error of at most 0.023.
The roundings to bfloat16 on the way count: a program that leaves them out, or rounds other values in their place, can miss the bound.
Values may be sent and summed in bfloat16 or wider, within the bound.
A program may use at most 384 MiB of HBM per device.

v0:
```python
import jax
import jax.numpy as jnp
from jax import lax
from jax.sharding import PartitionSpec as P

D = 1024
HEADS = 16
HDIM = 64
F = 512
TOPK = 4
ADAM_STEP = 10


EPS_NORM = 1e-05
BETA_ONE = 0.9
BETA_TWO = 0.95
ADAM_EPS = 1e-08
LEARN_RATE = 0.01
DECAY_RATE = 0.1
ROPE_BASE = 10000.0
MASK_FILL = -1e30


def combined_all(part, axis, combine):
    gathered = jax.tree.map(lambda a: lax.all_gather(a, axis), part)

    def take(source):
        return jax.tree.map(lambda a: lax.dynamic_index_in_dim(a, source, 0, False), gathered)

    return lax.fori_loop(
        1, lax.axis_size(axis), lambda source, state: combine(state, take(source)), take(0)
    )


def rms_norm(inputs, gain_row):
    return (
        inputs * lax.rsqrt(jnp.mean(inputs * inputs, axis=-1, keepdims=True) + EPS_NORM) * gain_row
    )


def norm_back(inputs, gain_row, upstream):
    _, pullback = jax.vjp(rms_norm, inputs, gain_row)
    return pullback(upstream)


def rotary(inputs):
    row_count = inputs.shape[0]
    split_heads = inputs.reshape(row_count, HEADS, HDIM)
    half_dim = HDIM // 2
    position = jnp.arange(row_count, dtype=jnp.float32)[:, None, None]
    frequency = ROPE_BASE ** (-jnp.arange(half_dim, dtype=jnp.float32) * 2.0 / HDIM)
    angles = position * frequency[None, None, :]
    cosines = jnp.cos(angles)
    sine_values = jnp.sin(angles)
    lower_half = split_heads[..., :half_dim]
    upper_half = split_heads[..., half_dim:]
    turned = jnp.concatenate(
        [
            lower_half * cosines - upper_half * sine_values,
            upper_half * cosines + lower_half * sine_values,
        ],
        axis=-1,
    )
    return turned.reshape(row_count, HEADS * HDIM)


def rotary_back(upstream):
    _, pullback = jax.vjp(rotary, upstream)
    return pullback(upstream)[0]


def rounded(values):
    return lax.optimization_barrier(values.astype(jnp.bfloat16)).astype(jnp.float32)


def slot_table(route_rows, expert_count, capacity):
    row_count = route_rows.shape[0]
    top_count = route_rows.shape[1]
    one_hot = (
        route_rows[:, :, None] == jnp.arange(expert_count, dtype=jnp.int32)[None, None, :]
    ).astype(jnp.int32)
    one_hot = one_hot.reshape(row_count * top_count, expert_count)
    before = jnp.cumsum(one_hot, axis=0) - one_hot
    slot_index = jnp.sum(before * one_hot, axis=1)
    kept_mask = slot_index < capacity
    flat_slot = jnp.where(
        kept_mask,
        route_rows.reshape(row_count * top_count) * capacity + slot_index,
        expert_count * capacity,
    )
    return (flat_slot, kept_mask)


def block_scores(query_block, key_heads, first_row, prefix_len):
    block_rows = query_block.shape[0]
    key_count = key_heads.shape[0]
    scores = jnp.einsum(
        "bhd,khd->hbk", query_block, key_heads, preferred_element_type=jnp.float32
    ) * HDIM ** (-0.5)
    query_place = first_row + jnp.arange(block_rows, dtype=jnp.int32)[:, None]
    key_place = jnp.arange(key_count, dtype=jnp.int32)[None, :]
    visible = (key_place <= query_place) | (key_place < prefix_len)
    return jnp.where(visible[None], scores, MASK_FILL)


def attend(queries, key_rows, value_rows, prefix_len):
    seq_len = queries.shape[0]
    block_rows = min(512, seq_len)
    key_heads = key_rows.reshape(seq_len, HEADS, HDIM)
    value_heads = value_rows.reshape(seq_len, HEADS, HDIM)

    def one_block(block_index):
        first_row = block_index * block_rows
        query_block = queries.reshape(block_rows, HEADS, HDIM)
        scores = block_scores(query_block, key_heads, first_row, prefix_len)
        peak_score = jnp.max(scores, axis=-1, keepdims=True)
        weights = jnp.exp(scores - peak_score)
        summed = jnp.sum(weights, axis=-1, keepdims=True)
        probs_low = (weights / summed).astype(jnp.bfloat16)
        attended = jnp.einsum(
            "hbk,khd->bhd", probs_low, value_heads, preferred_element_type=jnp.float32
        )
        return (attended.reshape(block_rows, HEADS * HDIM), (peak_score + jnp.log(summed))[..., 0])

    attended, log_total = lax.map(one_block, jnp.arange(seq_len // block_rows, dtype=jnp.int32))
    return (attended.reshape(seq_len, HEADS * HDIM), log_total)


def attend_back(queries, key_rows, value_rows, grad_low, log_total, prefix_len):
    seq_len = queries.shape[0]
    block_rows = min(512, seq_len)
    key_heads = key_rows.reshape(seq_len, HEADS, HDIM)
    value_heads = value_rows.reshape(seq_len, HEADS, HDIM)
    factor = HDIM ** (-0.5)

    def one_block(carry, block_index):
        key_grad, value_grad = carry
        first_row = block_index * block_rows
        query_block = queries.reshape(block_rows, HEADS, HDIM)
        grad_block = grad_low.reshape(block_rows, HEADS, HDIM)
        scores = block_scores(query_block, key_heads, first_row, prefix_len)
        probs = jnp.exp(scores - log_total[block_index][:, :, None])
        grad_probs = jnp.einsum(
            "bhd,khd->hbk", grad_block, value_heads, preferred_element_type=jnp.float32
        )
        row_dot = jnp.sum(probs * grad_probs, axis=-1, keepdims=True)
        grad_scores = (probs * (grad_probs - row_dot)).astype(jnp.bfloat16)
        query_grad = (
            jnp.einsum("hbk,khd->bhd", grad_scores, key_heads, preferred_element_type=jnp.float32)
            * factor
        )
        key_grad = (
            key_grad
            + jnp.einsum(
                "hbk,bhd->khd", grad_scores, query_block, preferred_element_type=jnp.float32
            )
            * factor
        )
        value_grad = value_grad + jnp.einsum(
            "hbk,bhd->khd",
            probs.astype(jnp.bfloat16),
            grad_block,
            preferred_element_type=jnp.float32,
        )
        return ((key_grad, value_grad), query_grad.reshape(block_rows, HEADS * HDIM))

    empty_grad = jnp.zeros((seq_len, HEADS, HDIM), jnp.float32)
    (key_grad, value_grad), query_grad = lax.scan(
        one_block, (empty_grad, empty_grad), jnp.arange(seq_len // block_rows, dtype=jnp.int32)
    )
    return (
        query_grad.reshape(seq_len, HEADS * HDIM),
        key_grad.reshape(seq_len, HEADS * HDIM),
        value_grad.reshape(seq_len, HEADS * HDIM),
    )


def join_stats(left_side, right_side):
    peak_value = jnp.maximum(left_side[0], right_side[0])
    summed = left_side[1] * jnp.exp(left_side[0] - peak_value) + right_side[1] * jnp.exp(
        right_side[0] - peak_value
    )
    return (peak_value, summed, left_side[2] + right_side[2])


def adam_step(weight, mean_old, square_old, gradient):
    mean_new = BETA_ONE * mean_old + (1.0 - BETA_ONE) * gradient
    square_new = BETA_TWO * square_old + (1.0 - BETA_TWO) * gradient * gradient
    bias_one = 1.0 - BETA_ONE**ADAM_STEP
    bias_two = 1.0 - BETA_TWO**ADAM_STEP
    update = -LEARN_RATE * (
        mean_new / bias_one / (jnp.sqrt(square_new / bias_two) + ADAM_EPS) + DECAY_RATE * weight
    )
    return (mean_new, square_new, update)


def shards(
    tokens,
    prefix,
    routes,
    picked,
    loss_ids,
    teacher_logits,
    embedding,
    embedding_mean,
    embedding_square,
    attention,
    attention_mean,
    attention_square,
    router,
    router_mean,
    router_square,
    norm_gains,
    gains_mean,
    gains_square,
    expert_up,
    upward_mean,
    upward_square,
    expert_down,
    downward_mean,
    downward_square,
    output_table,
    table_mean,
    table_square,
):
    devices_all = lax.axis_size(("expert", "shard"))
    seq_len = routes.shape[0]
    layer_count = attention.shape[0]
    experts_all = router.shape[2]
    capacity = 9 * seq_len * TOPK // (8 * experts_all)
    column_count = embedding.shape[1]
    prefix_len = prefix[0]
    slot_total = experts_all * capacity
    attention_low, router_low, gains_low = (
        lax.all_gather(attention.astype(jnp.bfloat16), ("expert", "shard"), axis=1, tiled=True),
        lax.all_gather(router.astype(jnp.bfloat16), ("expert", "shard"), axis=1, tiled=True),
        lax.all_gather(norm_gains.astype(jnp.bfloat16), ("expert", "shard"), axis=1, tiled=True),
    )
    gain_rows = gains_low.astype(jnp.float32)
    upward_low, downward_low = (
        lax.all_gather(expert_up.astype(jnp.bfloat16), "shard", axis=2, tiled=True),
        lax.all_gather(expert_down.astype(jnp.bfloat16), "shard", axis=3, tiled=True),
    )
    table_low = embedding.astype(jnp.bfloat16)
    looked_up = jnp.take(table_low, tokens, axis=0).reshape(devices_all, seq_len * column_count)
    arrived_rows = lax.all_to_all(
        looked_up, ("expert", "shard"), split_axis=0, concat_axis=0, tiled=True
    )
    hidden = (
        arrived_rows.reshape(devices_all, seq_len, column_count)
        .transpose(1, 0, 2)
        .reshape(seq_len, D)
        .astype(jnp.float32)
    )
    source_row = jnp.arange(seq_len * TOPK, dtype=jnp.int32) // TOPK
    flat_slot, kept_mask = slot_table(routes, experts_all, capacity)
    safe_slot = jnp.minimum(flat_slot, slot_total - 1)
    one_hot = (
        routes[:, :, None] == jnp.arange(experts_all, dtype=jnp.int32)[None, None, :]
    ).astype(jnp.float32)
    stored = []
    for layer_index in range(layer_count):
        weights_now = attention_low[layer_index]
        normed_low = rms_norm(hidden, gain_rows[4 * layer_index]).astype(jnp.bfloat16)
        projected = jnp.dot(normed_low, weights_now[:, : 3 * D], preferred_element_type=jnp.float32)
        queries = rotary(rms_norm(projected[:, :D], gain_rows[4 * layer_index + 1])).astype(
            jnp.bfloat16
        )
        key_rows = rotary(rms_norm(projected[:, D : 2 * D], gain_rows[4 * layer_index + 2])).astype(
            jnp.bfloat16
        )
        value_rows = projected[:, 2 * D :].astype(jnp.bfloat16)
        attended, log_total = attend(queries, key_rows, value_rows, prefix_len)
        attended_low = attended.astype(jnp.bfloat16)
        middle = hidden + jnp.dot(
            attended_low, weights_now[:, 3 * D :], preferred_element_type=jnp.float32
        )
        ffn_low = rms_norm(middle, gain_rows[4 * layer_index + 3]).astype(jnp.bfloat16)
        router_logits = jnp.dot(
            ffn_low, router_low[layer_index], preferred_element_type=jnp.float32
        )
        router_probs = jax.nn.softmax(router_logits, axis=-1)
        gate_weights = jnp.take_along_axis(router_probs, routes, axis=1)
        outgoing = (
            jnp.zeros((slot_total + 1, D), jnp.bfloat16)
            .at[flat_slot]
            .set(jnp.take(ffn_low, source_row, axis=0))
        )
        outgoing = outgoing[:slot_total].reshape(experts_all, capacity, D)
        received = lax.all_to_all(outgoing, "expert", split_axis=0, concat_axis=1, tiled=True)
        gate_up = jnp.einsum(
            "erd,edf->erf", received, upward_low[:, layer_index], preferred_element_type=jnp.float32
        )
        activated_low = (jax.nn.silu(gate_up[..., :F]) * gate_up[..., F:]).astype(jnp.bfloat16)
        produced = jnp.einsum(
            "erf,efd->erd",
            activated_low,
            downward_low[:, layer_index],
            preferred_element_type=jnp.float32,
        ).astype(jnp.bfloat16)
        returned = lax.all_to_all(produced, "expert", split_axis=1, concat_axis=0, tiled=True)
        collected = jnp.take(returned.reshape(slot_total, D), safe_slot, axis=0)
        collected = jnp.where(kept_mask[:, None], collected.astype(jnp.float32), 0.0).reshape(
            seq_len, TOPK, D
        )
        stored.append(
            (
                hidden,
                normed_low,
                projected,
                queries,
                key_rows,
                value_rows,
                log_total,
                attended_low,
                middle,
                ffn_low,
                router_probs,
                gate_weights,
                received,
                gate_up,
                activated_low,
                collected,
            )
        )
        hidden = middle + jnp.sum(gate_weights[:, :, None] * collected, axis=1)
    final_gain = gain_rows[4 * layer_count]
    final_rows = jnp.take(hidden, picked, axis=0)
    final_low = rms_norm(final_rows, final_gain).astype(jnp.bfloat16)
    all_rows = lax.all_gather(final_low, ("expert", "shard"), axis=0, tiled=True)
    head_low = output_table.astype(jnp.bfloat16)
    vocab_local = head_low.shape[0]
    logits = jnp.einsum("pd,vd->pv", all_rows, head_low, preferred_element_type=jnp.float32)
    local_ids = loss_ids - lax.axis_index(("expert", "shard")) * vocab_local
    in_range = (local_ids >= 0) & (local_ids < vocab_local)
    safe_ids = jnp.clip(local_ids, 0, vocab_local - 1)
    selected = jnp.where(in_range, jnp.take_along_axis(logits, safe_ids, axis=1), 0.0)
    local_peak = jnp.max(logits, axis=1)
    local_sum = jnp.sum(jnp.exp(logits - local_peak[:, None]), axis=1)
    peak_all, sum_all, selected_all = combined_all(
        (local_peak, local_sum, selected), ("expert", "shard"), join_stats
    )
    log_norm = peak_all + jnp.log(sum_all)
    teacher_log = jax.nn.log_softmax(teacher_logits, axis=1)
    teacher_prob = jnp.exp(teacher_log)
    row_loss = (
        log_norm
        - selected_all[:, 0]
        + jnp.sum(teacher_prob * (teacher_log - selected_all[:, 1:] + log_norm[:, None]), axis=1)
    )
    loss_value = jnp.mean(row_loss)
    position_count = all_rows.shape[0]
    coefficients = jnp.concatenate(
        [jnp.ones((position_count, 1), jnp.float32), teacher_prob], axis=1
    )
    grad_logits = (
        jnp.exp(logits - log_norm[:, None]) * (1.0 + jnp.sum(teacher_prob, axis=1))[:, None]
    )
    row_place = jnp.arange(position_count, dtype=jnp.int32)[:, None]
    grad_logits = grad_logits.at[row_place, safe_ids].add(-jnp.where(in_range, coefficients, 0.0))
    grad_logits_low = (grad_logits / position_count).astype(jnp.bfloat16)
    table_grad = jnp.einsum(
        "pv,pd->vd", grad_logits_low, all_rows, preferred_element_type=jnp.float32
    )
    final_grad = lax.psum_scatter(
        jnp.dot(grad_logits_low, head_low, preferred_element_type=jnp.float32),
        ("expert", "shard"),
        scatter_dimension=0,
        tiled=True,
    )
    rows_grad, final_gain_grad = norm_back(final_rows, final_gain, final_grad)
    grad_hidden = jnp.zeros((seq_len, D), jnp.float32).at[picked].add(rows_grad)
    gain_parts = [None] * (4 * layer_count + 1)
    gain_parts[4 * layer_count] = final_gain_grad
    attention_parts = [None] * layer_count
    router_parts = [None] * layer_count
    up_parts = [None] * layer_count
    down_parts = [None] * layer_count
    for layer_index in reversed(range(layer_count)):
        (
            hidden_in,
            normed_low,
            projected,
            queries,
            key_rows,
            value_rows,
            log_total,
            attended_low,
            middle,
            ffn_low,
            router_probs,
            gate_weights,
            received,
            gate_up,
            activated_low,
            collected,
        ) = stored[layer_index]
        weights_now = attention_low[layer_index]
        weight_grad = jnp.sum(grad_hidden[:, None, :] * collected, axis=2)
        sent_back = (
            (gate_weights[:, :, None] * grad_hidden[:, None, :])
            .astype(jnp.bfloat16)
            .reshape(seq_len * TOPK, D)
        )
        back_buffer = jnp.zeros((slot_total + 1, D), jnp.bfloat16).at[flat_slot].set(sent_back)
        back_buffer = back_buffer[:slot_total].reshape(experts_all, capacity, D)
        output_grad = lax.all_to_all(back_buffer, "expert", split_axis=0, concat_axis=1, tiled=True)
        activated_grad = rounded(
            jnp.einsum(
                "erd,efd->erf",
                output_grad,
                downward_low[:, layer_index],
                preferred_element_type=jnp.float32,
            )
        )
        down_parts[layer_index] = jnp.einsum(
            "erf,erd->efd", activated_low, output_grad, preferred_element_type=jnp.float32
        )
        gate_part = gate_up[..., :F]
        up_part = gate_up[..., F:]
        sigmoid_gate = jax.nn.sigmoid(gate_part)
        gate_side = (
            activated_grad * up_part * sigmoid_gate * (1.0 + gate_part * (1.0 - sigmoid_gate))
        )
        up_side = activated_grad * gate_part * sigmoid_gate
        gate_up_grad = jnp.concatenate([gate_side, up_side], axis=-1).astype(jnp.bfloat16)
        up_parts[layer_index] = jnp.einsum(
            "erd,erf->edf", received, gate_up_grad, preferred_element_type=jnp.float32
        )
        input_grad = jnp.einsum(
            "erf,edf->erd",
            gate_up_grad,
            upward_low[:, layer_index],
            preferred_element_type=jnp.float32,
        )
        back_inputs = lax.all_to_all(
            input_grad.astype(jnp.bfloat16), "expert", split_axis=1, concat_axis=0, tiled=True
        ).astype(input_grad.dtype)
        route_grad = jnp.take(back_inputs.reshape(slot_total, D), safe_slot, axis=0)
        route_grad = jnp.where(kept_mask[:, None], route_grad, 0.0).reshape(seq_len, TOPK, D)
        prob_grad = jnp.sum(one_hot * weight_grad[:, :, None], axis=1)
        logit_grad = router_probs * (
            prob_grad - jnp.sum(router_probs * prob_grad, axis=-1, keepdims=True)
        )
        logit_low = logit_grad.astype(jnp.bfloat16)
        router_parts[layer_index] = jnp.einsum(
            "ld,le->de", ffn_low, logit_low, preferred_element_type=jnp.float32
        )
        ffn_grad = jnp.sum(route_grad, axis=1) + jnp.einsum(
            "le,de->ld", logit_low, router_low[layer_index], preferred_element_type=jnp.float32
        )
        middle_grad, ffn_gain_grad = norm_back(middle, gain_rows[4 * layer_index + 3], ffn_grad)
        gain_parts[4 * layer_index + 3] = ffn_gain_grad
        grad_middle = grad_hidden + middle_grad
        branch_low = grad_middle.astype(jnp.bfloat16)
        out_weight_grad = jnp.einsum(
            "ld,le->de", attended_low, branch_low, preferred_element_type=jnp.float32
        )
        attended_grad = jnp.einsum(
            "le,de->ld", branch_low, weights_now[:, 3 * D :], preferred_element_type=jnp.float32
        ).astype(jnp.bfloat16)
        query_grad, key_grad, value_grad = attend_back(
            queries, key_rows, value_rows, attended_grad, log_total, prefix_len
        )
        query_pre = rotary_back(rounded(query_grad))
        key_pre = rotary_back(rounded(key_grad))
        query_in, query_gain_grad = norm_back(
            projected[:, :D], gain_rows[4 * layer_index + 1], query_pre
        )
        key_in, key_gain_grad = norm_back(
            projected[:, D : 2 * D], gain_rows[4 * layer_index + 2], key_pre
        )
        gain_parts[4 * layer_index + 1] = query_gain_grad
        gain_parts[4 * layer_index + 2] = key_gain_grad
        projected_grad = jnp.concatenate([query_in, key_in, value_grad], axis=1).astype(
            jnp.bfloat16
        )
        qkv_weight_grad = jnp.einsum(
            "ld,le->de", normed_low, projected_grad, preferred_element_type=jnp.float32
        )
        normed_grad = jnp.einsum(
            "le,de->ld", projected_grad, weights_now[:, : 3 * D], preferred_element_type=jnp.float32
        )
        hidden_grad, attn_gain_grad = norm_back(hidden_in, gain_rows[4 * layer_index], normed_grad)
        gain_parts[4 * layer_index] = attn_gain_grad
        attention_parts[layer_index] = jnp.concatenate([qkv_weight_grad, out_weight_grad], axis=1)
        grad_hidden = grad_middle + hidden_grad
    sending = (
        grad_hidden.reshape(seq_len, devices_all, column_count)
        .transpose(1, 0, 2)
        .reshape(devices_all, seq_len * column_count)
    )
    arrived_grads = lax.all_to_all(
        sending.astype(jnp.bfloat16), ("expert", "shard"), split_axis=0, concat_axis=0, tiled=True
    ).astype(sending.dtype)
    embedding_grad = jax.ops.segment_sum(
        arrived_grads.reshape(devices_all * seq_len, column_count),
        tokens,
        num_segments=embedding.shape[0],
    )
    attention_sum = jnp.stack(attention_parts)
    router_sum = jnp.stack(router_parts)
    gains_sum = jnp.stack(gain_parts)
    attention_grad, router_grad, gains_grad = (
        lax.psum_scatter(attention_sum, ("expert", "shard"), scatter_dimension=1, tiled=True),
        lax.psum_scatter(router_sum, ("expert", "shard"), scatter_dimension=1, tiled=True),
        lax.psum_scatter(gains_sum, ("expert", "shard"), scatter_dimension=1, tiled=True),
    )
    upward_grad, downward_grad = (
        lax.psum_scatter(
            jnp.stack(up_parts, axis=1).astype(jnp.bfloat16),
            "shard",
            scatter_dimension=2,
            tiled=True,
        ).astype(jnp.float32),
        lax.psum_scatter(
            jnp.stack(down_parts, axis=1).astype(jnp.bfloat16),
            "shard",
            scatter_dimension=3,
            tiled=True,
        ).astype(jnp.float32),
    )
    embedding_mean_next, embedding_square_next, embedding_update = adam_step(
        embedding, embedding_mean, embedding_square, embedding_grad
    )
    attention_mean_next, attention_square_next, attention_update = adam_step(
        attention, attention_mean, attention_square, attention_grad
    )
    router_mean_next, router_square_next, router_update = adam_step(
        router, router_mean, router_square, router_grad
    )
    gains_mean_next, gains_square_next, gains_update = adam_step(
        norm_gains, gains_mean, gains_square, gains_grad
    )
    upward_mean_next, upward_square_next, upward_update = adam_step(
        expert_up, upward_mean, upward_square, upward_grad
    )
    downward_mean_next, downward_square_next, downward_update = adam_step(
        expert_down, downward_mean, downward_square, downward_grad
    )
    table_mean_next, table_square_next, table_update = adam_step(
        output_table, table_mean, table_square, table_grad
    )
    return (
        loss_value,
        embedding_mean_next,
        embedding_square_next,
        embedding_update,
        attention_mean_next,
        attention_square_next,
        attention_update,
        router_mean_next,
        router_square_next,
        router_update,
        gains_mean_next,
        gains_square_next,
        gains_update,
        upward_mean_next,
        upward_square_next,
        upward_update,
        downward_mean_next,
        downward_square_next,
        downward_update,
        table_mean_next,
        table_square_next,
        table_update,
    )


def solution(mesh):
    return jax.shard_map(
        shards,
        mesh=mesh,
        in_specs=(
            P(),
            P(("expert", "shard")),
            P(("expert", "shard"), None),
            P(("expert", "shard")),
            P(),
            P(),
            P(None, ("expert", "shard")),
            P(None, ("expert", "shard")),
            P(None, ("expert", "shard")),
            P(None, ("expert", "shard"), None),
            P(None, ("expert", "shard"), None),
            P(None, ("expert", "shard"), None),
            P(None, ("expert", "shard"), None),
            P(None, ("expert", "shard"), None),
            P(None, ("expert", "shard"), None),
            P(None, ("expert", "shard")),
            P(None, ("expert", "shard")),
            P(None, ("expert", "shard")),
            P("expert", None, "shard", None),
            P("expert", None, "shard", None),
            P("expert", None, "shard", None),
            P("expert", None, None, "shard"),
            P("expert", None, None, "shard"),
            P("expert", None, None, "shard"),
            P(("expert", "shard"), None),
            P(("expert", "shard"), None),
            P(("expert", "shard"), None),
        ),
        out_specs=(
            P(),
            P(None, ("expert", "shard")),
            P(None, ("expert", "shard")),
            P(None, ("expert", "shard")),
            P(None, ("expert", "shard"), None),
            P(None, ("expert", "shard"), None),
            P(None, ("expert", "shard"), None),
            P(None, ("expert", "shard"), None),
            P(None, ("expert", "shard"), None),
            P(None, ("expert", "shard"), None),
            P(None, ("expert", "shard")),
            P(None, ("expert", "shard")),
            P(None, ("expert", "shard")),
            P("expert", None, "shard", None),
            P("expert", None, "shard", None),
            P("expert", None, "shard", None),
            P("expert", None, None, "shard"),
            P("expert", None, None, "shard"),
            P("expert", None, None, "shard"),
            P(("expert", "shard"), None),
            P(("expert", "shard"), None),
            P(("expert", "shard"), None),
        ),
        check_vma=False,
    )
```

profile of v0, /device:TPU:9, one launch (start us, length us, event | category | flops | bytes accessed | tf_op | source)
XLA Modules:
  0.0 2335.1 jit_solution(7185525881792155740)
XLA Ops:
  25.8 28.3 %gather_fusion = bf16[8192,32]{1,0:T(8,128)(2,1)S(1)} fusion(bf16[50304,32]{1,0:T(8,128)(2,1)} %copy.365, s32[8192]{0:T(1024)S(1)} %fusion.138), kind=kCustom, calls=%fused_computation.8 | custom fusion | bytes 1081344 | tf_op jit(solution)/shard_map/jit(_take)/gather | solution.py:245
  69.6 41.7 %all-gather.3 = bf16[32,32,9]{1,2,0:T(8,128)(2,1)S(1)} all-gather(bf16[1,32,9]{1,2,0:T(8,128)(2,1)S(1)} %convert_bitcast_fusion.2), channel_id=1, replica_groups=mesh['expert'=8,'shard'=4] {'expert','shard'}, dimensions={0}, use_global_device_ids=true | all-gather | bytes 19008 | tf_op jit(solution)/shard_map/all_gather | solution.py:237
  159.2 15.3 scatter_custom_fusion
  184.6 51.1 %all-to-all-done.1 = bf16[8,144,1024]{2,1,0:T(8,128)(2,1)} async-done(((bf16[8,144,1024]{2,1,0:T(8,128)(2,1)}), bf16[8,144,1024]{2,1,0:T(8,128)(2,1)}, u32[]{:S(2)}, u32[]{:S(2)}) %all-to-all-start.1) | async-done | bytes 2359328 | tf_op jit(solution)/shard_map/all_to_all | solution.py:290
  246.9 16.4 copy.482
  263.3 14.1 reduce.19
  288.2 78.3 %all_gather.38 = bf16[2,1024,8]{2,0,1:T(2,128)(2,1)S(1)} all-gather(bf16[2,32,8]{2,0,1:T(2,128)(2,1)S(1)} %copy.380), channel_id=1, replica_groups=mesh['expert'=8,'shard'=4] {'expert','shard'}, dimensions={1}, use_global_device_ids=true | all-gather | bytes 33792 | tf_op jit(solution)/shard_map/all_gather | solution.py:236
  427.6 15.5 scatter_custom_fusion.1
  443.4 57.7 %all_to_all.84 = bf16[8,144,1024]{2,1,0:T(8,128)(2,1)S(1)} all-to-all(bf16[8,144,1024]{2,1,0:T(8,128)(2,1)S(1)} %bitcast.314), channel_id=1, replica_groups=mesh['expert'=8,'shard'=4] {'expert'}, dimensions={0} | all-to-all | bytes 4718592 | tf_op jit(solution)/shard_map/all_to_all | solution.py:290
  508.6 16.4 copy.481
  525.1 14.1 reduce.20
  557.5 43.6 %all-to-all-done.4 = bf16[8,2,73728]{2,1,0:T(2,128)(2,1)} async-done(((bf16[8,2,73728]{2,1,0:T(2,128)(2,1)}), bf16[8,2,73728]{2,1,0:T(2,128)(2,1)}, u32[]{:S(2)}, u32[]{:S(2)}) %all-to-all-start.4) | async-done | bytes 2359328 | tf_op jit(solution)/shard_map/all_to_all | solution.py:301
  635.6 35.5 %all_gather.41 = bf16[256,1024]{1,0:T(8,128)(2,1)S(1)} all-gather(bf16[8,1024]{1,0:T(8,128)(2,1)S(1)} %multiply_convert_fusion.13), channel_id=1, replica_groups=mesh['expert'=8,'shard'=4] {'expert','shard'}, dimensions={0}, use_global_device_ids=true | all-gather | bytes 540672 | tf_op jit(solution)/shard_map/all_gather | solution.py:330
  675.2 126.3 %gather_fusion.2 = f32[16640]{0:T(1024)S(1)} fusion(f32[256,1572]{0,1:T(8,128)S(1)} %get-tuple-element.545, s32[16640]{0:T(1024)S(1)} %reshape.1054), kind=kCustom, calls=%fused_computation.10 | custom fusion | bytes 266240 | tf_op jit(solution)/shard_map/jit(take_along_axis)/gather | solution.py:337
  804.3 36.7 %all-gather.5 = f32[32,1,256]{2,1,0:T(1,128)S(1)} all-gather(f32[1,1,256]{2,1,0:T(1,128)S(1)} %bitcast.402), channel_id=3, replica_groups=mesh['expert'=8,'shard'=4] {'expert','shard'}, dimensions={0}, use_global_device_ids=true | all-gather | bytes 33792 | tf_op jit(solution)/shard_map/all_gather | solution.py:25
  841.0 38.1 %all-gather.4 = f32[32,1,256]{2,1,0:T(1,128)S(1)} all-gather(f32[1,1,256]{2,1,0:T(1,128)S(1)} %bitcast.401), channel_id=2, replica_groups=mesh['expert'=8,'shard'=4] {'expert','shard'}, dimensions={0}, use_global_device_ids=true | all-gather | bytes 33792 | tf_op jit(solution)/shard_map/all_gather | solution.py:25
  880.0 31.0 %while.12 = (s32[]{:T(128)}, f32[256]{0:T(256)S(1)}, f32[256]{0:T(256)S(1)}, f32[256,65]{1,0:T(8,128)S(1)}, f32[32,256]{1,0:T(8,128)S(1)}, /*index=5*/f32[32,256...) while((s32[]{:T(128)}, f32[256]{0:T(256)S(1)}, f32[256]{0:T(256)S(1)}, ...), condition=%wide.region_28.32_spmd, body=%wide.region_27.31_spmd.sunk | while | flops 18181 | bytes 210063 | solution.py:30
  913.3 113.0 %scatter_fusion = f32[402432]{0:T(1024)S(1)} fusion(f32[402432]{0:T(1024)S(1)} %reshape.958, s32[16640]{0:T(1024)} %reshape.1108, f32[16640]{0:T(1024)} %reshape.1110), kind=kCustom, calls=%fused_computation.17 | custom fusion | flops 16640 | bytes 266240
  1032.1 114.0 %reduce-scatter.11.cloned.1.call-done = f32[8,1024]{1,0:T(8,128)} async-done(((f32[256,1024]{1,0:T(8,128)}), f32[8,1024]{1,0:T(8,128)}) %reduce-scatter.11.cloned.1.call-update) | async-done | bytes 32784 | tf_op jit(solution)/shard_map/reduce_scatter | solution.py:365
  1164.8 72.6 %all_to_all.85 = bf16[8,144,1024]{2,1,0:T(8,128)(2,1)S(1)} all-to-all(bf16[8,144,1024]{2,1,0:T(8,128)(2,1)S(1)} %bitcast.315), channel_id=1, replica_groups=mesh['expert'=8,'shard'=4] {'expert'}, dimensions={0} | all-to-all | bytes 4718592 | tf_op jit(solution)/shard_map/all_to_all | solution.py:407
  1245.7 16.4 copy.480
  1262.2 14.1 reduce.21
  1286.9 49.4 %all-to-all-done.6 = bf16[8,2,73728]{2,1,0:T(2,128)(2,1)S(1)} async-done(((bf16[8,2,73728]{2,1,0:T(2,128)(2,1)}), bf16[8,2,73728]{2,1,0:T(2,128)(2,1)S(1)}, u32[]{:S(2)}, u32[]{:S(2)}) %all-to-all-start.6) | async-done | bytes 2359328 | tf_op jit(solution)/shard_map/all_to_all | solution.py:436
  1418.2 58.9 %all_to_all.86 = bf16[8,144,1024]{2,1,0:T(8,128)(2,1)S(1)} all-to-all(bf16[8,144,1024]{2,1,0:T(8,128)(2,1)S(1)} %bitcast.316), channel_id=1, replica_groups=mesh['expert'=8,'shard'=4] {'expert'}, dimensions={0} | all-to-all | bytes 4718592 | tf_op jit(solution)/shard_map/all_to_all | solution.py:407
  1485.5 16.4 copy.479
  1544.4 33.0 %all-to-all-done.8 = bf16[8,2,73728]{2,1,0:T(2,128)(2,1)S(1)} async-done(((bf16[8,2,73728]{2,1,0:T(2,128)(2,1)}), bf16[8,2,73728]{2,1,0:T(2,128)(2,1)S(1)}, u32[]{:S(2)}, u32[]{:S(2)}) %all-to-all-start.8) | async-done | bytes 2359328 | tf_op jit(solution)/shard_map/all_to_all | solution.py:436
  1730.6 32.9 %reduce-scatter.21.cloned.1.call-done = f32[32,9]{1,0:T(8,128)} async-done(((f32[1024,9]{1,0:T(8,128)}), f32[32,9]{1,0:T(8,128)}) %reduce-scatter.21.cloned.1.call-update) | async-done | bytes 1168
  1764.9 130.7 %reduce-scatter.19.cloned.1.call-done = f32[32,16]{1,0:T(8,128)} async-done(((f32[1024,16]{1,0:T(8,128)}), f32[32,16]{1,0:T(8,128)}) %reduce-scatter.19.cloned.1.call-update) | async-done | bytes 2064
  1903.5 54.6 %scatter_custom_fusion.5 = f32[50304,32]{1,0:T(8,128)} fusion(s32[8192]{0:T(1024)} %param.37, f32[8192,32]{1,0:T(8,128)} %reshape.1104, f32[]{:T(128)} %constant.264.clone.1), kind=kCustom, calls=%fused_computation.25 | custom fusion | flops 262144 | bytes 6439424 | tf_op jit(solution)/shard_map/scatter-add | solution.py:496
  1958.1 16.8 copy.426
  1974.9 17.2 add_multiply_fusion.1
  1998.6 324.3 %reduce-scatter.13.cloned.1.call-done = f32[2,32,4096]{2,1,0:T(8,128)} async-done(((f32[2,1024,4096]{2,1,0:T(8,128)}), f32[2,32,4096]{2,1,0:T(8,128)}) %reduce-scatter.13.cloned.1.call-update) | async-done | bytes 1048592 | tf_op jit(solution)/shard_map/reduce_scatter | solution.py:505
  (909 shorter events, 619.6 us)
Async XLA Ops:
  7.2 123.7 %all-gather.11.cloned.1.call-start = ((), (), s32[]{:S(2)}) async-start(), calls=%async_computation.16 | async-start | bytes 17301504 | tf_op jit(solution)/shard_map/all_gather | solution.py:235
  59.2 57.6 %all-to-all-start = ((bf16[32,2,4096]{2,1,0:T(2,128)(2,1)}), bf16[32,2,4096]{2,1,0:T(2,128)(2,1)S(1)}, u32[]{:S(2)}, u32[]{:S(2)}) async-start(bf16[32,2,4096]{2,1,0:T(2,128)(2,1)} %reshape.1212), calls=%async_computation | async-start | bytes 1048576 | tf_op jit(solution)/shard_map/all_to_all | solution.py:246
  65.6 119.0 %all-gather.13.cloned.1.call-start = ((), (), s32[]{:S(2)}) async-start(), calls=%async_computation.17 | async-start | bytes 5242880 | tf_op jit(solution)/shard_map/all_gather | solution.py:241
  116.8 290.1 %copy-start.114 = (f32[1,1024]{1,0:T(1,128)}, f32[1,1024]{1,0:T(1,128)S(1)}, u32[]{:S(2)}) copy-start(f32[1,1024]{1,0:T(1,128)S(1)} %get-tuple-element.513) | copy-start | bytes 12292
  158.6 248.0 %copy-start.6 = (f32[256,1024]{1,0:T(8,128)}, f32[256,1024]{1,0:T(8,128)S(1)}, u32[]{:S(2)}) copy-start(f32[256,1024]{1,0:T(8,128)S(1)} %get-tuple-element.535) | copy-start | bytes 3145732
  177.7 58.0 %all-to-all-start.1 = ((bf16[8,144,1024]{2,1,0:T(8,128)(2,1)}), bf16[8,144,1024]{2,1,0:T(8,128)(2,1)}, u32[]{:S(2)}, u32[]{:S(2)}) async-start(bf16[8,144,1024]{2,1,0:T(8,128)(2,1)} %bitcast.24), calls=%async_computation.1 | async-start | bytes 4718592 | tf_op jit(solution)/shard_map/all_to_all | solution.py:290
  183.5 60.3 %all-gather.15.cloned.1.call-start = ((), (), s32[]{:S(2)}) async-start(), calls=%async_computation.18 | async-start | bytes 2621440 | tf_op jit(solution)/shard_map/all_gather | solution.py:242
  281.5 95.6 %all-to-all-start.2 = ((bf16[8,2,73728]{2,1,0:T(2,128)(2,1)}), bf16[8,2,73728]{2,1,0:T(2,128)(2,1)}, u32[]{:S(2)}, u32[]{:S(2)}) async-start(bf16[8,2,73728]{2,1,0:T(2,128)(2,1)} %reshape.1214), calls=%async_computation.2 | async-start | bytes 4718592 | tf_op jit(solution)/shard_map/all_to_all | solution.py:301
  287.5 80.7 %copy-start.146 = (s32[1024]{0:T(1024)S(1)}, s32[1024]{0:T(1024)}, u32[]{:S(2)}) copy-start(s32[1024]{0:T(1024)} %copy-done.145) | copy-start | bytes 12292
  287.5 80.7 %copy-start.148 = (s32[1024]{0:T(1024)S(1)}, s32[1024]{0:T(1024)}, u32[]{:S(2)}) copy-start(s32[1024]{0:T(1024)} %copy-done.147) | copy-start | bytes 12292
  287.5 81.3 %copy-start.39 = (bf16[256,1024]{1,0:T(8,128)(2,1)S(1)}, bf16[256,1024]{1,0:T(8,128)(2,1)}, u32[]{:S(2)}) copy-start(bf16[256,1024]{1,0:T(8,128)(2,1)} %copy-done.38) | copy-start | bytes 1572868
  368.8 251.9 %copy-start.169 = (pred[1024]{0:T(1024)(128)(4,1)}, pred[1024]{0:T(1024)(128)(4,1)S(1)}, u32[]{:S(2)}) copy-start(pred[1024]{0:T(1024)(128)(4,1)S(1)} %get-tuple-element.524) | copy-start | bytes 3076
  368.9 243.9 %copy-start.129 = (s32[1024]{0:T(1024)}, s32[1024]{0:T(1024)S(1)}, u32[]{:S(2)}) copy-start(s32[1024]{0:T(1024)S(1)} %broadcast_clamp_fusion) | copy-start | bytes 12292
  426.4 208.1 %copy-start.4 = (f32[256,1024]{1,0:T(8,128)}, f32[256,1024]{1,0:T(8,128)S(1)}, u32[]{:S(2)}) copy-start(f32[256,1024]{1,0:T(8,128)S(1)} %get-tuple-element.541) | copy-start | bytes 3145732
  543.2 57.8 %all-to-all-start.4 = ((bf16[8,2,73728]{2,1,0:T(2,128)(2,1)}), bf16[8,2,73728]{2,1,0:T(2,128)(2,1)}, u32[]{:S(2)}, u32[]{:S(2)}) async-start(bf16[8,2,73728]{2,1,0:T(2,128)(2,1)} %reshape.1216), calls=%async_computation.4 | async-start | bytes 4718592 | tf_op jit(solution)/shard_map/all_to_all | solution.py:301
  548.9 330.2 %all-gather.17.cloned.1.call-start = ((), (), s32[]{:S(2)}) async-start(), calls=%async_computation.23 | async-start | bytes 4325376 | tf_op jit(solution)/shard_map/all_gather | solution.py:25
  675.2 127.3 %copy-start.118 = (f32[256,64]{0,1:T(8,128)S(1)}, f32[256,64]{0,1:T(8,128)}, u32[]{:S(2)}) copy-start(f32[256,64]{0,1:T(8,128)} %param.42) | copy-start | bytes 196612
  675.2 127.7 %copy-start.226 = (s32[2]{0:T(128)S(1)}, s32[2]{0:T(128)}, u32[]{:S(2)}) copy-start(s32[2]{0:T(128)} %constant.435) | copy-start | bytes 28
  675.2 127.8 %copy-start.225 = (s32[2]{0:T(128)S(1)}, s32[2]{0:T(128)}, u32[]{:S(2)}) copy-start(s32[2]{0:T(128)} %constant.438) | copy-start | bytes 28
  802.5 343.6 %reduce-scatter.11.cloned.1.call-start = ((), (), s32[]{:S(2)}) async-start(), calls=%async_computation.19 | async-start | bytes 1081344 | tf_op jit(solution)/shard_map/reduce_scatter | solution.py:365
  1280.3 56.0 %all-to-all-start.6 = ((bf16[8,2,73728]{2,1,0:T(2,128)(2,1)}), bf16[8,2,73728]{2,1,0:T(2,128)(2,1)S(1)}, u32[]{:S(2)}, u32[]{:S(2)}) async-start(bf16[8,2,73728]{2,1,0:T(2,128)(2,1)} %reshape.1218), calls=%async_computation.7 | async-start | bytes 4718592 | tf_op jit(solution)/shard_map/all_to_all | solution.py:436
  1520.1 57.3 %all-to-all-start.8 = ((bf16[8,2,73728]{2,1,0:T(2,128)(2,1)}), bf16[8,2,73728]{2,1,0:T(2,128)(2,1)S(1)}, u32[]{:S(2)}, u32[]{:S(2)}) async-start(bf16[8,2,73728]{2,1,0:T(2,128)(2,1)} %reshape.1220), calls=%async_computation.9 | async-start | bytes 4718592 | tf_op jit(solution)/shard_map/all_to_all | solution.py:436
  1525.2 201.5 %reduce-scatter.17.cloned.1.call-start = ((), (), s32[]{:S(2)}) async-start(), calls=%async_computation.22 | async-start | bytes 2621440 | tf_op jit(solution)/shard_map/reduce_scatter | solution.py:516
  1537.7 225.8 %reduce-scatter.21.cloned.1.call-start = ((), (), s32[]{:S(2)}) async-start(), calls=%async_computation.25 | async-start | bytes 540672
  1646.5 249.2 %reduce-scatter.19.cloned.1.call-start = ((), (), s32[]{:S(2)}) async-start(), calls=%async_computation.24 | async-start | bytes 540672
  1648.5 343.5 %reduce-scatter.15.cloned.1.call-start = ((), (), s32[]{:S(2)}) async-start(), calls=%async_computation.21 | async-start | bytes 5242880 | tf_op jit(solution)/shard_map/reduce_scatter | solution.py:510
  1652.7 670.2 %reduce-scatter.13.cloned.1.call-start = ((), (), s32[]{:S(2)}) async-start(), calls=%async_computation.20 | async-start | bytes 34603008 | tf_op jit(solution)/shard_map/reduce_scatter | solution.py:505
  1713.5 183.7 %all-to-all-start.9 = ((bf16[32,2,4096]{2,1,0:T(2,128)(2,1)}), bf16[32,2,4096]{2,1,0:T(2,128)(2,1)S(1)}, u32[]{:S(2)}, u32[]{:S(2)}) async-start(bf16[32,2,4096]{2,1,0:T(2,128)(2,1)} %reshape.1222), calls=%async_computation.10 | async-start | bytes 1048576 | tf_op jit(solution)/shard_map/all_to_all | solution.py:493
  1726.7 169.8 %copy-start.168 = (f32[2,32,8]{1,2,0:T(8,128)S(1)}, f32[2,32,8]{1,2,0:T(8,128)}, u32[]{:S(2)}) copy-start(f32[2,32,8]{1,2,0:T(8,128)} %param.49) | copy-start | bytes 6148
  1726.7 169.8 %copy-start.218 = (f32[2,32,8]{1,2,0:T(8,128)S(1)}, f32[2,32,8]{1,2,0:T(8,128)}, u32[]{:S(2)}) copy-start(f32[2,32,8]{1,2,0:T(8,128)} %param.51) | copy-start | bytes 6148
  1726.7 169.8 %copy-start.219 = (f32[2,32,8]{1,2,0:T(8,128)S(1)}, f32[2,32,8]{1,2,0:T(8,128)}, u32[]{:S(2)}) copy-start(f32[2,32,8]{1,2,0:T(8,128)} %param.50) | copy-start | bytes 6148
  1992.1 330.8 %copy-start.45 = (f32[2,32,4096]{2,1,0:T(8,128)S(1)}, f32[2,32,4096]{2,1,0:T(8,128)}, u32[]{:S(2)}) copy-start(f32[2,32,4096]{2,1,0:T(8,128)} %param.46) | copy-start | bytes 3145732
  (224 other events, 1595.1 us)
Sparse Core Ops, SparseCore 0:
  11.5 119.2 all-gather.10
  133.0 33.9 all-gather.12
  186.5 23.5 all-gather.14
  802.6 64.3 all-gather.16
  1032.1 113.9 reduce-scatter.10
  1537.8 38.7 reduce-scatter.16
  1646.6 116.8 reduce-scatter.20
  1765.8 129.8 reduce-scatter.18
  1898.2 64.3 reduce-scatter.14
  1964.8 358.0 reduce-scatter.12
where the time goes:
time: 2350 us; the launch traced here: 2340 us
  waiting for transfers between devices  782 us (33%)
  other arithmetic  471 us (20%)
  local copies, waits for them, and re-layouts  471 us (20%)
  blocking collectives  419 us (18%)
  matrix products  123 us (5%)
  starting transfers between devices  46.4 us (2%)
    reduce_scatter x1, waiting for transfers between devices, shards(): lax.psum_scatter(attention_sum, ('expert', 'shard'), scatter_dimension=1,...  324 us
    unnamed x13, other arithmetic  170 us
    unnamed x12, waiting for transfers between devices  164 us
    all_to_all x2, blocking collectives, shards(): lax.all_to_all(back_buffer, 'expert', split_axis=0, concat_axis=1, tiled=...  131 us
    gather x4, local copies, waits for them, and re-layouts, shards(): jnp.take_along_axis(logits, safe_ids, axis=1)  127 us
    reduce_scatter x1, waiting for transfers between devices, shards(): lax.psum_scatter(jnp.dot(grad_logits_low, head_low, preferred_element_typ...  114 us
    all_to_all x2, waiting for transfers between devices, shards(): lax.all_to_all(input_grad.astype(jnp.bfloat16), 'expert', split_axis=1, c...  82.4 us
    unnamed x507, local copies, waits for them, and re-layouts  81.2 us
  transfers between devices with their start and end apart: 17, of which 9 were waited for; matrix products, arithmetic and copies ran while one was open for 17% of the time, Pallas kernels for 0%

commit v1 on v0

v1 whole, which is shorter than its diff:
```python
import jax
import jax.numpy as jnp
from jax import lax
from jax.sharding import Mesh, PartitionSpec as P

D = 1024
HEADS = 16
HDIM = 64
F = 512
TOPK = 4
ADAM_STEP = 10


EPS_NORM = 1e-05
BETA_ONE = 0.9
BETA_TWO = 0.95
ADAM_EPS = 1e-08
LEARN_RATE = 0.01
DECAY_RATE = 0.1
ROPE_BASE = 10000.0
MASK_FILL = -1e30


def rms_norm(inputs, gain_row):
    return (
        inputs * lax.rsqrt(jnp.mean(inputs * inputs, axis=-1, keepdims=True) + EPS_NORM) * gain_row
    )


def norm_back(inputs, gain_row, upstream):
    _, pullback = jax.vjp(rms_norm, inputs, gain_row)
    return pullback(upstream)


def rotary(inputs):
    row_count = inputs.shape[0]
    split_heads = inputs.reshape(row_count, HEADS, HDIM)
    half_dim = HDIM // 2
    position = jnp.arange(row_count, dtype=jnp.float32)[:, None, None]
    frequency = ROPE_BASE ** (-jnp.arange(half_dim, dtype=jnp.float32) * 2.0 / HDIM)
    angles = position * frequency[None, None, :]
    cosines = jnp.cos(angles)
    sine_values = jnp.sin(angles)
    lower_half = split_heads[..., :half_dim]
    upper_half = split_heads[..., half_dim:]
    turned = jnp.concatenate(
        [
            lower_half * cosines - upper_half * sine_values,
            upper_half * cosines + lower_half * sine_values,
        ],
        axis=-1,
    )
    return turned.reshape(row_count, HEADS * HDIM)


def rotary_back(upstream):
    _, pullback = jax.vjp(rotary, upstream)
    return pullback(upstream)[0]


def rounded(values):
    return lax.optimization_barrier(values.astype(jnp.bfloat16)).astype(jnp.float32)


AXES = ("z", "x", "h", "y", "c")
PLANES = 4


def head_terms(values):
    high = lax.reduce_precision(values, 8, 7)
    rest = (values - high).astype(jnp.bfloat16)
    return high.astype(jnp.bfloat16), rest


def split_dot(left, right):
    high, rest = head_terms(left)
    return jnp.dot(high, right, preferred_element_type=jnp.float32) + jnp.dot(
        rest, right, preferred_element_type=jnp.float32
    )


def visible_mask(seq_len, prefix_len):
    query_place = jnp.arange(seq_len, dtype=jnp.int32)[:, None]
    key_place = jnp.arange(seq_len, dtype=jnp.int32)[None, :]
    return (key_place <= query_place) | (key_place < prefix_len)


def attend(queries, key_rows, value_rows, visible):
    seq_len = queries.shape[0]
    query_heads = queries.reshape(seq_len, HEADS, HDIM)
    key_heads = key_rows.reshape(seq_len, HEADS, HDIM)
    value_heads = value_rows.reshape(seq_len, HEADS, HDIM)
    scores = jnp.einsum(
        "bhd,khd->hbk", query_heads, key_heads, preferred_element_type=jnp.float32
    ) * HDIM ** (-0.5)
    scores = jnp.where(visible[None], scores, MASK_FILL)
    peak_score = jnp.max(scores, axis=-1, keepdims=True)
    weights = jnp.exp(scores - peak_score)
    summed = jnp.sum(weights, axis=-1, keepdims=True)
    probs_low = (weights / summed).astype(jnp.bfloat16)
    attended = jnp.einsum(
        "hbk,khd->bhd", probs_low, value_heads, preferred_element_type=jnp.float32
    )
    return attended.reshape(seq_len, HEADS * HDIM), peak_score + jnp.log(summed)


def attend_back(queries, key_rows, value_rows, grad_low, log_total, visible):
    seq_len = queries.shape[0]
    query_heads = queries.reshape(seq_len, HEADS, HDIM)
    key_heads = key_rows.reshape(seq_len, HEADS, HDIM)
    value_heads = value_rows.reshape(seq_len, HEADS, HDIM)
    grad_heads = grad_low.reshape(seq_len, HEADS, HDIM)
    factor = HDIM ** (-0.5)
    scores = (
        jnp.einsum("bhd,khd->hbk", query_heads, key_heads, preferred_element_type=jnp.float32)
        * factor
    )
    scores = jnp.where(visible[None], scores, MASK_FILL)
    probs = jnp.exp(scores - log_total)
    grad_probs = jnp.einsum(
        "bhd,khd->hbk", grad_heads, value_heads, preferred_element_type=jnp.float32
    )
    row_dot = jnp.sum(probs * grad_probs, axis=-1, keepdims=True)
    grad_scores = (probs * (grad_probs - row_dot)).astype(jnp.bfloat16)
    query_grad = (
        jnp.einsum("hbk,khd->bhd", grad_scores, key_heads, preferred_element_type=jnp.float32)
        * factor
    )
    key_grad = (
        jnp.einsum("hbk,bhd->khd", grad_scores, query_heads, preferred_element_type=jnp.float32)
        * factor
    )
    value_grad = jnp.einsum(
        "hbk,bhd->khd", probs.astype(jnp.bfloat16), grad_heads, preferred_element_type=jnp.float32
    )
    full = (seq_len, HEADS * HDIM)
    return query_grad.reshape(full), key_grad.reshape(full), value_grad.reshape(full)


def swap_pairs(planes, rows, turn_plane, turn_row):
    pairs = []
    for plane in range(planes):
        for row in range(rows):
            for part in range(planes):
                source = (plane * rows + row) * planes + part
                target = (
                    ((part + turn_plane) % planes) * rows + (row + turn_row) % rows
                ) * planes + plane
                pairs.append((source, target))
    return pairs


def take_piece(pieces, place):
    return lax.dynamic_index_in_dim(pieces, place, 0, False)


def spread_experts(piece, row_groups):
    me_plane = lax.axis_index("z")
    me_row = lax.axis_index("h")
    arrived = []
    for turn_row in range(row_groups):
        for turn_plane in range(PLANES):
            arrived.append(
                lax.ppermute(
                    piece,
                    ("z", "h", "y", "c"),
                    swap_pairs(PLANES, row_groups, turn_plane, turn_row),
                )
            )
    stacked = jnp.stack(arrived)
    places = jnp.arange(row_groups * PLANES)
    row, part = places // PLANES, places % PLANES
    order = ((me_row - row) % row_groups) * PLANES + (me_plane - part) % PLANES
    return jnp.take(stacked, order, axis=0)


def gather_expert_grads(pieces, row_groups):
    me_plane = lax.axis_index("z")
    me_row = lax.axis_index("h")
    total = None
    for turn_row in range(row_groups):
        for turn_plane in range(PLANES):
            place = ((me_row - turn_row) % row_groups) * PLANES + (me_plane - turn_plane) % PLANES
            back = [
                (target, source)
                for source, target in swap_pairs(PLANES, row_groups, turn_plane, turn_row)
            ]
            term = lax.ppermute(take_piece(pieces, place), ("z", "h", "y", "c"), back)
            term = term.astype(jnp.float32)
            total = term if total is None else total + term
    return total


def scatter_axis(values, axis_name, dim):
    count = lax.axis_size(axis_name)
    if count == 1:
        return jnp.squeeze(values, dim)
    me = lax.axis_index(axis_name)
    total = lax.dynamic_index_in_dim(values, me, dim, False).astype(jnp.float32)
    for turn in range(1, count):
        sent = lax.dynamic_index_in_dim(values, (me + turn) % count, dim, False)
        got = lax.ppermute(sent, axis_name, [(i, (i + turn) % count) for i in range(count)])
        total = total + got.astype(jnp.float32)
    return total.astype(jnp.bfloat16)


def scatter_all(values):
    sizes = [lax.axis_size(name) for name in AXES]
    rows, columns = values.shape
    count = 1
    for size in sizes:
        count *= size
    blocks = values.reshape(*sizes, rows // count, columns)
    blocks = scatter_axis(blocks, "c", 4)
    half = columns // 2
    first, second = blocks[..., :half], blocks[..., half:]
    first = scatter_axis(first, "x", 1)
    second = scatter_axis(second, "y", 3)
    first = scatter_axis(first, "y", 2)
    second = scatter_axis(second, "x", 1)
    joined = jnp.concatenate([first, second], axis=-1)
    joined = scatter_axis(joined, "h", 1)
    me = lax.axis_index("z")
    total = take_piece(joined, me).astype(jnp.float32)
    for turn in range(1, sizes[0]):
        sent = take_piece(joined, (me + turn) % sizes[0])
        got = lax.ppermute(sent, "z", [(i, (i + turn) % sizes[0]) for i in range(sizes[0])])
        total = total + got.astype(jnp.float32)
    return total


def send_all(values):
    return lax.all_to_all(values, AXES, split_axis=0, concat_axis=0, tiled=True)


def send_plane(values):
    return lax.all_to_all(values, ("x", "y", "c"), split_axis=0, concat_axis=0, tiled=True)


def three_terms(values):
    first = lax.reduce_precision(values, 8, 7)
    second = lax.reduce_precision(values - first, 8, 7)
    third = lax.reduce_precision(values - first - second, 8, 7)
    return [first, second, third]

def adam_step(weight, mean_old, square_old, gradient):
    mean_new = BETA_ONE * mean_old + (1.0 - BETA_ONE) * gradient
    square_new = BETA_TWO * square_old + (1.0 - BETA_TWO) * gradient * gradient
    bias_one = 1.0 - BETA_ONE**ADAM_STEP
    bias_two = 1.0 - BETA_TWO**ADAM_STEP
    update = -LEARN_RATE * (
        mean_new / bias_one / (jnp.sqrt(square_new / bias_two) + ADAM_EPS) + DECAY_RATE * weight
    )
    return (mean_new, square_new, update)


def shards(
    tokens,
    prefix,
    routes,
    picked,
    loss_ids,
    teacher_logits,
    embedding,
    embedding_mean,
    embedding_square,
    attention,
    attention_mean,
    attention_square,
    router,
    router_mean,
    router_square,
    norm_gains,
    gains_mean,
    gains_square,
    expert_up,
    upward_mean,
    upward_square,
    expert_down,
    downward_mean,
    downward_square,
    output_table,
    table_mean,
    table_square,
):
    devices_all = lax.axis_size(AXES)
    me_all = lax.axis_index(AXES)
    row_groups = lax.axis_size("h")
    columns_x = lax.axis_size("x")
    seq_len = routes.shape[0]
    layer_count = attention.shape[0]
    experts_all = router.shape[2]
    capacity = 9 * seq_len * TOPK // (8 * experts_all)
    column_count = embedding.shape[1]
    prefix_len = prefix[0]
    slot_total = experts_all * capacity
    piece_rows = expert_up.shape[2]
    gain_count = norm_gains.shape[0]
    group_experts = [
        (group % PLANES) * columns_x + group // PLANES for group in range(experts_all)
    ]
    group_order = jnp.array(group_experts, jnp.int32)
    group_back = jnp.array(
        [group_experts.index(expert) for expert in range(experts_all)], jnp.int32
    )

    attention_low = lax.all_gather(attention.astype(jnp.bfloat16), AXES, axis=1, tiled=True)

    table_low = embedding.astype(jnp.bfloat16)
    looked_up = jnp.take(table_low, tokens, axis=0).reshape(devices_all, seq_len * column_count)
    small_count = gain_count + layer_count * experts_all
    small = jnp.concatenate(
        [norm_gains.T, router.transpose(1, 0, 2).reshape(column_count, layer_count * experts_all)],
        axis=1,
    ).astype(jnp.bfloat16)
    small = jnp.broadcast_to(
        small.reshape(1, column_count * small_count), (devices_all, column_count * small_count)
    )
    arrived_rows = send_all(jnp.concatenate([looked_up, small], axis=1))
    hidden = (
        arrived_rows[:, : seq_len * column_count]
        .reshape(devices_all, seq_len, column_count)
        .transpose(1, 0, 2)
        .reshape(seq_len, D)
        .astype(jnp.float32)
    )
    small_all = arrived_rows[:, seq_len * column_count :].reshape(D, small_count)
    gain_rows = small_all[:, :gain_count].T.astype(jnp.float32)
    router_low = (
        small_all[:, gain_count:]
        .reshape(D, layer_count, experts_all)
        .transpose(1, 0, 2)[:, :, group_order]
    )

    upward_low, downward_low = [], []
    for layer_index in range(layer_count):
        down_piece = (
            expert_down[0, layer_index]
            .reshape(F // piece_rows, piece_rows, piece_rows)
            .transpose(1, 0, 2)
            .reshape(piece_rows, F)
        )
        piece = jnp.concatenate([expert_up[0, layer_index], down_piece], axis=1).astype(
            jnp.bfloat16
        )
        pieces = spread_experts(piece, row_groups)
        upward_low.append(pieces[:, :, : 2 * F].reshape(D, 2 * F))
        downward_low.append(
            pieces[:, :, 2 * F :]
            .reshape(D // piece_rows, piece_rows, F // piece_rows, piece_rows)
            .transpose(2, 1, 0, 3)
            .reshape(F, D)
        )

    member = jnp.any(routes[:, :, None] == group_order[None, None, :], axis=1)
    before = jnp.dot(
        jnp.tril(jnp.ones((seq_len, seq_len), jnp.bfloat16), -1),
        member.astype(jnp.bfloat16),
        preferred_element_type=jnp.float32,
    ).astype(jnp.int32)
    spread = (
        (before.T[:, None, :] == jnp.arange(capacity, dtype=jnp.int32)[None, :, None])
        & member.T[:, None, :]
    ).astype(jnp.bfloat16)
    spread_flat = spread.reshape(slot_total, seq_len)
    spread_back = spread_flat.T
    kept = (member & (before < capacity)).astype(jnp.float32)

    head_low = output_table.astype(jnp.bfloat16)
    vocab_local = head_low.shape[0]
    teacher_log = jax.nn.log_softmax(teacher_logits, axis=1)
    teacher_prob = jnp.exp(teacher_log)
    position_count = loss_ids.shape[0]
    teacher_mass = jnp.sum(teacher_prob, axis=1)
    coefficients = jnp.concatenate(
        [jnp.ones((position_count, 1), jnp.float32), teacher_prob], axis=1
    )
    local_ids = loss_ids - me_all * vocab_local
    vocab_place = jnp.arange(vocab_local, dtype=jnp.int32)
    marked = jnp.sum(
        jnp.where(
            local_ids[:, :, None] == vocab_place[None, None, :], coefficients[:, :, None], 0.0
        ),
        axis=1,
    )
    marked_pull = jnp.dot(
        marked.astype(jnp.bfloat16), head_low, preferred_element_type=jnp.float32
    )
    own_count = position_count // devices_all
    marked_arrived = send_all(
        marked_pull.astype(jnp.bfloat16).reshape(devices_all, own_count, D)
    )
    marked_total = jnp.sum(marked_arrived.astype(jnp.float32), axis=0)

    visible = visible_mask(seq_len, prefix_len)
    stored = []
    for layer_index in range(layer_count):
        weights_now = attention_low[layer_index]
        normed_low = rms_norm(hidden, gain_rows[4 * layer_index]).astype(jnp.bfloat16)
        projected = jnp.dot(normed_low, weights_now[:, : 3 * D], preferred_element_type=jnp.float32)
        queries = rotary(rms_norm(projected[:, :D], gain_rows[4 * layer_index + 1])).astype(
            jnp.bfloat16
        )
        key_rows = rotary(rms_norm(projected[:, D : 2 * D], gain_rows[4 * layer_index + 2])).astype(
            jnp.bfloat16
        )
        value_rows = projected[:, 2 * D :].astype(jnp.bfloat16)
        attended, log_total = attend(queries, key_rows, value_rows, visible)
        attended_low = attended.astype(jnp.bfloat16)
        middle = hidden + jnp.dot(
            attended_low, weights_now[:, 3 * D :], preferred_element_type=jnp.float32
        )
        ffn_low = rms_norm(middle, gain_rows[4 * layer_index + 3]).astype(jnp.bfloat16)
        outgoing = jnp.dot(spread_flat, ffn_low, preferred_element_type=jnp.float32).astype(
            jnp.bfloat16
        )
        received = send_plane(outgoing.reshape(experts_all, capacity, D)).reshape(slot_total, D)
        router_logits = jnp.dot(
            ffn_low, router_low[layer_index], preferred_element_type=jnp.float32
        )
        router_probs = jax.nn.softmax(router_logits, axis=-1)
        gates = router_probs * kept
        gate_up = jnp.dot(received, upward_low[layer_index], preferred_element_type=jnp.float32)
        activated_low = (jax.nn.silu(gate_up[:, :F]) * gate_up[:, F:]).astype(jnp.bfloat16)
        produced = jnp.dot(
            activated_low, downward_low[layer_index], preferred_element_type=jnp.float32
        ).astype(jnp.bfloat16)
        returned = send_plane(produced.reshape(experts_all, capacity, D)).reshape(slot_total, D)
        gate_spread = (
            spread_back.reshape(seq_len, experts_all, capacity).astype(jnp.float32)
            * gates[:, :, None]
        ).reshape(seq_len, slot_total)
        stored.append(
            (
                hidden,
                normed_low,
                projected,
                queries,
                key_rows,
                value_rows,
                log_total,
                attended_low,
                middle,
                ffn_low,
                router_probs,
                gates,
                received,
                gate_up,
                activated_low,
                returned,
            )
        )
        hidden = middle + split_dot(gate_spread, returned)

    final_gain = gain_rows[4 * layer_count]
    final_rows = jnp.take(hidden, picked, axis=0)
    final_low = rms_norm(final_rows, final_gain).astype(jnp.bfloat16)
    all_rows = send_all(jnp.broadcast_to(final_low[None], (devices_all, own_count, D))).reshape(
        position_count, D
    )
    logits = jnp.einsum("pd,vd->pv", all_rows, head_low, preferred_element_type=jnp.float32)
    local_peak = jnp.max(logits, axis=1)
    local_exp = jnp.exp(logits - local_peak[:, None])
    local_sum = jnp.sum(local_exp, axis=1)
    local_dot = jnp.sum(marked * logits, axis=1)
    pull = jnp.dot(local_exp.astype(jnp.bfloat16), head_low, preferred_element_type=jnp.float32)
    stats = jnp.stack(
        three_terms(local_peak) + three_terms(local_sum) + three_terms(local_dot), axis=1
    )
    stats = jnp.pad(stats, ((0, 0), (0, 128 - stats.shape[1])))
    pull_sent = jnp.concatenate([pull, stats], axis=1).astype(jnp.bfloat16)
    pull_got = send_all(pull_sent.reshape(devices_all, own_count, D + 128)).astype(jnp.float32)
    stats_got = pull_got[:, :, D:]
    peaks = jnp.sum(stats_got[:, :, 0:3], axis=2)
    sums = jnp.sum(stats_got[:, :, 3:6], axis=2)
    dots = jnp.sum(stats_got[:, :, 6:9], axis=2)
    peak_own = jnp.max(peaks, axis=0)
    log_norm_own = peak_own + jnp.log(jnp.sum(sums * jnp.exp(peaks - peak_own), axis=0))
    mass_own = lax.dynamic_slice_in_dim(teacher_mass, me_all * own_count, own_count)
    entropy_own = lax.dynamic_slice_in_dim(
        jnp.sum(teacher_prob * teacher_log, axis=1), me_all * own_count, own_count
    )
    loss_own = (1.0 + mass_own) * log_norm_own - jnp.sum(dots, axis=0) + entropy_own
    scale_own = (1.0 + mass_own)[None, :] * jnp.exp(peaks - log_norm_own[None, :])
    final_grad = (
        jnp.sum(scale_own[:, :, None] * pull_got[:, :, :D], axis=0) - marked_total
    ) / position_count
    spread_stats = jnp.concatenate([log_norm_own, loss_own]).reshape(1, 2 * own_count)
    stats_all = send_all(jnp.broadcast_to(spread_stats, (devices_all, 2 * own_count)))
    log_norm = stats_all[:, :own_count].reshape(position_count)
    loss_value = jnp.sum(stats_all[:, own_count:]) / position_count
    grad_logits = (
        jnp.exp(logits - log_norm[:, None]) * (1.0 + teacher_mass)[:, None] - marked
    ) / position_count
    table_grad = jnp.einsum(
        "pv,pd->vd",
        grad_logits.astype(jnp.bfloat16),
        all_rows,
        preferred_element_type=jnp.float32,
    )
    rows_grad, final_gain_grad = norm_back(final_rows, final_gain, final_grad)
    place = jnp.arange(seq_len, dtype=jnp.int32)
    grad_hidden = jnp.sum(
        jnp.where(picked[:, None, None] == place[None, :, None], rows_grad[:, None, :], 0.0), axis=0
    )

    gain_parts = [None] * (4 * layer_count + 1)
    gain_parts[4 * layer_count] = final_gain_grad
    attention_parts = [None] * layer_count
    router_parts = [None] * layer_count
    up_parts = [None] * layer_count
    down_parts = [None] * layer_count
    for layer_index in reversed(range(layer_count)):
        (
            hidden_in,
            normed_low,
            projected,
            queries,
            key_rows,
            value_rows,
            log_total,
            attended_low,
            middle,
            ffn_low,
            router_probs,
            gates,
            received,
            gate_up,
            activated_low,
            returned,
        ) = stored[layer_index]
        weights_now = attention_low[layer_index]
        gate_slots = jnp.sum(spread.astype(jnp.float32) * gates.T[:, None, :], axis=2).reshape(
            slot_total, 1
        )
        grad_high, grad_rest = head_terms(grad_hidden)
        grad_slots = jnp.dot(
            spread_flat, grad_high, preferred_element_type=jnp.float32
        ) + jnp.dot(spread_flat, grad_rest, preferred_element_type=jnp.float32)
        sent_back = (gate_slots * grad_slots).astype(jnp.bfloat16)
        output_grad = send_plane(sent_back.reshape(experts_all, capacity, D)).reshape(
            slot_total, D
        )
        gate_dots = (
            jnp.einsum("ld,rd->lr", grad_high, returned, preferred_element_type=jnp.float32)
            + jnp.einsum("ld,rd->lr", grad_rest, returned, preferred_element_type=jnp.float32)
        ) * spread_back.astype(jnp.float32)
        prob_grad = jnp.sum(gate_dots.reshape(seq_len, experts_all, capacity), axis=2)
        logit_grad = router_probs * (
            prob_grad - jnp.sum(router_probs * prob_grad, axis=-1, keepdims=True)
        )
        logit_low = logit_grad.astype(jnp.bfloat16)
        router_parts[layer_index] = jnp.einsum(
            "ld,le->de", ffn_low, logit_low, preferred_element_type=jnp.float32
        )
        activated_grad = rounded(
            jnp.einsum(
                "rd,fd->rf",
                output_grad,
                downward_low[layer_index],
                preferred_element_type=jnp.float32,
            )
        )
        gate_part = gate_up[:, :F]
        up_part = gate_up[:, F:]
        sigmoid_gate = jax.nn.sigmoid(gate_part)
        gate_side = (
            activated_grad * up_part * sigmoid_gate * (1.0 + gate_part * (1.0 - sigmoid_gate))
        )
        up_side = activated_grad * gate_part * sigmoid_gate
        gate_up_grad = jnp.concatenate([gate_side, up_side], axis=-1).astype(jnp.bfloat16)
        input_grad = jnp.einsum(
            "rf,df->rd",
            gate_up_grad,
            upward_low[layer_index],
            preferred_element_type=jnp.float32,
        ).astype(jnp.bfloat16)
        back_inputs = send_plane(input_grad.reshape(experts_all, capacity, D)).reshape(
            slot_total, D
        )
        up_grad = jnp.einsum(
            "rd,rf->df", received, gate_up_grad, preferred_element_type=jnp.float32
        )
        down_grad = jnp.einsum(
            "rf,rd->fd", activated_low, output_grad, preferred_element_type=jnp.float32
        )
        grad_pieces = jnp.concatenate(
            [
                up_grad.reshape(D // piece_rows, piece_rows, 2 * F),
                down_grad.reshape(F // piece_rows, piece_rows, D // piece_rows, piece_rows)
                .transpose(2, 1, 0, 3)
                .reshape(D // piece_rows, piece_rows, F),
            ],
            axis=2,
        ).astype(jnp.bfloat16)
        piece_grad = gather_expert_grads(grad_pieces, row_groups)
        up_parts[layer_index] = piece_grad[:, : 2 * F]
        down_parts[layer_index] = (
            piece_grad[:, 2 * F :]
            .reshape(piece_rows, F // piece_rows, piece_rows)
            .transpose(1, 0, 2)
            .reshape(F, piece_rows)
        )
        ffn_grad = jnp.dot(
            spread_back, back_inputs, preferred_element_type=jnp.float32
        ) + jnp.einsum(
            "le,de->ld", logit_low, router_low[layer_index], preferred_element_type=jnp.float32
        )
        middle_grad, ffn_gain_grad = norm_back(middle, gain_rows[4 * layer_index + 3], ffn_grad)
        gain_parts[4 * layer_index + 3] = ffn_gain_grad
        grad_middle = grad_hidden + middle_grad
        branch_low = grad_middle.astype(jnp.bfloat16)
        out_weight_grad = jnp.einsum(
            "ld,le->de", attended_low, branch_low, preferred_element_type=jnp.float32
        )
        attended_grad = jnp.einsum(
            "le,de->ld", branch_low, weights_now[:, 3 * D :], preferred_element_type=jnp.float32
        ).astype(jnp.bfloat16)
        query_grad, key_grad, value_grad = attend_back(
            queries, key_rows, value_rows, attended_grad, log_total, visible
        )
        query_pre = rotary_back(rounded(query_grad))
        key_pre = rotary_back(rounded(key_grad))
        query_in, query_gain_grad = norm_back(
            projected[:, :D], gain_rows[4 * layer_index + 1], query_pre
        )
        key_in, key_gain_grad = norm_back(
            projected[:, D : 2 * D], gain_rows[4 * layer_index + 2], key_pre
        )
        gain_parts[4 * layer_index + 1] = query_gain_grad
        gain_parts[4 * layer_index + 2] = key_gain_grad
        projected_grad = jnp.concatenate([query_in, key_in, value_grad], axis=1).astype(
            jnp.bfloat16
        )
        qkv_weight_grad = jnp.einsum(
            "ld,le->de", normed_low, projected_grad, preferred_element_type=jnp.float32
        )
        normed_grad = jnp.einsum(
            "le,de->ld", projected_grad, weights_now[:, : 3 * D], preferred_element_type=jnp.float32
        )
        hidden_grad, attn_gain_grad = norm_back(hidden_in, gain_rows[4 * layer_index], normed_grad)
        gain_parts[4 * layer_index] = attn_gain_grad
        attention_parts[layer_index] = scatter_all(
            jnp.concatenate([qkv_weight_grad, out_weight_grad], axis=1).astype(jnp.bfloat16)
        )
        grad_hidden = grad_middle + hidden_grad

    sending = (
        grad_hidden.astype(jnp.bfloat16)
        .reshape(seq_len, devices_all, column_count)
        .transpose(1, 0, 2)
        .reshape(devices_all, seq_len * column_count)
    )
    small_grads = jnp.concatenate(
        [jnp.stack(gain_parts, axis=1)] + [part[:, group_back] for part in router_parts], axis=1
    ).astype(jnp.bfloat16)
    arrived_grads = send_all(
        jnp.concatenate(
            [sending, small_grads.reshape(devices_all, column_count * small_count)], axis=1
        )
    )
    embedding_grad = jax.ops.segment_sum(
        arrived_grads[:, : seq_len * column_count]
        .astype(jnp.float32)
        .reshape(devices_all * seq_len, column_count),
        tokens,
        num_segments=embedding.shape[0],
    )
    small_total = jnp.sum(
        arrived_grads[:, seq_len * column_count :].astype(jnp.float32), axis=0
    ).reshape(column_count, small_count)
    gains_grad = small_total[:, :gain_count].T
    router_grad = (
        small_total[:, gain_count:]
        .reshape(column_count, layer_count, experts_all)
        .transpose(1, 0, 2)
    )
    attention_grad = jnp.stack(attention_parts)
    upward_grad = jnp.stack(up_parts)[None]
    downward_grad = jnp.stack(down_parts)[None]
    embedding_mean_next, embedding_square_next, embedding_update = adam_step(
        embedding, embedding_mean, embedding_square, embedding_grad
    )
    attention_mean_next, attention_square_next, attention_update = adam_step(
        attention, attention_mean, attention_square, attention_grad
    )
    router_mean_next, router_square_next, router_update = adam_step(
        router, router_mean, router_square, router_grad
    )
    gains_mean_next, gains_square_next, gains_update = adam_step(
        norm_gains, gains_mean, gains_square, gains_grad
    )
    upward_mean_next, upward_square_next, upward_update = adam_step(
        expert_up, upward_mean, upward_square, upward_grad
    )
    downward_mean_next, downward_square_next, downward_update = adam_step(
        expert_down, downward_mean, downward_square, downward_grad
    )
    table_mean_next, table_square_next, table_update = adam_step(
        output_table, table_mean, table_square, table_grad
    )
    return (
        loss_value,
        embedding_mean_next,
        embedding_square_next,
        embedding_update,
        attention_mean_next,
        attention_square_next,
        attention_update,
        router_mean_next,
        router_square_next,
        router_update,
        gains_mean_next,
        gains_square_next,
        gains_update,
        upward_mean_next,
        upward_square_next,
        upward_update,
        downward_mean_next,
        downward_square_next,
        downward_update,
        table_mean_next,
        table_square_next,
        table_update,
    )


def solution(mesh):
    expert_count, shard_count = mesh.devices.shape
    mesh = Mesh(
        mesh.devices.reshape(PLANES, expert_count // PLANES, shard_count // 4, 2, 2), AXES
    )
    return jax.shard_map(
        shards,
        mesh=mesh,
        in_specs=(
            P(),
            P(AXES),
            P(AXES, None),
            P(AXES),
            P(),
            P(),
            P(None, AXES),
            P(None, AXES),
            P(None, AXES),
            P(None, AXES, None),
            P(None, AXES, None),
            P(None, AXES, None),
            P(None, AXES, None),
            P(None, AXES, None),
            P(None, AXES, None),
            P(None, AXES),
            P(None, AXES),
            P(None, AXES),
            P(("z", "x"), None, ("h", "y", "c"), None),
            P(("z", "x"), None, ("h", "y", "c"), None),
            P(("z", "x"), None, ("h", "y", "c"), None),
            P(("z", "x"), None, None, ("h", "y", "c")),
            P(("z", "x"), None, None, ("h", "y", "c")),
            P(("z", "x"), None, None, ("h", "y", "c")),
            P(AXES, None),
            P(AXES, None),
            P(AXES, None),
        ),
        out_specs=(
            P(),
            P(None, AXES),
            P(None, AXES),
            P(None, AXES),
            P(None, AXES, None),
            P(None, AXES, None),
            P(None, AXES, None),
            P(None, AXES, None),
            P(None, AXES, None),
            P(None, AXES, None),
            P(None, AXES),
            P(None, AXES),
            P(None, AXES),
            P(("z", "x"), None, ("h", "y", "c"), None),
            P(("z", "x"), None, ("h", "y", "c"), None),
            P(("z", "x"), None, ("h", "y", "c"), None),
            P(("z", "x"), None, None, ("h", "y", "c")),
            P(("z", "x"), None, None, ("h", "y", "c")),
            P(("z", "x"), None, None, ("h", "y", "c")),
            P(AXES, None),
            P(AXES, None),
            P(AXES, None),
        ),
        check_vma=False,
    )
```

time: 2350 us -> 1360 us (0.58)
  blocking collectives: 419 us -> 0 us
  waiting for transfers between devices: 782 us -> 469 us
  other arithmetic: 471 us -> 237 us
  local copies, waits for them, and re-layouts: 471 us -> 248 us
  starting transfers between devices: 46.4 us -> 205 us
  matrix products: 123 us -> 171 us
    reduce_scatter x4 -> x0, waiting for transfers between devices: 438 us -> none  [the longest x1 324 us: shards(): lax.psum_scatter(attention_sum, ('expert', 'shard'), scatter_dimension=1,...]
    ppermute x0 -> x32, waiting for transfers between devices: none -> 316 us  [the longest x8 185 us: gather_expert_grads(): term = lax.ppermute(take_piece(pieces, place), ('z', 'h', 'y', 'c'), back)]
    all_gather x5 -> x0, blocking collectives: 230 us -> none  [the longest x1 78.3 us: shards(): lax.all_gather(router.astype(jnp.bfloat16), ('expert', 'shard'), axis=1,...]
    all_to_all x3 -> x0, blocking collectives: 189 us -> none  [the longest x2 131 us: shards(): lax.all_to_all(back_buffer, 'expert', split_axis=0, concat_axis=1, tiled=...]
    unnamed x13 -> x0, other arithmetic: 170 us -> none
    unnamed x12 -> x1, waiting for transfers between devices: 164 us -> 0.02 us
    gather x13 -> x5, local copies, waits for them, and re-layouts: 171 us -> 10.7 us  [the longest x2 8.6 us: spread_experts(): return jnp.take(stacked, order, axis=0)]
    all_to_all x7 -> x14, starting transfers between devices: 45.9 us -> 144 us  [the longest x8 77.4 us: send_plane(): lax.all_to_all(values, ('x', 'y', 'c'), split_axis=0, concat_axis=0, tile...]
  transfers between devices with their start and end apart: 17 -> 47, of which waited for: 9 -> 22; matrix products, arithmetic and copies ran while one was open for 17% -> 33% of each run, Pallas kernels for 0% -> 0%
where the time goes in v1:
time: 1360 us; the launch traced here: 1350 us
  waiting for transfers between devices  469 us (34%)
  local copies, waits for them, and re-layouts  248 us (18%)
  other arithmetic  237 us (17%)
  starting transfers between devices  205 us (15%)
  matrix products  171 us (13%)
  between operations  20.1 us (1%)
    ppermute x8, waiting for transfers between devices, gather_expert_grads(): term = lax.ppermute(take_piece(pieces, place), ('z', 'h', 'y', 'c'), back)  185 us
    all_to_all x8, starting transfers between devices, send_plane(): lax.all_to_all(values, ('x', 'y', 'c'), split_axis=0, concat_axis=0, tile...  77.4 us
    all_to_all x8, waiting for transfers between devices, send_plane(): lax.all_to_all(values, ('x', 'y', 'c'), split_axis=0, concat_axis=0, tile...  70.6 us
    all_to_all x6, starting transfers between devices, send_all(): return lax.all_to_all(values, AXES, split_axis=0, concat_axis=0, tiled=True)  66.3 us
    all_gather x1, waiting for transfers between devices, shards(): lax.all_gather(attention.astype(jnp.bfloat16), AXES, axis=1, tiled=True)  60.2 us
    scatter-add x1, other arithmetic, shards(): jax.ops.segment_sum(arrived_grads[:, :seq_len * column_count].astype(jnp....  54.7 us
    ppermute x8, waiting for transfers between devices, spread_experts(): lax.ppermute(piece, ('z', 'h', 'y', 'c'), swap_pairs(PLANES, row_groups,...  49.6 us
    ppermute x10, waiting for transfers between devices, scatter_axis(): lax.ppermute(sent, axis_name, [(i, (i + turn) % count) for i in range(cou...  46.6 us
  transfers between devices with their start and end apart: 47, of which 22 were waited for; matrix products, arithmetic and copies ran while one was open for 33% of the time, Pallas kernels for 0%

profile of v1, /device:TPU:9, one launch (start us, length us, event | category | flops | bytes accessed | tf_op | source)
XLA Modules:
  0.0 1349.5 jit_solution(11173723011915578766)
XLA Ops:
  18.9 8.6 copy.525
  27.5 28.3 %gather_fusion = bf16[8192,32]{1,0:T(8,128)(2,1)S(1)} fusion(bf16[50304,32]{1,0:T(8,128)(2,1)} %copy.525, s32[8192]{0:T(1024)S(1)} %fusion.212), kind=kCustom, calls=%fused_computation.2 | custom fusion | bytes 1081344 | tf_op jit(solution)/shard_map/jit(_take)/gather | solution.py:310
  61.3 6.4 all-to-all-start
  73.6 7.8 collective-permute-start
  86.0 15.2 %all-to-all-done = bf16[32,2,4496]{2,1,0:T(2,128)(2,1)} async-done(((bf16[32,2,4496]{2,1,0:T(2,128)(2,1)}), bf16[32,2,4496]{2,1,0:T(2,128)(2,1)}, u32[]{:S(2)}, u32[]{:S(2)}) %all-to-all-start) | async-done | bytes 575520 | tf_op jit(solution)/shard_map/all_to_all | solution.py:233
  118.4 60.2 %all-gather.2.cloned.1.call-done = bf16[2,1024,4096]{2,1,0:T(8,128)(2,1)} async-done(((bf16[2,32,4096]{2,1,0:T(8,128)(2,1)}), bf16[2,1024,4096]{2,1,0:T(8,128)(2,1)}) %all-gather.2.cloned.1.call-update) | async-done | bytes 16777232 | tf_op jit(solution)/shard_map/all_gather | solution.py:307
  178.6 10.1 slice_bitcast_fusion
  216.4 6.4 collective-permute-start.7
  226.0 7.5 collective-permute-start.4
  241.2 35.8 %collective-permute-done.7 = bf16[256,1536]{1,0:T(8,128)(2,1)S(1)} collective-permute-done((bf16[256,1536]{1,0:T(8,128)(2,1)}, bf16[256,1536]{1,0:T(8,128)(2,1)S(1)}, u32[]{:S(2)}, u32[]{:S(2)}) %collective-permute-start.7) | collective-permute-done | bytes 786464 | tf_op jit(solution)/shard_map/ppermute | solution.py:164
  277.0 13.8 %collective-permute-done.5 = bf16[256,1536]{1,0:T(8,128)(2,1)} collective-permute-done((bf16[256,1536]{1,0:T(8,128)(2,1)}, bf16[256,1536]{1,0:T(8,128)(2,1)}, u32[]{:S(2)}, u32[]{:S(2)}) %collective-permute-start.5) | collective-permute-done | bytes 786464 | tf_op jit(solution)/shard_map/ppermute | solution.py:164
  321.8 11.1 all-to-all-start.2
  336.7 23.8 %all-to-all-done.2 = bf16[8,144,1024]{2,1,0:T(8,128)(2,1)S(1)} async-done(((bf16[8,144,1024]{2,1,0:T(8,128)(2,1)}), bf16[8,144,1024]{2,1,0:T(8,128)(2,1)S(1)}, u32[]{:S(2)}, u32[]{:S(2)}) %all-to-all-start.2) | async-done | bytes 2359328 | tf_op jit(solution)/shard_map/all_to_all | solution.py:237
  408.5 17.0 %all-to-all-done.3 = bf16[8,144,1024]{2,1,0:T(8,128)(2,1)} async-done(((bf16[8,144,1024]{2,1,0:T(8,128)(2,1)}), bf16[8,144,1024]{2,1,0:T(8,128)(2,1)}, u32[]{:S(2)}, u32[]{:S(2)}) %all-to-all-start.3) | async-done | bytes 2359328 | tf_op jit(solution)/shard_map/all_to_all | solution.py:237
  452.3 16.5 %all-to-all-done.4 = bf16[8,144,1024]{2,1,0:T(8,128)(2,1)} async-done(((bf16[8,144,1024]{2,1,0:T(8,128)(2,1)}), bf16[8,144,1024]{2,1,0:T(8,128)(2,1)}, u32[]{:S(2)}, u32[]{:S(2)}) %all-to-all-start.4) | async-done | bytes 2359328 | tf_op jit(solution)/shard_map/all_to_all | solution.py:237
  486.4 15.8 %select_reduce_fusion = f32[256,1572]{0,1:T(8,128)} fusion(f32[256,65]{0,1:T(8,128)} %concatenate.162, s32[256,65]{0,1:T(8,128)} %broadcast_subtract_fusion), kind=kLoop, calls=%fused_computation.8 | loop fusion | flops 78071808 | bytes 1742848 | tf_op jit(solution)/shard_map/reduce_sum | solution.py:380
  508.8 6.6 all-to-all-start.8
  545.9 6.9 all-to-all-done.6
  649.6 7.4 collective-permute-start.28
  657.4 13.7 %add_multiply_fusion = (f32[1572,1024]{1,0:T(8,128)}, f32[1572,1024]{1,0:T(8,128)}, f32[1572,1024]{1,0:T(8,128)}) fusion(f32[1572,1024]{1,0:T(8,128)} %param.55, f32[1572,1024]{1,0:T(8,128)} %param.57, f32[1572,1024]{1,0:T(8,128)} %param.56, bf16[32,8,1024]{2,1,0:T(8,128)(2,1)} %all-to-all-done.5, f32[256,1572]{0,1:T(8,128)S(1)} %copy-done.26, ...), kind=kOutput, calls=%fused_computation.30 | convolution fusion | flops 848729088 | bytes 42379264 | tf_op jit(solution)/shard_map/pv,pd->vd/dot_general | solution.py:495
  671.8 89.7 %collective-permute-done.29 = bf16[256,1536]{1,0:T(8,128)(2,1)} collective-permute-done((bf16[256,1536]{1,0:T(8,128)(2,1)}, bf16[256,1536]{1,0:T(8,128)(2,1)}, u32[]{:S(2)}, u32[]{:S(2)}) %collective-permute-start.29) | collective-permute-done | bytes 786464 | tf_op jit(solution)/shard_map/ppermute | solution.py:188
  815.7 36.5 %all-to-all-start.11 = ((bf16[8,144,1024]{2,1,0:T(8,128)(2,1)}), bf16[8,144,1024]{2,1,0:T(8,128)(2,1)}, u32[]{:S(2)}, u32[]{:S(2)}) async-start(bf16[8,144,1024]{2,1,0:T(8,128)(2,1)} %bitcast.490), calls=%async_computation.11 | async-start | bytes 4718592 | tf_op jit(solution)/shard_map/all_to_all | solution.py:237
  868.1 11.9 all-to-all-done.11
  922.5 95.4 %collective-permute-done.25 = bf16[256,1536]{1,0:T(8,128)(2,1)S(1)} collective-permute-done((bf16[256,1536]{1,0:T(8,128)(2,1)}, bf16[256,1536]{1,0:T(8,128)(2,1)S(1)}, u32[]{:S(2)}, u32[]{:S(2)}) %collective-permute-start.25) | collective-permute-done | bytes 786464 | tf_op jit(solution)/shard_map/ppermute | solution.py:188
  1083.9 37.3 %all-to-all-start.13 = ((bf16[32,2,4496]{2,1,0:T(2,128)(2,1)}), bf16[32,2,4496]{2,1,0:T(2,128)(2,1)}, u32[]{:S(2)}, u32[]{:S(2)}) async-start(bf16[32,2,4496]{2,1,0:T(2,128)(2,1)} %reshape.1501), calls=%async_computation.13 | async-start | bytes 1179648 | tf_op jit(solution)/shard_map/all_to_all | solution.py:233
  1134.2 19.3 %collective-permute-done.17 = bf16[4,1,2,32,2048]{4,3,0,2,1:T(8,128)(2,1)S(1)} collective-permute-done((bf16[4,1,2,32,2048]{4,3,0,2,1:T(8,128)(2,1)S(1)}, bf16[4,1,2,32,2048]{4,3,0,2,1:T(8,128)(2,1)S(1)}, u32[]{:S(2)}, u32[]{:S(2)}) %collective-permute-start.17) | collective-permute-done | bytes 1048608 | tf_op jit(solution)/shard_map/ppermute | solution.py:202
  1166.8 54.7 %scatter_custom_fusion = f32[50304,32]{1,0:T(8,128)} fusion(s32[8192]{0:T(1024)} %param.31, f32[8192,32]{1,0:T(8,128)} %reshape.1462, f32[]{:T(128)} %constant.451.clone.1), kind=kCustom, calls=%fused_computation.10 | custom fusion | flops 262144 | bytes 6439424 | tf_op jit(solution)/shard_map/scatter-add | solution.py:662
  1221.5 16.9 %copy.579 = f32[50304,32]{0,1:T(8,128)} copy(f32[50304,32]{1,0:T(8,128)} %scatter_custom_fusion) | data formatting | bytes 12877824 | tf_op jit(solution)/shard_map/scatter-add | solution.py:662
  1238.4 17.1 %add_multiply_fusion.1 = (f32[50304,32]{0,1:T(8,128)}, f32[50304,32]{0,1:T(8,128)}, f32[50304,32]{0,1:T(8,128)}) fusion(f32[50304,32]{0,1:T(8,128)} %param.37, f32[50304,32]{0,1:T(8,128)} %copy.579, f32[50304,32]{0,1:T(8,128)} %param.39, f32[50304,32]{0,1:T(8,128)} %param.38), kind=kLoop, calls=%fused_computation.33 | loop fusion | flops 22536192 | bytes 45072384 | tf_op jit(solution)/shard_map/mul | solution.py:251
  1267.3 18.9 %collective-permute-done.11 = bf16[4,2,1,32,2048]{4,3,1,0,2:T(8,128)(2,1)S(1)} collective-permute-done((bf16[4,2,1,32,2048]{4,3,1,0,2:T(8,128)(2,1)S(1)}, bf16[4,2,1,32,2048]{4,3,1,0,2:T(8,128)(2,1)S(1)}, u32[]{:S(2)}, u32[]{:S(2)}) %collective-permute-start.11) | collective-permute-done | bytes 1048608 | tf_op jit(solution)/shard_map/ppermute | solution.py:202
  1293.4 6.9 collective-permute-done.12
  1309.8 17.9 %collective-permute-done.23 = bf16[32,4096]{1,0:T(8,128)(2,1)S(1)} collective-permute-done((bf16[32,4096]{1,0:T(8,128)(2,1)S(1)}, bf16[32,4096]{1,0:T(8,128)(2,1)S(1)}, u32[]{:S(2)}, u32[]{:S(2)}) %collective-permute-start.23) | collective-permute-done | bytes 262176 | tf_op jit(solution)/shard_map/ppermute | solution.py:227
  (862 shorter events, 587.9 us)
Async XLA Ops:
  7.2 171.4 %all-gather.2.cloned.1.call-start = ((), (), s32[]{:S(2)}) async-start(), calls=%async_computation.14 | async-start | bytes 17301504 | tf_op jit(solution)/shard_map/all_gather | solution.py:307
  61.3 40.0 %all-to-all-start = ((bf16[32,2,4496]{2,1,0:T(2,128)(2,1)}), bf16[32,2,4496]{2,1,0:T(2,128)(2,1)}, u32[]{:S(2)}, u32[]{:S(2)}) async-start(bf16[32,2,4496]{2,1,0:T(2,128)(2,1)} %reshape.1499), calls=%async_computation | async-start | bytes 1179648 | tf_op jit(solution)/shard_map/all_to_all | solution.py:233
  69.8 153.0 %collective-permute-start.3 = (bf16[256,1536]{1,0:T(8,128)(2,1)}, bf16[256,1536]{1,0:T(8,128)(2,1)}, u32[]{:S(2)}, u32[]{:S(2)}) collective-permute-start(bf16[256,1536]{1,0:T(8,128)(2,1)} %pad_maximum_fusion.13), channel_id=1, source_target_pairs={{0,24},{1,0},{2,8},{3,16},{8,25},{9,1},{10,9},{11,17},{16,26},{17,... | collective-permute-start | bytes 2359304 | tf_op jit(solution)/shard_map/ppermute | solution.py:164
  69.9 156.1 %collective-permute-start.2 = (bf16[256,1536]{1,0:T(8,128)(2,1)}, bf16[256,1536]{1,0:T(8,128)(2,1)}, u32[]{:S(2)}, u32[]{:S(2)}) collective-permute-start(bf16[256,1536]{1,0:T(8,128)(2,1)} %pad_maximum_fusion.13), channel_id=1, source_target_pairs={{0,16},{1,24},{2,0},{3,8},{8,17},{9,25},{10,1},{11,9},{16,18},{17,... | collective-permute-start | bytes 2359304 | tf_op jit(solution)/shard_map/ppermute | solution.py:164
  73.1 152.9 %collective-permute-start.1 = (bf16[256,1536]{1,0:T(8,128)(2,1)}, bf16[256,1536]{1,0:T(8,128)(2,1)}, u32[]{:S(2)}, u32[]{:S(2)}) collective-permute-start(bf16[256,1536]{1,0:T(8,128)(2,1)} %pad_maximum_fusion.13), channel_id=1, source_target_pairs={{0,8},{1,16},{2,24},{3,0},{8,9},{9,17},{10,25},{11,1},{16,10},{17,... | collective-permute-start | bytes 2359304 | tf_op jit(solution)/shard_map/ppermute | solution.py:164
  73.6 159.9 %collective-permute-start = (bf16[256,1536]{1,0:T(8,128)(2,1)}, bf16[256,1536]{1,0:T(8,128)(2,1)}, u32[]{:S(2)}, u32[]{:S(2)}) collective-permute-start(bf16[256,1536]{1,0:T(8,128)(2,1)} %pad_maximum_fusion.13), channel_id=1, source_target_pairs={{0,0},{1,8},{2,16},{3,24},{8,1},{9,9},{10,17},{11,25},{16,2},{17,1... | collective-permute-start | bytes 2359304 | tf_op jit(solution)/shard_map/ppermute | solution.py:164
  211.3 100.0 %all-to-all-start.1 = ((bf16[8,144,1024]{2,1,0:T(8,128)(2,1)}), bf16[8,144,1024]{2,1,0:T(8,128)(2,1)S(1)}, u32[]{:S(2)}, u32[]{:S(2)}) async-start(bf16[8,144,1024]{2,1,0:T(8,128)(2,1)} %bitcast.493), calls=%async_computation.1 | async-start | bytes 4718592 | tf_op jit(solution)/shard_map/all_to_all | solution.py:237
  216.4 60.6 %collective-permute-start.7 = (bf16[256,1536]{1,0:T(8,128)(2,1)}, bf16[256,1536]{1,0:T(8,128)(2,1)S(1)}, u32[]{:S(2)}, u32[]{:S(2)}) collective-permute-start(bf16[256,1536]{1,0:T(8,128)(2,1)} %pad_maximum_fusion.14), channel_id=1, source_target_pairs={{0,24},{1,0},{2,8},{3,16},{8,25},{9,1},{10,9},{11,17},{16,26},{17,... | collective-permute-start | bytes 2359304 | tf_op jit(solution)/shard_map/ppermute | solution.py:164
  222.8 54.2 %collective-permute-start.6 = (bf16[256,1536]{1,0:T(8,128)(2,1)}, bf16[256,1536]{1,0:T(8,128)(2,1)}, u32[]{:S(2)}, u32[]{:S(2)}) collective-permute-start(bf16[256,1536]{1,0:T(8,128)(2,1)} %pad_maximum_fusion.14), channel_id=1, source_target_pairs={{0,16},{1,24},{2,0},{3,8},{8,17},{9,25},{10,1},{11,9},{16,18},{17,... | collective-permute-start | bytes 2359304 | tf_op jit(solution)/shard_map/ppermute | solution.py:164
  226.0 64.8 %collective-permute-start.5 = (bf16[256,1536]{1,0:T(8,128)(2,1)}, bf16[256,1536]{1,0:T(8,128)(2,1)}, u32[]{:S(2)}, u32[]{:S(2)}) collective-permute-start(bf16[256,1536]{1,0:T(8,128)(2,1)} %pad_maximum_fusion.14), channel_id=1, source_target_pairs={{0,8},{1,16},{2,24},{3,0},{8,9},{9,17},{10,25},{11,1},{16,10},{17,... | collective-permute-start | bytes 2359304 | tf_op jit(solution)/shard_map/ppermute | solution.py:164
  226.0 64.8 %collective-permute-start.4 = (bf16[256,1536]{1,0:T(8,128)(2,1)}, bf16[256,1536]{1,0:T(8,128)(2,1)}, u32[]{:S(2)}, u32[]{:S(2)}) collective-permute-start(bf16[256,1536]{1,0:T(8,128)(2,1)} %pad_maximum_fusion.14), channel_id=1, source_target_pairs={{0,0},{1,8},{2,16},{3,24},{8,1},{9,9},{10,17},{11,25},{16,2},{17,1... | collective-permute-start | bytes 2359304 | tf_op jit(solution)/shard_map/ppermute | solution.py:164
  321.8 38.7 %all-to-all-start.2 = ((bf16[8,144,1024]{2,1,0:T(8,128)(2,1)}), bf16[8,144,1024]{2,1,0:T(8,128)(2,1)S(1)}, u32[]{:S(2)}, u32[]{:S(2)}) async-start(bf16[8,144,1024]{2,1,0:T(8,128)(2,1)} %bitcast.524), calls=%async_computation.2 | async-start | bytes 4718592 | tf_op jit(solution)/shard_map/all_to_all | solution.py:237
  392.4 33.1 %all-to-all-start.3 = ((bf16[8,144,1024]{2,1,0:T(8,128)(2,1)}), bf16[8,144,1024]{2,1,0:T(8,128)(2,1)}, u32[]{:S(2)}, u32[]{:S(2)}) async-start(bf16[8,144,1024]{2,1,0:T(8,128)(2,1)} %bitcast.494), calls=%async_computation.3 | async-start | bytes 4718592 | tf_op jit(solution)/shard_map/all_to_all | solution.py:237
  435.8 33.0 %all-to-all-start.4 = ((bf16[8,144,1024]{2,1,0:T(8,128)(2,1)}), bf16[8,144,1024]{2,1,0:T(8,128)(2,1)}, u32[]{:S(2)}, u32[]{:S(2)}) async-start(bf16[8,144,1024]{2,1,0:T(8,128)(2,1)} %bitcast.522), calls=%async_computation.4 | async-start | bytes 4718592 | tf_op jit(solution)/shard_map/all_to_all | solution.py:237
  575.2 33.1 %all-to-all-start.9 = ((bf16[8,144,1024]{2,1,0:T(8,128)(2,1)}), bf16[8,144,1024]{2,1,0:T(8,128)(2,1)}, u32[]{:S(2)}, u32[]{:S(2)}) async-start(bf16[8,144,1024]{2,1,0:T(8,128)(2,1)} %bitcast.489), calls=%async_computation.9 | async-start | bytes 4718592 | tf_op jit(solution)/shard_map/all_to_all | solution.py:237
  640.7 125.1 %all-to-all-start.10 = ((bf16[8,144,1024]{2,1,0:T(8,128)(2,1)}), bf16[8,144,1024]{2,1,0:T(8,128)(2,1)}, u32[]{:S(2)}, u32[]{:S(2)}) async-start(bf16[8,144,1024]{2,1,0:T(8,128)(2,1)} %bitcast.521), calls=%async_computation.10 | async-start | bytes 4718592 | tf_op jit(solution)/shard_map/all_to_all | solution.py:237
  657.1 104.5 %collective-permute-start.29 = (bf16[256,1536]{1,0:T(8,128)(2,1)}, bf16[256,1536]{1,0:T(8,128)(2,1)}, u32[]{:S(2)}, u32[]{:S(2)}) collective-permute-start(bf16[256,1536]{1,0:T(8,128)(2,1)} %get-tuple-element.219), channel_id=1, source_target_pairs={{8,0},{16,1},{24,2},{0,3},{9,8},{17,9},{25,10},{1,11},{10,16},{18,... | collective-permute-start | bytes 2359304 | tf_op jit(solution)/shard_map/ppermute | solution.py:188
  657.1 104.5 %collective-permute-start.30 = (bf16[256,1536]{1,0:T(8,128)(2,1)}, bf16[256,1536]{1,0:T(8,128)(2,1)}, u32[]{:S(2)}, u32[]{:S(2)}) collective-permute-start(bf16[256,1536]{1,0:T(8,128)(2,1)} %get-tuple-element.220), channel_id=1, source_target_pairs={{16,0},{24,1},{0,2},{8,3},{17,8},{25,9},{1,10},{9,11},{18,16},{26,... | collective-permute-start | bytes 2359304 | tf_op jit(solution)/shard_map/ppermute | solution.py:188
  657.4 104.2 %collective-permute-start.31 = (bf16[256,1536]{1,0:T(8,128)(2,1)}, bf16[256,1536]{1,0:T(8,128)(2,1)}, u32[]{:S(2)}, u32[]{:S(2)}) collective-permute-start(bf16[256,1536]{1,0:T(8,128)(2,1)} %get-tuple-element.221), channel_id=1, source_target_pairs={{24,0},{0,1},{8,2},{16,3},{25,8},{1,9},{9,10},{17,11},{26,16},{2,1... | collective-permute-start | bytes 2359304 | tf_op jit(solution)/shard_map/ppermute | solution.py:188
  815.7 64.3 %all-to-all-start.11 = ((bf16[8,144,1024]{2,1,0:T(8,128)(2,1)}), bf16[8,144,1024]{2,1,0:T(8,128)(2,1)}, u32[]{:S(2)}, u32[]{:S(2)}) async-start(bf16[8,144,1024]{2,1,0:T(8,128)(2,1)} %bitcast.490), calls=%async_computation.11 | async-start | bytes 4718592 | tf_op jit(solution)/shard_map/all_to_all | solution.py:237
  906.4 111.5 %collective-permute-start.25 = (bf16[256,1536]{1,0:T(8,128)(2,1)}, bf16[256,1536]{1,0:T(8,128)(2,1)S(1)}, u32[]{:S(2)}, u32[]{:S(2)}) collective-permute-start(bf16[256,1536]{1,0:T(8,128)(2,1)} %get-tuple-element.215), channel_id=1, source_target_pairs={{8,0},{16,1},{24,2},{0,3},{9,8},{17,9},{25,10},{1,11},{10,16},{18,... | collective-permute-start | bytes 2359304 | tf_op jit(solution)/shard_map/ppermute | solution.py:188
  908.9 109.0 %collective-permute-start.26 = (bf16[256,1536]{1,0:T(8,128)(2,1)}, bf16[256,1536]{1,0:T(8,128)(2,1)S(1)}, u32[]{:S(2)}, u32[]{:S(2)}) collective-permute-start(bf16[256,1536]{1,0:T(8,128)(2,1)} %get-tuple-element.216), channel_id=1, source_target_pairs={{16,0},{24,1},{0,2},{8,3},{17,8},{25,9},{1,10},{9,11},{18,16},{26,... | collective-permute-start | bytes 2359304 | tf_op jit(solution)/shard_map/ppermute | solution.py:188
  913.1 104.8 %collective-permute-start.27 = (bf16[256,1536]{1,0:T(8,128)(2,1)}, bf16[256,1536]{1,0:T(8,128)(2,1)}, u32[]{:S(2)}, u32[]{:S(2)}) collective-permute-start(bf16[256,1536]{1,0:T(8,128)(2,1)} %get-tuple-element.217), channel_id=1, source_target_pairs={{24,0},{0,1},{8,2},{16,3},{25,8},{1,9},{9,10},{17,11},{26,16},{2,1... | collective-permute-start | bytes 2359304 | tf_op jit(solution)/shard_map/ppermute | solution.py:188
  917.1 112.8 %all-to-all-start.12 = ((bf16[8,144,1024]{2,1,0:T(8,128)(2,1)}), bf16[8,144,1024]{2,1,0:T(8,128)(2,1)}, u32[]{:S(2)}, u32[]{:S(2)}) async-start(bf16[8,144,1024]{2,1,0:T(8,128)(2,1)} %bitcast.86), calls=%async_computation.12 | async-start | bytes 4718592 | tf_op jit(solution)/shard_map/all_to_all | solution.py:237
  922.4 198.8 %collective-permute-start.16 = (bf16[4,2,1,2,32,4096]{5,4,0,1,3,2:T(8,128)(2,1)}, bf16[4,2,1,2,32,4096]{5,4,0,1,3,2:T(8,128)(2,1)}, u32[]{:S(2)}, u32[]{:S(2)}) collective-permute-start(bf16[4,2,1,2,32,4096]{5,4,0,1,3,2:T(8,128)(2,1)} %fusion.17), channel_id=1, source_target_pairs={{0,1},{1,0},{2,3},{3,2},{4,5},{5,4},{6,7},{7,6},{8,9},{9,8},{10,11... | collective-permute-start | bytes 12582920 | tf_op jit(solution)/shard_map/ppermute | solution.py:202
  1083.9 75.3 %all-to-all-start.13 = ((bf16[32,2,4496]{2,1,0:T(2,128)(2,1)}), bf16[32,2,4496]{2,1,0:T(2,128)(2,1)}, u32[]{:S(2)}, u32[]{:S(2)}) async-start(bf16[32,2,4496]{2,1,0:T(2,128)(2,1)} %reshape.1501), calls=%async_computation.13 | async-start | bytes 1179648 | tf_op jit(solution)/shard_map/all_to_all | solution.py:233
  1133.4 124.6 %collective-permute-start.8 = (bf16[4,2,1,2,32,4096]{5,4,3,1,0,2:T(8,128)(2,1)}, bf16[4,2,1,2,32,4096]{5,4,3,1,0,2:T(8,128)(2,1)}, u32[]{:S(2)}, u32[]{:S(2)}) collective-permute-start(bf16[4,2,1,2,32,4096]{5,4,3,1,0,2:T(8,128)(2,1)} %fusion.21), channel_id=1, source_target_pairs={{0,1},{1,0},{2,3},{3,2},{4,5},{5,4},{6,7},{7,6},{8,9},{9,8},{10,11... | collective-permute-start | bytes 12582920 | tf_op jit(solution)/shard_map/ppermute | solution.py:202
  1154.8 108.7 %collective-permute-start.18 = (bf16[4,1,32,2048]{3,2,0,1:T(8,128)(2,1)}, bf16[4,1,32,2048]{3,2,0,1:T(8,128)(2,1)}, u32[]{:S(2)}, u32[]{:S(2)}) collective-permute-start(bf16[4,1,32,2048]{3,2,0,1:T(8,128)(2,1)} %dynamic-slice_bitcast_fusion.4), channel_id=1, source_target_pairs={{0,2},{2,0},{1,3},{3,1},{4,6},{6,4},{5,7},{7,5},{8,10},{10,8},{9,1... | collective-permute-start | bytes 1572872 | tf_op jit(solution)/shard_map/ppermute | solution.py:202
  1158.5 107.6 %collective-permute-start.20 = (bf16[4,1,32,2048]{3,2,1,0:T(8,128)(2,1)}, bf16[4,1,32,2048]{3,2,1,0:T(8,128)(2,1)}, u32[]{:S(2)}, u32[]{:S(2)}) collective-permute-start(bf16[4,1,32,2048]{3,2,1,0:T(8,128)(2,1)} %dynamic-slice_bitcast_fusion.3), channel_id=1, source_target_pairs={{0,4},{4,0},{1,5},{5,1},{2,6},{6,2},{3,7},{7,3},{8,12},{12,8},{9,1... | collective-permute-start | bytes 1572872 | tf_op jit(solution)/shard_map/ppermute | solution.py:202
  1293.0 34.7 %collective-permute-start.23 = (bf16[32,4096]{1,0:T(8,128)(2,1)S(1)}, bf16[32,4096]{1,0:T(8,128)(2,1)S(1)}, u32[]{:S(2)}, u32[]{:S(2)}) collective-permute-start(bf16[32,4096]{1,0:T(8,128)(2,1)S(1)} %get-tuple-element.255), channel_id=1, source_target_pairs={{0,24},{8,0},{16,8},{24,16},{1,25},{9,1},{17,9},{25,17},{2,26},{10... | collective-permute-start | bytes 786440 | tf_op jit(solution)/shard_map/ppermute | solution.py:227
  1301.9 32.1 %collective-permute-start.14 = (bf16[32,4096]{1,0:T(8,128)(2,1)S(1)}, bf16[32,4096]{1,0:T(8,128)(2,1)S(1)}, u32[]{:S(2)}, u32[]{:S(2)}) collective-permute-start(bf16[32,4096]{1,0:T(8,128)(2,1)S(1)} %get-tuple-element.251), channel_id=1, source_target_pairs={{0,16},{8,24},{16,0},{24,8},{1,17},{9,25},{17,1},{25,9},{2,18},{10... | collective-permute-start | bytes 786440 | tf_op jit(solution)/shard_map/ppermute | solution.py:227
  1303.4 35.5 %collective-permute-start.15 = (bf16[32,4096]{1,0:T(8,128)(2,1)S(1)}, bf16[32,4096]{1,0:T(8,128)(2,1)S(1)}, u32[]{:S(2)}, u32[]{:S(2)}) collective-permute-start(bf16[32,4096]{1,0:T(8,128)(2,1)S(1)} %get-tuple-element.252), channel_id=1, source_target_pairs={{0,24},{8,0},{16,8},{24,16},{1,25},{9,1},{17,9},{25,17},{2,26},{10... | collective-permute-start | bytes 786440 | tf_op jit(solution)/shard_map/ppermute | solution.py:227
  (236 other events, 1740.3 us)
Sparse Core Ops, SparseCore 0:
  11.5 166.9 all-gather.1

commit v2 on v1

v2 whole, which is shorter than its diff:
```python
import functools

import jax
import jax.numpy as jnp
from jax import lax
from jax.experimental import pallas as pl
from jax.experimental.pallas import tpu as pltpu
from jax.sharding import Mesh, PartitionSpec as P

D = 1024
HEADS = 16
HDIM = 64
F = 512
TOPK = 4
ADAM_STEP = 10


EPS_NORM = 1e-05
BETA_ONE = 0.9
BETA_TWO = 0.95
ADAM_EPS = 1e-08
LEARN_RATE = 0.01
DECAY_RATE = 0.1
ROPE_BASE = 10000.0
MASK_FILL = -1e30


def rms_norm(inputs, gain_row):
    return (
        inputs * lax.rsqrt(jnp.mean(inputs * inputs, axis=-1, keepdims=True) + EPS_NORM) * gain_row
    )


def norm_back(inputs, gain_row, upstream):
    _, pullback = jax.vjp(rms_norm, inputs, gain_row)
    return pullback(upstream)


AXES = ("z", "x", "h", "y", "c")
PLANES = 4
SHIFTS = (0, 2, 1, 3)
LANES = 128
CHUNKS = D // LANES


def dot_nn(left, right):
    return lax.dot_general(
        left, right, (((1,), (0,)), ((), ())), preferred_element_type=jnp.float32
    )


def dot_nt(left, right):
    return lax.dot_general(
        left, right, (((1,), (1,)), ((), ())), preferred_element_type=jnp.float32
    )


def dot_tn(left, right):
    return lax.dot_general(
        left, right, (((0,), (0,)), ((), ())), preferred_element_type=jnp.float32
    )


def inverse_root(values):
    return lax.rsqrt(jnp.mean(values * values, axis=-1, keepdims=True) + EPS_NORM)


def two_terms(values):
    high = values.astype(jnp.bfloat16)
    return high, (values - high.astype(jnp.float32)).astype(jnp.bfloat16)


def chunk(values, place):
    return values[:, place * LANES : (place + 1) * LANES]


def half_turn(values):
    lane = lax.broadcasted_iota(jnp.int32, values.shape, 1)
    ahead = pltpu.roll(values, LANES - HDIM // 2, 1)
    behind = pltpu.roll(values, HDIM // 2, 1)
    return jnp.where(lane % HDIM < HDIM // 2, ahead, behind)


def slot_gates(spread, gates, capacity):
    high, rest = two_terms(gates)
    full = dot_nn(spread, high) + dot_nn(spread, rest)
    expert = lax.broadcasted_iota(jnp.int32, full.shape, 0) // capacity
    lane = lax.broadcasted_iota(jnp.int32, full.shape, 1)
    return jnp.sum(jnp.where(lane == expert, full, 0.0), axis=1, keepdims=True)


def combine(middle, spread, spread_back, gates, returned, capacity):
    weighted = slot_gates(spread, gates, capacity) * returned.astype(jnp.float32)
    high, rest = two_terms(weighted)
    return middle + (dot_nn(spread_back, high) + dot_nn(spread_back, rest))


def masked_probs(query, key, visible):
    scores = dot_nt(query, key) * HDIM ** (-0.5)
    scores = jnp.where(visible, scores, MASK_FILL)
    weights = jnp.exp(scores - jnp.max(scores, axis=-1, keepdims=True))
    return weights / jnp.sum(weights, axis=-1, keepdims=True)


def visible_keys(prefix_ref, seq_len):
    query_place = lax.broadcasted_iota(jnp.int32, (seq_len, seq_len), 0)
    key_place = lax.broadcasted_iota(jnp.int32, (seq_len, seq_len), 1)
    return (key_place <= query_place) | (key_place < prefix_ref[0])


def head_masks(seq_len):
    lane = lax.broadcasted_iota(jnp.int32, (seq_len, LANES), 1)
    return lane < HDIM, lane >= HDIM


def fetch_weights(weight_ref, held_ref, copy_sem, layer_index, order):
    copies = {}
    for part in order:
        copies[part] = pltpu.make_async_copy(
            weight_ref.at[layer_index, :, pl.ds(part * D, D)], held_ref.at[part], copy_sem.at[part]
        )
        copies[part].start()
    return copies


def forward_kernel(
    layer_index,
    capacity,
    expert_count,
    prefix_ref,
    hidden_ref,
    *refs,
):
    if layer_index > 0:
        gates_in_ref, returned_ref, refs = refs[0], refs[1], refs[2:]
    (
        weight_ref,
        gain_ref,
        turn_ref,
        router_ref,
        kept_ref,
        spread_ref,
        spread_back_ref,
        hidden_out_ref,
        projected_ref,
        query_ref,
        key_ref,
        value_ref,
        attended_ref,
        middle_ref,
        ffn_ref,
        probs_ref,
        gates_ref,
        outgoing_ref,
        held_ref,
        copy_sem,
    ) = refs
    copies = fetch_weights(weight_ref, held_ref, copy_sem, layer_index, (0, 1, 2, 3))
    seq_len = hidden_ref.shape[0]
    hidden = hidden_ref[...]
    if layer_index > 0:
        hidden = combine(
            hidden,
            spread_ref[...],
            spread_back_ref[...],
            gates_in_ref[...],
            returned_ref[...],
            capacity,
        )
    hidden_out_ref[...] = hidden
    row = 4 * layer_index
    normed = (hidden * inverse_root(hidden) * gain_ref[row : row + 1, :]).astype(jnp.bfloat16)
    cosines, sines = turn_ref[0], turn_ref[1]
    for part, out_ref in ((0, query_ref), (1, key_ref)):
        columns = slice(part * D, (part + 1) * D)
        copies[part].wait()
        projected = dot_nn(normed, held_ref[part])
        projected_ref[:, columns] = projected
        scaled = projected * inverse_root(projected) * gain_ref[row + 1 + part : row + 2 + part, :]
        for place in range(CHUNKS):
            block = chunk(scaled, place)
            out_ref[:, place * LANES : (place + 1) * LANES] = (
                block * cosines + half_turn(block) * sines
            ).astype(jnp.bfloat16)
    copies[2].wait()
    value_ref[...] = dot_nn(normed, held_ref[2]).astype(jnp.bfloat16)
    visible = visible_keys(prefix_ref, seq_len)
    masks = head_masks(seq_len)
    zero = jnp.zeros((), jnp.bfloat16)
    for place in range(CHUNKS):
        columns = slice(place * LANES, (place + 1) * LANES)
        query, key, value = query_ref[:, columns], key_ref[:, columns], value_ref[:, columns]
        total = None
        for mask in masks:
            probs = masked_probs(query, jnp.where(mask, key, zero), visible).astype(jnp.bfloat16)
            term = dot_nn(probs, jnp.where(mask, value, zero))
            total = term if total is None else total + term
        attended_ref[:, columns] = total.astype(jnp.bfloat16)
    copies[3].wait()
    middle = hidden + dot_nn(attended_ref[...], held_ref[3])
    middle_ref[...] = middle
    ffn = (middle * inverse_root(middle) * gain_ref[row + 3 : row + 4, :]).astype(jnp.bfloat16)
    ffn_ref[...] = ffn
    outgoing_ref[...] = dot_nn(spread_ref[...], ffn).astype(jnp.bfloat16)
    logits = dot_nn(ffn, router_ref[layer_index])
    lane = lax.broadcasted_iota(jnp.int32, logits.shape, 1)
    logits = jnp.where(lane < expert_count, logits, MASK_FILL)
    weights = jnp.exp(logits - jnp.max(logits, axis=-1, keepdims=True))
    probs = weights / jnp.sum(weights, axis=-1, keepdims=True)
    probs_ref[...] = probs
    gates_ref[...] = probs * kept_ref[...]


def forward_layer(
    layer_index,
    capacity,
    expert_count,
    prefix,
    hidden,
    extra,
    weights,
    gains,
    turns,
    router,
    kept,
    spread,
    spread_back,
):
    seq_len = hidden.shape[0]
    whole = pl.BlockSpec(memory_space=pltpu.VMEM)
    wide = jax.ShapeDtypeStruct((seq_len, D), jnp.float32)
    low = jax.ShapeDtypeStruct((seq_len, D), jnp.bfloat16)
    small = jax.ShapeDtypeStruct((seq_len, LANES), jnp.float32)
    return pl.pallas_call(
        functools.partial(forward_kernel, layer_index, capacity, expert_count),
        out_shape=(
            wide,
            jax.ShapeDtypeStruct((seq_len, 2 * D), jnp.float32),
            low,
            low,
            low,
            low,
            wide,
            low,
            small,
            small,
            jax.ShapeDtypeStruct((spread.shape[0], D), jnp.bfloat16),
        ),
        in_specs=[pl.BlockSpec(memory_space=pltpu.SMEM), whole]
        + [whole] * len(extra)
        + [pl.BlockSpec(memory_space=pl.ANY)]
        + [whole] * 6,
        out_specs=[whole] * 11,
        scratch_shapes=[
            pltpu.VMEM((4, D, D), jnp.bfloat16),
            pltpu.SemaphoreType.DMA((4,)),
        ],
        compiler_params=pltpu.CompilerParams(vmem_limit_bytes=60 * 1024 * 1024),
        cost_estimate=pl.CostEstimate(
            flops=4 * seq_len * D * D * 3, bytes_accessed=24 * 1024 * 1024, transcendentals=1 << 20
        ),
    )(prefix, hidden, *extra, weights, gains, turns, router, kept, spread, spread_back)


def norm_pull(values, gain, upstream):
    root = inverse_root(values)
    scaled = values * root
    weighted = upstream * gain
    mean = jnp.mean(weighted * scaled, axis=-1, keepdims=True)
    return root * (weighted - scaled * mean), jnp.sum(upstream * scaled, axis=0, keepdims=True)


def backward_kernel(
    layer_index,
    capacity,
    prefix_ref,
    grad_ref,
    back_ref,
    logit_ref,
    hidden_ref,
    projected_ref,
    query_ref,
    key_ref,
    value_ref,
    attended_ref,
    middle_ref,
    weight_ref,
    gain_ref,
    turn_ref,
    router_ref,
    spread_back_ref,
    *refs,
):
    if layer_index > 0:
        spread_ref, gates_ref, refs = refs[0], refs[1], refs[2:]
        outgoing_ref, refs = refs[3], refs[:3] + refs[4:]
    grad_out_ref, weight_grad_ref, gain_grad_ref, pull_ref, key_pull_ref, held_ref, copy_sem = refs
    copies = fetch_weights(weight_ref, held_ref, copy_sem, layer_index, (3, 2, 0, 1))
    seq_len = hidden_ref.shape[0]
    row = 4 * layer_index
    ffn_grad = dot_nn(spread_back_ref[...], back_ref[...]) + dot_nt(
        logit_ref[...], router_ref[layer_index]
    )
    middle_grad, gain_three = norm_pull(
        middle_ref[...], gain_ref[row + 3 : row + 4, :], ffn_grad
    )
    grad_middle = grad_ref[...] + middle_grad
    grad_out_ref[...] = grad_middle
    branch = grad_middle.astype(jnp.bfloat16)
    weight_grad_ref[:, 3 * D :] = dot_tn(attended_ref[...], branch).astype(jnp.bfloat16)
    copies[3].wait()
    pull_ref[...] = dot_nt(branch, held_ref[3]).astype(jnp.bfloat16)
    visible = visible_keys(prefix_ref, seq_len)
    masks = head_masks(seq_len)
    zero = jnp.zeros((), jnp.bfloat16)
    cosines, sines = turn_ref[0], turn_ref[1]
    factor = HDIM ** (-0.5)
    hidden = hidden_ref[...]
    normed = (hidden * inverse_root(hidden) * gain_ref[row : row + 1, :]).astype(jnp.bfloat16)
    for place in range(CHUNKS):
        columns = slice(place * LANES, (place + 1) * LANES)
        query, key, value = query_ref[:, columns], key_ref[:, columns], value_ref[:, columns]
        pull = pull_ref[:, columns]
        totals = [None, None, None]
        for mask in masks:
            key_half = jnp.where(mask, key, zero)
            probs = masked_probs(query, key_half, visible)
            pulled = dot_nt(pull, jnp.where(mask, value, zero))
            inner = jnp.sum(probs * pulled, axis=-1, keepdims=True)
            score_grad = (probs * (pulled - inner)).astype(jnp.bfloat16)
            terms = (
                dot_nn(score_grad, key_half),
                dot_tn(score_grad, jnp.where(mask, query, zero)),
                dot_tn(probs.astype(jnp.bfloat16), jnp.where(mask, pull, zero)),
            )
            totals = [b if a is None else a + b for a, b in zip(totals, terms)]
        for part, target_ref in ((0, key_pull_ref.at[0]), (1, key_pull_ref.at[1])):
            turned = (totals[part] * factor).astype(jnp.bfloat16).astype(jnp.float32)
            target_ref[:, columns] = turned * cosines - half_turn(turned) * sines
        pull_ref[:, columns] = totals[2].astype(jnp.bfloat16)
    gain_rows = []
    value_pull = pull_ref[...]
    copies[2].wait()
    back = dot_nt(value_pull, held_ref[2])
    weight_grad_ref[:, 2 * D : 3 * D] = dot_tn(normed, value_pull).astype(jnp.bfloat16)
    for part in range(2):
        columns = slice(part * D, (part + 1) * D)
        input_pull, gain_row = norm_pull(
            projected_ref[:, columns],
            gain_ref[row + 1 + part : row + 2 + part, :],
            key_pull_ref[part],
        )
        gain_rows.append(gain_row)
        low_pull = input_pull.astype(jnp.bfloat16)
        weight_grad_ref[:, columns] = dot_tn(normed, low_pull).astype(jnp.bfloat16)
        copies[part].wait()
        back = back + dot_nt(low_pull, held_ref[part])
    hidden_grad, gain_zero = norm_pull(hidden, gain_ref[row : row + 1, :], back)
    grad_out = grad_out_ref[...] + hidden_grad
    grad_out_ref[...] = grad_out
    if layer_index > 0:
        outgoing_ref[...] = outgoing_pull(grad_out, spread_ref[...], gates_ref[...], capacity)
    gain_grad_ref[...] = jnp.concatenate(
        [gain_zero] + gain_rows + [gain_three, jnp.zeros((4, D), jnp.float32)], axis=0
    )


def backward_layer(
    layer_index,
    capacity,
    prefix,
    grad,
    back_inputs,
    logit_low,
    hidden,
    projected,
    queries,
    keys,
    values,
    attended,
    middle,
    weights,
    gains,
    turns,
    router,
    spread_back,
    extra,
):
    seq_len = hidden.shape[0]
    whole = pl.BlockSpec(memory_space=pltpu.VMEM)
    out_shape = [
        jax.ShapeDtypeStruct((seq_len, D), jnp.float32),
        jax.ShapeDtypeStruct((D, 4 * D), jnp.bfloat16),
        jax.ShapeDtypeStruct((8, D), jnp.float32),
    ]
    if layer_index > 0:
        out_shape.append(jax.ShapeDtypeStruct((spread_back.shape[1], D), jnp.bfloat16))
    return pl.pallas_call(
        functools.partial(backward_kernel, layer_index, capacity),
        out_shape=out_shape,
        in_specs=[pl.BlockSpec(memory_space=pltpu.SMEM)]
        + [whole] * 10
        + [pl.BlockSpec(memory_space=pl.ANY)]
        + [whole] * (4 + len(extra)),
        out_specs=[whole] * len(out_shape),
        scratch_shapes=[
            pltpu.VMEM((seq_len, D), jnp.bfloat16),
            pltpu.VMEM((2, seq_len, D), jnp.float32),
            pltpu.VMEM((4, D, D), jnp.bfloat16),
            pltpu.SemaphoreType.DMA((4,)),
        ],
        compiler_params=pltpu.CompilerParams(vmem_limit_bytes=60 * 1024 * 1024),
        cost_estimate=pl.CostEstimate(
            flops=8 * seq_len * D * D * 3, bytes_accessed=32 * 1024 * 1024, transcendentals=1 << 20
        ),
    )(
        prefix,
        grad,
        back_inputs,
        logit_low,
        hidden,
        projected,
        queries,
        keys,
        values,
        attended,
        middle,
        weights,
        gains,
        turns,
        router,
        spread_back,
        *extra,
    )


def turn_tables(seq_len):
    position = jnp.arange(seq_len, dtype=jnp.float32)[:, None]
    frequency = ROPE_BASE ** (-jnp.arange(HDIM // 2, dtype=jnp.float32) * 2.0 / HDIM)
    angles = position * frequency[None, :]
    cosines, sines = jnp.cos(angles), jnp.sin(angles)
    return jnp.stack(
        [
            jnp.concatenate([cosines] * 4, axis=1),
            jnp.concatenate([-sines, sines, -sines, sines], axis=1),
        ]
    )


def silu_parts(gate_up):
    gate_part, up_part = gate_up[:, :F], gate_up[:, F:]
    sigmoid = 1.0 / (1.0 + jnp.exp(-gate_part))
    return gate_part, up_part, sigmoid


def fetch_expert(place_ref, part_refs, up_ref, down_ref, copy_sem):
    copies = []
    rows = part_refs[0].shape[0]
    for turn, part_ref in enumerate(part_refs):
        place = pl.multiple_of(place_ref[turn] * rows, rows)
        copies.append(
            pltpu.make_async_copy(
                part_ref.at[:, pl.ds(0, 2 * F)],
                up_ref.at[pl.ds(place, rows), :],
                copy_sem.at[len(copies)],
            )
        )
        for block in range(F // rows):
            copies.append(
                pltpu.make_async_copy(
                    part_ref.at[:, pl.ds(2 * F + block * rows, rows)],
                    down_ref.at[pl.ds(block * rows, rows), pl.ds(place, rows)],
                    copy_sem.at[len(copies)],
                )
            )
    for copy in copies:
        copy.start()
    for copy in copies:
        copy.wait()


def expert_kernel(part_count, row_block, place_ref, received_ref, *refs):
    part_refs, (produced_ref, up_ref, down_ref, copy_sem) = refs[:part_count], refs[part_count:]
    fetch_expert(place_ref, part_refs, up_ref, down_ref, copy_sem)

    @pl.loop(0, received_ref.shape[0] // row_block)
    def _(step):
        rows = pl.ds(pl.multiple_of(step * row_block, row_block), row_block)
        gate_part, up_part, sigmoid = silu_parts(dot_nn(received_ref[rows, :], up_ref[...]))
        activated = (gate_part * sigmoid * up_part).astype(jnp.bfloat16)
        produced_ref[rows, :] = dot_nn(activated, down_ref[...]).astype(jnp.bfloat16)


def expert_specs(parts):
    rows = parts[0].shape[0]
    whole = pl.BlockSpec(memory_space=pltpu.VMEM)
    specs = [pl.BlockSpec(memory_space=pltpu.SMEM)]
    apart = [pl.BlockSpec(memory_space=pl.ANY)] * len(parts)
    scratch = [
        pltpu.VMEM((D, 2 * F), jnp.bfloat16),
        pltpu.VMEM((F, D), jnp.bfloat16),
        pltpu.SemaphoreType.DMA((len(parts) * (1 + F // rows),)),
    ]
    return whole, specs, apart, scratch


def run_expert(places, received, parts):
    whole, specs, apart, scratch = expert_specs(parts)
    slot_total = received.shape[0]
    return pl.pallas_call(
        functools.partial(expert_kernel, len(parts), slot_total // 4),
        out_shape=jax.ShapeDtypeStruct((slot_total, D), jnp.bfloat16),
        in_specs=specs + [whole] + apart,
        out_specs=whole,
        scratch_shapes=scratch,
        compiler_params=pltpu.CompilerParams(vmem_limit_bytes=56 * 1024 * 1024),
        cost_estimate=pl.CostEstimate(
            flops=slot_total * D * F * 6, bytes_accessed=8 * 1024 * 1024, transcendentals=1 << 19
        ),
    )(places, received, *parts)


def expert_back_kernel(part_count, row_block, place_ref, received_ref, pull_ref, *refs):
    part_refs, refs = refs[:part_count], refs[part_count:]
    input_grad_ref, gate_grad_ref, activated_ref, up_ref, down_ref, copy_sem = refs
    fetch_expert(place_ref, part_refs, up_ref, down_ref, copy_sem)

    @pl.loop(0, received_ref.shape[0] // row_block)
    def _(step):
        rows = pl.ds(pl.multiple_of(step * row_block, row_block), row_block)
        gate_part, up_part, sigmoid = silu_parts(dot_nn(received_ref[rows, :], up_ref[...]))
        side = gate_part * sigmoid
        activated_ref[rows, :] = (side * up_part).astype(jnp.bfloat16)
        pulled = dot_nt(pull_ref[rows, :], down_ref[...]).astype(jnp.bfloat16)
        pulled = pulled.astype(jnp.float32)
        gate_side = pulled * up_part * sigmoid * (1.0 + gate_part * (1.0 - sigmoid))
        gate_grad_ref[rows, :F] = gate_side.astype(jnp.bfloat16)
        gate_grad_ref[rows, F:] = (pulled * side).astype(jnp.bfloat16)
        input_grad_ref[rows, :] = dot_nt(gate_grad_ref[rows, :], up_ref[...]).astype(jnp.bfloat16)


def run_expert_back(places, received, pull, parts):
    whole, specs, apart, scratch = expert_specs(parts)
    slot_total = received.shape[0]
    return pl.pallas_call(
        functools.partial(expert_back_kernel, len(parts), slot_total // 4),
        out_shape=(
            jax.ShapeDtypeStruct((slot_total, D), jnp.bfloat16),
            jax.ShapeDtypeStruct((slot_total, 2 * F), jnp.bfloat16),
            jax.ShapeDtypeStruct((slot_total, F), jnp.bfloat16),
        ),
        in_specs=specs + [whole] * 2 + apart,
        out_specs=[whole] * 3,
        scratch_shapes=scratch,
        compiler_params=pltpu.CompilerParams(vmem_limit_bytes=56 * 1024 * 1024),
        cost_estimate=pl.CostEstimate(
            flops=slot_total * D * F * 12, bytes_accessed=12 * 1024 * 1024, transcendentals=1 << 19
        ),
    )(places, received, pull, *parts)


def expert_grad_kernel(
    part_count, place_ref, received_ref, pull_ref, gate_grad_ref, activated_ref, *refs
):
    out_refs, (up_ref, down_ref) = refs[:part_count], refs[part_count:]
    block = 256

    @pl.loop(0, D // block)
    def _(step):
        columns = pl.ds(pl.multiple_of(step * block, block), block)
        up_ref[columns, :] = dot_tn(received_ref[:, columns], gate_grad_ref[...]).astype(
            jnp.bfloat16
        )

    @pl.loop(0, F // block)
    def _(step):
        columns = pl.ds(pl.multiple_of(step * block, block), block)
        down_ref[columns, :] = dot_tn(activated_ref[:, columns], pull_ref[...]).astype(
            jnp.bfloat16
        )

    rows = out_refs[0].shape[0]
    for turn, out_ref in enumerate(out_refs):
        place = pl.multiple_of(place_ref[turn] * rows, rows)
        out_ref[:, : 2 * F] = up_ref[pl.ds(place, rows), :]
        for part in range(F // rows):
            out_ref[:, 2 * F + part * rows : 2 * F + (part + 1) * rows] = down_ref[
                part * rows : (part + 1) * rows, pl.ds(place, rows)
            ]


def run_expert_grad(places, received, pull, gate_grad, activated, piece_rows):
    whole = pl.BlockSpec(memory_space=pltpu.VMEM)
    part_count = D // piece_rows
    slot_total = received.shape[0]
    return pl.pallas_call(
        functools.partial(expert_grad_kernel, part_count),
        out_shape=[jax.ShapeDtypeStruct((piece_rows, 3 * F), jnp.bfloat16)] * part_count,
        in_specs=[pl.BlockSpec(memory_space=pltpu.SMEM)] + [whole] * 4,
        out_specs=[whole] * part_count,
        scratch_shapes=[
            pltpu.VMEM((D, 2 * F), jnp.bfloat16),
            pltpu.VMEM((F, D), jnp.bfloat16),
        ],
        compiler_params=pltpu.CompilerParams(vmem_limit_bytes=56 * 1024 * 1024),
        cost_estimate=pl.CostEstimate(
            flops=slot_total * D * F * 6, bytes_accessed=12 * 1024 * 1024, transcendentals=0
        ),
    )(places, received, pull, gate_grad, activated)


def outgoing_pull(grad, spread, gates, capacity):
    high, rest = two_terms(grad)
    wide = dot_nn(spread, high) + dot_nn(spread, rest)
    return (slot_gates(spread, gates, capacity) * wide).astype(jnp.bfloat16)


def first_pull_kernel(capacity, picked_ref, rows_ref, spread_ref, gates_ref, grad_ref, out_ref):
    grad_ref[...] = jnp.zeros_like(grad_ref)
    for place in range(rows_ref.shape[0]):
        grad_ref[pl.ds(picked_ref[place], 1), :] = rows_ref[place : place + 1, :]
    out_ref[...] = outgoing_pull(grad_ref[...], spread_ref[...], gates_ref[...], capacity)


def first_pull(capacity, picked, rows, spread, gates):
    whole = pl.BlockSpec(memory_space=pltpu.VMEM)
    return pl.pallas_call(
        functools.partial(first_pull_kernel, capacity),
        out_shape=(
            jax.ShapeDtypeStruct((spread.shape[1], D), jnp.float32),
            jax.ShapeDtypeStruct((spread.shape[0], D), jnp.bfloat16),
        ),
        in_specs=[pl.BlockSpec(memory_space=pltpu.SMEM)] + [whole] * 3,
        out_specs=[whole] * 2,
        compiler_params=pltpu.CompilerParams(vmem_limit_bytes=48 * 1024 * 1024),
        cost_estimate=pl.CostEstimate(
            flops=4 * spread.shape[0] * spread.shape[1] * D,
            bytes_accessed=5 * 1024 * 1024,
            transcendentals=0,
        ),
    )(picked, rows, spread, gates)


def router_kernel(
    capacity, grad_ref, returned_ref, spread_back_ref, probs_ref, ffn_ref, low_ref, router_grad_ref
):
    high, rest = two_terms(grad_ref[...])
    dots = dot_nt(high, returned_ref[...]) + dot_nt(rest, returned_ref[...])
    dots = dots * spread_back_ref[...].astype(jnp.float32)
    slot_total = returned_ref.shape[0]
    slot = lax.broadcasted_iota(jnp.int32, (slot_total, LANES), 0) // capacity
    lane = lax.broadcasted_iota(jnp.int32, (slot_total, LANES), 1)
    owner = jnp.where(slot == lane, 1.0, 0.0).astype(jnp.bfloat16)
    high, rest = two_terms(dots)
    pull = dot_nn(high, owner) + dot_nn(rest, owner)
    probs = probs_ref[...]
    low = (probs * (pull - jnp.sum(probs * pull, axis=-1, keepdims=True))).astype(jnp.bfloat16)
    low_ref[...] = low
    router_grad_ref[...] = dot_tn(ffn_ref[...], low)


def router_back(capacity, grad, returned, spread_back, probs, ffn):
    whole = pl.BlockSpec(memory_space=pltpu.VMEM)
    seq_len = grad.shape[0]
    return pl.pallas_call(
        functools.partial(router_kernel, capacity),
        out_shape=(
            jax.ShapeDtypeStruct((seq_len, LANES), jnp.bfloat16),
            jax.ShapeDtypeStruct((D, LANES), jnp.float32),
        ),
        in_specs=[whole] * 5,
        out_specs=[whole] * 2,
        compiler_params=pltpu.CompilerParams(vmem_limit_bytes=48 * 1024 * 1024),
        cost_estimate=pl.CostEstimate(
            flops=4 * seq_len * returned.shape[0] * D,
            bytes_accessed=6 * 1024 * 1024,
            transcendentals=0,
        ),
    )(grad, returned, spread_back, probs, ffn)


def final_kernel(
    capacity,
    gain_row,
    picked_ref,
    middle_ref,
    gates_ref,
    returned_ref,
    spread_ref,
    spread_back_ref,
    gain_ref,
    rows_ref,
    low_ref,
):
    count = rows_ref.shape[0]
    for place in range(count):
        rows_ref[place : place + 1, :] = middle_ref[pl.ds(picked_ref[place], 1), :]
    sublane = lax.broadcasted_iota(jnp.int32, (count, LANES), 0)
    wanted = jnp.zeros((count, LANES), jnp.int32)
    for place in range(count):
        wanted = jnp.where(sublane == place, picked_ref[place], wanted)
    seq_len = middle_ref.shape[0]
    token = lax.broadcasted_iota(jnp.int32, (count, seq_len), 1)
    wanted = jnp.concatenate([wanted] * (seq_len // LANES), axis=1)
    chosen = jnp.where(token == wanted, 1.0, 0.0).astype(jnp.bfloat16)
    slots = dot_nn(chosen, spread_back_ref[...]).astype(jnp.bfloat16)
    weighted = slot_gates(spread_ref[...], gates_ref[...], capacity) * returned_ref[...].astype(
        jnp.float32
    )
    high, rest = two_terms(weighted)
    rows = rows_ref[...] + (dot_nn(slots, high) + dot_nn(slots, rest))
    rows_ref[...] = rows
    low_ref[...] = (rows * inverse_root(rows) * gain_ref[gain_row : gain_row + 1, :]).astype(
        jnp.bfloat16
    )


def final_rows_of(capacity, gain_row, picked, middle, gates, returned, spread, spread_back, gains):
    whole = pl.BlockSpec(memory_space=pltpu.VMEM)
    count = picked.shape[0]
    return pl.pallas_call(
        functools.partial(final_kernel, capacity, gain_row),
        out_shape=(
            jax.ShapeDtypeStruct((count, D), jnp.float32),
            jax.ShapeDtypeStruct((count, D), jnp.bfloat16),
        ),
        in_specs=[pl.BlockSpec(memory_space=pltpu.SMEM)] + [whole] * 6,
        out_specs=[whole] * 2,
        compiler_params=pltpu.CompilerParams(vmem_limit_bytes=48 * 1024 * 1024),
        cost_estimate=pl.CostEstimate(
            flops=1 << 28, bytes_accessed=5 * 1024 * 1024, transcendentals=0
        ),
    )(picked, middle, gates, returned, spread, spread_back, gains)


def tie(first, second):
    return lax.optimization_barrier((first, second))


def swap_pairs(row_groups, turn_plane, turn_row):
    pairs = []
    for plane in range(PLANES):
        for row in range(row_groups):
            for part in range(PLANES):
                source = (plane * row_groups + row) * PLANES + part
                target_plane = (plane + SHIFTS[part ^ turn_plane]) % PLANES
                target_row = (row + turn_row) % row_groups
                pairs.append((source, (target_plane * row_groups + target_row) * PLANES + plane))
    return pairs


def all_turns(row_groups):
    return [(plane, row) for row in range(row_groups) for plane in range(PLANES)]


def shift_inverse(shift):
    return jnp.array(SHIFTS, jnp.int32)[shift]


def part_of_turn(turn_plane):
    me_plane = lax.axis_index("z")
    me_part = lax.axis_index(("y", "c"))
    return shift_inverse((me_plane - me_part) % PLANES) ^ turn_plane


def piece_place(turn, row_groups):
    turn_plane, turn_row = turn
    row = (lax.axis_index("h") - turn_row) % row_groups
    return row * PLANES + part_of_turn(turn_plane)


def spread_experts(piece, row_groups):
    return [
        lax.ppermute(
            piece, ("z", "h", "y", "c"), swap_pairs(row_groups, turn_plane, turn_row)
        )
        for turn_plane, turn_row in all_turns(row_groups)
    ]


def return_expert_grads(pieces, row_groups):
    arrived = []
    for piece, turn in zip(pieces, all_turns(row_groups)):
        back = [(target, source) for source, target in swap_pairs(row_groups, *turn)]
        arrived.append(lax.ppermute(piece, ("z", "h", "y", "c"), back))
    return arrived


def take_piece(pieces, place):
    return lax.dynamic_index_in_dim(pieces, place, 0, False)


def scatter_axis(values, axis_name, dim):
    count = lax.axis_size(axis_name)
    if count == 1:
        return jnp.squeeze(values, dim)
    me = lax.axis_index(axis_name)
    total = lax.dynamic_index_in_dim(values, me, dim, False).astype(jnp.float32)
    for turn in range(1, count):
        sent = lax.dynamic_index_in_dim(values, (me + turn) % count, dim, False)
        got = lax.ppermute(sent, axis_name, [(i, (i + turn) % count) for i in range(count)])
        total = total + got.astype(jnp.float32)
    return total.astype(jnp.bfloat16)


def scatter_near(values):
    sizes = [lax.axis_size(name) for name in AXES]
    rows, columns = values.shape
    count = 1
    for size in sizes:
        count *= size
    blocks = values.reshape(*sizes, rows // count, columns)
    return scatter_axis(blocks, "c", 4)


def scatter_middle(blocks):
    half = blocks.shape[-1] // 2
    return [
        scatter_axis(blocks[..., :half], "x", 1),
        scatter_axis(blocks[..., half:], "y", 3),
    ]


def scatter_turn(parts):
    first = scatter_axis(parts[0], "y", 2)
    second = scatter_axis(parts[1], "x", 1)
    return scatter_axis(jnp.concatenate([first, second], axis=-1), "h", 1)


def scatter_planes(joined):
    planes = lax.axis_size("z")
    me = lax.axis_index("z")
    parts = [take_piece(joined, me)]
    for turn in range(1, planes):
        sent = take_piece(joined, (me + turn) % planes)
        parts.append(lax.ppermute(sent, "z", [(i, (i + turn) % planes) for i in range(planes)]))
    return parts


def scatter_sum(parts):
    total = parts[0].astype(jnp.float32)
    for part in parts[1:]:
        total = total + part.astype(jnp.float32)
    return total


def send_all(values):
    return lax.all_to_all(values, AXES, split_axis=0, concat_axis=0, tiled=True)


def send_plane(values):
    return lax.all_to_all(values, ("x", "y", "c"), split_axis=0, concat_axis=0, tiled=True)


def three_terms(values):
    first = lax.reduce_precision(values, 8, 7)
    second = lax.reduce_precision(values - first, 8, 7)
    third = lax.reduce_precision(values - first - second, 8, 7)
    return [first, second, third]

def adam_step(weight, mean_old, square_old, gradient):
    mean_new = BETA_ONE * mean_old + (1.0 - BETA_ONE) * gradient
    square_new = BETA_TWO * square_old + (1.0 - BETA_TWO) * gradient * gradient
    bias_one = 1.0 - BETA_ONE**ADAM_STEP
    bias_two = 1.0 - BETA_TWO**ADAM_STEP
    update = -LEARN_RATE * (
        mean_new / bias_one / (jnp.sqrt(square_new / bias_two) + ADAM_EPS) + DECAY_RATE * weight
    )
    return (mean_new, square_new, update)


def shards(
    tokens,
    prefix,
    routes,
    picked,
    loss_ids,
    teacher_logits,
    embedding,
    embedding_mean,
    embedding_square,
    attention,
    attention_mean,
    attention_square,
    router,
    router_mean,
    router_square,
    norm_gains,
    gains_mean,
    gains_square,
    expert_up,
    upward_mean,
    upward_square,
    expert_down,
    downward_mean,
    downward_square,
    output_table,
    table_mean,
    table_square,
):
    devices_all = lax.axis_size(AXES)
    me_all = lax.axis_index(AXES)
    row_groups = lax.axis_size("h")
    columns_x = lax.axis_size("x")
    seq_len = routes.shape[0]
    layer_count = attention.shape[0]
    experts_all = router.shape[2]
    capacity = 9 * seq_len * TOPK // (8 * experts_all)
    column_count = embedding.shape[1]
    prefix_len = prefix[0]
    slot_total = experts_all * capacity
    piece_rows = expert_up.shape[2]
    gain_count = norm_gains.shape[0]
    group_experts = [
        (group % PLANES) * columns_x + group // PLANES for group in range(experts_all)
    ]
    group_order = jnp.array(group_experts, jnp.int32)
    group_back = jnp.array(
        [group_experts.index(expert) for expert in range(experts_all)], jnp.int32
    )

    attention_low = lax.all_gather(attention.astype(jnp.bfloat16), AXES, axis=1, tiled=True)

    table_low = embedding.astype(jnp.bfloat16)
    looked_up = jnp.take(table_low, tokens, axis=0).reshape(devices_all, seq_len * column_count)
    small_count = gain_count + layer_count * experts_all
    small = jnp.concatenate(
        [norm_gains.T, router.transpose(1, 0, 2).reshape(column_count, layer_count * experts_all)],
        axis=1,
    ).astype(jnp.bfloat16)
    small = jnp.broadcast_to(
        small.reshape(1, column_count * small_count), (devices_all, column_count * small_count)
    )
    arrived_rows = send_all(jnp.concatenate([looked_up, small], axis=1))
    hidden = (
        arrived_rows[:, : seq_len * column_count]
        .reshape(devices_all, seq_len, column_count)
        .transpose(1, 0, 2)
        .reshape(seq_len, D)
        .astype(jnp.float32)
    )
    small_all = arrived_rows[:, seq_len * column_count :].reshape(D, small_count)
    gain_rows = jnp.pad(
        small_all[:, :gain_count].T.astype(jnp.float32), ((0, 16 - gain_count), (0, 0))
    )
    router_low = jnp.pad(
        small_all[:, gain_count:]
        .reshape(D, layer_count, experts_all)
        .transpose(1, 0, 2)[:, :, group_order],
        ((0, 0), (0, 0), (0, LANES - experts_all)),
    )

    head_low = output_table.astype(jnp.bfloat16)
    vocab_local = head_low.shape[0]
    teacher_log = jax.nn.log_softmax(teacher_logits, axis=1)
    teacher_prob = jnp.exp(teacher_log)
    position_count = loss_ids.shape[0]
    teacher_mass = jnp.sum(teacher_prob, axis=1)
    coefficients = jnp.concatenate(
        [jnp.ones((position_count, 1), jnp.float32), teacher_prob], axis=1
    )
    local_ids = loss_ids - me_all * vocab_local
    vocab_place = jnp.arange(vocab_local, dtype=jnp.int32)
    marked = jnp.sum(
        jnp.where(
            local_ids[:, :, None] == vocab_place[None, None, :], coefficients[:, :, None], 0.0
        ),
        axis=1,
    )
    marked_pull = jnp.dot(
        marked.astype(jnp.bfloat16), head_low, preferred_element_type=jnp.float32
    )
    own_count = position_count // devices_all
    marked_arrived = send_all(
        marked_pull.astype(jnp.bfloat16).reshape(devices_all, own_count, D)
    )

    expert_parts = []
    for layer_index in range(layer_count):
        if layer_index == 1:
            attention_low, marked, marked_arrived = lax.optimization_barrier(
                (attention_low, marked, marked_arrived)
            )
        down_piece = (
            expert_down[0, layer_index]
            .reshape(F // piece_rows, piece_rows, piece_rows)
            .transpose(1, 0, 2)
            .reshape(piece_rows, F)
        )
        piece = jnp.concatenate([expert_up[0, layer_index], down_piece], axis=1).astype(
            jnp.bfloat16
        )
        if layer_index > 0:
            piece, attention_low = tie(piece, attention_low)
        expert_parts.append(spread_experts(piece, row_groups))

    member = jnp.any(routes[:, :, None] == group_order[None, None, :], axis=1)
    before = jnp.dot(
        jnp.tril(jnp.ones((seq_len, seq_len), jnp.bfloat16), -1),
        member.astype(jnp.bfloat16),
        preferred_element_type=jnp.float32,
    ).astype(jnp.int32)
    spread = (
        (before.T[:, None, :] == jnp.arange(capacity, dtype=jnp.int32)[None, :, None])
        & member.T[:, None, :]
    ).astype(jnp.bfloat16)
    spread_flat = spread.reshape(slot_total, seq_len)
    spread_back = spread_flat.T
    kept = jnp.pad(
        (member & (before < capacity)).astype(jnp.float32), ((0, 0), (0, LANES - experts_all))
    )
    turns = turn_tables(seq_len)
    places = jnp.stack([piece_place(turn, row_groups) for turn in all_turns(row_groups)]).astype(
        jnp.int32
    )

    stored = []
    extra = ()
    for layer_index in range(layer_count):
        saved = forward_layer(
            layer_index,
            capacity,
            experts_all,
            prefix,
            hidden,
            extra,
            attention_low,
            gain_rows,
            turns,
            router_low,
            kept,
            spread_flat,
            spread_back,
        )
        hidden = saved[6]
        gates, outgoing = saved[9], saved[10]
        if layer_index > 0:
            expert_parts[layer_index][2], outgoing = tie(expert_parts[layer_index][2], outgoing)
        received = send_plane(outgoing.reshape(experts_all, capacity, D)).reshape(slot_total, D)
        upcoming = expert_parts[layer_index + 1] if layer_index + 1 < layer_count else None
        if upcoming is not None:
            upcoming[0], received = tie(upcoming[0], received)
        produced = run_expert(places, received, expert_parts[layer_index])
        returned = send_plane(produced.reshape(experts_all, capacity, D)).reshape(slot_total, D)
        if upcoming is not None:
            upcoming[1], returned = tie(upcoming[1], returned)
        stored.append((saved, received, returned))
        extra = (gates, returned)

    final_gain = gain_rows[4 * layer_count]
    final_rows, final_low = final_rows_of(
        capacity,
        4 * layer_count,
        picked,
        hidden,
        *extra,
        spread_flat,
        spread_back,
        gain_rows,
    )
    all_rows = send_all(jnp.broadcast_to(final_low[None], (devices_all, own_count, D))).reshape(
        position_count, D
    )
    logits = jnp.einsum("pd,vd->pv", all_rows, head_low, preferred_element_type=jnp.float32)
    local_peak = jnp.max(logits, axis=1)
    local_exp = jnp.exp(logits - local_peak[:, None])
    local_sum = jnp.sum(local_exp, axis=1)
    local_dot = jnp.sum(marked * logits, axis=1)
    pull = jnp.dot(local_exp.astype(jnp.bfloat16), head_low, preferred_element_type=jnp.float32)
    stats = jnp.stack(
        three_terms(local_peak) + three_terms(local_sum) + three_terms(local_dot), axis=1
    )
    stats = jnp.pad(stats, ((0, 0), (0, 128 - stats.shape[1])))
    pull_sent = jnp.concatenate([pull, stats], axis=1).astype(jnp.bfloat16)
    pull_got = send_all(pull_sent.reshape(devices_all, own_count, D + 128)).astype(jnp.float32)
    stats_got = pull_got[:, :, D:]
    peaks = jnp.sum(stats_got[:, :, 0:3], axis=2)
    sums = jnp.sum(stats_got[:, :, 3:6], axis=2)
    dots = jnp.sum(stats_got[:, :, 6:9], axis=2)
    peak_own = jnp.max(peaks, axis=0)
    log_norm_own = peak_own + jnp.log(jnp.sum(sums * jnp.exp(peaks - peak_own), axis=0))
    mass_own = lax.dynamic_slice_in_dim(teacher_mass, me_all * own_count, own_count)
    entropy_own = lax.dynamic_slice_in_dim(
        jnp.sum(teacher_prob * teacher_log, axis=1), me_all * own_count, own_count
    )
    loss_own = (1.0 + mass_own) * log_norm_own - jnp.sum(dots, axis=0) + entropy_own
    scale_own = (1.0 + mass_own)[None, :] * jnp.exp(peaks - log_norm_own[None, :])
    marked_total = jnp.sum(marked_arrived.astype(jnp.float32), axis=0)
    final_grad = (
        jnp.sum(scale_own[:, :, None] * pull_got[:, :, :D], axis=0) - marked_total
    ) / position_count
    spread_stats = jnp.concatenate([log_norm_own, loss_own]).reshape(1, 2 * own_count)
    stats_all = send_all(jnp.broadcast_to(spread_stats, (devices_all, 2 * own_count)))
    log_norm = stats_all[:, :own_count].reshape(position_count)
    loss_value = jnp.sum(stats_all[:, own_count:]) / position_count
    grad_logits = (
        jnp.exp(logits - log_norm[:, None]) * (1.0 + teacher_mass)[:, None] - marked
    ) / position_count
    table_grad = jnp.einsum(
        "pv,pd->vd",
        grad_logits.astype(jnp.bfloat16),
        all_rows,
        preferred_element_type=jnp.float32,
    )
    rows_grad, final_gain_grad = norm_back(final_rows, final_gain, final_grad)
    grad_hidden, sent_back = first_pull(capacity, picked, rows_grad, spread_flat, extra[0])
    gain_parts = [None] * (4 * layer_count) + [final_gain_grad]
    attention_parts = [None] * layer_count
    router_parts = [None] * layer_count
    piece_parts = [None] * layer_count
    for layer_index in reversed(range(layer_count)):
        saved, received, returned = stored[layer_index]
        hidden_in, projected, queries, keys, values, attended, middle, ffn_low, probs = saved[:9]
        upper = layer_index + 1 if layer_index + 1 < layer_count else None
        output_grad = send_plane(sent_back.reshape(experts_all, capacity, D)).reshape(
            slot_total, D
        )
        logit_low, router_parts[layer_index] = router_back(
            capacity, grad_hidden, returned, spread_back, probs, ffn_low
        )
        if upper is not None:
            near, output_grad = tie(attention_parts[upper], output_grad)
            middle_parts = scatter_middle(near)
        input_grad, gate_grad, activated = run_expert_back(
            places, received, output_grad, expert_parts[layer_index]
        )
        back_inputs = send_plane(input_grad.reshape(experts_all, capacity, D)).reshape(
            slot_total, D
        )
        grad_pieces = run_expert_grad(
            places, received, output_grad, gate_grad, activated, piece_rows
        )
        piece_parts[layer_index] = return_expert_grads(grad_pieces, row_groups)
        if upper is not None:
            piece_parts[upper][2:], back_inputs = tie(piece_parts[upper][2:], back_inputs)
        lower = (spread_flat, stored[layer_index - 1][0][9]) if layer_index > 0 else ()
        results = backward_layer(
            layer_index,
            capacity,
            prefix,
            grad_hidden,
            back_inputs,
            logit_low,
            hidden_in,
            projected,
            queries,
            keys,
            values,
            attended,
            middle,
            attention_low,
            gain_rows,
            turns,
            router_low,
            spread_back,
            lower,
        )
        grad_hidden, weight_grad, gain_grads = results[:3]
        gain_parts[4 * layer_index : 4 * layer_index + 4] = list(gain_grads[:4])
        if layer_index > 0:
            sent_back = results[3]
            piece_parts[layer_index][:2], sent_back = tie(piece_parts[layer_index][:2], sent_back)
        attention_parts[layer_index] = scatter_near(weight_grad)
        if upper is not None:
            middle_parts, grad_hidden = tie(middle_parts, grad_hidden)
            attention_parts[upper] = scatter_sum(scatter_planes(scatter_turn(middle_parts)))

    sending = (
        grad_hidden.astype(jnp.bfloat16)
        .reshape(seq_len, devices_all, column_count)
        .transpose(1, 0, 2)
        .reshape(devices_all, seq_len * column_count)
    )
    small_grads = jnp.concatenate(
        [jnp.stack(gain_parts, axis=1)] + [part[:, group_back] for part in router_parts], axis=1
    ).astype(jnp.bfloat16)
    arrived_grads = send_all(
        jnp.concatenate(
            [sending, small_grads.reshape(devices_all, column_count * small_count)], axis=1
        )
    )
    attention_parts[0], arrived_grads, piece_parts = lax.optimization_barrier(
        (attention_parts[0], arrived_grads, piece_parts)
    )
    attention_parts[0] = scatter_sum(
        scatter_planes(scatter_turn(scatter_middle(attention_parts[0])))
    )
    up_parts, down_parts = [], []
    for parts in piece_parts:
        piece_grad = scatter_sum(parts)
        up_parts.append(piece_grad[:, : 2 * F])
        down_parts.append(
            piece_grad[:, 2 * F :]
            .reshape(piece_rows, F // piece_rows, piece_rows)
            .transpose(1, 0, 2)
            .reshape(F, piece_rows)
        )
    embedding_grad = jax.ops.segment_sum(
        arrived_grads[:, : seq_len * column_count]
        .astype(jnp.float32)
        .reshape(devices_all * seq_len, column_count),
        tokens,
        num_segments=embedding.shape[0],
    )
    small_total = jnp.sum(
        arrived_grads[:, seq_len * column_count :].astype(jnp.float32), axis=0
    ).reshape(column_count, small_count)
    gains_grad = small_total[:, :gain_count].T
    router_grad = (
        small_total[:, gain_count:]
        .reshape(column_count, layer_count, experts_all)
        .transpose(1, 0, 2)
    )
    attention_grad = jnp.stack(attention_parts)
    upward_grad = jnp.stack(up_parts)[None]
    downward_grad = jnp.stack(down_parts)[None]
    embedding_mean_next, embedding_square_next, embedding_update = adam_step(
        embedding, embedding_mean, embedding_square, embedding_grad
    )
    attention_mean_next, attention_square_next, attention_update = adam_step(
        attention, attention_mean, attention_square, attention_grad
    )
    router_mean_next, router_square_next, router_update = adam_step(
        router, router_mean, router_square, router_grad
    )
    gains_mean_next, gains_square_next, gains_update = adam_step(
        norm_gains, gains_mean, gains_square, gains_grad
    )
    upward_mean_next, upward_square_next, upward_update = adam_step(
        expert_up, upward_mean, upward_square, upward_grad
    )
    downward_mean_next, downward_square_next, downward_update = adam_step(
        expert_down, downward_mean, downward_square, downward_grad
    )
    table_mean_next, table_square_next, table_update = adam_step(
        output_table, table_mean, table_square, table_grad
    )
    return (
        loss_value,
        embedding_mean_next,
        embedding_square_next,
        embedding_update,
        attention_mean_next,
        attention_square_next,
        attention_update,
        router_mean_next,
        router_square_next,
        router_update,
        gains_mean_next,
        gains_square_next,
        gains_update,
        upward_mean_next,
        upward_square_next,
        upward_update,
        downward_mean_next,
        downward_square_next,
        downward_update,
        table_mean_next,
        table_square_next,
        table_update,
    )


def solution(mesh):
    expert_count, shard_count = mesh.devices.shape
    mesh = Mesh(
        mesh.devices.reshape(PLANES, expert_count // PLANES, shard_count // 4, 2, 2), AXES
    )
    return jax.shard_map(
        shards,
        mesh=mesh,
        in_specs=(
            P(),
            P(AXES),
            P(AXES, None),
            P(AXES),
            P(),
            P(),
            P(None, AXES),
            P(None, AXES),
            P(None, AXES),
            P(None, AXES, None),
            P(None, AXES, None),
            P(None, AXES, None),
            P(None, AXES, None),
            P(None, AXES, None),
            P(None, AXES, None),
            P(None, AXES),
            P(None, AXES),
            P(None, AXES),
            P(("z", "x"), None, ("h", "y", "c"), None),
            P(("z", "x"), None, ("h", "y", "c"), None),
            P(("z", "x"), None, ("h", "y", "c"), None),
            P(("z", "x"), None, None, ("h", "y", "c")),
            P(("z", "x"), None, None, ("h", "y", "c")),
            P(("z", "x"), None, None, ("h", "y", "c")),
            P(AXES, None),
            P(AXES, None),
            P(AXES, None),
        ),
        out_specs=(
            P(),
            P(None, AXES),
            P(None, AXES),
            P(None, AXES),
            P(None, AXES, None),
            P(None, AXES, None),
            P(None, AXES, None),
            P(None, AXES, None),
            P(None, AXES, None),
            P(None, AXES, None),
            P(None, AXES),
            P(None, AXES),
            P(None, AXES),
            P(("z", "x"), None, ("h", "y", "c"), None),
            P(("z", "x"), None, ("h", "y", "c"), None),
            P(("z", "x"), None, ("h", "y", "c"), None),
            P(("z", "x"), None, None, ("h", "y", "c")),
            P(("z", "x"), None, None, ("h", "y", "c")),
            P(("z", "x"), None, None, ("h", "y", "c")),
            P(AXES, None),
            P(AXES, None),
            P(AXES, None),
        ),
        check_vma=False,
    )
```

time: 1360 us -> 1240 us (0.912)
  Pallas kernels: 0 us -> 151 us
  matrix products: 171 us -> 25.3 us
  blocking collectives: 0 us -> 95.1 us
  local copies, waits for them, and re-layouts: 248 us -> 153 us
  other arithmetic: 237 us -> 165 us
  waiting for transfers between devices: 469 us -> 424 us
    pallas_call x0 -> x14, Pallas kernels: none -> 151 us  [the longest x2 41.8 us: backward_layer(): pl.pallas_call(functools.partial(backward_kernel, layer_index, capacity),...]
    dot_general x58 -> x0, matrix products: 142 us -> none  [the longest x2 10.6 us: shards(): jnp.dot(received, upward_low[layer_index], preferred_element_type=jnp.flo...]
    all_to_all x0 -> x3, blocking collectives: none -> 95.1 us  [the longest x2 63.7 us: send_plane(): lax.all_to_all(values, ('x', 'y', 'c'), split_axis=0, concat_axis=0, tile...]
    ppermute x22, starting transfers between devices: 52.1 us -> 122 us  [the longest x8 66.8 us: return_expert_grads(): arrived.append(lax.ppermute(piece, ('z', 'h', 'y', 'c'), back))]
    all_to_all x6 -> x5, waiting for transfers between devices: 22.3 us -> 76.9 us  [send_all(): return lax.all_to_all(values, AXES, split_axis=0, concat_axis=0, tiled=True)]
    all_gather x1, waiting for transfers between devices: 60.2 us -> 7.21 us  [shards(): lax.all_gather(attention.astype(jnp.bfloat16), AXES, axis=1, tiled=True)]
    all_to_all x8 -> x6, starting transfers between devices: 77.4 us -> 31.3 us  [send_plane(): lax.all_to_all(values, ('x', 'y', 'c'), split_axis=0, concat_axis=0, tile...]
    reshape x21 -> x3, local copies, waits for them, and re-layouts: 41 us -> 3.32 us  [the longest x2 3.28 us: shards(): down_parts.append(piece_grad[:, 2 * F:].reshape(piece_rows, F // piece_ro...]
  transfers between devices with their start and end apart: 47 -> 44, of which waited for: 22 -> 23; matrix products, arithmetic and copies ran while one was open for 33% -> 22% of each run, Pallas kernels for 0% -> 5%
where the time goes in v2:
time: 1240 us; the launch traced here: 1220 us
  waiting for transfers between devices  424 us (34%)
  starting transfers between devices  192 us (15%)
  other arithmetic  165 us (13%)
  local copies, waits for them, and re-layouts  153 us (12%)
  Pallas kernels  151 us (12%)
  blocking collectives  95.1 us (8%)
  matrix products  25.3 us (2%)
  between operations  20.6 us (2%)
    ppermute x8, waiting for transfers between devices, return_expert_grads(): arrived.append(lax.ppermute(piece, ('z', 'h', 'y', 'c'), back))  138 us
    ppermute x8, waiting for transfers between devices, spread_experts(): lax.ppermute(piece, ('z', 'h', 'y', 'c'), swap_pairs(row_groups, turn_pla...  86.3 us
    all_to_all x5, waiting for transfers between devices, send_all(): return lax.all_to_all(values, AXES, split_axis=0, concat_axis=0, tiled=True)  76.9 us
    ppermute x8, starting transfers between devices, return_expert_grads(): arrived.append(lax.ppermute(piece, ('z', 'h', 'y', 'c'), back))  66.8 us
    all_to_all x2, blocking collectives, send_plane(): lax.all_to_all(values, ('x', 'y', 'c'), split_axis=0, concat_axis=0, tile...  63.7 us
    all_to_all x6, waiting for transfers between devices, send_plane(): lax.all_to_all(values, ('x', 'y', 'c'), split_axis=0, concat_axis=0, tile...  63.1 us
    scatter-add x1, other arithmetic, shards(): jax.ops.segment_sum(arrived_grads[:, :seq_len * column_count].astype(jnp....  54.7 us
    ppermute x8, starting transfers between devices, spread_experts(): lax.ppermute(piece, ('z', 'h', 'y', 'c'), swap_pairs(row_groups, turn_pla...  50 us
  transfers between devices with their start and end apart: 44, of which 23 were waited for; matrix products, arithmetic and copies ran while one was open for 22% of the time, Pallas kernels for 5%

profile of v2, /device:TPU:9, one launch (start us, length us, event | category | flops | bytes accessed | tf_op | source)
XLA Modules:
  0.0 1224.7 jit_solution(15411202695648176672)
XLA Ops:
  27.5 28.3 %gather_fusion = bf16[8192,32]{1,0:T(8,128)(2,1)S(1)} fusion(bf16[50304,32]{1,0:T(8,128)(2,1)} %copy.333, s32[8192]{0:T(1024)S(1)} %fusion.64), kind=kCustom, calls=%fused_computation | custom fusion | bytes 1081344 | tf_op jit(solution)/shard_map/jit(_take)/gather | solution.py:925
  73.0 12.9 %select_reduce_fusion = f32[256,1572]{0,1:T(8,128)S(1)} fusion(f32[256,65]{0,1:T(8,128)S(1)} %concatenate.92, s32[256,65]{0,1:T(8,128)S(1)} %broadcast_subtract_fusion), kind=kLoop, calls=%fused_computation.5 | loop fusion | flops 78071808 | bytes 1742848 | tf_op jit(solution)/shard_map/reduce_sum | solution.py:964
  117.9 12.5 %all-to-all-done.1 = bf16[32,8,1024]{2,1,0:T(8,128)(2,1)S(1)} async-done(((bf16[32,8,1024]{2,1,0:T(8,128)(2,1)}), bf16[32,8,1024]{2,1,0:T(8,128)(2,1)S(1)}, u32[]{:S(2)}, u32[]{:S(2)}) %all-to-all-start.1) | async-done | bytes 524320 | tf_op jit(solution)/shard_map/all_to_all | solution.py:848
  137.6 13.6 %shard_map.480 = (f32[256,1024]{1,0:T(8,128)}, f32[256,2048]{1,0:T(8,128)}, bf16[256,1024]{1,0:T(8,128)(2,1)}, bf16[256,1024]{1,0:T(8,128)(2,1)}, bf16[256,1024]...) custom-call(s32[1]{0:T(128)S(6)} %copy.402.prefix_ref, ...), custom_call_target="tpu_custom_call" | custom-call | flops 3221225472 | bytes 25165824 | tf_op jit(solution)/shard_map/pallas_call | solution.py:234
  184.3 20.2 %collective-permute-done.1.refs_0_ = bf16[256,1536]{1,0:T(8,128)(2,1)} collective-permute-done((bf16[256,1536]{1,0:T(8,128)(2,1)}, bf16[256,1536]{1,0:T(8,128)(2,1)}, u32[]{:S(2)}, u32[]{:S(2)}) %collective-permute-start.1) | collective-permute-done | bytes 786464 | tf_op jit(solution)/shard_map/ppermute | solution.py:774
  204.5 34.7 %collective-permute-done.5.refs_3_ = bf16[256,1536]{1,0:T(8,128)(2,1)S(1)} collective-permute-done((bf16[256,1536]{1,0:T(8,128)(2,1)}, bf16[256,1536]{1,0:T(8,128)(2,1)S(1)}, u32[]{:S(2)}, u32[]{:S(2)}) %collective-permute-start.5) | collective-permute-done | bytes 786464 | tf_op jit(solution)/shard_map/ppermute | solution.py:774
  264.1 10.9 collective-permute-start.6
  275.0 23.1 %all-to-all-done.3 = bf16[8,144,1024]{2,1,0:T(8,128)(2,1)S(1)} async-done(((bf16[8,144,1024]{2,1,0:T(8,128)(2,1)}), bf16[8,144,1024]{2,1,0:T(8,128)(2,1)S(1)}, u32[]{:S(2)}, u32[]{:S(2)}) %all-to-all-start.3) | async-done | bytes 2359328 | tf_op jit(solution)/shard_map/all_to_all | solution.py:852
  299.6 16.7 %shard_map.482 = (f32[256,1024]{1,0:T(8,128)}, f32[256,2048]{1,0:T(8,128)}, bf16[256,1024]{1,0:T(8,128)(2,1)}, bf16[256,1024]{1,0:T(8,128)(2,1)}, bf16[256,1024]...) custom-call(s32[1]{0:T(128)S(6)} %copy.402.prefix_ref, ...), custom_call_target="tpu_custom_call" | custom-call | flops 3221225472 | bytes 25165824 | tf_op jit(solution)/shard_map/pallas_call | solution.py:234
  323.2 14.0 %collective-permute-start.7 = (bf16[256,1536]{1,0:T(8,128)(2,1)S(1)}, bf16[256,1536]{1,0:T(8,128)(2,1)}, u32[]{:S(2)}, u32[]{:S(2)}) collective-permute-start(bf16[256,1536]{1,0:T(8,128)(2,1)S(1)} %copy-done.63), channel_id=1, source_target_pairs={{0,24},{1,8},{2,16},{3,0},{8,1},{9,17},{10,25},{11,9},{16,10},{17,... | collective-permute-start | bytes 2359304 | tf_op jit(solution)/shard_map/ppermute | solution.py:774
  337.2 22.3 %collective-permute-done.7.refs_3_ = bf16[256,1536]{1,0:T(8,128)(2,1)} collective-permute-done((bf16[256,1536]{1,0:T(8,128)(2,1)S(1)}, bf16[256,1536]{1,0:T(8,128)(2,1)}, u32[]{:S(2)}, u32[]{:S(2)}) %collective-permute-start.7) | collective-permute-done | bytes 786464 | tf_op jit(solution)/shard_map/ppermute | solution.py:774
  370.7 31.6 %all_to_all.88 = bf16[8,144,1024]{2,1,0:T(8,128)(2,1)S(1)} all-to-all(bf16[8,144,1024]{2,1,0:T(8,128)(2,1)} %bitcast.260), channel_id=1, replica_groups=mesh['z'=4,'x'=2,'h'=1,'y'=2,'c'=2] {'x','y','c'}, dimensions={0} | all-to-all | bytes 4718592 | tf_op jit(solution)/shard_map/all_to_all | solution.py:852
  404.9 31.4 %all_to_all.89 = bf16[32,8,1024]{2,1,0:T(8,128)(2,1)S(1)} all-to-all(bf16[32,8,1024]{2,1,0:T(8,128)(2,1)S(1)} %broadcast_in_dim.102), channel_id=1, replica_groups=mesh['z'=4,'x'=2,'h'=1,'y'=2,'c'=2] {'z','x','h','y','c'}, dimensions={0} | all-to-all | bytes 1048576 | tf_op jit(solution)/shard_map/all_to_all | solution.py:848
  458.3 12.1 all-to-all-done.7
  484.2 32.1 %all_to_all.90 = bf16[8,144,1024]{2,1,0:T(8,128)(2,1)} all-to-all(bf16[8,144,1024]{2,1,0:T(8,128)(2,1)S(1)} %bitcast.233), channel_id=1, replica_groups=mesh['z'=4,'x'=2,'h'=1,'y'=2,'c'=2] {'x','y','c'}, dimensions={0} | all-to-all | bytes 4718592 | tf_op jit(solution)/shard_map/all_to_all | solution.py:852
  516.3 13.8 %shard_map.486 = (bf16[1152,1024]{1,0:T(8,128)(2,1)}, bf16[1152,1024]{1,0:T(8,128)(2,1)}, bf16[1152,512]{1,0:T(8,128)(2,1)}) custom-call(s32[4]{0:T(128)} %pad_add_fusion.place_ref, bf16[1152,1024]{1,0:T(8,128)(2,1)} %bitcast.251, bf16[1152,1024]{1,0:T(8,128)(2,1)} %bitcast.253, bf16[256,1536]{1,0:T(8,128)(2,1)} %collective-permute-done.1.refs_0_, ...), custom_call_target="tpu_custom_call" | custom-call | flops 7247757312 | bytes 12582912 | tf_op jit(solution)/shard_map/pallas_call | solution.py:545
  541.9 21.1 %all-to-all-done.10 = bf16[8,144,1024]{2,1,0:T(8,128)(2,1)} async-done(((bf16[8,144,1024]{2,1,0:T(8,128)(2,1)}), bf16[8,144,1024]{2,1,0:T(8,128)(2,1)}, u32[]{:S(2)}, u32[]{:S(2)}) %all-to-all-start.10) | async-done | bytes 2359328 | tf_op jit(solution)/shard_map/all_to_all | solution.py:852
  563.0 21.4 %shard_map.488 = (f32[256,1024]{1,0:T(8,128)}, bf16[1024,4096]{1,0:T(8,128)(2,1)}, f32[8,1024]{1,0:T(8,128)}, bf16[1152,1024]{1,0:T(8,128)(2,1)}) custom-call(s32[1]{0:T(128)S(6)} %copy.402.prefix_ref, f32[256,1024]{1,0:T(8,128)} %copy-done.8, bf16[1152,1024]{1,0:T(8,128)(2,1)} %bitcast.43.back_ref, bf16[256,128]{1,0:T(8,128)(2,1)} %copy-done.22, ...), custom_call_target="tpu_custom_call" | custom-call | flops 6442450944 | bytes 33554432 | tf_op jit(solution)/shard_map/pallas_call | solution.py:398
  625.2 52.3 %all-to-all-done.8 = f32[32,1,16]{2,1,0:T(1,128)S(1)} async-done(((f32[32,1,16]{2,1,0:T(1,128)}), f32[32,1,16]{2,1,0:T(1,128)S(1)}, u32[]{:S(2)}, u32[]{:S(2)}) %all-to-all-start.8) | async-done | bytes 2080 | tf_op jit(solution)/shard_map/all_to_all | solution.py:848
  690.7 18.9 %all-to-all-done.11 = bf16[8,144,1024]{2,1,0:T(8,128)(2,1)S(1)} async-done(((bf16[8,144,1024]{2,1,0:T(8,128)(2,1)}), bf16[8,144,1024]{2,1,0:T(8,128)(2,1)S(1)}, u32[]{:S(2)}, u32[]{:S(2)}) %all-to-all-start.11) | async-done | bytes 2359328 | tf_op jit(solution)/shard_map/all_to_all | solution.py:852
  717.1 13.8 %shard_map.490 = (bf16[1152,1024]{1,0:T(8,128)(2,1)}, bf16[1152,1024]{1,0:T(8,128)(2,1)}, bf16[1152,512]{1,0:T(8,128)(2,1)}) custom-call(s32[4]{0:T(128)} %pad_add_fusion.place_ref, bf16[1152,1024]{1,0:T(8,128)(2,1)} %bitcast.245, bf16[1152,1024]{1,0:T(8,128)(2,1)} %bitcast.247, bf16[256,1536]{1,0:T(8,128)(2,1)} %collective-permute-done.2.refs_0_, ...), custom_call_target="tpu_custom_call" | custom-call | flops 7247757312 | bytes 12582912 | tf_op jit(solution)/shard_map/pallas_call | solution.py:545
  736.5 14.1 %add_multiply_fusion = (f32[1572,1024]{1,0:T(8,128)}, f32[1572,1024]{1,0:T(8,128)}, f32[1572,1024]{1,0:T(8,128)}) fusion(f32[1572,1024]{1,0:T(8,128)} %param.57, f32[1572,1024]{1,0:T(8,128)} %param.59, f32[1572,1024]{1,0:T(8,128)} %param.58, bf16[32,8,1024]{2,1,0:T(8,128)(2,1)} %copy-done.52, f32[256,1572]{0,1:T(8,128)} %copy-done.24, ...), kind=kOutput, calls=%fused_computation.16 | convolution fusion | flops 848729088 | bytes 42379264 | tf_op jit(solution)/shard_map/pv,pd->vd/dot_general | solution.py:1099
  771.5 19.5 %collective-permute-done.8 = bf16[256,1536]{1,0:T(8,128)(2,1)} collective-permute-done((bf16[256,1536]{1,0:T(8,128)(2,1)}, bf16[256,1536]{1,0:T(8,128)(2,1)}, u32[]{:S(2)}, u32[]{:S(2)}) %collective-permute-start.8) | collective-permute-done | bytes 786464 | tf_op jit(solution)/shard_map/ppermute | solution.py:785
  791.0 30.2 %collective-permute-done.9 = bf16[256,1536]{1,0:T(8,128)(2,1)} collective-permute-done((bf16[256,1536]{1,0:T(8,128)(2,1)}, bf16[256,1536]{1,0:T(8,128)(2,1)}, u32[]{:S(2)}, u32[]{:S(2)}) %collective-permute-start.9) | collective-permute-done | bytes 786464 | tf_op jit(solution)/shard_map/ppermute | solution.py:785
  821.2 20.4 %shard_map.492 = (f32[256,1024]{1,0:T(8,128)}, bf16[1024,4096]{1,0:T(8,128)(2,1)}, f32[8,1024]{1,0:T(8,128)}) custom-call(s32[1]{0:T(128)S(6)} %copy.402.prefix_ref, f32[256,1024]{1,0:T(8,128)} %get-tuple-element.136.grad_ref, bf16[1152,1024]{1,0:T(8,128)(2,1)} %bitcast.50.back_ref, bf16[256,128]{1,0:T(8,128)(2,1)} %copy-done.21, ...), custom_call_target="tpu_custom_call" | custom-call | flops 6442450944 | bytes 33554432 | tf_op jit(solution)/shard_map/pallas_call | solution.py:398
  907.4 46.3 %collective-permute-start.18 = (bf16[256,1536]{1,0:T(8,128)(2,1)}, bf16[256,1536]{1,0:T(8,128)(2,1)}, u32[]{:S(2)}, u32[]{:S(2)}) collective-permute-start(bf16[256,1536]{1,0:T(8,128)(2,1)} %get-tuple-element.170), channel_id=1, source_target_pairs={{8,0},{24,1},{0,2},{16,3},{17,8},{1,9},{9,10},{25,11},{26,16},{10,... | collective-permute-start | bytes 2359304 | tf_op jit(solution)/shard_map/ppermute | solution.py:785
  965.4 16.8 %collective-permute-done.18 = bf16[256,1536]{1,0:T(8,128)(2,1)} collective-permute-done((bf16[256,1536]{1,0:T(8,128)(2,1)}, bf16[256,1536]{1,0:T(8,128)(2,1)}, u32[]{:S(2)}, u32[]{:S(2)}) %collective-permute-start.18) | collective-permute-done | bytes 786464 | tf_op jit(solution)/shard_map/ppermute | solution.py:785
  982.2 62.1 %collective-permute-done.19 = bf16[256,1536]{1,0:T(8,128)(2,1)} collective-permute-done((bf16[256,1536]{1,0:T(8,128)(2,1)}, bf16[256,1536]{1,0:T(8,128)(2,1)}, u32[]{:S(2)}, u32[]{:S(2)}) %collective-permute-start.19) | collective-permute-done | bytes 786464 | tf_op jit(solution)/shard_map/ppermute | solution.py:785
  1058.9 54.7 %scatter_custom_fusion = f32[50304,32]{1,0:T(8,128)} fusion(s32[8192]{0:T(1024)} %param.33, f32[8192,32]{1,0:T(8,128)} %reshape.792, f32[]{:T(128)} %constant.325.clone.1), kind=kCustom, calls=%fused_computation.7 | custom fusion | flops 262144 | bytes 6439424 | tf_op jit(solution)/shard_map/scatter-add | solution.py:1198
  1113.6 16.9 %copy.366 = f32[50304,32]{0,1:T(8,128)} copy(f32[50304,32]{1,0:T(8,128)} %scatter_custom_fusion) | data formatting | bytes 12877824 | tf_op jit(solution)/shard_map/scatter-add | solution.py:1198
  1130.5 17.1 %add_multiply_fusion.1 = (f32[50304,32]{0,1:T(8,128)}, f32[50304,32]{0,1:T(8,128)}, f32[50304,32]{0,1:T(8,128)}) fusion(f32[50304,32]{0,1:T(8,128)} %param.39, f32[50304,32]{0,1:T(8,128)} %copy.366, f32[50304,32]{0,1:T(8,128)} %param.41, f32[50304,32]{0,1:T(8,128)} %param.40), kind=kLoop, calls=%fused_computation.19 | loop fusion | flops 22536192 | bytes 45072384 | tf_op jit(solution)/shard_map/mul | solution.py:866
  1198.9 15.1 %collective-permute-done.25 = bf16[32,4096]{1,0:T(8,128)(2,1)S(1)} collective-permute-done((bf16[32,4096]{1,0:T(8,128)(2,1)}, bf16[32,4096]{1,0:T(8,128)(2,1)S(1)}, u32[]{:S(2)}, u32[]{:S(2)}) %collective-permute-start.25) | collective-permute-done | bytes 262176 | tf_op jit(solution)/shard_map/ppermute | solution.py:836
  (435 shorter events, 433.2 us)
Async XLA Ops:
  7.2 130.4 %all-gather.2.cloned.1.call-start = ((), (), s32[]{:S(2)}) async-start(), calls=%async_computation.14 | async-start | bytes 17301504 | tf_op jit(solution)/shard_map/all_gather | solution.py:922
  61.4 35.7 %all-to-all-start = ((bf16[32,2,4496]{2,1,0:T(2,128)(2,1)}), bf16[32,2,4496]{2,1,0:T(2,128)(2,1)}, u32[]{:S(2)}, u32[]{:S(2)}) async-start(bf16[32,2,4496]{2,1,0:T(2,128)(2,1)} %reshape.802), calls=%async_computation | async-start | bytes 1179648 | tf_op jit(solution)/shard_map/all_to_all | solution.py:848
  97.1 33.3 %all-to-all-start.1 = ((bf16[32,8,1024]{2,1,0:T(8,128)(2,1)}), bf16[32,8,1024]{2,1,0:T(8,128)(2,1)S(1)}, u32[]{:S(2)}, u32[]{:S(2)}) async-start(bf16[32,8,1024]{2,1,0:T(8,128)(2,1)} %fusion.13), calls=%async_computation.1 | async-start | bytes 1048576 | tf_op jit(solution)/shard_map/all_to_all | solution.py:848
  151.3 53.3 %all-to-all-start.2 = ((bf16[8,144,1024]{2,1,0:T(8,128)(2,1)}), bf16[8,144,1024]{2,1,0:T(8,128)(2,1)S(1)}, u32[]{:S(2)}, u32[]{:S(2)}) async-start(bf16[8,144,1024]{2,1,0:T(8,128)(2,1)} %bitcast.255), calls=%async_computation.2 | async-start | bytes 4718592 | tf_op jit(solution)/shard_map/all_to_all | solution.py:852
  156.0 48.6 %collective-permute-start.1 = (bf16[256,1536]{1,0:T(8,128)(2,1)}, bf16[256,1536]{1,0:T(8,128)(2,1)}, u32[]{:S(2)}, u32[]{:S(2)}) collective-permute-start(bf16[256,1536]{1,0:T(8,128)(2,1)} %pad_maximum_fusion.3), channel_id=1, source_target_pairs={{0,0},{1,16},{2,8},{3,24},{8,9},{9,25},{10,17},{11,1},{16,18},{17,... | collective-permute-start | bytes 2359304 | tf_op jit(solution)/shard_map/ppermute | solution.py:774
  164.4 74.8 %collective-permute-start.5 = (bf16[256,1536]{1,0:T(8,128)(2,1)}, bf16[256,1536]{1,0:T(8,128)(2,1)S(1)}, u32[]{:S(2)}, u32[]{:S(2)}) collective-permute-start(bf16[256,1536]{1,0:T(8,128)(2,1)} %pad_maximum_fusion.4), channel_id=1, source_target_pairs={{0,24},{1,8},{2,16},{3,0},{8,1},{9,17},{10,25},{11,9},{16,10},{17,... | collective-permute-start | bytes 2359304 | tf_op jit(solution)/shard_map/ppermute | solution.py:774
  168.8 70.4 %collective-permute-start.4 = (bf16[256,1536]{1,0:T(8,128)(2,1)}, bf16[256,1536]{1,0:T(8,128)(2,1)}, u32[]{:S(2)}, u32[]{:S(2)}) collective-permute-start(bf16[256,1536]{1,0:T(8,128)(2,1)} %pad_maximum_fusion.4), channel_id=1, source_target_pairs={{0,8},{1,24},{2,0},{3,16},{8,17},{9,1},{10,9},{11,25},{16,26},{17,... | collective-permute-start | bytes 2359304 | tf_op jit(solution)/shard_map/ppermute | solution.py:774
  170.8 68.5 %collective-permute-start.3 = (bf16[256,1536]{1,0:T(8,128)(2,1)}, bf16[256,1536]{1,0:T(8,128)(2,1)}, u32[]{:S(2)}, u32[]{:S(2)}) collective-permute-start(bf16[256,1536]{1,0:T(8,128)(2,1)} %pad_maximum_fusion.4), channel_id=1, source_target_pairs={{0,16},{1,0},{2,24},{3,8},{8,25},{9,9},{10,1},{11,17},{16,2},{17,1... | collective-permute-start | bytes 2359304 | tf_op jit(solution)/shard_map/ppermute | solution.py:774
  178.2 70.1 %collective-permute-start.2 = (bf16[256,1536]{1,0:T(8,128)(2,1)}, bf16[256,1536]{1,0:T(8,128)(2,1)}, u32[]{:S(2)}, u32[]{:S(2)}) collective-permute-start(bf16[256,1536]{1,0:T(8,128)(2,1)} %pad_maximum_fusion.4), channel_id=1, source_target_pairs={{0,0},{1,16},{2,8},{3,24},{8,9},{9,25},{10,17},{11,1},{16,18},{17,... | collective-permute-start | bytes 2359304 | tf_op jit(solution)/shard_map/ppermute | solution.py:774
  258.0 40.2 %all-to-all-start.3 = ((bf16[8,144,1024]{2,1,0:T(8,128)(2,1)}), bf16[8,144,1024]{2,1,0:T(8,128)(2,1)S(1)}, u32[]{:S(2)}, u32[]{:S(2)}) async-start(bf16[8,144,1024]{2,1,0:T(8,128)(2,1)} %bitcast.259), calls=%async_computation.3 | async-start | bytes 4718592 | tf_op jit(solution)/shard_map/all_to_all | solution.py:852
  264.1 52.1 %collective-permute-start.6 = (bf16[256,1536]{1,0:T(8,128)(2,1)S(1)}, bf16[256,1536]{1,0:T(8,128)(2,1)}, u32[]{:S(2)}, u32[]{:S(2)}) collective-permute-start(bf16[256,1536]{1,0:T(8,128)(2,1)S(1)} %copy-done.63), channel_id=1, source_target_pairs={{0,8},{1,24},{2,0},{3,16},{8,17},{9,1},{10,9},{11,25},{16,26},{17,... | collective-permute-start | bytes 2359304 | tf_op jit(solution)/shard_map/ppermute | solution.py:774
  316.3 43.3 %all-to-all-start.4 = ((bf16[8,144,1024]{2,1,0:T(8,128)(2,1)}), bf16[8,144,1024]{2,1,0:T(8,128)(2,1)S(1)}, u32[]{:S(2)}, u32[]{:S(2)}) async-start(bf16[8,144,1024]{2,1,0:T(8,128)(2,1)} %bitcast.258), calls=%async_computation.4 | async-start | bytes 4718592 | tf_op jit(solution)/shard_map/all_to_all | solution.py:852
  323.2 36.4 %collective-permute-start.7 = (bf16[256,1536]{1,0:T(8,128)(2,1)S(1)}, bf16[256,1536]{1,0:T(8,128)(2,1)}, u32[]{:S(2)}, u32[]{:S(2)}) collective-permute-start(bf16[256,1536]{1,0:T(8,128)(2,1)S(1)} %copy-done.63), channel_id=1, source_target_pairs={{0,24},{1,8},{2,16},{3,0},{8,1},{9,17},{10,25},{11,9},{16,10},{17,... | collective-permute-start | bytes 2359304 | tf_op jit(solution)/shard_map/ppermute | solution.py:774
  530.1 32.9 %all-to-all-start.10 = ((bf16[8,144,1024]{2,1,0:T(8,128)(2,1)}), bf16[8,144,1024]{2,1,0:T(8,128)(2,1)}, u32[]{:S(2)}, u32[]{:S(2)}) async-start(bf16[8,144,1024]{2,1,0:T(8,128)(2,1)} %bitcast.257), calls=%async_computation.10 | async-start | bytes 4718592 | tf_op jit(solution)/shard_map/all_to_all | solution.py:852
  593.0 90.4 %collective-permute-start.10 = (bf16[4,2,1,2,32,4096]{5,4,0,1,3,2:T(8,128)(2,1)}, bf16[4,2,1,2,32,4096]{5,4,0,1,3,2:T(8,128)(2,1)}, u32[]{:S(2)}, u32[]{:S(2)}) collective-permute-start(bf16[4,2,1,2,32,4096]{5,4,0,1,3,2:T(8,128)(2,1)} %bitcast.216), channel_id=1, source_target_pairs={{0,1},{1,0},{2,3},{3,2},{4,5},{5,4},{6,7},{7,6},{8,9},{9,8},{10,11... | collective-permute-start | bytes 12582920 | tf_op jit(solution)/shard_map/ppermute | solution.py:801
  609.0 68.6 %all-to-all-start.8 = ((f32[32,1,16]{2,1,0:T(1,128)}), f32[32,1,16]{2,1,0:T(1,128)S(1)}, u32[]{:S(2)}, u32[]{:S(2)}) async-start(f32[32,1,16]{2,1,0:T(1,128)} %broadcast_in_dim.103), calls=%async_computation.8 | async-start | bytes 32768 | tf_op jit(solution)/shard_map/all_to_all | solution.py:848
  677.6 32.0 %all-to-all-start.11 = ((bf16[8,144,1024]{2,1,0:T(8,128)(2,1)}), bf16[8,144,1024]{2,1,0:T(8,128)(2,1)S(1)}, u32[]{:S(2)}, u32[]{:S(2)}) async-start(bf16[8,144,1024]{2,1,0:T(8,128)(2,1)} %bitcast.249), calls=%async_computation.11 | async-start | bytes 4718592 | tf_op jit(solution)/shard_map/all_to_all | solution.py:852
  714.4 52.5 %collective-permute-start.14 = (bf16[4,1,2,32,2048]{4,3,0,2,1:T(8,128)(2,1)}, bf16[4,1,2,32,2048]{4,3,0,2,1:T(8,128)(2,1)}, u32[]{:S(2)}, u32[]{:S(2)}) collective-permute-start(bf16[4,1,2,32,2048]{4,3,0,2,1:T(8,128)(2,1)} %dynamic-slice_bitcast_fusion.3), channel_id=1, source_target_pairs={{0,4},{4,0},{1,5},{5,1},{2,6},{6,2},{3,7},{7,3},{8,12},{12,8},{9,1... | collective-permute-start | bytes 3145736 | tf_op jit(solution)/shard_map/ppermute | solution.py:801
  715.9 53.0 %collective-permute-start.15 = (bf16[4,2,1,32,2048]{4,3,0,2,1:T(8,128)(2,1)}, bf16[4,2,1,32,2048]{4,3,0,2,1:T(8,128)(2,1)}, u32[]{:S(2)}, u32[]{:S(2)}) collective-permute-start(bf16[4,2,1,32,2048]{4,3,0,2,1:T(8,128)(2,1)} %dynamic-slice_bitcast_fusion.2), channel_id=1, source_target_pairs={{0,2},{2,0},{1,3},{3,1},{4,6},{6,4},{5,7},{7,5},{8,10},{10,8},{9,1... | collective-permute-start | bytes 3145736 | tf_op jit(solution)/shard_map/ppermute | solution.py:801
  730.9 90.3 %all-to-all-start.12 = ((bf16[8,144,1024]{2,1,0:T(8,128)(2,1)}), bf16[8,144,1024]{2,1,0:T(8,128)(2,1)}, u32[]{:S(2)}, u32[]{:S(2)}) async-start(bf16[8,144,1024]{2,1,0:T(8,128)(2,1)} %bitcast.256), calls=%async_computation.12 | async-start | bytes 4718592 | tf_op jit(solution)/shard_map/all_to_all | solution.py:852
  751.3 39.7 %collective-permute-start.8 = (bf16[256,1536]{1,0:T(8,128)(2,1)}, bf16[256,1536]{1,0:T(8,128)(2,1)}, u32[]{:S(2)}, u32[]{:S(2)}) collective-permute-start(bf16[256,1536]{1,0:T(8,128)(2,1)} %get-tuple-element.139), channel_id=1, source_target_pairs={{8,0},{24,1},{0,2},{16,3},{17,8},{1,9},{9,10},{25,11},{26,16},{10,... | collective-permute-start | bytes 2359304 | tf_op jit(solution)/shard_map/ppermute | solution.py:785
  754.9 66.4 %collective-permute-start.9 = (bf16[256,1536]{1,0:T(8,128)(2,1)}, bf16[256,1536]{1,0:T(8,128)(2,1)}, u32[]{:S(2)}, u32[]{:S(2)}) collective-permute-start(bf16[256,1536]{1,0:T(8,128)(2,1)} %get-tuple-element.140), channel_id=1, source_target_pairs={{24,0},{8,1},{16,2},{0,3},{1,8},{17,9},{25,10},{9,11},{10,16},{26,... | collective-permute-start | bytes 2359304 | tf_op jit(solution)/shard_map/ppermute | solution.py:785
  850.3 109.8 %collective-permute-start.13 = (bf16[4,2,1,2,32,4096]{5,4,0,1,3,2:T(8,128)(2,1)}, bf16[4,2,1,2,32,4096]{5,4,0,1,3,2:T(8,128)(2,1)}, u32[]{:S(2)}, u32[]{:S(2)}) collective-permute-start(bf16[4,2,1,2,32,4096]{5,4,0,1,3,2:T(8,128)(2,1)} %bitcast.215), channel_id=1, source_target_pairs={{0,1},{1,0},{2,3},{3,2},{4,5},{5,4},{6,7},{7,6},{8,9},{9,8},{10,11... | collective-permute-start | bytes 12582920 | tf_op jit(solution)/shard_map/ppermute | solution.py:801
  866.2 92.8 %all-to-all-start.13 = ((bf16[32,2,4496]{2,1,0:T(2,128)(2,1)}), bf16[32,2,4496]{2,1,0:T(2,128)(2,1)S(1)}, u32[]{:S(2)}, u32[]{:S(2)}) async-start(bf16[32,2,4496]{2,1,0:T(2,128)(2,1)} %reshape.804), calls=%async_computation.13 | async-start | bytes 1179648 | tf_op jit(solution)/shard_map/all_to_all | solution.py:848
  874.6 27.2 %collective-permute-start.29 = (bf16[32,4096]{1,0:T(8,128)(2,1)S(1)}, bf16[32,4096]{1,0:T(8,128)(2,1)S(1)}, u32[]{:S(2)}, u32[]{:S(2)}) collective-permute-start(bf16[32,4096]{1,0:T(8,128)(2,1)S(1)} %get-tuple-element.341), channel_id=1, source_target_pairs={{0,8},{8,16},{16,24},{24,0},{1,9},{9,17},{17,25},{25,1},{2,10},{10... | collective-permute-start | bytes 786440 | tf_op jit(solution)/shard_map/ppermute | solution.py:836
  875.9 31.5 %collective-permute-start.30 = (bf16[32,4096]{1,0:T(8,128)(2,1)S(1)}, bf16[32,4096]{1,0:T(8,128)(2,1)S(1)}, u32[]{:S(2)}, u32[]{:S(2)}) collective-permute-start(bf16[32,4096]{1,0:T(8,128)(2,1)S(1)} %get-tuple-element.342), channel_id=1, source_target_pairs={{0,16},{8,24},{16,0},{24,8},{1,17},{9,25},{17,1},{25,9},{2,18},{10... | collective-permute-start | bytes 786440 | tf_op jit(solution)/shard_map/ppermute | solution.py:836
  877.0 76.8 %collective-permute-start.31 = (bf16[32,4096]{1,0:T(8,128)(2,1)S(1)}, bf16[32,4096]{1,0:T(8,128)(2,1)S(1)}, u32[]{:S(2)}, u32[]{:S(2)}) collective-permute-start(bf16[32,4096]{1,0:T(8,128)(2,1)S(1)} %get-tuple-element.343), channel_id=1, source_target_pairs={{0,24},{8,0},{16,8},{24,16},{1,25},{9,1},{17,9},{25,17},{2,26},{10... | collective-permute-start | bytes 786440 | tf_op jit(solution)/shard_map/ppermute | solution.py:836
  888.9 76.4 %collective-permute-start.16 = (bf16[256,1536]{1,0:T(8,128)(2,1)}, bf16[256,1536]{1,0:T(8,128)(2,1)S(1)}, u32[]{:S(2)}, u32[]{:S(2)}) collective-permute-start(bf16[256,1536]{1,0:T(8,128)(2,1)} %get-tuple-element.168), channel_id=1, source_target_pairs={{0,0},{16,1},{8,2},{24,3},{9,8},{25,9},{17,10},{1,11},{18,16},{2,1... | collective-permute-start | bytes 2359304 | tf_op jit(solution)/shard_map/ppermute | solution.py:785
  901.8 63.5 %collective-permute-start.17 = (bf16[256,1536]{1,0:T(8,128)(2,1)}, bf16[256,1536]{1,0:T(8,128)(2,1)S(1)}, u32[]{:S(2)}, u32[]{:S(2)}) collective-permute-start(bf16[256,1536]{1,0:T(8,128)(2,1)} %get-tuple-element.169), channel_id=1, source_target_pairs={{16,0},{0,1},{24,2},{8,3},{25,8},{9,9},{1,10},{17,11},{2,16},{18,1... | collective-permute-start | bytes 2359304 | tf_op jit(solution)/shard_map/ppermute | solution.py:785
  907.4 74.8 %collective-permute-start.18 = (bf16[256,1536]{1,0:T(8,128)(2,1)}, bf16[256,1536]{1,0:T(8,128)(2,1)}, u32[]{:S(2)}, u32[]{:S(2)}) collective-permute-start(bf16[256,1536]{1,0:T(8,128)(2,1)} %get-tuple-element.170), channel_id=1, source_target_pairs={{8,0},{24,1},{0,2},{16,3},{17,8},{1,9},{9,10},{25,11},{26,16},{10,... | collective-permute-start | bytes 2359304 | tf_op jit(solution)/shard_map/ppermute | solution.py:785
  953.7 90.6 %collective-permute-start.19 = (bf16[256,1536]{1,0:T(8,128)(2,1)}, bf16[256,1536]{1,0:T(8,128)(2,1)}, u32[]{:S(2)}, u32[]{:S(2)}) collective-permute-start(bf16[256,1536]{1,0:T(8,128)(2,1)} %get-tuple-element.171), channel_id=1, source_target_pairs={{24,0},{8,1},{16,2},{0,3},{1,8},{17,9},{25,10},{9,11},{10,16},{26,... | collective-permute-start | bytes 2359304 | tf_op jit(solution)/shard_map/ppermute | solution.py:785
  1055.0 107.8 %collective-permute-start.20 = (bf16[4,1,2,32,2048]{4,3,0,2,1:T(8,128)(2,1)}, bf16[4,1,2,32,2048]{4,3,0,2,1:T(8,128)(2,1)}, u32[]{:S(2)}, u32[]{:S(2)}) collective-permute-start(bf16[4,1,2,32,2048]{4,3,0,2,1:T(8,128)(2,1)} %dynamic-slice_bitcast_fusion.1), channel_id=1, source_target_pairs={{0,4},{4,0},{1,5},{5,1},{2,6},{6,2},{3,7},{7,3},{8,12},{12,8},{9,1... | collective-permute-start | bytes 3145736 | tf_op jit(solution)/shard_map/ppermute | solution.py:801
  (100 other events, 1427.5 us)
Sparse Core Ops, SparseCore 0:
  11.5 125.9 all-gather.1

commit v3 on v2

--- a/solution.py
+++ b/solution.py
@@ -113,11 +113,11 @@
     return lane < HDIM, lane >= HDIM
 
 
-def fetch_weights(weight_ref, held_ref, copy_sem, layer_index, order):
+def fetch_weights(weight_ref, held_ref, copy_sem, order):
     copies = {}
     for part in order:
         copies[part] = pltpu.make_async_copy(
-            weight_ref.at[layer_index, :, pl.ds(part * D, D)], held_ref.at[part], copy_sem.at[part]
+            weight_ref.at[:, pl.ds(part * D, D)], held_ref.at[part], copy_sem.at[part]
         )
         copies[part].start()
     return copies
@@ -155,7 +155,7 @@
         held_ref,
         copy_sem,
     ) = refs
-    copies = fetch_weights(weight_ref, held_ref, copy_sem, layer_index, (0, 1, 2, 3))
+    copies = fetch_weights(weight_ref, held_ref, copy_sem, (0, 1, 2, 3))
     seq_len = hidden_ref.shape[0]
     hidden = hidden_ref[...]
     if layer_index > 0:
@@ -295,7 +295,7 @@
         spread_ref, gates_ref, refs = refs[0], refs[1], refs[2:]
         outgoing_ref, refs = refs[3], refs[:3] + refs[4:]
     grad_out_ref, weight_grad_ref, gain_grad_ref, pull_ref, key_pull_ref, held_ref, copy_sem = refs
-    copies = fetch_weights(weight_ref, held_ref, copy_sem, layer_index, (3, 2, 0, 1))
+    copies = fetch_weights(weight_ref, held_ref, copy_sem, (3, 2, 0, 1))
     seq_len = hidden_ref.shape[0]
     row = 4 * layer_index
     ffn_grad = dot_nn(spread_back_ref[...], back_ref[...]) + dot_nt(
@@ -786,57 +786,6 @@
     return arrived
 
 
-def take_piece(pieces, place):
-    return lax.dynamic_index_in_dim(pieces, place, 0, False)
-
-
-def scatter_axis(values, axis_name, dim):
-    count = lax.axis_size(axis_name)
-    if count == 1:
-        return jnp.squeeze(values, dim)
-    me = lax.axis_index(axis_name)
-    total = lax.dynamic_index_in_dim(values, me, dim, False).astype(jnp.float32)
-    for turn in range(1, count):
-        sent = lax.dynamic_index_in_dim(values, (me + turn) % count, dim, False)
-        got = lax.ppermute(sent, axis_name, [(i, (i + turn) % count) for i in range(count)])
-        total = total + got.astype(jnp.float32)
-    return total.astype(jnp.bfloat16)
-
-
-def scatter_near(values):
-    sizes = [lax.axis_size(name) for name in AXES]
-    rows, columns = values.shape
-    count = 1
-    for size in sizes:
-        count *= size
-    blocks = values.reshape(*sizes, rows // count, columns)
-    return scatter_axis(blocks, "c", 4)
-
-
-def scatter_middle(blocks):
-    half = blocks.shape[-1] // 2
-    return [
-        scatter_axis(blocks[..., :half], "x", 1),
-        scatter_axis(blocks[..., half:], "y", 3),
-    ]
-
-
-def scatter_turn(parts):
-    first = scatter_axis(parts[0], "y", 2)
-    second = scatter_axis(parts[1], "x", 1)
-    return scatter_axis(jnp.concatenate([first, second], axis=-1), "h", 1)
-
-
-def scatter_planes(joined):
-    planes = lax.axis_size("z")
-    me = lax.axis_index("z")
-    parts = [take_piece(joined, me)]
-    for turn in range(1, planes):
-        sent = take_piece(joined, (me + turn) % planes)
-        parts.append(lax.ppermute(sent, "z", [(i, (i + turn) % planes) for i in range(planes)]))
-    return parts
-
-
 def scatter_sum(parts):
     total = parts[0].astype(jnp.float32)
     for part in parts[1:]:
@@ -857,6 +806,192 @@
     second = lax.reduce_precision(values - first, 8, 7)
     third = lax.reduce_precision(values - first - second, 8, 7)
     return [first, second, third]
+
+RING = ("z", "x", "y", "c")
+
+
+def owner_sum_kernel(
+    layers,
+    *refs,
+):
+    grads, refs = refs[:layers], refs[layers:]
+    (
+        out_ref,
+        own_ref,
+        core_ref,
+        near_ref,
+        joined_ref,
+        turn_ref,
+        last_ref,
+        got_ref,
+        local_sem,
+        send_sem,
+        recv_sem,
+    ) = refs
+    at = {name: lax.axis_index(name) for name in RING}
+    planes = lax.axis_size("z")
+    barrier = pltpu.get_barrier_semaphore()
+    partners = [{name: 1 - at[name]} for name in ("c", "x", "y")]
+    partners += [{"z": lax.rem(at["z"] + turn, planes)} for turn in range(1, planes)]
+    for partner in partners:
+        pl.semaphore_signal(
+            barrier, inc=1, device_id=partner, device_id_type=pl.DeviceIdType.MESH
+        )
+    pl.semaphore_wait(barrier, len(partners))
+
+    width = own_ref.shape[-1]
+    half = width // 2
+    per_layer = grads[0].shape[-1] // width
+    chunk_count = layers * per_layer
+    copies = {}
+
+    def send(chunk_index, step, source, target, partner):
+        place = chunk_index * 8 + step
+        copy = pltpu.make_async_remote_copy(
+            src_ref=source,
+            dst_ref=target,
+            send_sem=send_sem.at[place],
+            recv_sem=recv_sem.at[place],
+            device_id=partner,
+            device_id_type=pl.DeviceIdType.MESH,
+        )
+        copy.start()
+        copies[place] = copy
+
+    def arrived(chunk_index, *steps):
+        for step in steps:
+            copies[chunk_index * 8 + step].wait()
+
+    def source_of(chunk_index, core):
+        layer, part = chunk_index // per_layer, chunk_index % per_layer
+        return grads[layer].at[:, :, :, core, :, pl.ds(part * width, width)]
+
+    def added(left, right):
+        return (left.astype(jnp.float32) + right.astype(jnp.float32)).astype(jnp.bfloat16)
+
+    local = []
+    for index in range(chunk_count):
+        copy = pltpu.make_async_copy(
+            source_of(index, at["c"]), own_ref.at[index], local_sem.at[index]
+        )
+        copy.start()
+        local.append(copy)
+        send(index, 0, source_of(index, 1 - at["c"]), core_ref.at[index], partners[0])
+
+    def stage_core(index):
+        local[index].wait()
+        arrived(index, 0)
+        for plane in range(planes):
+            own_ref[index, plane] = added(own_ref[index, plane], core_ref[index, plane])
+        send(
+            index,
+            1,
+            own_ref.at[index, :, 1 - at["x"], :, :, pl.ds(0, half)],
+            near_ref.at[index, 0],
+            partners[1],
+        )
+        send(
+            index,
+            2,
+            own_ref.at[index, :, :, 1 - at["y"], :, pl.ds(half, half)],
+            near_ref.at[index, 1],
+            partners[2],
+        )
+
+    def stage_near(index):
+        arrived(index, 1, 2)
+        for plane in range(planes):
+            for other in range(2):
+                joined_ref[index, 0, plane, other] = added(
+                    own_ref[index, plane, at["x"], other, :, :half],
+                    near_ref[index, 0, plane, other],
+                )
+                joined_ref[index, 1, plane, other] = added(
+                    own_ref[index, plane, other, at["y"], :, half:],
+                    near_ref[index, 1, plane, other],
+                )
+        send(
+            index,
+            3,
+            joined_ref.at[index, 0, :, 1 - at["y"]],
+            turn_ref.at[index, 0],
+            partners[2],
+        )
+        send(
+            index,
+            4,
+            joined_ref.at[index, 1, :, 1 - at["x"]],
+            turn_ref.at[index, 1],
+            partners[1],
+        )
+
+    def stage_turn(index):
+        arrived(index, 3, 4)
+        for plane in range(planes):
+            last_ref[index, plane, :, :half] = added(
+                joined_ref[index, 0, plane, at["y"]], turn_ref[index, 0, plane]
+            )
+            last_ref[index, plane, :, half:] = added(
+                joined_ref[index, 1, plane, at["x"]], turn_ref[index, 1, plane]
+            )
+        for turn in range(1, planes):
+            send(
+                index,
+                4 + turn,
+                last_ref.at[index, partners[2 + turn]["z"]],
+                got_ref.at[index, turn - 1],
+                partners[2 + turn],
+            )
+
+    def stage_planes(index):
+        arrived(index, *[4 + turn for turn in range(1, planes)])
+        total = last_ref[index, at["z"]].astype(jnp.float32)
+        for turn in range(1, planes):
+            total = total + got_ref[index, turn - 1].astype(jnp.float32)
+        layer, part = index // per_layer, index % per_layer
+        out_ref[layer, :, part * width : (part + 1) * width] = total
+
+    stages = (stage_core, stage_near, stage_turn, stage_planes)
+    for step in range(chunk_count + len(stages) - 1):
+        for number, stage in enumerate(stages):
+            if 0 <= step - number < chunk_count:
+                stage(step - number)
+
+
+def owner_sums(grads, width=2048):
+    layers = len(grads)
+    sizes = [lax.axis_size(name) for name in RING]
+    rows, columns = grads[0].shape
+    own_rows = rows // (sizes[0] * sizes[1] * sizes[2] * sizes[3])
+    chunks = layers * columns // width
+    blocks = [grad.reshape(*sizes, own_rows, columns) for grad in grads]
+    half = width // 2
+    low = jnp.bfloat16
+    return pl.pallas_call(
+        functools.partial(owner_sum_kernel, layers),
+        out_shape=jax.ShapeDtypeStruct((layers, own_rows, columns), jnp.float32),
+        in_specs=[pl.BlockSpec(memory_space=pl.ANY)] * layers,
+        out_specs=pl.BlockSpec(memory_space=pltpu.VMEM),
+        scratch_shapes=[
+            pltpu.VMEM((chunks, sizes[0], 2, 2, own_rows, width), low),
+            pltpu.VMEM((chunks, sizes[0], 2, 2, own_rows, width), low),
+            pltpu.VMEM((chunks, 2, sizes[0], 2, own_rows, half), low),
+            pltpu.VMEM((chunks, 2, sizes[0], 2, own_rows, half), low),
+            pltpu.VMEM((chunks, 2, sizes[0], own_rows, half), low),
+            pltpu.VMEM((chunks, sizes[0], own_rows, width), low),
+            pltpu.VMEM((chunks, sizes[0] - 1, own_rows, width), low),
+            pltpu.SemaphoreType.DMA((chunks,)),
+            pltpu.SemaphoreType.DMA((chunks * 8,)),
+            pltpu.SemaphoreType.DMA((chunks * 8,)),
+        ],
+        compiler_params=pltpu.CompilerParams(
+            vmem_limit_bytes=56 * 1024 * 1024, collective_id=1, has_side_effects=True
+        ),
+        cost_estimate=pl.CostEstimate(
+            flops=1 << 26, bytes_accessed=200 * 1024 * 1024, transcendentals=0
+        ),
+    )(*blocks)
+
 
 def adam_step(weight, mean_old, square_old, gradient):
     mean_new = BETA_ONE * mean_old + (1.0 - BETA_ONE) * gradient
@@ -867,6 +1002,131 @@
         mean_new / bias_one / (jnp.sqrt(square_new / bias_two) + ADAM_EPS) + DECAY_RATE * weight
     )
     return (mean_new, square_new, update)
+
+
+VOCAB_BLOCK = 2048
+VOCAB_PART = 512
+
+
+def embedding_kernel(
+    row_ref,
+    low_ref,
+    high_ref,
+    arrived_ref,
+    word_ref,
+    group_ref,
+    weight_ref,
+    mean_ref,
+    square_ref,
+    mean_out_ref,
+    square_out_ref,
+    update_ref,
+    wide_ref,
+    sorted_ref,
+    turned_ref,
+    total_ref,
+):
+    step = pl.program_id(0)
+    device_count = arrived_ref.shape[0]
+    token_count = sorted_ref.shape[0]
+    columns = weight_ref.shape[0]
+    groups = LANES // columns
+
+    @pl.when(step == 0)
+    def _():
+        for part in range(wide_ref.shape[0] // device_count):
+            wide_ref[part * device_count : (part + 1) * device_count, :] = arrived_ref[
+                :, part * LANES : (part + 1) * LANES
+            ].astype(jnp.float32)
+
+        @pl.loop(0, token_count // 32)
+        def _(block):
+            start = pl.multiple_of(block * 32, 32)
+            for place in range(32):
+                sorted_ref[pl.ds(start + place, 1), :] = wide_ref[pl.ds(row_ref[start + place], 1), :]
+
+        row_place = lax.broadcasted_iota(jnp.int32, (LANES, LANES), 0)
+        lane = lax.broadcasted_iota(jnp.int32, (LANES, LANES), 1)
+        same = jnp.where(row_place == lane, 1.0, 0.0).astype(jnp.bfloat16)
+
+        @pl.loop(0, token_count // LANES)
+        def _(block):
+            rows = pl.ds(pl.multiple_of(block * LANES, LANES), LANES)
+            turned = dot_nt(same, sorted_ref[rows, :].astype(jnp.bfloat16))
+            group = group_ref[pl.ds(block, 1), :]
+            kept = jnp.where(group == 0, turned[:columns, :], 0.0)
+            for place in range(1, groups):
+                kept += jnp.where(
+                    group == place, turned[place * columns : (place + 1) * columns, :], 0.0
+                )
+            turned_ref[:, rows] = kept.astype(jnp.bfloat16)
+
+    for part in range(VOCAB_BLOCK // VOCAB_PART):
+        total_ref[...] = jnp.zeros_like(total_ref)
+        place = step * (VOCAB_BLOCK // VOCAB_PART) + part
+        first = place * VOCAB_PART
+
+        @pl.loop(low_ref[place], high_ref[place])
+        def _(block):
+            rows = pl.ds(pl.multiple_of(block * LANES, LANES), LANES)
+            word = lax.broadcasted_iota(jnp.int32, (VOCAB_PART, LANES), 0)
+            hit = word == word_ref[pl.ds(block, 1), :] - first
+            hit = jnp.where(hit, 1.0, 0.0).astype(jnp.bfloat16)
+            total_ref[...] += dot_nt(turned_ref[:, rows], hit)
+
+        gradient = total_ref[...]
+        words = slice(part * VOCAB_PART, (part + 1) * VOCAB_PART)
+        mean_new, square_new, update = adam_step(
+            weight_ref[:, words], mean_ref[:, words], square_ref[:, words], gradient
+        )
+        mean_out_ref[:, words] = mean_new
+        square_out_ref[:, words] = square_new
+        update_ref[:, words] = update
+
+
+def token_order(tokens, seq_len, vocabulary, groups):
+    count = tokens.shape[0]
+    devices = count // seq_len
+    keys = lax.sort(tokens * count + jnp.arange(count, dtype=jnp.int32))
+    words, origin = keys // count, keys % count
+    device, place = origin // seq_len, origin % seq_len
+    row = (place // groups) * devices + device
+    words = words.reshape(count // LANES, LANES)
+    group = (place % groups).reshape(count // LANES, LANES)
+    steps = -(-vocabulary // VOCAB_BLOCK) * (VOCAB_BLOCK // VOCAB_PART)
+    edges = jnp.arange(steps + 1, dtype=jnp.int32) * VOCAB_PART
+    below = jnp.sum((tokens[None, :] < edges[:, None]).astype(jnp.int32), axis=1)
+    low = below[:-1] // LANES
+    high = (below[1:] + LANES - 1) // LANES
+    high = jnp.where(below[1:] > below[:-1], high, low)
+    return row, low, high, words, group
+
+
+def embedding_update_of(order, arrived, weight, mean, square):
+    row, low, high, words, group = order
+    count = row.shape[0]
+    columns, vocabulary = weight.shape
+    block = pl.BlockSpec((columns, VOCAB_BLOCK), lambda step: (0, step))
+    whole = pl.BlockSpec(memory_space=pltpu.VMEM)
+    scalar = pl.BlockSpec(memory_space=pltpu.SMEM)
+    wide = count * columns // LANES
+    return pl.pallas_call(
+        embedding_kernel,
+        grid=(-(-vocabulary // VOCAB_BLOCK),),
+        out_shape=[jax.ShapeDtypeStruct(weight.shape, jnp.float32)] * 3,
+        in_specs=[scalar] * 3 + [whole] * 3 + [block] * 3,
+        out_specs=[block] * 3,
+        scratch_shapes=[
+            pltpu.VMEM((wide, LANES), jnp.float32),
+            pltpu.VMEM((count, LANES), jnp.float32),
+            pltpu.VMEM((columns, count), jnp.bfloat16),
+            pltpu.VMEM((columns, VOCAB_PART), jnp.float32),
+        ],
+        compiler_params=pltpu.CompilerParams(vmem_limit_bytes=48 * 1024 * 1024),
+        cost_estimate=pl.CostEstimate(
+            flops=1 << 32, bytes_accessed=50 * 1024 * 1024, transcendentals=1 << 20
+        ),
+    )(row, low, high, arrived, words, group, weight, mean, square)
 
 
 def shards(
@@ -919,36 +1179,6 @@
         [group_experts.index(expert) for expert in range(experts_all)], jnp.int32
     )
 
-    attention_low = lax.all_gather(attention.astype(jnp.bfloat16), AXES, axis=1, tiled=True)
-
-    table_low = embedding.astype(jnp.bfloat16)
-    looked_up = jnp.take(table_low, tokens, axis=0).reshape(devices_all, seq_len * column_count)
-    small_count = gain_count + layer_count * experts_all
-    small = jnp.concatenate(
-        [norm_gains.T, router.transpose(1, 0, 2).reshape(column_count, layer_count * experts_all)],
-        axis=1,
-    ).astype(jnp.bfloat16)
-    small = jnp.broadcast_to(
-        small.reshape(1, column_count * small_count), (devices_all, column_count * small_count)
-    )
-    arrived_rows = send_all(jnp.concatenate([looked_up, small], axis=1))
-    hidden = (
-        arrived_rows[:, : seq_len * column_count]
-        .reshape(devices_all, seq_len, column_count)
-        .transpose(1, 0, 2)
-        .reshape(seq_len, D)
-        .astype(jnp.float32)
-    )
-    small_all = arrived_rows[:, seq_len * column_count :].reshape(D, small_count)
-    gain_rows = jnp.pad(
-        small_all[:, :gain_count].T.astype(jnp.float32), ((0, 16 - gain_count), (0, 0))
-    )
-    router_low = jnp.pad(
-        small_all[:, gain_count:]
-        .reshape(D, layer_count, experts_all)
-        .transpose(1, 0, 2)[:, :, group_order],
-        ((0, 0), (0, 0), (0, LANES - experts_all)),
-    )
 
     head_low = output_table.astype(jnp.bfloat16)
     vocab_local = head_low.shape[0]
@@ -959,28 +1189,25 @@
     coefficients = jnp.concatenate(
         [jnp.ones((position_count, 1), jnp.float32), teacher_prob], axis=1
     )
-    local_ids = loss_ids - me_all * vocab_local
-    vocab_place = jnp.arange(vocab_local, dtype=jnp.int32)
-    marked = jnp.sum(
-        jnp.where(
-            local_ids[:, :, None] == vocab_place[None, None, :], coefficients[:, :, None], 0.0
-        ),
+    table_low = embedding.astype(jnp.bfloat16)
+    looked_up = jnp.take(table_low, tokens, axis=0).reshape(devices_all, seq_len * column_count)
+    attention_low = []
+    for layer_index in range(layer_count):
+        rows_low = attention[layer_index].astype(jnp.bfloat16)
+        if layer_index > 0:
+            rows_low, looked_up = tie(rows_low, looked_up)
+        attention_low.append(lax.all_gather(rows_low, AXES, axis=0, tiled=True))
+    small_count = gain_count + layer_count * experts_all
+    small = jnp.concatenate(
+        [norm_gains.T, router.transpose(1, 0, 2).reshape(column_count, layer_count * experts_all)],
         axis=1,
-    )
-    marked_pull = jnp.dot(
-        marked.astype(jnp.bfloat16), head_low, preferred_element_type=jnp.float32
-    )
-    own_count = position_count // devices_all
-    marked_arrived = send_all(
-        marked_pull.astype(jnp.bfloat16).reshape(devices_all, own_count, D)
-    )
-
+    ).astype(jnp.bfloat16)
+    small = jnp.broadcast_to(
+        small.reshape(1, column_count * small_count), (devices_all, column_count * small_count)
+    )
+    arrived_rows = send_all(jnp.concatenate([looked_up, small], axis=1))
     expert_parts = []
     for layer_index in range(layer_count):
-        if layer_index == 1:
-            attention_low, marked, marked_arrived = lax.optimization_barrier(
-                (attention_low, marked, marked_arrived)
-            )
         down_piece = (
             expert_down[0, layer_index]
             .reshape(F // piece_rows, piece_rows, piece_rows)
@@ -991,8 +1218,30 @@
             jnp.bfloat16
         )
         if layer_index > 0:
-            piece, attention_low = tie(piece, attention_low)
+            piece, attention_low[0] = tie(piece, attention_low[0])
+        else:
+            piece, arrived_rows = tie(piece, arrived_rows)
         expert_parts.append(spread_experts(piece, row_groups))
+
+    hidden = (
+        arrived_rows[:, : seq_len * column_count]
+        .reshape(devices_all, seq_len, column_count)
+        .transpose(1, 0, 2)
+        .reshape(seq_len, D)
+        .astype(jnp.float32)
+    )
+    small_all = arrived_rows[:, seq_len * column_count :].reshape(D, small_count)
+    gain_rows = jnp.pad(
+        small_all[:, :gain_count].T.astype(jnp.float32), ((0, 16 - gain_count), (0, 0))
+    )
+    router_low = jnp.pad(
+        small_all[:, gain_count:]
+        .reshape(D, layer_count, experts_all)
+        .transpose(1, 0, 2)[:, :, group_order],
+        ((0, 0), (0, 0), (0, LANES - experts_all)),
+    )
+
+    fits_sum = [lax.axis_size(name) for name in AXES] == [PLANES, 2, 1, 2, 2]
 
     member = jnp.any(routes[:, :, None] == group_order[None, None, :], axis=1)
     before = jnp.dot(
@@ -1024,7 +1273,7 @@
             prefix,
             hidden,
             extra,
-            attention_low,
+            attention_low[layer_index],
             gain_rows,
             turns,
             router_low,
@@ -1035,15 +1284,34 @@
         hidden = saved[6]
         gates, outgoing = saved[9], saved[10]
         if layer_index > 0:
-            expert_parts[layer_index][2], outgoing = tie(expert_parts[layer_index][2], outgoing)
+            expert_parts[layer_index][2:], outgoing = tie(expert_parts[layer_index][2:], outgoing)
         received = send_plane(outgoing.reshape(experts_all, capacity, D)).reshape(slot_total, D)
+        if layer_index == 0:
+            ids_now, tokens_now, outgoing = lax.optimization_barrier((loss_ids, tokens, outgoing))
+            local_ids = ids_now - me_all * vocab_local
+            vocab_place = jnp.arange(vocab_local, dtype=jnp.int32)
+            marked = jnp.sum(
+                jnp.where(
+                    local_ids[:, :, None] == vocab_place[None, None, :], coefficients[:, :, None], 0.0
+                ),
+                axis=1,
+            )
+            order = token_order(tokens_now, seq_len, embedding.shape[0], LANES // column_count)
+            marked, order, received = lax.optimization_barrier((marked, order, received))
         upcoming = expert_parts[layer_index + 1] if layer_index + 1 < layer_count else None
-        if upcoming is not None:
-            upcoming[0], received = tie(upcoming[0], received)
         produced = run_expert(places, received, expert_parts[layer_index])
         returned = send_plane(produced.reshape(experts_all, capacity, D)).reshape(slot_total, D)
+        if layer_index == 0:
+            marked_pull = jnp.dot(
+                marked.astype(jnp.bfloat16), head_low, preferred_element_type=jnp.float32
+            )
+            own_count = position_count // devices_all
+            marked_arrived = send_all(
+                marked_pull.astype(jnp.bfloat16).reshape(devices_all, own_count, D)
+            )
+            marked_arrived, returned = tie(marked_arrived, returned)
         if upcoming is not None:
-            upcoming[1], returned = tie(upcoming[1], returned)
+            upcoming[:2], returned = tie(upcoming[:2], returned)
         stored.append((saved, received, returned))
         extra = (gates, returned)
 
@@ -1118,9 +1386,6 @@
         logit_low, router_parts[layer_index] = router_back(
             capacity, grad_hidden, returned, spread_back, probs, ffn_low
         )
-        if upper is not None:
-            near, output_grad = tie(attention_parts[upper], output_grad)
-            middle_parts = scatter_middle(near)
         input_grad, gate_grad, activated = run_expert_back(
             places, received, output_grad, expert_parts[layer_index]
         )
@@ -1130,7 +1395,8 @@
         grad_pieces = run_expert_grad(
             places, received, output_grad, gate_grad, activated, piece_rows
         )
-        piece_parts[layer_index] = return_expert_grads(grad_pieces, row_groups)
+        if layer_index > 0:
+            piece_parts[layer_index] = return_expert_grads(grad_pieces, row_groups)
         if upper is not None:
             piece_parts[upper][2:], back_inputs = tie(piece_parts[upper][2:], back_inputs)
         lower = (spread_flat, stored[layer_index - 1][0][9]) if layer_index > 0 else ()
@@ -1148,7 +1414,7 @@
             values,
             attended,
             middle,
-            attention_low,
+            attention_low[layer_index],
             gain_rows,
             turns,
             router_low,
@@ -1160,10 +1426,11 @@
         if layer_index > 0:
             sent_back = results[3]
             piece_parts[layer_index][:2], sent_back = tie(piece_parts[layer_index][:2], sent_back)
-        attention_parts[layer_index] = scatter_near(weight_grad)
-        if upper is not None:
-            middle_parts, grad_hidden = tie(middle_parts, grad_hidden)
-            attention_parts[upper] = scatter_sum(scatter_planes(scatter_turn(middle_parts)))
+        attention_parts[layer_index] = weight_grad
+        if not fits_sum:
+            attention_parts[layer_index] = lax.psum_scatter(
+                weight_grad, AXES, scatter_dimension=0, tiled=True
+            ).astype(jnp.float32)
 
     sending = (
         grad_hidden.astype(jnp.bfloat16)
@@ -1179,12 +1446,20 @@
             [sending, small_grads.reshape(devices_all, column_count * small_count)], axis=1
         )
     )
-    attention_parts[0], arrived_grads, piece_parts = lax.optimization_barrier(
-        (attention_parts[0], arrived_grads, piece_parts)
-    )
-    attention_parts[0] = scatter_sum(
-        scatter_planes(scatter_turn(scatter_middle(attention_parts[0])))
-    )
+    if fits_sum:
+        attention_parts = list(owner_sums(attention_parts[::-1], 2048))[::-1]
+    grad_pieces, arrived_grads, attention_parts = lax.optimization_barrier(
+        (grad_pieces, arrived_grads, attention_parts)
+    )
+    piece_parts[0] = return_expert_grads(grad_pieces, row_groups)
+    embedding_next = embedding_update_of(
+        order,
+        arrived_grads[:, : seq_len * column_count],
+        embedding.T,
+        embedding_mean.T,
+        embedding_square.T,
+    )
+    piece_parts[0], embedding_next = tie(piece_parts[0], embedding_next)
     up_parts, down_parts = [], []
     for parts in piece_parts:
         piece_grad = scatter_sum(parts)
@@ -1195,13 +1470,6 @@
             .transpose(1, 0, 2)
             .reshape(F, piece_rows)
         )
-    embedding_grad = jax.ops.segment_sum(
-        arrived_grads[:, : seq_len * column_count]
-        .astype(jnp.float32)
-        .reshape(devices_all * seq_len, column_count),
-        tokens,
-        num_segments=embedding.shape[0],
-    )
     small_total = jnp.sum(
         arrived_grads[:, seq_len * column_count :].astype(jnp.float32), axis=0
     ).reshape(column_count, small_count)
@@ -1214,9 +1482,9 @@
     attention_grad = jnp.stack(attention_parts)
     upward_grad = jnp.stack(up_parts)[None]
     downward_grad = jnp.stack(down_parts)[None]
-    embedding_mean_next, embedding_square_next, embedding_update = adam_step(
-        embedding, embedding_mean, embedding_square, embedding_grad
-    )
+    embedding_mean_next, embedding_square_next, embedding_update = [
+        part.T for part in embedding_next
+    ]
     attention_mean_next, attention_square_next, attention_update = adam_step(
         attention, attention_mean, attention_square, attention_grad
     )

time: 1240 us -> 1030 us (0.83)
  waiting for transfers between devices: 424 us -> 227 us
  Pallas kernels: 151 us -> 306 us
  other arithmetic: 165 us -> 69.9 us
  local copies, waits for them, and re-layouts: 153 us -> 102 us
  starting transfers between devices: 192 us -> 145 us
  blocking collectives: 95.1 us -> 124 us
    pallas_call x0 -> x2, Pallas kernels: none -> 155 us  [the longest x1 99.5 us: owner_sums(): pl.pallas_call(functools.partial(owner_sum_kernel, layers), out_shape=jax...]
    ppermute x8, waiting for transfers between devices: 86.3 us -> 12.4 us  [spread_experts(): lax.ppermute(piece, ('z', 'h', 'y', 'c'), swap_pairs(row_groups, turn_pla...]
    ppermute x8, waiting for transfers between devices: 138 us -> 67.5 us  [return_expert_grads(): arrived.append(lax.ppermute(piece, ('z', 'h', 'y', 'c'), back))]
    scatter-add x1 -> x0, other arithmetic: 54.7 us -> none  [shards(): jax.ops.segment_sum(arrived_grads[:, :seq_len * column_count].astype(jnp....]
    ppermute x16 -> x0, waiting for transfers between devices: 52.2 us -> none  [the longest x6 33.6 us: scatter_planes(): lax.ppermute(sent, 'z', [(i, (i + turn) % planes) for i in range(planes)])]
    all_to_all x6 -> x5, waiting for transfers between devices: 63.1 us -> 104 us  [send_plane(): lax.all_to_all(values, ('x', 'y', 'c'), split_axis=0, concat_axis=0, tile...]
    ppermute x8, starting transfers between devices: 66.8 us -> 28.4 us  [return_expert_grads(): arrived.append(lax.ppermute(piece, ('z', 'h', 'y', 'c'), back))]
    all_to_all x2 -> x3, blocking collectives: 63.7 us -> 101 us  [send_plane(): lax.all_to_all(values, ('x', 'y', 'c'), split_axis=0, concat_axis=0, tile...]
  transfers between devices with their start and end apart: 44 -> 28, of which waited for: 23 -> 10; matrix products, arithmetic and copies ran while one was open for 22% -> 13% of each run, Pallas kernels for 5% -> 25%
where the time goes in v3:
time: 1030 us; the launch traced here: 1020 us
  Pallas kernels  306 us (30%)
  waiting for transfers between devices  227 us (22%)
  starting transfers between devices  145 us (14%)
  blocking collectives  124 us (12%)
  local copies, waits for them, and re-layouts  102 us (10%)
  other arithmetic  69.9 us (7%)
  matrix products  25.5 us (2%)
  between operations  20.3 us (2%)
    all_to_all x5, waiting for transfers between devices, send_plane(): lax.all_to_all(values, ('x', 'y', 'c'), split_axis=0, concat_axis=0, tile...  104 us
    all_to_all x3, blocking collectives, send_plane(): lax.all_to_all(values, ('x', 'y', 'c'), split_axis=0, concat_axis=0, tile...  101 us
    pallas_call x1, Pallas kernels, owner_sums(): pl.pallas_call(functools.partial(owner_sum_kernel, layers), out_shape=jax...  99.5 us
    ppermute x8, waiting for transfers between devices, return_expert_grads(): arrived.append(lax.ppermute(piece, ('z', 'h', 'y', 'c'), back))  67.5 us
    all_to_all x5, starting transfers between devices, send_all(): return lax.all_to_all(values, AXES, split_axis=0, concat_axis=0, tiled=True)  62.3 us
    pallas_call x1, Pallas kernels, embedding_update_of(): pl.pallas_call(embedding_kernel, grid=(-(-vocabulary // VOCAB_BLOCK),), o...  55.5 us
    all_to_all x5, waiting for transfers between devices, send_all(): return lax.all_to_all(values, AXES, split_axis=0, concat_axis=0, tiled=True)  43 us
    pallas_call x2, Pallas kernels, backward_layer(): pl.pallas_call(functools.partial(backward_kernel, layer_index, capacity),...  41.6 us
  transfers between devices with their start and end apart: 28, of which 10 were waited for; matrix products, arithmetic and copies ran while one was open for 13% of the time, Pallas kernels for 25%

profile of v3, /device:TPU:9, one launch (start us, length us, event | category | flops | bytes accessed | tf_op | source)
XLA Modules:
  0.0 1019.8 jit_solution(7909307634591512281)
XLA Ops:
  16.4 8.8 copy.270
  25.2 28.2 %gather_fusion = bf16[8192,32]{1,0:T(8,128)(2,1)S(1)} fusion(bf16[50304,32]{1,0:T(8,128)(2,1)} %copy.270, s32[8192]{0:T(1024)S(1)} %fusion.34), kind=kCustom, calls=%fused_computation | custom fusion | bytes 1081344 | tf_op jit(solution)/shard_map/jit(_take)/gather | solution.py:1193
  79.3 17.2 %all-to-all-done = bf16[32,2,4496]{2,1,0:T(2,128)(2,1)} async-done(((bf16[32,2,4496]{2,1,0:T(2,128)(2,1)}), bf16[32,2,4496]{2,1,0:T(2,128)(2,1)}, u32[]{:S(2)}, u32[]{:S(2)}) %all-to-all-start) | async-done | bytes 575520 | tf_op jit(solution)/shard_map/all_to_all | solution.py:797
  105.7 7.8 collective-permute-start.3
  126.3 13.7 %shard_map.480 = (f32[256,1024]{1,0:T(8,128)}, f32[256,2048]{1,0:T(8,128)}, bf16[256,1024]{1,0:T(8,128)(2,1)}, bf16[256,1024]{1,0:T(8,128)(2,1)}, bf16[256,1024]...) custom-call(s32[1]{0:T(128)S(6)} %copy.317.prefix_ref, ...), custom_call_target="tpu_custom_call" | custom-call | flops 3221225472 | bytes 25165824 | tf_op jit(solution)/shard_map/pallas_call | solution.py:234
  155.3 13.1 %select_reduce_fusion = f32[256,1572]{0,1:T(8,128)S(1)} fusion(f32[256,65]{0,1:T(8,128)S(1)} %concatenate.89, s32[256,65]{0,1:T(8,128)S(1)} %broadcast_subtract_fusion), kind=kLoop, calls=%fused_computation.4 | loop fusion | flops 78071808 | bytes 1742848 | tf_op jit(solution)/shard_map/reduce_sum | solution.py:1293
  168.4 22.5 %all-to-all-done.1 = bf16[8,144,1024]{2,1,0:T(8,128)(2,1)} async-done(((bf16[8,144,1024]{2,1,0:T(8,128)(2,1)}), bf16[8,144,1024]{2,1,0:T(8,128)(2,1)}, u32[]{:S(2)}, u32[]{:S(2)}) %all-to-all-start.1) | async-done | bytes 2359328 | tf_op jit(solution)/shard_map/all_to_all | solution.py:801
  205.1 9.8 shard_map.481
  214.9 14.2 %all-to-all-done.2 = bf16[32,8,1024]{2,1,0:T(8,128)(2,1)S(1)} async-done(((bf16[32,8,1024]{2,1,0:T(8,128)(2,1)}), bf16[32,8,1024]{2,1,0:T(8,128)(2,1)S(1)}, u32[]{:S(2)}, u32[]{:S(2)}) %all-to-all-start.2) | async-done | bytes 524320 | tf_op jit(solution)/shard_map/all_to_all | solution.py:797
  247.2 28.9 %all-to-all-done.3 = bf16[8,144,1024]{2,1,0:T(8,128)(2,1)S(1)} async-done(((bf16[8,144,1024]{2,1,0:T(8,128)(2,1)}), bf16[8,144,1024]{2,1,0:T(8,128)(2,1)S(1)}, u32[]{:S(2)}, u32[]{:S(2)}) %all-to-all-start.3) | async-done | bytes 2359328 | tf_op jit(solution)/shard_map/all_to_all | solution.py:801
  282.5 16.7 %shard_map.482 = (f32[256,1024]{1,0:T(8,128)}, f32[256,2048]{1,0:T(8,128)}, bf16[256,1024]{1,0:T(8,128)(2,1)}, bf16[256,1024]{1,0:T(8,128)(2,1)}, bf16[256,1024]...) custom-call(s32[1]{0:T(128)S(6)} %copy.317.prefix_ref, ...), custom_call_target="tpu_custom_call" | custom-call | flops 3221225472 | bytes 25165824 | tf_op jit(solution)/shard_map/pallas_call | solution.py:234
  305.2 36.1 %all_to_all.88 = bf16[8,144,1024]{2,1,0:T(8,128)(2,1)} all-to-all(bf16[8,144,1024]{2,1,0:T(8,128)(2,1)} %bitcast.192), channel_id=1, replica_groups=mesh['z'=4,'x'=2,'h'=1,'y'=2,'c'=2] {'x','y','c'}, dimensions={0} | all-to-all | bytes 4718592 | tf_op jit(solution)/shard_map/all_to_all | solution.py:801
  341.4 9.7 shard_map.483
  351.2 33.0 %all_to_all.89 = bf16[8,144,1024]{2,1,0:T(8,128)(2,1)S(1)} all-to-all(bf16[8,144,1024]{2,1,0:T(8,128)(2,1)} %bitcast.193), channel_id=1, replica_groups=mesh['z'=4,'x'=2,'h'=1,'y'=2,'c'=2] {'x','y','c'}, dimensions={0} | all-to-all | bytes 4718592 | tf_op jit(solution)/shard_map/all_to_all | solution.py:801
  386.8 22.6 %all_to_all.90 = bf16[32,8,1024]{2,1,0:T(8,128)(2,1)S(1)} all-to-all(bf16[32,8,1024]{2,1,0:T(8,128)(2,1)S(1)} %broadcast_in_dim.98), channel_id=1, replica_groups=mesh['z'=4,'x'=2,'h'=1,'y'=2,'c'=2] {'z','x','h','y','c'}, dimensions={0} | all-to-all | bytes 1048576 | tf_op jit(solution)/shard_map/all_to_all | solution.py:797
  433.8 11.6 %all-to-all-done.7 = bf16[32,8,1152]{2,1,0:T(8,128)(2,1)} async-done(((bf16[32,8,1152]{2,1,0:T(8,128)(2,1)}), bf16[32,8,1152]{2,1,0:T(8,128)(2,1)}, u32[]{:S(2)}, u32[]{:S(2)}) %all-to-all-start.7) | async-done | bytes 589856 | tf_op jit(solution)/shard_map/all_to_all | solution.py:797
  460.2 32.1 %all_to_all.91 = bf16[8,144,1024]{2,1,0:T(8,128)(2,1)} all-to-all(bf16[8,144,1024]{2,1,0:T(8,128)(2,1)S(1)} %bitcast.166), channel_id=1, replica_groups=mesh['z'=4,'x'=2,'h'=1,'y'=2,'c'=2] {'x','y','c'}, dimensions={0} | all-to-all | bytes 4718592 | tf_op jit(solution)/shard_map/all_to_all | solution.py:801
  492.4 13.9 %shard_map.486 = (bf16[1152,1024]{1,0:T(8,128)(2,1)}, bf16[1152,1024]{1,0:T(8,128)(2,1)}, bf16[1152,512]{1,0:T(8,128)(2,1)}) custom-call(s32[4]{0:T(128)} %pad_add_fusion.place_ref, bf16[1152,1024]{1,0:T(8,128)(2,1)} %bitcast.181, bf16[1152,1024]{1,0:T(8,128)(2,1)} %bitcast.190, bf16[256,1536]{1,0:T(8,128)(2,1)} %collective-permute-done.refs_0_, ...), custom_call_target="tpu_custom_call" | custom-call | flops 7247757312 | bytes 12582912 | tf_op jit(solution)/shard_map/pallas_call | solution.py:545
  511.3 10.7 %shard_map.487 = (bf16[256,1536]{1,0:T(8,128)(2,1)}, bf16[256,1536]{1,0:T(8,128)(2,1)}, bf16[256,1536]{1,0:T(8,128)(2,1)}, bf16[256,1536]{1,0:T(8,128)(2,1)}) custom-call(s32[4]{0:T(128)} %pad_add_fusion.place_ref, bf16[1152,1024]{1,0:T(8,128)(2,1)} %bitcast.182, bf16[1152,1024]{1,0:T(8,128)(2,1)} %bitcast.191, ...), custom_call_target="tpu_custom_call" | custom-call | flops 3623878656 | bytes 12582912 | tf_op jit(solution)/shard_map/pallas_call | solution.py:596
  524.1 7.4 collective-permute-start.9
  534.9 19.0 %all-to-all-done.10 = bf16[8,144,1024]{2,1,0:T(8,128)(2,1)} async-done(((bf16[8,144,1024]{2,1,0:T(8,128)(2,1)}), bf16[8,144,1024]{2,1,0:T(8,128)(2,1)}, u32[]{:S(2)}, u32[]{:S(2)}) %all-to-all-start.10) | async-done | bytes 2359328 | tf_op jit(solution)/shard_map/all_to_all | solution.py:801
  554.6 21.7 %all-to-all-start.8 = ((f32[32,1,16]{2,1,0:T(1,128)}), f32[32,1,16]{2,1,0:T(1,128)S(1)}, u32[]{:S(2)}, u32[]{:S(2)}) async-start(f32[32,1,16]{2,1,0:T(1,128)} %broadcast_in_dim.99), calls=%async_computation.8 | async-start | bytes 32768 | tf_op jit(solution)/shard_map/all_to_all | solution.py:797
  576.3 21.3 %shard_map.489 = (f32[256,1024]{1,0:T(8,128)}, bf16[1024,4096]{1,0:T(8,128)(2,1)}, f32[8,1024]{1,0:T(8,128)}, bf16[1152,1024]{1,0:T(8,128)(2,1)}) custom-call(s32[1]{0:T(128)S(6)} %copy.317.prefix_ref, f32[256,1024]{1,0:T(8,128)} %copy-done.8, bf16[1152,1024]{1,0:T(8,128)(2,1)} %bitcast.47.back_ref, bf16[256,128]{1,0:T(8,128)(2,1)} %copy-done.24, ...), custom_call_target="tpu_custom_call" | custom-call | flops 6442450944 | bytes 33554432 | tf_op jit(solution)/shard_map/pallas_call | solution.py:398
  611.4 33.2 %all-to-all-done.11 = bf16[8,144,1024]{2,1,0:T(8,128)(2,1)S(1)} async-done(((bf16[8,144,1024]{2,1,0:T(8,128)(2,1)}), bf16[8,144,1024]{2,1,0:T(8,128)(2,1)S(1)}, u32[]{:S(2)}, u32[]{:S(2)}) %all-to-all-start.11) | async-done | bytes 2359328 | tf_op jit(solution)/shard_map/all_to_all | solution.py:801
  646.0 13.9 %shard_map.490 = (bf16[1152,1024]{1,0:T(8,128)(2,1)}, bf16[1152,1024]{1,0:T(8,128)(2,1)}, bf16[1152,512]{1,0:T(8,128)(2,1)}) custom-call(s32[4]{0:T(128)} %pad_add_fusion.place_ref, bf16[1152,1024]{1,0:T(8,128)(2,1)} %bitcast.28.received_ref, bf16[1152,1024]{1,0:T(8,128)(2,1)} %bitcast.183, bf16[256,1536]{1,0:T(8,128)(2,1)} %collective-permute-done.2.refs_0_, ...), custom_call_target="tpu_custom_call" | custom-call | flops 7247757312 | bytes 12582912 | tf_op jit(solution)/shard_map/pallas_call | solution.py:545
  665.5 14.1 %add_multiply_fusion = (f32[1572,1024]{1,0:T(8,128)}, f32[1572,1024]{1,0:T(8,128)}, f32[1572,1024]{1,0:T(8,128)}) fusion(f32[1572,1024]{1,0:T(8,128)} %param.57, f32[1572,1024]{1,0:T(8,128)} %param.59, f32[1572,1024]{1,0:T(8,128)} %param.58, bf16[32,8,1024]{2,1,0:T(8,128)(2,1)} %copy-done.43, f32[256,1572]{0,1:T(8,128)} %copy-done.25, ...), kind=kOutput, calls=%fused_computation.8 | convolution fusion | flops 848729088 | bytes 42379264 | tf_op jit(solution)/shard_map/pv,pd->vd/dot_general | solution.py:1367
  688.4 11.0 %shard_map.491 = (bf16[256,1536]{1,0:T(8,128)(2,1)}, bf16[256,1536]{1,0:T(8,128)(2,1)}, bf16[256,1536]{1,0:T(8,128)(2,1)}, bf16[256,1536]{1,0:T(8,128)(2,1)}) custom-call(s32[4]{0:T(128)} %pad_add_fusion.place_ref, bf16[1152,1024]{1,0:T(8,128)(2,1)} %bitcast.28.received_ref, bf16[1152,1024]{1,0:T(8,128)(2,1)} %bitcast.184, ...), custom_call_target="tpu_custom_call" | custom-call | flops 3623878656 | bytes 12582912 | tf_op jit(solution)/shard_map/pallas_call | solution.py:596
  699.4 20.3 %shard_map.493 = (f32[256,1024]{1,0:T(8,128)}, bf16[1024,4096]{1,0:T(8,128)(2,1)}, f32[8,1024]{1,0:T(8,128)}) custom-call(s32[1]{0:T(128)S(6)} %copy.317.prefix_ref, f32[256,1024]{1,0:T(8,128)} %get-tuple-element.172.grad_ref, bf16[1152,1024]{1,0:T(8,128)(2,1)} %bitcast.51.back_ref, bf16[256,128]{1,0:T(8,128)(2,1)} %copy-done.23, ...), custom_call_target="tpu_custom_call" | custom-call | flops 6442450944 | bytes 33554432 | tf_op jit(solution)/shard_map/pallas_call | solution.py:398
  732.9 24.2 %all-to-all-start.13 = ((bf16[32,2,4496]{2,1,0:T(2,128)(2,1)}), bf16[32,2,4496]{2,1,0:T(2,128)(2,1)S(1)}, u32[]{:S(2)}, u32[]{:S(2)}) async-start(bf16[32,2,4496]{2,1,0:T(2,128)(2,1)} %reshape.626), calls=%async_computation.13 | async-start | bytes 1179648 | tf_op jit(solution)/shard_map/all_to_all | solution.py:797
  757.1 99.5 %shard_map.494 = f32[2,32,4096]{2,1,0:T(8,128)} custom-call(bf16[4,2,2,2,32,4096]{5,4,3,2,1,0:T(8,128)(2,1)} %bitcast.172, bf16[4,2,2,2,32,4096]{5,4,3,2,1,0:T(8,128)(2,1)} %bitcast.173), custom_call_target="tpu_custom_call" | custom-call | flops 67108864 | bytes 209715200 | tf_op jit(solution)/shard_map/pallas_call | solution.py:970
  873.0 55.5 %shard_map.495 = (f32[32,50304]{1,0:T(8,128)}, f32[32,50304]{1,0:T(8,128)}, f32[32,50304]{1,0:T(8,128)}) custom-call(s32[8192]{0:T(1024)S(1)} %copy-done.16, s32[100]{0:T(128)S(1)} %get-tuple-element.198.low_ref, s32[100]{0:T(128)S(1)} %get-tuple-element.199.high_ref, bf16[32,8192]{1,0:T(8,128)(2,1)S(1)} %slice.122.arrived_ref, s32[64,128]{1,0:T(8,128)S(1)} %copy-done.17, ...), custom_call_target="tpu_custom_call" | custom-call | flops 4294967296 | bytes 52428800 | tf_op jit(solution)/shard_map/pallas_call | solution.py:1113
  930.7 67.5 %collective-permute-done.15 = bf16[256,1536]{1,0:T(8,128)(2,1)S(1)} collective-permute-done((bf16[256,1536]{1,0:T(8,128)(2,1)}, bf16[256,1536]{1,0:T(8,128)(2,1)S(1)}, u32[]{:S(2)}, u32[]{:S(2)}) %collective-permute-start.15) | collective-permute-done | bytes 786464 | tf_op jit(solution)/shard_map/ppermute | solution.py:785
  (369 shorter events, 240.3 us)
Async XLA Ops:
  7.2 119.1 %all-gather.6.cloned.1.call-start = ((), (), s32[]{:S(2)}) async-start(), calls=%async_computation.15 | async-start | bytes 8650752 | tf_op jit(solution)/shard_map/all_gather | solution.py:1199
  9.4 273.2 %all-gather.4.cloned.1.call-start = ((), (), s32[]{:S(2)}) async-start(), calls=%async_computation.14 | async-start | bytes 8650752 | tf_op jit(solution)/shard_map/all_gather | solution.py:1199
  59.7 36.7 %all-to-all-start = ((bf16[32,2,4496]{2,1,0:T(2,128)(2,1)}), bf16[32,2,4496]{2,1,0:T(2,128)(2,1)}, u32[]{:S(2)}, u32[]{:S(2)}) async-start(bf16[32,2,4496]{2,1,0:T(2,128)(2,1)} %reshape.624), calls=%async_computation | async-start | bytes 1179648 | tf_op jit(solution)/shard_map/all_to_all | solution.py:797
  100.5 104.6 %collective-permute-start.5 = (bf16[256,1536]{1,0:T(8,128)(2,1)}, bf16[256,1536]{1,0:T(8,128)(2,1)}, u32[]{:S(2)}, u32[]{:S(2)}) collective-permute-start(bf16[256,1536]{1,0:T(8,128)(2,1)} %pad_maximum_fusion.3), channel_id=1, source_target_pairs={{0,24},{1,8},{2,16},{3,0},{8,1},{9,17},{10,25},{11,9},{16,10},{17,... | collective-permute-start | bytes 2359304 | tf_op jit(solution)/shard_map/ppermute | solution.py:774
  102.9 102.2 %collective-permute-start.4 = (bf16[256,1536]{1,0:T(8,128)(2,1)}, bf16[256,1536]{1,0:T(8,128)(2,1)}, u32[]{:S(2)}, u32[]{:S(2)}) collective-permute-start(bf16[256,1536]{1,0:T(8,128)(2,1)} %pad_maximum_fusion.3), channel_id=1, source_target_pairs={{0,8},{1,24},{2,0},{3,16},{8,17},{9,1},{10,9},{11,25},{16,26},{17,... | collective-permute-start | bytes 2359304 | tf_op jit(solution)/shard_map/ppermute | solution.py:774
  105.7 99.4 %collective-permute-start.3 = (bf16[256,1536]{1,0:T(8,128)(2,1)}, bf16[256,1536]{1,0:T(8,128)(2,1)}, u32[]{:S(2)}, u32[]{:S(2)}) collective-permute-start(bf16[256,1536]{1,0:T(8,128)(2,1)} %pad_maximum_fusion.3), channel_id=1, source_target_pairs={{0,16},{1,0},{2,24},{3,8},{8,25},{9,9},{10,1},{11,17},{16,2},{17,1... | collective-permute-start | bytes 2359304 | tf_op jit(solution)/shard_map/ppermute | solution.py:774
  113.4 91.7 %collective-permute-start.2 = (bf16[256,1536]{1,0:T(8,128)(2,1)}, bf16[256,1536]{1,0:T(8,128)(2,1)}, u32[]{:S(2)}, u32[]{:S(2)}) collective-permute-start(bf16[256,1536]{1,0:T(8,128)(2,1)} %pad_maximum_fusion.3), channel_id=1, source_target_pairs={{0,0},{1,16},{2,8},{3,24},{8,9},{9,25},{10,17},{11,1},{16,18},{17,... | collective-permute-start | bytes 2359304 | tf_op jit(solution)/shard_map/ppermute | solution.py:774
  140.0 51.0 %all-to-all-start.1 = ((bf16[8,144,1024]{2,1,0:T(8,128)(2,1)}), bf16[8,144,1024]{2,1,0:T(8,128)(2,1)}, u32[]{:S(2)}, u32[]{:S(2)}) async-start(bf16[8,144,1024]{2,1,0:T(8,128)(2,1)} %bitcast.187), calls=%async_computation.1 | async-start | bytes 4718592 | tf_op jit(solution)/shard_map/all_to_all | solution.py:801
  195.8 33.3 %all-to-all-start.2 = ((bf16[32,8,1024]{2,1,0:T(8,128)(2,1)}), bf16[32,8,1024]{2,1,0:T(8,128)(2,1)S(1)}, u32[]{:S(2)}, u32[]{:S(2)}) async-start(bf16[32,8,1024]{2,1,0:T(8,128)(2,1)} %fusion.4), calls=%async_computation.2 | async-start | bytes 1048576 | tf_op jit(solution)/shard_map/all_to_all | solution.py:797
  229.9 46.2 %all-to-all-start.3 = ((bf16[8,144,1024]{2,1,0:T(8,128)(2,1)}), bf16[8,144,1024]{2,1,0:T(8,128)(2,1)S(1)}, u32[]{:S(2)}, u32[]{:S(2)}) async-start(bf16[8,144,1024]{2,1,0:T(8,128)(2,1)} %bitcast.189), calls=%async_computation.3 | async-start | bytes 4718592 | tf_op jit(solution)/shard_map/all_to_all | solution.py:801
  233.5 42.6 %collective-permute-start.1 = (bf16[256,1536]{1,0:T(8,128)(2,1)S(1)}, bf16[256,1536]{1,0:T(8,128)(2,1)}, u32[]{:S(2)}, u32[]{:S(2)}) collective-permute-start(bf16[256,1536]{1,0:T(8,128)(2,1)S(1)} %pad_maximum_fusion.4), channel_id=1, source_target_pairs={{0,16},{1,0},{2,24},{3,8},{8,25},{9,9},{10,1},{11,17},{16,2},{17,1... | collective-permute-start | bytes 2359304 | tf_op jit(solution)/shard_map/ppermute | solution.py:774
  235.0 47.5 %collective-permute-start = (bf16[256,1536]{1,0:T(8,128)(2,1)S(1)}, bf16[256,1536]{1,0:T(8,128)(2,1)}, u32[]{:S(2)}, u32[]{:S(2)}) collective-permute-start(bf16[256,1536]{1,0:T(8,128)(2,1)S(1)} %pad_maximum_fusion.4), channel_id=1, source_target_pairs={{0,0},{1,16},{2,8},{3,24},{8,9},{9,25},{10,17},{11,1},{16,18},{17,... | collective-permute-start | bytes 2359304 | tf_op jit(solution)/shard_map/ppermute | solution.py:774
  240.0 65.2 %collective-permute-start.7 = (bf16[256,1536]{1,0:T(8,128)(2,1)S(1)}, bf16[256,1536]{1,0:T(8,128)(2,1)}, u32[]{:S(2)}, u32[]{:S(2)}) collective-permute-start(bf16[256,1536]{1,0:T(8,128)(2,1)S(1)} %pad_maximum_fusion.4), channel_id=1, source_target_pairs={{0,24},{1,8},{2,16},{3,0},{8,1},{9,17},{10,25},{11,9},{16,10},{17,... | collective-permute-start | bytes 2359304 | tf_op jit(solution)/shard_map/ppermute | solution.py:774
  244.0 61.3 %collective-permute-start.6 = (bf16[256,1536]{1,0:T(8,128)(2,1)S(1)}, bf16[256,1536]{1,0:T(8,128)(2,1)}, u32[]{:S(2)}, u32[]{:S(2)}) collective-permute-start(bf16[256,1536]{1,0:T(8,128)(2,1)S(1)} %pad_maximum_fusion.4), channel_id=1, source_target_pairs={{0,8},{1,24},{2,0},{3,16},{8,17},{9,1},{10,9},{11,25},{16,26},{17,... | collective-permute-start | bytes 2359304 | tf_op jit(solution)/shard_map/ppermute | solution.py:774
  424.8 20.5 %all-to-all-start.7 = ((bf16[32,8,1152]{2,1,0:T(8,128)(2,1)}), bf16[32,8,1152]{2,1,0:T(8,128)(2,1)}, u32[]{:S(2)}, u32[]{:S(2)}) async-start(bf16[32,8,1152]{2,1,0:T(8,128)(2,1)} %pad_maximum_fusion.5), calls=%async_computation.7 | async-start | bytes 1179648 | tf_op jit(solution)/shard_map/all_to_all | solution.py:797
  506.3 47.7 %all-to-all-start.10 = ((bf16[8,144,1024]{2,1,0:T(8,128)(2,1)}), bf16[8,144,1024]{2,1,0:T(8,128)(2,1)}, u32[]{:S(2)}, u32[]{:S(2)}) async-start(bf16[8,144,1024]{2,1,0:T(8,128)(2,1)} %bitcast.188), calls=%async_computation.10 | async-start | bytes 4718592 | tf_op jit(solution)/shard_map/all_to_all | solution.py:801
  522.0 75.6 %collective-permute-start.8 = (bf16[256,1536]{1,0:T(8,128)(2,1)}, bf16[256,1536]{1,0:T(8,128)(2,1)}, u32[]{:S(2)}, u32[]{:S(2)}) collective-permute-start(bf16[256,1536]{1,0:T(8,128)(2,1)} %get-tuple-element.151), channel_id=1, source_target_pairs={{0,0},{16,1},{8,2},{24,3},{9,8},{25,9},{17,10},{1,11},{18,16},{2,1... | collective-permute-start | bytes 2359304 | tf_op jit(solution)/shard_map/ppermute | solution.py:785
  524.1 73.5 %collective-permute-start.9 = (bf16[256,1536]{1,0:T(8,128)(2,1)}, bf16[256,1536]{1,0:T(8,128)(2,1)}, u32[]{:S(2)}, u32[]{:S(2)}) collective-permute-start(bf16[256,1536]{1,0:T(8,128)(2,1)} %get-tuple-element.152), channel_id=1, source_target_pairs={{16,0},{0,1},{24,2},{8,3},{25,8},{9,9},{1,10},{17,11},{2,16},{18,1... | collective-permute-start | bytes 2359304 | tf_op jit(solution)/shard_map/ppermute | solution.py:785
  554.6 43.0 %all-to-all-start.8 = ((f32[32,1,16]{2,1,0:T(1,128)}), f32[32,1,16]{2,1,0:T(1,128)S(1)}, u32[]{:S(2)}, u32[]{:S(2)}) async-start(f32[32,1,16]{2,1,0:T(1,128)} %broadcast_in_dim.99), calls=%async_computation.8 | async-start | bytes 32768 | tf_op jit(solution)/shard_map/all_to_all | solution.py:797
  597.7 46.9 %all-to-all-start.11 = ((bf16[8,144,1024]{2,1,0:T(8,128)(2,1)}), bf16[8,144,1024]{2,1,0:T(8,128)(2,1)S(1)}, u32[]{:S(2)}, u32[]{:S(2)}) async-start(bf16[8,144,1024]{2,1,0:T(8,128)(2,1)} %bitcast.185), calls=%async_computation.11 | async-start | bytes 4718592 | tf_op jit(solution)/shard_map/all_to_all | solution.py:801
  604.0 95.5 %collective-permute-start.10 = (bf16[256,1536]{1,0:T(8,128)(2,1)}, bf16[256,1536]{1,0:T(8,128)(2,1)}, u32[]{:S(2)}, u32[]{:S(2)}) collective-permute-start(bf16[256,1536]{1,0:T(8,128)(2,1)} %get-tuple-element.173), channel_id=1, source_target_pairs={{8,0},{24,1},{0,2},{16,3},{17,8},{1,9},{9,10},{25,11},{26,16},{10,... | collective-permute-start | bytes 2359304 | tf_op jit(solution)/shard_map/ppermute | solution.py:785
  607.5 91.9 %collective-permute-start.11 = (bf16[256,1536]{1,0:T(8,128)(2,1)}, bf16[256,1536]{1,0:T(8,128)(2,1)}, u32[]{:S(2)}, u32[]{:S(2)}) collective-permute-start(bf16[256,1536]{1,0:T(8,128)(2,1)} %get-tuple-element.174), channel_id=1, source_target_pairs={{24,0},{8,1},{16,2},{0,3},{1,8},{17,9},{25,10},{9,11},{10,16},{26,... | collective-permute-start | bytes 2359304 | tf_op jit(solution)/shard_map/ppermute | solution.py:785
  659.9 39.6 %all-to-all-start.12 = ((bf16[8,144,1024]{2,1,0:T(8,128)(2,1)}), bf16[8,144,1024]{2,1,0:T(8,128)(2,1)}, u32[]{:S(2)}, u32[]{:S(2)}) async-start(bf16[8,144,1024]{2,1,0:T(8,128)(2,1)} %bitcast.186), calls=%async_computation.12 | async-start | bytes 4718592 | tf_op jit(solution)/shard_map/all_to_all | solution.py:801
  732.9 125.9 %all-to-all-start.13 = ((bf16[32,2,4496]{2,1,0:T(2,128)(2,1)}), bf16[32,2,4496]{2,1,0:T(2,128)(2,1)S(1)}, u32[]{:S(2)}, u32[]{:S(2)}) async-start(bf16[32,2,4496]{2,1,0:T(2,128)(2,1)} %reshape.626), calls=%async_computation.13 | async-start | bytes 1179648 | tf_op jit(solution)/shard_map/all_to_all | solution.py:797
  757.0 99.5 %copy-start.31 = (f32[256,1536]{1,0:T(8,128)S(1)}, f32[256,1536]{1,0:T(8,128)}, u32[]{:S(2)}) copy-start(f32[256,1536]{1,0:T(8,128)} %copy-done.30) | copy-start | bytes 4718596
  860.2 70.5 %collective-permute-start.12 = (bf16[256,1536]{1,0:T(8,128)(2,1)}, bf16[256,1536]{1,0:T(8,128)(2,1)S(1)}, u32[]{:S(2)}, u32[]{:S(2)}) collective-permute-start(bf16[256,1536]{1,0:T(8,128)(2,1)} %get-tuple-element.193), channel_id=1, source_target_pairs={{0,0},{16,1},{8,2},{24,3},{9,8},{25,9},{17,10},{1,11},{18,16},{2,1... | collective-permute-start | bytes 2359304 | tf_op jit(solution)/shard_map/ppermute | solution.py:785
  862.7 68.0 %collective-permute-start.13 = (bf16[256,1536]{1,0:T(8,128)(2,1)}, bf16[256,1536]{1,0:T(8,128)(2,1)S(1)}, u32[]{:S(2)}, u32[]{:S(2)}) collective-permute-start(bf16[256,1536]{1,0:T(8,128)(2,1)} %get-tuple-element.194), channel_id=1, source_target_pairs={{16,0},{0,1},{24,2},{8,3},{25,8},{9,9},{1,10},{17,11},{2,16},{18,1... | collective-permute-start | bytes 2359304 | tf_op jit(solution)/shard_map/ppermute | solution.py:785
  864.5 66.2 %collective-permute-start.14 = (bf16[256,1536]{1,0:T(8,128)(2,1)}, bf16[256,1536]{1,0:T(8,128)(2,1)S(1)}, u32[]{:S(2)}, u32[]{:S(2)}) collective-permute-start(bf16[256,1536]{1,0:T(8,128)(2,1)} %get-tuple-element.195), channel_id=1, source_target_pairs={{8,0},{24,1},{0,2},{16,3},{17,8},{1,9},{9,10},{25,11},{26,16},{10,... | collective-permute-start | bytes 2359304 | tf_op jit(solution)/shard_map/ppermute | solution.py:785
  867.7 130.5 %collective-permute-start.15 = (bf16[256,1536]{1,0:T(8,128)(2,1)}, bf16[256,1536]{1,0:T(8,128)(2,1)S(1)}, u32[]{:S(2)}, u32[]{:S(2)}) collective-permute-start(bf16[256,1536]{1,0:T(8,128)(2,1)} %get-tuple-element.196), channel_id=1, source_target_pairs={{24,0},{8,1},{16,2},{0,3},{1,8},{17,9},{25,10},{9,11},{10,16},{26,... | collective-permute-start | bytes 2359304 | tf_op jit(solution)/shard_map/ppermute | solution.py:785
  873.0 55.5 %copy-start.34 = (f32[2,32,4096]{2,1,0:T(8,128)S(1)}, f32[2,32,4096]{2,1,0:T(8,128)}, u32[]{:S(2)}) copy-start(f32[2,32,4096]{2,1,0:T(8,128)} %param.42) | copy-start | bytes 3145732
  873.0 55.5 %copy-start.39 = (f32[32,4096]{1,0:T(8,128)S(1)}, f32[32,4096]{1,0:T(8,128)}, u32[]{:S(2)}) copy-start(f32[32,4096]{1,0:T(8,128)} %get-tuple-element.209) | copy-start | bytes 1572868
  873.0 55.5 %copy-start.44 = (f32[2,32,4096]{2,1,0:T(8,128)S(1)}, f32[2,32,4096]{2,1,0:T(8,128)}, u32[]{:S(2)}) copy-start(f32[2,32,4096]{2,1,0:T(8,128)} %param.44) | copy-start | bytes 3145732
  (76 other events, 852.3 us)
Sparse Core Ops, SparseCore 0:
  11.5 85.8 all-gather.5
  100.8 130.4 all-gather.3

commit v4 on v3

--- a/solution.py
+++ b/solution.py
@@ -453,11 +453,11 @@
     return gate_part, up_part, sigmoid
 
 
-def fetch_expert(place_ref, part_refs, up_ref, down_ref, copy_sem):
+def fetch_expert(places, part_refs, up_ref, down_ref, copy_sem):
     copies = []
     rows = part_refs[0].shape[0]
     for turn, part_ref in enumerate(part_refs):
-        place = pl.multiple_of(place_ref[turn] * rows, rows)
+        place = pl.multiple_of(places[turn] * rows, rows)
         copies.append(
             pltpu.make_async_copy(
                 part_ref.at[:, pl.ds(0, 2 * F)],
@@ -745,7 +745,10 @@
                 source = (plane * row_groups + row) * PLANES + part
                 target_plane = (plane + SHIFTS[part ^ turn_plane]) % PLANES
                 target_row = (row + turn_row) % row_groups
-                pairs.append((source, (target_plane * row_groups + target_row) * PLANES + plane))
+                target_part = (plane // 2 + target_plane) % 2 * 2 + plane % 2
+                pairs.append(
+                    (source, (target_plane * row_groups + target_row) * PLANES + target_part)
+                )
     return pairs
 
 
@@ -759,8 +762,8 @@
 
 def part_of_turn(turn_plane):
     me_plane = lax.axis_index("z")
-    me_part = lax.axis_index(("y", "c"))
-    return shift_inverse((me_plane - me_part) % PLANES) ^ turn_plane
+    expert_plane = (lax.axis_index("y") + me_plane) % 2 * 2 + lax.axis_index("c")
+    return shift_inverse((me_plane - expert_plane) % PLANES) ^ turn_plane
 
 
 def piece_place(turn, row_groups):
@@ -778,9 +781,11 @@
     ]
 
 
-def return_expert_grads(pieces, row_groups):
+def return_expert_grads(pieces, row_groups, chosen=None):
     arrived = []
-    for piece, turn in zip(pieces, all_turns(row_groups)):
+    for place, (piece, turn) in enumerate(zip(pieces, all_turns(row_groups))):
+        if chosen is not None and place not in chosen:
+            continue
         back = [(target, source) for source, target in swap_pairs(row_groups, *turn)]
         arrived.append(lax.ppermute(piece, ("z", "h", "y", "c"), back))
     return arrived
@@ -806,6 +811,291 @@
     second = lax.reduce_precision(values - first, 8, 7)
     third = lax.reduce_precision(values - first - second, 8, 7)
     return [first, second, third]
+
+PLANE_RING = ("x", "y", "c")
+
+
+def plane_partners():
+    at = {name: lax.axis_index(name) for name in PLANE_RING}
+    partners, groups = [None], [at["x"] * 4 + at["y"] * 2 + at["c"]]
+    for turn in range(1, 8):
+        flips = {"x": turn // 4, "y": turn // 2 % 2, "c": turn % 2}
+        there = {name: 1 - at[name] if flips[name] else at[name] for name in PLANE_RING}
+        partners.append({name: there[name] for name in PLANE_RING if flips[name]})
+        groups.append(there["x"] * 4 + there["y"] * 2 + there["c"])
+    return partners, groups
+
+
+def part_places(part_count):
+    plane = lax.axis_index("z")
+    expert_plane = lax.rem(lax.axis_index("y") + plane, 2) * 2 + lax.axis_index("c")
+    shift = lax.rem(plane - expert_plane + PLANES, PLANES)
+    upper, lower = lax.rem(shift, 2), shift // 2
+    places = []
+    for turn in range(part_count):
+        first = 1 - upper if turn // 2 else upper
+        second = 1 - lower if turn % 2 else lower
+        places.append(first * 2 + second)
+    return places
+
+
+def greet(partners):
+    barrier = pltpu.get_barrier_semaphore()
+    for partner in partners:
+        pl.semaphore_signal(
+            barrier, inc=1, device_id=partner, device_id_type=pl.DeviceIdType.MESH
+        )
+    pl.semaphore_wait(barrier, len(partners))
+
+
+def push(source, target, send_sem, recv_sem, place, partner):
+    copy = pltpu.make_async_remote_copy(
+        src_ref=source,
+        dst_ref=target,
+        send_sem=send_sem.at[place],
+        recv_sem=recv_sem.at[place],
+        device_id=partner,
+        device_id_type=pl.DeviceIdType.MESH,
+    )
+    copy.start()
+    return copy
+
+
+FAR_FIRST = (6, 7, 4, 5, 2, 3, 1)
+
+
+def exchange_out(outgoing_ref, received_ref, send_sem, recv_sem, partners, groups):
+    copies = {}
+    for turn in FAR_FIRST:
+        copies[turn] = push(
+            outgoing_ref.at[groups[turn]],
+            received_ref.at[turn],
+            send_sem,
+            recv_sem,
+            turn,
+            partners[turn],
+        )
+    received_ref[0] = outgoing_ref[groups[0]]
+    return copies
+
+
+def flat_rows(block):
+    return block.reshape(block.shape[0] * block.shape[1], block.shape[2])
+
+
+def two_blocks(ref, pair):
+    return flat_rows(ref[2 * pair : 2 * pair + 2])
+
+
+def put_two(ref, pair, values):
+    rows = values.shape[0] // 2
+    ref[2 * pair] = values[:rows]
+    ref[2 * pair + 1] = values[rows:]
+
+
+def forward_exchange_kernel(part_count, outgoing_ref, *refs):
+    part_refs, refs = refs[:part_count], refs[part_count:]
+    returned_ref, received_ref, up_ref, down_ref, produced_ref, copy_sem, send_sem, recv_sem = refs
+    partners, groups = plane_partners()
+    greet(partners[1:])
+    copies = exchange_out(outgoing_ref, received_ref, send_sem, recv_sem, partners, groups)
+    fetch_expert(part_places(part_count), part_refs, up_ref, down_ref, copy_sem)
+    back = {}
+    for pair in range(4):
+        for turn in (2 * pair, 2 * pair + 1):
+            if turn:
+                copies[turn].wait_recv()
+        gate_part, up_part, sigmoid = silu_parts(
+            dot_nn(two_blocks(received_ref, pair), up_ref[...])
+        )
+        activated = (gate_part * sigmoid * up_part).astype(jnp.bfloat16)
+        put_two(produced_ref, pair, dot_nn(activated, down_ref[...]).astype(jnp.bfloat16))
+        for turn in (2 * pair, 2 * pair + 1):
+            if turn:
+                back[turn] = push(
+                    produced_ref.at[turn],
+                    returned_ref.at[groups[0]],
+                    send_sem,
+                    recv_sem,
+                    8 + turn,
+                    partners[turn],
+                )
+    returned_ref[groups[0]] = produced_ref[0]
+    for turn in range(1, 8):
+        copies[turn].wait_send()
+        back[turn].wait()
+
+
+def forward_exchange(outgoing, parts):
+    whole, _, apart, scratch = expert_specs(parts)
+    shape = jax.ShapeDtypeStruct(outgoing.shape, jnp.bfloat16)
+    slot_total = outgoing.shape[0] * outgoing.shape[1]
+    return pl.pallas_call(
+        functools.partial(forward_exchange_kernel, len(parts)),
+        out_shape=(shape, shape),
+        in_specs=[whole] + apart,
+        out_specs=[whole] * 2,
+        scratch_shapes=scratch[:2]
+        + [
+            pltpu.VMEM(outgoing.shape, jnp.bfloat16),
+            scratch[2],
+            pltpu.SemaphoreType.DMA((16,)),
+            pltpu.SemaphoreType.DMA((16,)),
+        ],
+        compiler_params=pltpu.CompilerParams(
+            vmem_limit_bytes=56 * 1024 * 1024, collective_id=2, has_side_effects=True
+        ),
+        cost_estimate=pl.CostEstimate(
+            flops=slot_total * D * F * 6, bytes_accessed=150 * 1024 * 1024, transcendentals=1 << 19
+        ),
+    )(outgoing, *parts)
+
+
+def backward_exchange_kernel(
+    part_count,
+    capacity,
+    outgoing_ref,
+    received_ref,
+    grad_ref,
+    returned_ref,
+    spread_back_ref,
+    probs_ref,
+    ffn_ref,
+    *refs,
+):
+    part_refs, refs = refs[:part_count], refs[part_count:]
+    out_refs, refs = refs[:part_count], refs[part_count:]
+    (
+        back_ref,
+        low_ref,
+        router_grad_ref,
+        pull_ref,
+        gate_grad_ref,
+        activated_ref,
+        input_grad_ref,
+        up_ref,
+        down_ref,
+        up_grad_ref,
+        down_grad_ref,
+        copy_sem,
+        send_sem,
+        recv_sem,
+    ) = refs
+    partners, groups = plane_partners()
+    greet(partners[1:])
+    copies = exchange_out(outgoing_ref, pull_ref, send_sem, recv_sem, partners, groups)
+    fetch_expert(part_places(part_count), part_refs, up_ref, down_ref, copy_sem)
+    back = {}
+    for pair in range(4):
+        rows = slice(pair * 2 * capacity, (pair + 1) * 2 * capacity)
+        gate_part, up_part, sigmoid = silu_parts(
+            dot_nn(two_blocks(received_ref, pair), up_ref[...])
+        )
+        side = gate_part * sigmoid
+        activated_ref[rows, :] = (side * up_part).astype(jnp.bfloat16)
+        slope = up_part * sigmoid * (1.0 + gate_part * (1.0 - sigmoid))
+        for turn in (2 * pair, 2 * pair + 1):
+            if turn:
+                copies[turn].wait_recv()
+        pulled = dot_nt(two_blocks(pull_ref, pair), down_ref[...]).astype(jnp.bfloat16)
+        pulled = pulled.astype(jnp.float32)
+        gate_grad_ref[rows, :F] = (pulled * slope).astype(jnp.bfloat16)
+        gate_grad_ref[rows, F:] = (pulled * side).astype(jnp.bfloat16)
+        put_two(
+            input_grad_ref, pair, dot_nt(gate_grad_ref[rows, :], up_ref[...]).astype(jnp.bfloat16)
+        )
+        for turn in (2 * pair, 2 * pair + 1):
+            if turn:
+                back[turn] = push(
+                    input_grad_ref.at[turn],
+                    back_ref.at[groups[0]],
+                    send_sem,
+                    recv_sem,
+                    8 + turn,
+                    partners[turn],
+                )
+        if pair == 0:
+            router_kernel(
+                capacity,
+                grad_ref,
+                returned_ref,
+                spread_back_ref,
+                probs_ref,
+                ffn_ref,
+                low_ref,
+                router_grad_ref,
+            )
+    back_ref[groups[0]] = input_grad_ref[0]
+    block = 256
+
+    @pl.loop(0, D // block)
+    def _(step):
+        columns = pl.ds(pl.multiple_of(step * block, block), block)
+        up_grad_ref[columns, :] = dot_tn(
+            flat_rows(received_ref[:, :, columns]), gate_grad_ref[...]
+        ).astype(jnp.bfloat16)
+
+    @pl.loop(0, F // block)
+    def _(step):
+        columns = pl.ds(pl.multiple_of(step * block, block), block)
+        down_grad_ref[columns, :] = dot_tn(
+            activated_ref[:, columns], flat_rows(pull_ref[...])
+        ).astype(jnp.bfloat16)
+
+    rows = out_refs[0].shape[0]
+    for out_ref, own_place in zip(out_refs, part_places(part_count)):
+        place = pl.multiple_of(own_place * rows, rows)
+        out_ref[:, : 2 * F] = up_grad_ref[pl.ds(place, rows), :]
+        for part in range(F // rows):
+            out_ref[:, 2 * F + part * rows : 2 * F + (part + 1) * rows] = down_grad_ref[
+                part * rows : (part + 1) * rows, pl.ds(place, rows)
+            ]
+    for turn in range(1, 8):
+        copies[turn].wait_send()
+        back[turn].wait()
+
+
+def backward_exchange(
+    capacity, outgoing, received, grad, returned, spread_back, probs, ffn, parts
+):
+    whole, _, apart, scratch = expert_specs(parts)
+    slot_total = outgoing.shape[0] * outgoing.shape[1]
+    piece_rows = parts[0].shape[0]
+    seq_len = grad.shape[0]
+    low = jnp.bfloat16
+    return pl.pallas_call(
+        functools.partial(backward_exchange_kernel, len(parts), capacity),
+        out_shape=[jax.ShapeDtypeStruct((piece_rows, 3 * F), low)] * len(parts)
+        + [
+            jax.ShapeDtypeStruct(outgoing.shape, low),
+            jax.ShapeDtypeStruct((seq_len, LANES), low),
+            jax.ShapeDtypeStruct((D, LANES), jnp.float32),
+        ],
+        in_specs=[whole] * 7 + apart,
+        out_specs=[whole] * (len(parts) + 3),
+        scratch_shapes=[
+            pltpu.VMEM(outgoing.shape, low),
+            pltpu.VMEM((slot_total, 2 * F), low),
+            pltpu.VMEM((slot_total, F), low),
+            pltpu.VMEM(outgoing.shape, low),
+        ]
+        + scratch[:2]
+        + scratch[:2]
+        + [
+            scratch[2],
+            pltpu.SemaphoreType.DMA((16,)),
+            pltpu.SemaphoreType.DMA((16,)),
+        ],
+        compiler_params=pltpu.CompilerParams(
+            vmem_limit_bytes=58 * 1024 * 1024, collective_id=3, has_side_effects=True
+        ),
+        cost_estimate=pl.CostEstimate(
+            flops=slot_total * D * F * 18,
+            bytes_accessed=180 * 1024 * 1024,
+            transcendentals=1 << 19,
+        ),
+    )(outgoing, received, grad, returned, spread_back, probs, ffn, *parts)
+
 
 RING = ("z", "x", "y", "c")
 
@@ -1171,12 +1461,17 @@
     slot_total = experts_all * capacity
     piece_rows = expert_up.shape[2]
     gain_count = norm_gains.shape[0]
-    group_experts = [
-        (group % PLANES) * columns_x + group // PLANES for group in range(experts_all)
-    ]
-    group_order = jnp.array(group_experts, jnp.int32)
-    group_back = jnp.array(
-        [group_experts.index(expert) for expert in range(experts_all)], jnp.int32
+    me_plane = lax.axis_index("z")
+    member_place = jnp.arange(experts_all, dtype=jnp.int32)
+    member_part = member_place % PLANES
+    group_order = (
+        (member_part // 2 + me_plane) % 2 * 2 + member_part % 2
+    ) * columns_x + member_place // PLANES
+    expert_plane = member_place // columns_x
+    group_back = (
+        member_place % columns_x * PLANES
+        + (expert_plane // 2 + me_plane) % 2 * 2
+        + expert_plane % 2
     )
 
 
@@ -1190,7 +1485,7 @@
         [jnp.ones((position_count, 1), jnp.float32), teacher_prob], axis=1
     )
     table_low = embedding.astype(jnp.bfloat16)
-    looked_up = jnp.take(table_low, tokens, axis=0).reshape(devices_all, seq_len * column_count)
+    looked_up = jnp.take(table_low, tokens, axis=0, mode="clip").reshape(devices_all, seq_len * column_count)
     attention_low = []
     for layer_index in range(layer_count):
         rows_low = attention[layer_index].astype(jnp.bfloat16)
@@ -1206,7 +1501,7 @@
         small.reshape(1, column_count * small_count), (devices_all, column_count * small_count)
     )
     arrived_rows = send_all(jnp.concatenate([looked_up, small], axis=1))
-    expert_parts = []
+    expert_parts, expert_pieces = [], []
     for layer_index in range(layer_count):
         down_piece = (
             expert_down[0, layer_index]
@@ -1217,11 +1512,9 @@
         piece = jnp.concatenate([expert_up[0, layer_index], down_piece], axis=1).astype(
             jnp.bfloat16
         )
-        if layer_index > 0:
-            piece, attention_low[0] = tie(piece, attention_low[0])
-        else:
-            piece, arrived_rows = tie(piece, arrived_rows)
-        expert_parts.append(spread_experts(piece, row_groups))
+        expert_pieces.append(piece)
+    expert_pieces[0], arrived_rows = tie(expert_pieces[0], arrived_rows)
+    expert_parts.append(spread_experts(expert_pieces[0], row_groups))
 
     hidden = (
         arrived_rows[:, : seq_len * column_count]
@@ -1283,37 +1576,35 @@
         )
         hidden = saved[6]
         gates, outgoing = saved[9], saved[10]
-        if layer_index > 0:
-            expert_parts[layer_index][2:], outgoing = tie(expert_parts[layer_index][2:], outgoing)
-        received = send_plane(outgoing.reshape(experts_all, capacity, D)).reshape(slot_total, D)
-        if layer_index == 0:
-            ids_now, tokens_now, outgoing = lax.optimization_barrier((loss_ids, tokens, outgoing))
-            local_ids = ids_now - me_all * vocab_local
-            vocab_place = jnp.arange(vocab_local, dtype=jnp.int32)
-            marked = jnp.sum(
-                jnp.where(
-                    local_ids[:, :, None] == vocab_place[None, None, :], coefficients[:, :, None], 0.0
-                ),
-                axis=1,
-            )
-            order = token_order(tokens_now, seq_len, embedding.shape[0], LANES // column_count)
-            marked, order, received = lax.optimization_barrier((marked, order, received))
-        upcoming = expert_parts[layer_index + 1] if layer_index + 1 < layer_count else None
-        produced = run_expert(places, received, expert_parts[layer_index])
-        returned = send_plane(produced.reshape(experts_all, capacity, D)).reshape(slot_total, D)
-        if layer_index == 0:
-            marked_pull = jnp.dot(
-                marked.astype(jnp.bfloat16), head_low, preferred_element_type=jnp.float32
-            )
-            own_count = position_count // devices_all
-            marked_arrived = send_all(
-                marked_pull.astype(jnp.bfloat16).reshape(devices_all, own_count, D)
-            )
-            marked_arrived, returned = tie(marked_arrived, returned)
-        if upcoming is not None:
-            upcoming[:2], returned = tie(upcoming[:2], returned)
+        if layer_index + 1 < layer_count:
+            piece, outgoing = tie(expert_pieces[layer_index + 1], outgoing)
+            expert_parts.append(spread_experts(piece, row_groups))
+        blocks = outgoing.reshape(experts_all, capacity, D)
+        if fits_sum:
+            returned, received = forward_exchange(blocks, expert_parts[layer_index])
+        else:
+            received = send_plane(blocks).reshape(slot_total, D)
+            produced = run_expert(places, received, expert_parts[layer_index])
+            returned = send_plane(produced.reshape(experts_all, capacity, D))
+        returned = returned.reshape(slot_total, D)
+        if layer_index + 1 < layer_count:
+            expert_parts[-1][:2], returned = tie(expert_parts[-1][:2], returned)
         stored.append((saved, received, returned))
         extra = (gates, returned)
+
+    order = token_order(tokens, seq_len, embedding.shape[0], LANES // column_count)
+    local_ids = loss_ids - me_all * vocab_local
+    vocab_place = jnp.arange(vocab_local, dtype=jnp.int32)
+    marked = jnp.sum(
+        jnp.where(
+            local_ids[:, :, None] == vocab_place[None, None, :], coefficients[:, :, None], 0.0
+        ),
+        axis=1,
+    )
+    marked_pull = jnp.dot(
+        marked.astype(jnp.bfloat16), head_low, preferred_element_type=jnp.float32
+    )
+    own_count = position_count // devices_all
 
     final_gain = gain_rows[4 * layer_count]
     final_rows, final_low = final_rows_of(
@@ -1339,9 +1630,9 @@
         three_terms(local_peak) + three_terms(local_sum) + three_terms(local_dot), axis=1
     )
     stats = jnp.pad(stats, ((0, 0), (0, 128 - stats.shape[1])))
-    pull_sent = jnp.concatenate([pull, stats], axis=1).astype(jnp.bfloat16)
-    pull_got = send_all(pull_sent.reshape(devices_all, own_count, D + 128)).astype(jnp.float32)
-    stats_got = pull_got[:, :, D:]
+    pull_sent = jnp.concatenate([pull, marked_pull, stats], axis=1).astype(jnp.bfloat16)
+    pull_got = send_all(pull_sent.reshape(devices_all, own_count, 2 * D + 128)).astype(jnp.float32)
+    stats_got = pull_got[:, :, 2 * D :]
     peaks = jnp.sum(stats_got[:, :, 0:3], axis=2)
     sums = jnp.sum(stats_got[:, :, 3:6], axis=2)
     dots = jnp.sum(stats_got[:, :, 6:9], axis=2)
@@ -1353,7 +1644,7 @@
     )
     loss_own = (1.0 + mass_own) * log_norm_own - jnp.sum(dots, axis=0) + entropy_own
     scale_own = (1.0 + mass_own)[None, :] * jnp.exp(peaks - log_norm_own[None, :])
-    marked_total = jnp.sum(marked_arrived.astype(jnp.float32), axis=0)
+    marked_total = jnp.sum(pull_got[:, :, D : 2 * D], axis=0)
     final_grad = (
         jnp.sum(scale_own[:, :, None] * pull_got[:, :, :D], axis=0) - marked_total
     ) / position_count
@@ -1380,25 +1671,40 @@
         saved, received, returned = stored[layer_index]
         hidden_in, projected, queries, keys, values, attended, middle, ffn_low, probs = saved[:9]
         upper = layer_index + 1 if layer_index + 1 < layer_count else None
-        output_grad = send_plane(sent_back.reshape(experts_all, capacity, D)).reshape(
-            slot_total, D
-        )
-        logit_low, router_parts[layer_index] = router_back(
-            capacity, grad_hidden, returned, spread_back, probs, ffn_low
-        )
-        input_grad, gate_grad, activated = run_expert_back(
-            places, received, output_grad, expert_parts[layer_index]
-        )
-        back_inputs = send_plane(input_grad.reshape(experts_all, capacity, D)).reshape(
-            slot_total, D
-        )
-        grad_pieces = run_expert_grad(
-            places, received, output_grad, gate_grad, activated, piece_rows
-        )
+        blocks = sent_back.reshape(experts_all, capacity, D)
+        if fits_sum:
+            *grad_pieces, back_inputs, logit_low, router_parts[layer_index] = backward_exchange(
+                capacity,
+                blocks,
+                received,
+                grad_hidden,
+                returned,
+                spread_back,
+                probs,
+                ffn_low,
+                expert_parts[layer_index],
+            )
+        else:
+            output_grad = send_plane(blocks).reshape(slot_total, D)
+            logit_low, router_parts[layer_index] = router_back(
+                capacity, grad_hidden, returned, spread_back, probs, ffn_low
+            )
+            input_grad, gate_grad, activated = run_expert_back(
+                places, received, output_grad, expert_parts[layer_index]
+            )
+            back_inputs = send_plane(input_grad.reshape(experts_all, capacity, D))
+            grad_pieces = run_expert_grad(
+                places, received, output_grad, gate_grad, activated, piece_rows
+            )
+        back_inputs = back_inputs.reshape(slot_total, D)
+        if upper is not None:
+            piece_parts[upper][1:], back_inputs = tie(piece_parts[upper][1:], back_inputs)
         if layer_index > 0:
             piece_parts[layer_index] = return_expert_grads(grad_pieces, row_groups)
-        if upper is not None:
-            piece_parts[upper][2:], back_inputs = tie(piece_parts[upper][2:], back_inputs)
+        else:
+            turns_all = len(grad_pieces)
+            early = range(turns_all // 2)
+            piece_parts[0] = return_expert_grads(grad_pieces, row_groups, early)
         lower = (spread_flat, stored[layer_index - 1][0][9]) if layer_index > 0 else ()
         results = backward_layer(
             layer_index,
@@ -1425,7 +1731,7 @@
         gain_parts[4 * layer_index : 4 * layer_index + 4] = list(gain_grads[:4])
         if layer_index > 0:
             sent_back = results[3]
-            piece_parts[layer_index][:2], sent_back = tie(piece_parts[layer_index][:2], sent_back)
+            piece_parts[layer_index][:1], sent_back = tie(piece_parts[layer_index][:1], sent_back)
         attention_parts[layer_index] = weight_grad
         if not fits_sum:
             attention_parts[layer_index] = lax.psum_scatter(
@@ -1446,12 +1752,14 @@
             [sending, small_grads.reshape(devices_all, column_count * small_count)], axis=1
         )
     )
+    piece_parts[0], attention_parts = tie(piece_parts[0], attention_parts)
     if fits_sum:
         attention_parts = list(owner_sums(attention_parts[::-1], 2048))[::-1]
     grad_pieces, arrived_grads, attention_parts = lax.optimization_barrier(
         (grad_pieces, arrived_grads, attention_parts)
     )
-    piece_parts[0] = return_expert_grads(grad_pieces, row_groups)
+    late = range(turns_all // 2, turns_all)
+    piece_parts[0] = piece_parts[0] + return_expert_grads(grad_pieces, row_groups, late)
     embedding_next = embedding_update_of(
         order,
         arrived_grads[:, : seq_len * column_count],

time: 1030 us -> 931 us (0.904)
  Pallas kernels: 306 us -> 502 us
  waiting for transfers between devices: 227 us -> 68.5 us
  blocking collectives: 124 us -> 0 us
  local copies, waits for them, and re-layouts: 102 us -> 90.6 us
    pallas_call x8 -> x4, Pallas kernels: 74.4 us -> 272 us  [the longest x2 136 us: forward_exchange(): pl.pallas_call(functools.partial(forward_exchange_kernel, len(parts)), ou...]
    all_to_all x4 -> x0, blocking collectives: 124 us -> none  [the longest x3 101 us: send_plane(): lax.all_to_all(values, ('x', 'y', 'c'), split_axis=0, concat_axis=0, tile...]
    all_to_all x5 -> x0, waiting for transfers between devices: 104 us -> none  [send_plane(): lax.all_to_all(values, ('x', 'y', 'c'), split_axis=0, concat_axis=0, tile...]
    ppermute x8, waiting for transfers between devices: 67.5 us -> 0.02 us  [return_expert_grads(): arrived.append(lax.ppermute(piece, ('z', 'h', 'y', 'c'), back))]
    ppermute x8, starting transfers between devices: 29 us -> 85.4 us  [spread_experts(): lax.ppermute(piece, ('z', 'h', 'y', 'c'), swap_pairs(row_groups, turn_pla...]
    all_to_all x5, starting transfers between devices: 62.3 us -> 29.5 us  [send_all(): return lax.all_to_all(values, AXES, split_axis=0, concat_axis=0, tiled=True)]
    all_to_all x5 -> x0, starting transfers between devices: 25.5 us -> none  [send_plane(): lax.all_to_all(values, ('x', 'y', 'c'), split_axis=0, concat_axis=0, tile...]
    ppermute x8, waiting for transfers between devices: 12.4 us -> 31.9 us  [spread_experts(): lax.ppermute(piece, ('z', 'h', 'y', 'c'), swap_pairs(row_groups, turn_pla...]
  transfers between devices with their start and end apart: 28 -> 23, of which waited for: 10 -> 4; matrix products, arithmetic and copies ran while one was open for 13% -> 15% of each run, Pallas kernels for 25% -> 47%
where the time goes in v4:
time: 931 us; the launch traced here: 917 us
  Pallas kernels  502 us (54%)
  starting transfers between devices  151 us (16%)
  local copies, waits for them, and re-layouts  90.6 us (10%)
  waiting for transfers between devices  68.5 us (7%)
  other arithmetic  59.9 us (6%)
  matrix products  27.3 us (3%)
  between operations  18.4 us (2%)
    pallas_call x2, Pallas kernels, forward_exchange(): pl.pallas_call(functools.partial(forward_exchange_kernel, len(parts)), ou...  136 us
    pallas_call x2, Pallas kernels, backward_exchange(): pl.pallas_call(functools.partial(backward_exchange_kernel, len(parts), ca...  136 us
    pallas_call x1, Pallas kernels, owner_sums(): pl.pallas_call(functools.partial(owner_sum_kernel, layers), out_shape=jax...  97.1 us
    ppermute x8, starting transfers between devices, spread_experts(): lax.ppermute(piece, ('z', 'h', 'y', 'c'), swap_pairs(row_groups, turn_pla...  85.4 us
    pallas_call x1, Pallas kernels, embedding_update_of(): pl.pallas_call(embedding_kernel, grid=(-(-vocabulary // VOCAB_BLOCK),), o...  55.2 us
    pallas_call x2, Pallas kernels, backward_layer(): pl.pallas_call(functools.partial(backward_kernel, layer_index, capacity),...  41.9 us
    all_to_all x5, waiting for transfers between devices, send_all(): return lax.all_to_all(values, AXES, split_axis=0, concat_axis=0, tiled=True)  36.5 us
    ppermute x8, starting transfers between devices, return_expert_grads(): arrived.append(lax.ppermute(piece, ('z', 'h', 'y', 'c'), back))  36 us
  transfers between devices with their start and end apart: 23, of which 4 were waited for; matrix products, arithmetic and copies ran while one was open for 15% of the time, Pallas kernels for 47%

profile of v4, /device:TPU:9, one launch (start us, length us, event | category | flops | bytes accessed | tf_op | source)
XLA Modules:
  0.0 917.4 jit_solution(11383645755911615293)
XLA Ops:
  12.6 8.7 copy.264
  21.9 28.3 %gather_fusion = bf16[8192,32]{1,0:T(8,128)(2,1)S(1)} fusion(bf16[50304,32]{1,0:T(8,128)(2,1)} %copy.264, s32[8192]{0:T(1024)S(1)} %get-tuple-element.351), kind=kCustom, calls=%fused_computation | custom fusion | bytes 1081344 | tf_op jit(solution)/shard_map/jit(_take)/gather | solution.py:1488
  56.1 6.4 all-to-all-start
  74.2 19.0 %all-to-all-done = bf16[32,2,4496]{2,1,0:T(2,128)(2,1)} async-done(((bf16[32,2,4496]{2,1,0:T(2,128)(2,1)}), bf16[32,2,4496]{2,1,0:T(2,128)(2,1)}, u32[]{:S(2)}, u32[]{:S(2)}) %all-to-all-start) | async-done | bytes 575520 | tf_op jit(solution)/shard_map/all_to_all | solution.py:802
  97.2 4.4 collective-permute-start.2
  103.6 7.0 collective-permute-start.4
  123.3 13.7 %shard_map.426 = (f32[256,1024]{1,0:T(8,128)}, f32[256,2048]{1,0:T(8,128)}, bf16[256,1024]{1,0:T(8,128)(2,1)}, bf16[256,1024]{1,0:T(8,128)(2,1)}, bf16[256,1024]...) custom-call(s32[1]{0:T(128)S(6)} %copy.311.prefix_ref, ...), custom_call_target="tpu_custom_call" | custom-call | flops 3221225472 | bytes 25165824 | tf_op jit(solution)/shard_map/pallas_call | solution.py:234
  140.4 23.7 %collective-permute-done.2.refs_0_ = bf16[256,1536]{1,0:T(8,128)(2,1)} collective-permute-done((bf16[256,1536]{1,0:T(8,128)(2,1)}, bf16[256,1536]{1,0:T(8,128)(2,1)}, u32[]{:S(2)}, u32[]{:S(2)}) %collective-permute-start.2) | collective-permute-done | bytes 786464 | tf_op jit(solution)/shard_map/ppermute | solution.py:777
  168.5 8.2 collective-permute-done.4.refs_2_
  176.7 62.7 %collective-permute-start.7 = (bf16[256,1536]{1,0:T(8,128)(2,1)S(1)}, bf16[256,1536]{1,0:T(8,128)(2,1)}, u32[]{:S(2)}, u32[]{:S(2)}) collective-permute-start(bf16[256,1536]{1,0:T(8,128)(2,1)S(1)} %pad_maximum_fusion.5), channel_id=1, source_target_pairs={{0,26},{1,10},{2,16},{3,0},{8,1},{9,17},{10,27},{11,11},{16,8},{17... | collective-permute-start | bytes 2359304 | tf_op jit(solution)/shard_map/ppermute | solution.py:777
  240.1 71.0 %shard_map.427 = (bf16[8,144,1024]{2,1,0:T(8,128)(2,1)}, bf16[8,144,1024]{2,1,0:T(8,128)(2,1)}) custom-call(bf16[8,144,1024]{2,1,0:T(8,128)(2,1)} %bitcast.211, bf16[256,1536]{1,0:T(8,128)(2,1)} %collective-permute-done.2.refs_0_, bf16[256,1536]{1,0:T(8,128)(2,1)} %collective-permute-done.3.refs_1_, bf16[256,1536]{1,0:T(8,128)(2,1)} %collective-permute-done.4.refs_2_, ...), custom_call_target="tpu_custom_call" | custom-call | flops 3623878656 | bytes 157286400 | tf_op jit(solution)/shard_map/pallas_call | solution.py:933
  311.2 17.1 %shard_map.428 = (f32[256,1024]{1,0:T(8,128)}, f32[256,2048]{1,0:T(8,128)}, bf16[256,1024]{1,0:T(8,128)(2,1)}, bf16[256,1024]{1,0:T(8,128)(2,1)}, bf16[256,1024]...) custom-call(s32[1]{0:T(128)S(6)} %copy.311.prefix_ref, ...), custom_call_target="tpu_custom_call" | custom-call | flops 3221225472 | bytes 25165824 | tf_op jit(solution)/shard_map/pallas_call | solution.py:234
  328.4 65.0 %shard_map.429 = (bf16[8,144,1024]{2,1,0:T(8,128)(2,1)}, bf16[8,144,1024]{2,1,0:T(8,128)(2,1)}) custom-call(bf16[8,144,1024]{2,1,0:T(8,128)(2,1)} %bitcast.209, bf16[256,1536]{1,0:T(8,128)(2,1)} %copy-done.49, bf16[256,1536]{1,0:T(8,128)(2,1)} %collective-permute-done.1.refs_1_, bf16[256,1536]{1,0:T(8,128)(2,1)} %collective-permute-done.6.refs_2_, ...), custom_call_target="tpu_custom_call" | custom-call | flops 3623878656 | bytes 157286400 | tf_op jit(solution)/shard_map/pallas_call | solution.py:933
  398.6 4.1 all-to-all-start.1
  402.7 13.0 %select_reduce_fusion = f32[256,1572]{0,1:T(8,128)S(1)} fusion(f32[256,65]{0,1:T(8,128)S(1)} %concatenate.92, s32[256,65]{0,1:T(8,128)S(1)} %copy-done.32), kind=kLoop, calls=%fused_computation.4 | loop fusion | flops 78071808 | bytes 1742848 | tf_op jit(solution)/shard_map/reduce_sum | solution.py:1598
  419.8 4.1 fusion.79
  424.4 4.1 fusion.4
  429.9 5.9 all-to-all-start.2
  435.8 6.8 sort.14
  444.9 17.6 %all-to-all-done.2 = bf16[32,8,2176]{2,1,0:T(8,128)(2,1)} async-done(((bf16[32,8,2176]{2,1,0:T(8,128)(2,1)}), bf16[32,8,2176]{2,1,0:T(8,128)(2,1)}, u32[]{:S(2)}, u32[]{:S(2)}) %all-to-all-start.2) | async-done | bytes 1114144 | tf_op jit(solution)/shard_map/all_to_all | solution.py:802
  466.4 5.1 all-to-all-start.3
  478.4 66.4 %shard_map.432 = (bf16[256,1536]{1,0:T(8,128)(2,1)}, bf16[256,1536]{1,0:T(8,128)(2,1)}, bf16[256,1536]{1,0:T(8,128)(2,1)}, bf16[256,1536]{1,0:T(8,128)(2,1)}, bf...) custom-call(bf16[8,144,1024]{2,1,0:T(8,128)(2,1)} %bitcast.160, ...), custom_call_target="tpu_custom_call" | custom-call | flops 10871635968 | bytes 188743680 | tf_op jit(solution)/shard_map/pallas_call | solution.py:1066
  558.7 21.4 %shard_map.433 = (f32[256,1024]{1,0:T(8,128)}, bf16[1024,4096]{1,0:T(8,128)(2,1)}, f32[8,1024]{1,0:T(8,128)}, bf16[1152,1024]{1,0:T(8,128)(2,1)}) custom-call(s32[1]{0:T(128)S(6)} %copy.311.prefix_ref, f32[256,1024]{1,0:T(8,128)} %copy-done.9, bf16[1152,1024]{1,0:T(8,128)(2,1)} %bitcast.213, bf16[256,128]{1,0:T(8,128)(2,1)} %get-tuple-element.135.logit_ref, ...), custom_call_target="tpu_custom_call" | custom-call | flops 6442450944 | bytes 33554432 | tf_op jit(solution)/shard_map/pallas_call | solution.py:398
  582.5 14.7 %add_multiply_fusion = (f32[1572,1024]{1,0:T(8,128)}, f32[1572,1024]{1,0:T(8,128)}, f32[1572,1024]{1,0:T(8,128)}) fusion(f32[1572,1024]{1,0:T(8,128)} %param.51, f32[1572,1024]{1,0:T(8,128)} %param.53, f32[1572,1024]{1,0:T(8,128)} %param.52, bf16[32,8,1024]{2,1,0:T(8,128)(2,1)S(1)} %copy-done.21, f32[256,1572]{0,1:T(8,128)S(1)} %select_reduce_fusion, ...), kind=kOutput, calls=%fused_computation.8 | convolution fusion | flops 848729088 | bytes 42379264 | tf_op jit(solution)/shard_map/pv,pd->vd/dot_general | solution.py:1658
  597.9 69.2 %shard_map.434 = (bf16[256,1536]{1,0:T(8,128)(2,1)}, bf16[256,1536]{1,0:T(8,128)(2,1)}, bf16[256,1536]{1,0:T(8,128)(2,1)}, bf16[256,1536]{1,0:T(8,128)(2,1)}, bf...) custom-call(bf16[8,144,1024]{2,1,0:T(8,128)(2,1)} %bitcast.210, ...), custom_call_target="tpu_custom_call" | custom-call | flops 10871635968 | bytes 188743680 | tf_op jit(solution)/shard_map/pallas_call | solution.py:1066
  667.1 11.5 %collective-permute-start.9 = (bf16[256,1536]{1,0:T(8,128)(2,1)}, bf16[256,1536]{1,0:T(8,128)(2,1)}, u32[]{:S(2)}, u32[]{:S(2)}) collective-permute-start(bf16[256,1536]{1,0:T(8,128)(2,1)} %get-tuple-element.148), channel_id=1, source_target_pairs={{0,0},{16,1},{10,2},{26,3},{11,8},{27,9},{17,10},{1,11},{18,16},{2... | collective-permute-start | bytes 2359304 | tf_op jit(solution)/shard_map/ppermute | solution.py:790
  681.5 20.5 %shard_map.435 = (f32[256,1024]{1,0:T(8,128)}, bf16[1024,4096]{1,0:T(8,128)(2,1)}, f32[8,1024]{1,0:T(8,128)}) custom-call(s32[1]{0:T(128)S(6)} %copy.311.prefix_ref, f32[256,1024]{1,0:T(8,128)} %get-tuple-element.145.grad_ref, bf16[1152,1024]{1,0:T(8,128)(2,1)} %bitcast.212, bf16[256,128]{1,0:T(8,128)(2,1)} %get-tuple-element.155.logit_ref, ...), custom_call_target="tpu_custom_call" | custom-call | flops 6442450944 | bytes 33554432 | tf_op jit(solution)/shard_map/pallas_call | solution.py:398
  710.8 8.0 all-to-all-start.4
  722.4 97.1 %shard_map.436 = f32[2,32,4096]{2,1,0:T(8,128)} custom-call(bf16[4,2,2,2,32,4096]{5,4,3,2,1,0:T(8,128)(2,1)} %bitcast.164, bf16[4,2,2,2,32,4096]{5,4,3,2,1,0:T(8,128)(2,1)} %bitcast.165), custom_call_target="tpu_custom_call" | custom-call | flops 67108864 | bytes 209715200 | tf_op jit(solution)/shard_map/pallas_call | solution.py:1260
  826.0 4.1 collective-permute-start.14
  835.4 55.2 %shard_map.437 = (f32[32,50304]{1,0:T(8,128)}, f32[32,50304]{1,0:T(8,128)}, f32[32,50304]{1,0:T(8,128)}) custom-call(s32[8192]{0:T(1024)S(1)} %get-tuple-element.348.row_ref, s32[100]{0:T(128)S(1)} %get-tuple-element.335.low_ref, s32[100]{0:T(128)S(1)} %get-tuple-element.334.high_ref, bf16[32,8192]{1,0:T(8,128)(2,1)S(1)} %slice.126.arrived_ref, ...), custom_call_target="tpu_custom_call" | custom-call | flops 4294967296 | bytes 52428800 | tf_op jit(solution)/shard_map/pallas_call | solution.py:1403
  900.2 6.6 add_multiply_fusion.1
  (284 shorter events, 128.3 us)
Async XLA Ops:
  7.2 116.1 %all-gather.6.cloned.1.call-start = ((), (), s32[]{:S(2)}) async-start(), calls=%async_computation.6 | async-start | bytes 8650752 | tf_op jit(solution)/shard_map/all_gather | solution.py:1494
  9.4 301.8 %all-gather.4.cloned.1.call-start = ((), (), s32[]{:S(2)}) async-start(), calls=%async_computation.5 | async-start | bytes 8650752 | tf_op jit(solution)/shard_map/all_gather | solution.py:1494
  56.1 37.1 %all-to-all-start = ((bf16[32,2,4496]{2,1,0:T(2,128)(2,1)}), bf16[32,2,4496]{2,1,0:T(2,128)(2,1)}, u32[]{:S(2)}, u32[]{:S(2)}) async-start(bf16[32,2,4496]{2,1,0:T(2,128)(2,1)} %reshape.966), calls=%async_computation | async-start | bytes 1179648 | tf_op jit(solution)/shard_map/all_to_all | solution.py:802
  97.2 66.8 %collective-permute-start.2 = (bf16[256,1536]{1,0:T(8,128)(2,1)}, bf16[256,1536]{1,0:T(8,128)(2,1)}, u32[]{:S(2)}, u32[]{:S(2)}) collective-permute-start(bf16[256,1536]{1,0:T(8,128)(2,1)} %pad_maximum_fusion.4), channel_id=1, source_target_pairs={{0,0},{1,16},{2,10},{3,26},{8,11},{9,27},{10,17},{11,1},{16,18},{1... | collective-permute-start | bytes 2359304 | tf_op jit(solution)/shard_map/ppermute | solution.py:777
  101.6 65.0 %collective-permute-start.3 = (bf16[256,1536]{1,0:T(8,128)(2,1)}, bf16[256,1536]{1,0:T(8,128)(2,1)}, u32[]{:S(2)}, u32[]{:S(2)}) collective-permute-start(bf16[256,1536]{1,0:T(8,128)(2,1)} %pad_maximum_fusion.4), channel_id=1, source_target_pairs={{0,16},{1,0},{2,26},{3,10},{8,27},{9,11},{10,1},{11,17},{16,2},{17... | collective-permute-start | bytes 2359304 | tf_op jit(solution)/shard_map/ppermute | solution.py:777
  103.6 73.2 %collective-permute-start.4 = (bf16[256,1536]{1,0:T(8,128)(2,1)}, bf16[256,1536]{1,0:T(8,128)(2,1)}, u32[]{:S(2)}, u32[]{:S(2)}) collective-permute-start(bf16[256,1536]{1,0:T(8,128)(2,1)} %pad_maximum_fusion.4), channel_id=1, source_target_pairs={{0,10},{1,26},{2,0},{3,16},{8,17},{9,1},{10,11},{11,27},{16,24},{1... | collective-permute-start | bytes 2359304 | tf_op jit(solution)/shard_map/ppermute | solution.py:777
  110.7 129.4 %collective-permute-start.5 = (bf16[256,1536]{1,0:T(8,128)(2,1)}, bf16[256,1536]{1,0:T(8,128)(2,1)}, u32[]{:S(2)}, u32[]{:S(2)}) collective-permute-start(bf16[256,1536]{1,0:T(8,128)(2,1)} %pad_maximum_fusion.4), channel_id=1, source_target_pairs={{0,26},{1,10},{2,16},{3,0},{8,1},{9,17},{10,27},{11,11},{16,8},{17... | collective-permute-start | bytes 2359304 | tf_op jit(solution)/shard_map/ppermute | solution.py:777
  123.3 116.1 %copy-start.37 = (s32[256,65]{0,1:T(8,128)S(1)}, s32[256,65]{0,1:T(8,128)}, u32[]{:S(2)}) copy-start(s32[256,65]{0,1:T(8,128)} %param.31) | copy-start | bytes 199684
  137.0 174.1 %collective-permute-start = (bf16[256,1536]{1,0:T(8,128)(2,1)S(1)}, bf16[256,1536]{1,0:T(8,128)(2,1)S(1)}, u32[]{:S(2)}, u32[]{:S(2)}) collective-permute-start(bf16[256,1536]{1,0:T(8,128)(2,1)S(1)} %pad_maximum_fusion.5), channel_id=1, source_target_pairs={{0,0},{1,16},{2,10},{3,26},{8,11},{9,27},{10,17},{11,1},{16,18},{1... | collective-permute-start | bytes 2359304 | tf_op jit(solution)/shard_map/ppermute | solution.py:777
  164.1 147.1 %collective-permute-start.1 = (bf16[256,1536]{1,0:T(8,128)(2,1)S(1)}, bf16[256,1536]{1,0:T(8,128)(2,1)}, u32[]{:S(2)}, u32[]{:S(2)}) collective-permute-start(bf16[256,1536]{1,0:T(8,128)(2,1)S(1)} %pad_maximum_fusion.5), channel_id=1, source_target_pairs={{0,16},{1,0},{2,26},{3,10},{8,27},{9,11},{10,1},{11,17},{16,2},{17... | collective-permute-start | bytes 2359304 | tf_op jit(solution)/shard_map/ppermute | solution.py:777
  166.6 161.7 %collective-permute-start.6 = (bf16[256,1536]{1,0:T(8,128)(2,1)S(1)}, bf16[256,1536]{1,0:T(8,128)(2,1)}, u32[]{:S(2)}, u32[]{:S(2)}) collective-permute-start(bf16[256,1536]{1,0:T(8,128)(2,1)S(1)} %pad_maximum_fusion.5), channel_id=1, source_target_pairs={{0,10},{1,26},{2,0},{3,16},{8,17},{9,1},{10,11},{11,27},{16,24},{1... | collective-permute-start | bytes 2359304 | tf_op jit(solution)/shard_map/ppermute | solution.py:777
  176.7 151.6 %collective-permute-start.7 = (bf16[256,1536]{1,0:T(8,128)(2,1)S(1)}, bf16[256,1536]{1,0:T(8,128)(2,1)}, u32[]{:S(2)}, u32[]{:S(2)}) collective-permute-start(bf16[256,1536]{1,0:T(8,128)(2,1)S(1)} %pad_maximum_fusion.5), channel_id=1, source_target_pairs={{0,26},{1,10},{2,16},{3,0},{8,1},{9,17},{10,27},{11,11},{16,8},{17... | collective-permute-start | bytes 2359304 | tf_op jit(solution)/shard_map/ppermute | solution.py:777
  328.3 65.1 %copy-start.1 = (bf16[1152,256]{0,1:T(8,128)(2,1)S(1)}, bf16[1152,256]{0,1:T(8,128)(2,1)}, u32[]{:S(2)}) copy-start(bf16[1152,256]{0,1:T(8,128)(2,1)} %copy-done) | copy-start | bytes 1769476
  328.3 65.1 %copy-start.2 = (bf16[1152,256]{1,0:T(8,128)(2,1)S(1)}, bf16[1152,256]{1,0:T(8,128)(2,1)}, u32[]{:S(2)}) copy-start(bf16[1152,256]{1,0:T(8,128)(2,1)} %copy.279.refs_5_.refs_7_.spread_ref.refs_0_) | copy-start | bytes 1769476
  328.3 65.1 %copy-start.4 = (f32[256,1024]{1,0:T(8,128)S(1)}, f32[256,1024]{1,0:T(8,128)}, u32[]{:S(2)}) copy-start(f32[256,1024]{1,0:T(8,128)} %get-tuple-element.120.middle_ref) | copy-start | bytes 3145732
  328.4 65.1 %copy-start.5 = (f32[16,1024]{1,0:T(8,128)S(1)}, f32[16,1024]{1,0:T(8,128)}, u32[]{:S(2)}) copy-start(f32[16,1024]{1,0:T(8,128)} %pad.20.refs_1_.refs_3_.gain_ref) | copy-start | bytes 196612
  328.4 65.1 %copy-start.6 = (f32[256,128]{1,0:T(8,128)S(1)}, f32[256,128]{1,0:T(8,128)}, u32[]{:S(2)}) copy-start(f32[256,128]{1,0:T(8,128)} %get-tuple-element.121.gates_ref) | copy-start | bytes 393220
  328.4 65.1 %copy-start.7 = (s32[8]{0:T(128)S(1)}, s32[8]{0:T(128)}, u32[]{:S(2)}) copy-start(s32[8]{0:T(128)} %picked_ref.3) | copy-start | bytes 100
  398.6 21.2 %all-to-all-start.1 = ((bf16[32,8,1024]{2,1,0:T(8,128)(2,1)}), bf16[32,8,1024]{2,1,0:T(8,128)(2,1)S(1)}, u32[]{:S(2)}, u32[]{:S(2)}) async-start(bf16[32,8,1024]{2,1,0:T(8,128)(2,1)} %broadcast_in_dim.38), calls=%async_computation.1 | async-start | bytes 1048576 | tf_op jit(solution)/shard_map/all_to_all | solution.py:802
  429.9 32.6 %all-to-all-start.2 = ((bf16[32,8,2176]{2,1,0:T(8,128)(2,1)}), bf16[32,8,2176]{2,1,0:T(8,128)(2,1)}, u32[]{:S(2)}, u32[]{:S(2)}) async-start(bf16[32,8,2176]{2,1,0:T(8,128)(2,1)} %pad_maximum_fusion.1), calls=%async_computation.2 | async-start | bytes 2228224 | tf_op jit(solution)/shard_map/all_to_all | solution.py:802
  466.4 115.3 %all-to-all-start.3 = ((f32[32,1,16]{2,1,0:T(1,128)}), f32[32,1,16]{2,1,0:T(1,128)S(1)}, u32[]{:S(2)}, u32[]{:S(2)}) async-start(f32[32,1,16]{2,1,0:T(1,128)} %broadcast_in_dim.41), calls=%async_computation.3 | async-start | bytes 32768 | tf_op jit(solution)/shard_map/all_to_all | solution.py:802
  544.8 53.1 %collective-permute-start.8 = (bf16[256,1536]{1,0:T(8,128)(2,1)}, bf16[256,1536]{1,0:T(8,128)(2,1)}, u32[]{:S(2)}, u32[]{:S(2)}) collective-permute-start(bf16[256,1536]{1,0:T(8,128)(2,1)} %get-tuple-element.133), channel_id=1, source_target_pairs={{0,0},{16,1},{10,2},{26,3},{11,8},{27,9},{17,10},{1,11},{18,16},{2... | collective-permute-start | bytes 2359304 | tf_op jit(solution)/shard_map/ppermute | solution.py:790
  548.9 132.6 %collective-permute-start.11 = (bf16[256,1536]{1,0:T(8,128)(2,1)}, bf16[256,1536]{1,0:T(8,128)(2,1)}, u32[]{:S(2)}, u32[]{:S(2)}) collective-permute-start(bf16[256,1536]{1,0:T(8,128)(2,1)} %get-tuple-element.150), channel_id=1, source_target_pairs={{16,0},{0,1},{26,2},{10,3},{27,8},{11,9},{1,10},{17,11},{2,16},{18... | collective-permute-start | bytes 2359304 | tf_op jit(solution)/shard_map/ppermute | solution.py:790
  552.1 129.4 %collective-permute-start.12 = (bf16[256,1536]{1,0:T(8,128)(2,1)}, bf16[256,1536]{1,0:T(8,128)(2,1)}, u32[]{:S(2)}, u32[]{:S(2)}) collective-permute-start(bf16[256,1536]{1,0:T(8,128)(2,1)} %get-tuple-element.151), channel_id=1, source_target_pairs={{10,0},{26,1},{0,2},{16,3},{17,8},{1,9},{11,10},{27,11},{24,16},{8... | collective-permute-start | bytes 2359304 | tf_op jit(solution)/shard_map/ppermute | solution.py:790
  555.8 125.7 %collective-permute-start.13 = (bf16[256,1536]{1,0:T(8,128)(2,1)}, bf16[256,1536]{1,0:T(8,128)(2,1)}, u32[]{:S(2)}, u32[]{:S(2)}) collective-permute-start(bf16[256,1536]{1,0:T(8,128)(2,1)} %get-tuple-element.152), channel_id=1, source_target_pairs={{26,0},{10,1},{16,2},{0,3},{1,8},{17,9},{27,10},{11,11},{8,16},{24... | collective-permute-start | bytes 2359304 | tf_op jit(solution)/shard_map/ppermute | solution.py:790
  667.1 55.3 %collective-permute-start.9 = (bf16[256,1536]{1,0:T(8,128)(2,1)}, bf16[256,1536]{1,0:T(8,128)(2,1)}, u32[]{:S(2)}, u32[]{:S(2)}) collective-permute-start(bf16[256,1536]{1,0:T(8,128)(2,1)} %get-tuple-element.148), channel_id=1, source_target_pairs={{0,0},{16,1},{10,2},{26,3},{11,8},{27,9},{17,10},{1,11},{18,16},{2... | collective-permute-start | bytes 2359304 | tf_op jit(solution)/shard_map/ppermute | solution.py:790
  678.6 43.8 %collective-permute-start.10 = (bf16[256,1536]{1,0:T(8,128)(2,1)}, bf16[256,1536]{1,0:T(8,128)(2,1)}, u32[]{:S(2)}, u32[]{:S(2)}) collective-permute-start(bf16[256,1536]{1,0:T(8,128)(2,1)} %get-tuple-element.149), channel_id=1, source_target_pairs={{16,0},{0,1},{26,2},{10,3},{27,8},{11,9},{1,10},{17,11},{2,16},{18... | collective-permute-start | bytes 2359304 | tf_op jit(solution)/shard_map/ppermute | solution.py:790
  710.8 111.0 %all-to-all-start.4 = ((bf16[32,2,4496]{2,1,0:T(2,128)(2,1)}), bf16[32,2,4496]{2,1,0:T(2,128)(2,1)}, u32[]{:S(2)}, u32[]{:S(2)}) async-start(bf16[32,2,4496]{2,1,0:T(2,128)(2,1)} %reshape.968), calls=%async_computation.4 | async-start | bytes 1179648 | tf_op jit(solution)/shard_map/all_to_all | solution.py:802
  826.0 66.8 %collective-permute-start.14 = (bf16[256,1536]{1,0:T(8,128)(2,1)}, bf16[256,1536]{1,0:T(8,128)(2,1)}, u32[]{:S(2)}, u32[]{:S(2)}) collective-permute-start(bf16[256,1536]{1,0:T(8,128)(2,1)} %get-tuple-element.175), channel_id=1, source_target_pairs={{10,0},{26,1},{0,2},{16,3},{17,8},{1,9},{11,10},{27,11},{24,16},{8... | collective-permute-start | bytes 2359304 | tf_op jit(solution)/shard_map/ppermute | solution.py:790
  830.1 62.7 %collective-permute-start.15 = (bf16[256,1536]{1,0:T(8,128)(2,1)}, bf16[256,1536]{1,0:T(8,128)(2,1)}, u32[]{:S(2)}, u32[]{:S(2)}) collective-permute-start(bf16[256,1536]{1,0:T(8,128)(2,1)} %get-tuple-element.176), channel_id=1, source_target_pairs={{26,0},{10,1},{16,2},{0,3},{1,8},{17,9},{27,10},{11,11},{8,16},{24... | collective-permute-start | bytes 2359304 | tf_op jit(solution)/shard_map/ppermute | solution.py:790
  835.4 55.3 %copy-start.22 = (f32[2,32,4096]{2,1,0:T(8,128)S(1)}, f32[2,32,4096]{2,1,0:T(8,128)}, u32[]{:S(2)}) copy-start(f32[2,32,4096]{2,1,0:T(8,128)} %param.38) | copy-start | bytes 3145732
  835.4 55.3 %copy-start.23 = (f32[2,32,4096]{2,1,0:T(8,128)S(1)}, f32[2,32,4096]{2,1,0:T(8,128)}, u32[]{:S(2)}) copy-start(f32[2,32,4096]{2,1,0:T(8,128)} %param.37) | copy-start | bytes 3145732
  (41 other events, 497.6 us)
Sparse Core Ops, SparseCore 0:
  11.5 87.9 all-gather.5
  102.9 150.8 all-gather.3

commit v5 on v4

--- a/solution.py
+++ b/solution.py
@@ -25,17 +25,6 @@
 MASK_FILL = -1e30
 
 
-def rms_norm(inputs, gain_row):
-    return (
-        inputs * lax.rsqrt(jnp.mean(inputs * inputs, axis=-1, keepdims=True) + EPS_NORM) * gain_row
-    )
-
-
-def norm_back(inputs, gain_row, upstream):
-    _, pullback = jax.vjp(rms_norm, inputs, gain_row)
-    return pullback(upstream)
-
-
 AXES = ("z", "x", "h", "y", "c")
 PLANES = 4
 SHIFTS = (0, 2, 1, 3)
@@ -113,11 +102,11 @@
     return lane < HDIM, lane >= HDIM
 
 
-def fetch_weights(weight_ref, held_ref, copy_sem, order):
+def fetch_weights(weight_ref, held_ref, copy_sem, layer_index, order):
     copies = {}
     for part in order:
         copies[part] = pltpu.make_async_copy(
-            weight_ref.at[:, pl.ds(part * D, D)], held_ref.at[part], copy_sem.at[part]
+            weight_ref.at[layer_index, :, pl.ds(part * D, D)], held_ref.at[part], copy_sem.at[part]
         )
         copies[part].start()
     return copies
@@ -155,7 +144,7 @@
         held_ref,
         copy_sem,
     ) = refs
-    copies = fetch_weights(weight_ref, held_ref, copy_sem, (0, 1, 2, 3))
+    copies = fetch_weights(weight_ref, held_ref, copy_sem, layer_index, (0, 1, 2, 3))
     seq_len = hidden_ref.shape[0]
     hidden = hidden_ref[...]
     if layer_index > 0:
@@ -295,7 +284,7 @@
         spread_ref, gates_ref, refs = refs[0], refs[1], refs[2:]
         outgoing_ref, refs = refs[3], refs[:3] + refs[4:]
     grad_out_ref, weight_grad_ref, gain_grad_ref, pull_ref, key_pull_ref, held_ref, copy_sem = refs
-    copies = fetch_weights(weight_ref, held_ref, copy_sem, (3, 2, 0, 1))
+    copies = fetch_weights(weight_ref, held_ref, copy_sem, layer_index, (3, 2, 0, 1))
     seq_len = hidden_ref.shape[0]
     row = 4 * layer_index
     ffn_grad = dot_nn(spread_back_ref[...], back_ref[...]) + dot_nt(
@@ -615,30 +604,68 @@
     return (slot_gates(spread, gates, capacity) * wide).astype(jnp.bfloat16)
 
 
-def first_pull_kernel(capacity, picked_ref, rows_ref, spread_ref, gates_ref, grad_ref, out_ref):
+def first_pull_kernel(
+    capacity,
+    gain_row,
+    position_count,
+    picked_ref,
+    got_ref,
+    own_ref,
+    rows_ref,
+    gain_ref,
+    spread_ref,
+    gates_ref,
+    grad_ref,
+    out_ref,
+    gain_grad_ref,
+    stat_ref,
+):
+    stats = got_ref[:, :, 2 * D :].astype(jnp.float32)
+
+    def joined(place):
+        return sum(stats[:, :, place + term : place + term + 1] for term in range(3))
+
+    peaks, sums, dots = joined(0), joined(3), joined(6)
+    peak = jnp.max(peaks, axis=0)
+    log_norm = peak + jnp.log(jnp.sum(sums * jnp.exp(peaks - peak[None]), axis=0))
+    mass, entropy = own_ref[:, 0:1], own_ref[:, 1:2]
+    loss = (1.0 + mass) * log_norm - jnp.sum(dots, axis=0) + entropy
+    scale = (1.0 + mass)[None] * jnp.exp(peaks - log_norm[None])
+    total = jnp.zeros(rows_ref.shape, jnp.float32)
+    for device in range(got_ref.shape[0]):
+        total += scale[device] * got_ref[device, :, :D].astype(jnp.float32)
+        total -= got_ref[device, :, D : 2 * D].astype(jnp.float32)
+    rows_grad, gain_grad = norm_pull(
+        rows_ref[...], gain_ref[gain_row : gain_row + 1, :], total / position_count
+    )
+    gain_grad_ref[...] = gain_grad
+    lane = lax.broadcasted_iota(jnp.int32, stat_ref.shape, 1)
+    stat_ref[...] = jnp.where(lane == 0, log_norm, jnp.where(lane == 1, loss, 0.0))
     grad_ref[...] = jnp.zeros_like(grad_ref)
     for place in range(rows_ref.shape[0]):
-        grad_ref[pl.ds(picked_ref[place], 1), :] = rows_ref[place : place + 1, :]
+        grad_ref[pl.ds(picked_ref[place], 1), :] = rows_grad[place : place + 1, :]
     out_ref[...] = outgoing_pull(grad_ref[...], spread_ref[...], gates_ref[...], capacity)
 
 
-def first_pull(capacity, picked, rows, spread, gates):
+def first_pull(capacity, gain_row, position_count, picked, got, own, rows, gains, spread, gates):
     whole = pl.BlockSpec(memory_space=pltpu.VMEM)
     return pl.pallas_call(
-        functools.partial(first_pull_kernel, capacity),
+        functools.partial(first_pull_kernel, capacity, gain_row, position_count),
         out_shape=(
             jax.ShapeDtypeStruct((spread.shape[1], D), jnp.float32),
             jax.ShapeDtypeStruct((spread.shape[0], D), jnp.bfloat16),
-        ),
-        in_specs=[pl.BlockSpec(memory_space=pltpu.SMEM)] + [whole] * 3,
-        out_specs=[whole] * 2,
+            jax.ShapeDtypeStruct((1, D), jnp.float32),
+            jax.ShapeDtypeStruct(own.shape, jnp.float32),
+        ),
+        in_specs=[pl.BlockSpec(memory_space=pltpu.SMEM)] + [whole] * 6,
+        out_specs=[whole] * 4,
         compiler_params=pltpu.CompilerParams(vmem_limit_bytes=48 * 1024 * 1024),
         cost_estimate=pl.CostEstimate(
             flops=4 * spread.shape[0] * spread.shape[1] * D,
-            bytes_accessed=5 * 1024 * 1024,
+            bytes_accessed=6 * 1024 * 1024,
             transcendentals=0,
         ),
-    )(picked, rows, spread, gates)
+    )(picked, got, own, rows, gains, spread, gates)
 
 
 def router_kernel(
@@ -839,13 +866,80 @@
     return places
 
 
-def greet(partners):
+def swap_routes():
+    z, y, c = (lax.axis_index(name) for name in ("z", "y", "c"))
+    expert_plane = lax.rem(y + z, 2) * 2 + c
+    shift_in = lax.rem(z - expert_plane + PLANES, PLANES)
+    routes = []
+    for turn in range(PLANES):
+        upper = 1 - y if turn // 2 else y
+        lower = 1 - c if turn % 2 else c
+        plane = lax.rem(z + lower * 2 + upper, PLANES)
+        target = {"z": plane, "y": lax.rem(z // 2 + plane, 2), "c": lax.rem(z, 2)}
+        first, second = lax.rem(shift_in, 2), shift_in // 2
+        source = {
+            "z": expert_plane,
+            "y": 1 - first if turn // 2 else first,
+            "c": 1 - second if turn % 2 else second,
+        }
+        own = (target["z"] == z) & (target["y"] == y) & (target["c"] == c)
+        routes.append((target, source, own))
+    return routes
+
+
+def swap_copies(route, turn, held_ref, slot_ref, sems, backward):
+    target, source, _ = route
+    send_sem, recv_sem, local_sem = sems
+    away = pltpu.make_async_remote_copy(
+        src_ref=held_ref,
+        dst_ref=slot_ref,
+        send_sem=send_sem.at[turn],
+        recv_sem=recv_sem.at[turn],
+        device_id=source if backward else target,
+        device_id_type=pl.DeviceIdType.MESH,
+    )
+    return away, pltpu.make_async_copy(held_ref, slot_ref, local_sem.at[turn])
+
+
+def swap_start(routes, held_refs, slot_refs, sems, backward):
+    for turn, route in enumerate(routes):
+        away, stay = swap_copies(route, turn, held_refs[turn], slot_refs[turn], sems, backward)
+        pl.when(jnp.logical_not(route[2]))(away.start)
+        pl.when(route[2])(stay.start)
+
+
+def swap_wait(routes, held_refs, slot_refs, sems, backward):
+    for turn, route in enumerate(routes):
+        away, stay = swap_copies(route, turn, held_refs[turn], slot_refs[turn], sems, backward)
+        pl.when(jnp.logical_not(route[2]))(away.wait)
+        pl.when(route[2])(stay.wait)
+
+
+def greet(partners, routes=()):
     barrier = pltpu.get_barrier_semaphore()
-    for partner in partners:
+
+    def hello(partner):
         pl.semaphore_signal(
             barrier, inc=1, device_id=partner, device_id_type=pl.DeviceIdType.MESH
         )
-    pl.semaphore_wait(barrier, len(partners))
+
+    for partner in partners:
+        hello(partner)
+    for target, source, own in routes:
+
+        @pl.when(jnp.logical_not(own))
+        def _(target=target, source=source):
+            hello(target)
+            hello(source)
+
+    count = len(partners)
+    for _, _, own in routes:
+        count = count + jnp.where(own, 0, 2)
+    pl.semaphore_wait(barrier, count)
+
+
+def swap_scratch(count):
+    return [pltpu.SemaphoreType.DMA((PLANES,))] * (3 * count)
 
 
 def push(source, target, send_sem, recv_sem, place, partner):
@@ -893,13 +987,40 @@
     ref[2 * pair + 1] = values[rows:]
 
 
-def forward_exchange_kernel(part_count, outgoing_ref, *refs):
-    part_refs, refs = refs[:part_count], refs[part_count:]
-    returned_ref, received_ref, up_ref, down_ref, produced_ref, copy_sem, send_sem, recv_sem = refs
+def forward_exchange_kernel(spread_count, outgoing_ref, *refs):
+    routes = ()
+    if spread_count:
+        routes = swap_routes()
+        pieces, refs = refs[:spread_count], refs[spread_count:]
+        returned_ref, received_ref = refs[:2]
+        slots, refs = refs[2 : 2 + spread_count * PLANES], refs[2 + spread_count * PLANES :]
+        sems, refs = refs[-3 * spread_count :], refs[: -3 * spread_count]
+        swaps = [
+            (
+                routes,
+                [piece] * PLANES,
+                slots[place * PLANES : (place + 1) * PLANES],
+                sems[3 * place : 3 * place + 3],
+                False,
+            )
+            for place, piece in enumerate(pieces)
+        ]
+        part_refs = slots[:PLANES]
+    else:
+        part_refs, refs = refs[:PLANES], refs[PLANES:]
+        returned_ref, received_ref = refs[:2]
+        swaps, refs = [], refs[2:]
+    up_ref, down_ref, produced_ref, copy_sem, send_sem, recv_sem = refs
     partners, groups = plane_partners()
-    greet(partners[1:])
+    greet(partners[1:], routes)
+    for swap in swaps[:1]:
+        swap_start(*swap)
     copies = exchange_out(outgoing_ref, received_ref, send_sem, recv_sem, partners, groups)
-    fetch_expert(part_places(part_count), part_refs, up_ref, down_ref, copy_sem)
+    for swap in swaps[:1]:
+        swap_wait(*swap)
+    for swap in swaps[1:]:
+        swap_start(*swap)
+    fetch_expert(part_places(PLANES), part_refs, up_ref, down_ref, copy_sem)
     back = {}
     for pair in range(4):
         for turn in (2 * pair, 2 * pair + 1):
@@ -924,31 +1045,43 @@
     for turn in range(1, 8):
         copies[turn].wait_send()
         back[turn].wait()
-
-
-def forward_exchange(outgoing, parts):
-    whole, _, apart, scratch = expert_specs(parts)
+    for swap in swaps[1:]:
+        swap_wait(*swap)
+
+
+def forward_exchange(outgoing, parts, pieces=()):
+    whole = pl.BlockSpec(memory_space=pltpu.VMEM)
+    apart = [pl.BlockSpec(memory_space=pl.ANY)]
+    sources = list(pieces) if pieces else list(parts)
+    rows = sources[0].shape[0]
     shape = jax.ShapeDtypeStruct(outgoing.shape, jnp.bfloat16)
     slot_total = outgoing.shape[0] * outgoing.shape[1]
+    slots = [
+        jax.ShapeDtypeStruct(piece.shape, piece.dtype) for piece in pieces for _ in range(PLANES)
+    ]
     return pl.pallas_call(
-        functools.partial(forward_exchange_kernel, len(parts)),
-        out_shape=(shape, shape),
-        in_specs=[whole] + apart,
-        out_specs=[whole] * 2,
-        scratch_shapes=scratch[:2]
-        + [
+        functools.partial(forward_exchange_kernel, len(pieces)),
+        out_shape=[shape, shape] + slots,
+        in_specs=[whole] + apart * len(sources),
+        out_specs=[whole] * 2 + apart * len(slots),
+        scratch_shapes=[
+            pltpu.VMEM((D, 2 * F), jnp.bfloat16),
+            pltpu.VMEM((F, D), jnp.bfloat16),
             pltpu.VMEM(outgoing.shape, jnp.bfloat16),
-            scratch[2],
+            pltpu.SemaphoreType.DMA((PLANES * (1 + F // rows),)),
             pltpu.SemaphoreType.DMA((16,)),
             pltpu.SemaphoreType.DMA((16,)),
-        ],
+        ]
+        + swap_scratch(len(pieces)),
         compiler_params=pltpu.CompilerParams(
-            vmem_limit_bytes=56 * 1024 * 1024, collective_id=2, has_side_effects=True
+            vmem_limit_bytes=56 * 1024 * 1024,
+            collective_id=5 if pieces else 2,
+            has_side_effects=True,
         ),
         cost_estimate=pl.CostEstimate(
             flops=slot_total * D * F * 6, bytes_accessed=150 * 1024 * 1024, transcendentals=1 << 19
         ),
-    )(outgoing, *parts)
+    )(outgoing, *sources)
 
 
 def backward_exchange_kernel(
@@ -1486,12 +1619,7 @@
     )
     table_low = embedding.astype(jnp.bfloat16)
     looked_up = jnp.take(table_low, tokens, axis=0, mode="clip").reshape(devices_all, seq_len * column_count)
-    attention_low = []
-    for layer_index in range(layer_count):
-        rows_low = attention[layer_index].astype(jnp.bfloat16)
-        if layer_index > 0:
-            rows_low, looked_up = tie(rows_low, looked_up)
-        attention_low.append(lax.all_gather(rows_low, AXES, axis=0, tiled=True))
+    attention_low = lax.all_gather(attention.astype(jnp.bfloat16), AXES, axis=1, tiled=True)
     small_count = gain_count + layer_count * experts_all
     small = jnp.concatenate(
         [norm_gains.T, router.transpose(1, 0, 2).reshape(column_count, layer_count * experts_all)],
@@ -1501,6 +1629,8 @@
         small.reshape(1, column_count * small_count), (devices_all, column_count * small_count)
     )
     arrived_rows = send_all(jnp.concatenate([looked_up, small], axis=1))
+    fits_sum = [lax.axis_size(name) for name in AXES] == [PLANES, 2, 1, 2, 2]
+
     expert_parts, expert_pieces = [], []
     for layer_index in range(layer_count):
         down_piece = (
@@ -1513,8 +1643,8 @@
             jnp.bfloat16
         )
         expert_pieces.append(piece)
-    expert_pieces[0], arrived_rows = tie(expert_pieces[0], arrived_rows)
-    expert_parts.append(spread_experts(expert_pieces[0], row_groups))
+    if not fits_sum:
+        expert_parts.append(spread_experts(expert_pieces[0], row_groups))
 
     hidden = (
         arrived_rows[:, : seq_len * column_count]
@@ -1533,8 +1663,6 @@
         .transpose(1, 0, 2)[:, :, group_order],
         ((0, 0), (0, 0), (0, LANES - experts_all)),
     )
-
-    fits_sum = [lax.axis_size(name) for name in AXES] == [PLANES, 2, 1, 2, 2]
 
     member = jnp.any(routes[:, :, None] == group_order[None, None, :], axis=1)
     before = jnp.dot(
@@ -1566,7 +1694,7 @@
             prefix,
             hidden,
             extra,
-            attention_low[layer_index],
+            attention_low,
             gain_rows,
             turns,
             router_low,
@@ -1576,19 +1704,20 @@
         )
         hidden = saved[6]
         gates, outgoing = saved[9], saved[10]
-        if layer_index + 1 < layer_count:
-            piece, outgoing = tie(expert_pieces[layer_index + 1], outgoing)
-            expert_parts.append(spread_experts(piece, row_groups))
         blocks = outgoing.reshape(experts_all, capacity, D)
         if fits_sum:
-            returned, received = forward_exchange(blocks, expert_parts[layer_index])
+            here = expert_parts[layer_index] if layer_index < len(expert_parts) else ()
+            ahead = () if here else expert_pieces[layer_index : layer_index + 2]
+            returned, received, *arrived = forward_exchange(blocks, here, ahead)
+            for place in range(len(ahead)):
+                expert_parts.append(arrived[place * PLANES : (place + 1) * PLANES])
         else:
+            for piece in expert_pieces[layer_index + 1 : layer_index + 2]:
+                expert_parts.append(spread_experts(piece, row_groups))
             received = send_plane(blocks).reshape(slot_total, D)
             produced = run_expert(places, received, expert_parts[layer_index])
             returned = send_plane(produced.reshape(experts_all, capacity, D))
         returned = returned.reshape(slot_total, D)
-        if layer_index + 1 < layer_count:
-            expert_parts[-1][:2], returned = tie(expert_parts[-1][:2], returned)
         stored.append((saved, received, returned))
         extra = (gates, returned)
 
@@ -1606,7 +1735,6 @@
     )
     own_count = position_count // devices_all
 
-    final_gain = gain_rows[4 * layer_count]
     final_rows, final_low = final_rows_of(
         capacity,
         4 * layer_count,
@@ -1631,38 +1759,26 @@
     )
     stats = jnp.pad(stats, ((0, 0), (0, 128 - stats.shape[1])))
     pull_sent = jnp.concatenate([pull, marked_pull, stats], axis=1).astype(jnp.bfloat16)
-    pull_got = send_all(pull_sent.reshape(devices_all, own_count, 2 * D + 128)).astype(jnp.float32)
-    stats_got = pull_got[:, :, 2 * D :]
-    peaks = jnp.sum(stats_got[:, :, 0:3], axis=2)
-    sums = jnp.sum(stats_got[:, :, 3:6], axis=2)
-    dots = jnp.sum(stats_got[:, :, 6:9], axis=2)
-    peak_own = jnp.max(peaks, axis=0)
-    log_norm_own = peak_own + jnp.log(jnp.sum(sums * jnp.exp(peaks - peak_own), axis=0))
-    mass_own = lax.dynamic_slice_in_dim(teacher_mass, me_all * own_count, own_count)
-    entropy_own = lax.dynamic_slice_in_dim(
-        jnp.sum(teacher_prob * teacher_log, axis=1), me_all * own_count, own_count
-    )
-    loss_own = (1.0 + mass_own) * log_norm_own - jnp.sum(dots, axis=0) + entropy_own
-    scale_own = (1.0 + mass_own)[None, :] * jnp.exp(peaks - log_norm_own[None, :])
-    marked_total = jnp.sum(pull_got[:, :, D : 2 * D], axis=0)
-    final_grad = (
-        jnp.sum(scale_own[:, :, None] * pull_got[:, :, :D], axis=0) - marked_total
-    ) / position_count
-    spread_stats = jnp.concatenate([log_norm_own, loss_own]).reshape(1, 2 * own_count)
-    stats_all = send_all(jnp.broadcast_to(spread_stats, (devices_all, 2 * own_count)))
-    log_norm = stats_all[:, :own_count].reshape(position_count)
-    loss_value = jnp.sum(stats_all[:, own_count:]) / position_count
-    grad_logits = (
-        jnp.exp(logits - log_norm[:, None]) * (1.0 + teacher_mass)[:, None] - marked
-    ) / position_count
-    table_grad = jnp.einsum(
-        "pv,pd->vd",
-        grad_logits.astype(jnp.bfloat16),
-        all_rows,
-        preferred_element_type=jnp.float32,
-    )
-    rows_grad, final_gain_grad = norm_back(final_rows, final_gain, final_grad)
-    grad_hidden, sent_back = first_pull(capacity, picked, rows_grad, spread_flat, extra[0])
+    pull_got = send_all(pull_sent.reshape(devices_all, own_count, 2 * D + LANES))
+    entropy = jnp.sum(teacher_prob * teacher_log, axis=1)
+    own = lax.dynamic_slice_in_dim(
+        jnp.pad(jnp.stack([teacher_mass, entropy], axis=1), ((0, 0), (0, LANES - 2))),
+        me_all * own_count,
+        own_count,
+    )
+    grad_hidden, sent_back, final_gain_grad, own_stats = first_pull(
+        capacity,
+        4 * layer_count,
+        position_count,
+        picked,
+        pull_got,
+        own,
+        final_rows,
+        gain_rows,
+        spread_flat,
+        extra[0],
+    )
+    final_gain_grad = final_gain_grad[0]
     gain_parts = [None] * (4 * layer_count) + [final_gain_grad]
     attention_parts = [None] * layer_count
     router_parts = [None] * layer_count
@@ -1697,14 +1813,15 @@
                 places, received, output_grad, gate_grad, activated, piece_rows
             )
         back_inputs = back_inputs.reshape(slot_total, D)
+        if upper is None:
+            own_stats, back_inputs = tie(own_stats, back_inputs)
         if upper is not None:
             piece_parts[upper][1:], back_inputs = tie(piece_parts[upper][1:], back_inputs)
         if layer_index > 0:
             piece_parts[layer_index] = return_expert_grads(grad_pieces, row_groups)
         else:
             turns_all = len(grad_pieces)
-            early = range(turns_all // 2)
-            piece_parts[0] = return_expert_grads(grad_pieces, row_groups, early)
+            piece_parts[0] = []
         lower = (spread_flat, stored[layer_index - 1][0][9]) if layer_index > 0 else ()
         results = backward_layer(
             layer_index,
@@ -1720,7 +1837,7 @@
             values,
             attended,
             middle,
-            attention_low[layer_index],
+            attention_low,
             gain_rows,
             turns,
             router_low,
@@ -1738,6 +1855,21 @@
                 weight_grad, AXES, scatter_dimension=0, tiled=True
             ).astype(jnp.float32)
 
+    log_norm_own, loss_own = own_stats[:, 0], own_stats[:, 1]
+    spread_stats = jnp.concatenate([log_norm_own, loss_own]).reshape(1, 2 * own_count)
+    stats_all = send_all(jnp.broadcast_to(spread_stats, (devices_all, 2 * own_count)))
+    log_norm = stats_all[:, :own_count].reshape(position_count)
+    loss_value = jnp.sum(stats_all[:, own_count:]) / position_count
+    grad_logits = (
+        jnp.exp(logits - log_norm[:, None]) * (1.0 + teacher_mass)[:, None] - marked
+    ) / position_count
+    table_grad = jnp.einsum(
+        "pv,pd->vd",
+        grad_logits.astype(jnp.bfloat16),
+        all_rows,
+        preferred_element_type=jnp.float32,
+    )
+
     sending = (
         grad_hidden.astype(jnp.bfloat16)
         .reshape(seq_len, devices_all, column_count)
@@ -1752,13 +1884,12 @@
             [sending, small_grads.reshape(devices_all, column_count * small_count)], axis=1
         )
     )
-    piece_parts[0], attention_parts = tie(piece_parts[0], attention_parts)
     if fits_sum:
         attention_parts = list(owner_sums(attention_parts[::-1], 2048))[::-1]
     grad_pieces, arrived_grads, attention_parts = lax.optimization_barrier(
         (grad_pieces, arrived_grads, attention_parts)
     )
-    late = range(turns_all // 2, turns_all)
+    late = range(turns_all)
     piece_parts[0] = piece_parts[0] + return_expert_grads(grad_pieces, row_groups, late)
     embedding_next = embedding_update_of(
         order,

time: 931 us -> 907 us (0.974)
  starting transfers between devices: 151 us -> 67 us
  Pallas kernels: 502 us -> 584 us
    ppermute x8 -> x0, starting transfers between devices: 85.4 us -> none  [spread_experts(): lax.ppermute(piece, ('z', 'h', 'y', 'c'), swap_pairs(row_groups, turn_pla...]
    pallas_call x3, Pallas kernels: 139 us -> 218 us  [the longest x2 215 us: forward_exchange(): pl.pallas_call(functools.partial(forward_exchange_kernel, len(pieces)), o...]
    all_gather x2 -> x1, waiting for transfers between devices: 0.02 us -> 36.8 us  [shards(): lax.all_gather(attention.astype(jnp.bfloat16), AXES, axis=1, tiled=True)]
    ppermute x8 -> x0, waiting for transfers between devices: 31.9 us -> none  [spread_experts(): lax.ppermute(piece, ('z', 'h', 'y', 'c'), swap_pairs(row_groups, turn_pla...]
    all_to_all x5, waiting for transfers between devices: 36.5 us -> 24.9 us  [send_all(): return lax.all_to_all(values, AXES, split_axis=0, concat_axis=0, tiled=True)]
  transfers between devices with their start and end apart: 23 -> 14, of which waited for: 4 -> 3; matrix products, arithmetic and copies ran while one was open for 15% -> 13% of each run, Pallas kernels for 47% -> 27%
where the time goes in v5:
time: 907 us; the launch traced here: 897 us
  Pallas kernels  584 us (64%)
  local copies, waits for them, and re-layouts  86.3 us (10%)
  starting transfers between devices  67 us (7%)
  waiting for transfers between devices  61.7 us (7%)
  other arithmetic  53.7 us (6%)
  matrix products  26.7 us (3%)
  between operations  18.1 us (2%)
    pallas_call x2, Pallas kernels, forward_exchange(): pl.pallas_call(functools.partial(forward_exchange_kernel, len(pieces)), o...  215 us
    pallas_call x2, Pallas kernels, backward_exchange(): pl.pallas_call(functools.partial(backward_exchange_kernel, len(parts), ca...  135 us
    pallas_call x1, Pallas kernels, owner_sums(): pl.pallas_call(functools.partial(owner_sum_kernel, layers), out_shape=jax...  99.4 us
    pallas_call x1, Pallas kernels, embedding_update_of(): pl.pallas_call(embedding_kernel, grid=(-(-vocabulary // VOCAB_BLOCK),), o...  55.7 us
    pallas_call x2, Pallas kernels, backward_layer(): pl.pallas_call(functools.partial(backward_kernel, layer_index, capacity),...  41.6 us
    all_to_all x5, starting transfers between devices, send_all(): return lax.all_to_all(values, AXES, split_axis=0, concat_axis=0, tiled=True)  38.7 us
    all_gather x1, waiting for transfers between devices, shards(): lax.all_gather(attention.astype(jnp.bfloat16), AXES, axis=1, tiled=True)  36.8 us
    pallas_call x2, Pallas kernels, forward_layer(): pl.pallas_call(functools.partial(forward_kernel, layer_index, capacity, e...  30.5 us
  transfers between devices with their start and end apart: 14, of which 3 were waited for; matrix products, arithmetic and copies ran while one was open for 13% of the time, Pallas kernels for 27%

profile of v5, /device:TPU:9, one launch (start us, length us, event | category | flops | bytes accessed | tf_op | source)
XLA Modules:
  0.0 897.1 jit_solution(1917831239618396156)
XLA Ops:
  12.9 8.8 copy.270
  22.4 28.4 %gather_fusion = bf16[8192,32]{1,0:T(8,128)(2,1)S(1)} fusion(bf16[50304,32]{1,0:T(8,128)(2,1)} %copy.270, s32[8192]{0:T(1024)S(1)} %get-tuple-element.344), kind=kCustom, calls=%fused_computation | custom fusion | bytes 1081344 | tf_op jit(solution)/shard_map/jit(_take)/gather | solution.py:1621
  56.2 6.7 all-to-all-start
  75.4 6.4 all-to-all-done
  81.9 4.0 reshape.909
  96.8 36.8 %all-gather.2.cloned.1.call-done.refs_0_.refs_2_.weight_ref = bf16[2,1024,4096]{2,1,0:T(8,128)(2,1)} async-done(((bf16[2,32,4096]{2,1,0:T(8,128)(2,1)}), bf16[2,1024,4096]{2,1,0:T(8,128)(2,1)}) %all-gather.2.cloned.1.call-update) | async-done | bytes 16777232 | tf_op jit(solution)/shard_map/all_gather | solution.py:1622
  133.5 13.6 %shard_map.426 = (f32[256,1024]{1,0:T(8,128)}, f32[256,2048]{1,0:T(8,128)}, bf16[256,1024]{1,0:T(8,128)(2,1)}, bf16[256,1024]{1,0:T(8,128)(2,1)}, bf16[256,1024]...) custom-call(s32[1]{0:T(128)S(6)} %copy.319.prefix_ref, ...), custom_call_target="tpu_custom_call" | custom-call | flops 3221225472 | bytes 25165824 | tf_op jit(solution)/shard_map/pallas_call | solution.py:223
  147.2 145.0 %shard_map.427 = (bf16[8,144,1024]{2,1,0:T(8,128)(2,1)}, bf16[8,144,1024]{2,1,0:T(8,128)(2,1)}, bf16[256,1536]{1,0:T(8,128)(2,1)}, bf16[256,1536]{1,0:T(8,128)(2...) custom-call(bf16[8,144,1024]{2,1,0:T(8,128)(2,1)} %bitcast.210, ...), custom_call_target="tpu_custom_call" | custom-call | flops 3623878656 | bytes 157286400 | tf_op jit(solution)/shard_map/pallas_call | solution.py:1062
  292.2 16.9 %shard_map.428 = (f32[256,1024]{1,0:T(8,128)}, f32[256,2048]{1,0:T(8,128)}, bf16[256,1024]{1,0:T(8,128)(2,1)}, bf16[256,1024]{1,0:T(8,128)(2,1)}, bf16[256,1024]...) custom-call(s32[1]{0:T(128)S(6)} %copy.319.prefix_ref, ...), custom_call_target="tpu_custom_call" | custom-call | flops 3221225472 | bytes 25165824 | tf_op jit(solution)/shard_map/pallas_call | solution.py:223
  309.2 70.4 %shard_map.429 = (bf16[8,144,1024]{2,1,0:T(8,128)(2,1)}, bf16[8,144,1024]{2,1,0:T(8,128)(2,1)}) custom-call(bf16[8,144,1024]{2,1,0:T(8,128)(2,1)} %bitcast.211, bf16[256,1536]{1,0:T(8,128)(2,1)} %get-tuple-element.117.refs_0_, bf16[256,1536]{1,0:T(8,128)(2,1)} %get-tuple-element.118.refs_1_, bf16[256,1536]{1,0:T(8,128)(2,1)} %get-tuple-element.119.refs_2_, ...), custom_call_target="tpu_custom_call" | custom-call | flops 3623878656 | bytes 157286400 | tf_op jit(solution)/shard_map/pallas_call | solution.py:1062
  384.7 6.5 all-to-all-start.1
  391.2 13.0 %select_reduce_fusion = f32[256,1572]{0,1:T(8,128)S(1)} fusion(f32[256,65]{0,1:T(8,128)S(1)} %concatenate.92, s32[256,65]{0,1:T(8,128)S(1)} %broadcast_subtract_fusion), kind=kLoop, calls=%fused_computation.4 | loop fusion | flops 78071808 | bytes 1742848 | tf_op jit(solution)/shard_map/reduce_sum | solution.py:1727
  404.3 4.6 fusion.5
  409.0 4.1 fusion.76
  413.5 4.1 fusion.4
  419.1 6.3 all-to-all-start.2
  425.6 6.8 sort.14
  433.2 18.4 %all-to-all-done.2.got_ref = bf16[32,8,2176]{2,1,0:T(8,128)(2,1)S(1)} async-done(((bf16[32,8,2176]{2,1,0:T(8,128)(2,1)}), bf16[32,8,2176]{2,1,0:T(8,128)(2,1)S(1)}, u32[]{:S(2)}, u32[]{:S(2)}) %all-to-all-start.2) | async-done | bytes 1114144 | tf_op jit(solution)/shard_map/all_to_all | solution.py:829
  457.1 66.3 %shard_map.432 = (bf16[256,1536]{1,0:T(8,128)(2,1)}, bf16[256,1536]{1,0:T(8,128)(2,1)}, bf16[256,1536]{1,0:T(8,128)(2,1)}, bf16[256,1536]{1,0:T(8,128)(2,1)}, bf...) custom-call(bf16[8,144,1024]{2,1,0:T(8,128)(2,1)} %bitcast.159, ...), custom_call_target="tpu_custom_call" | custom-call | flops 10871635968 | bytes 188743680 | tf_op jit(solution)/shard_map/pallas_call | solution.py:1199
  524.2 3.8 all-to-all-start.3
  528.1 4.0 collective-permute-start
  532.1 3.8 collective-permute-start.1
  535.9 21.3 %shard_map.433 = (f32[256,1024]{1,0:T(8,128)}, bf16[1024,4096]{1,0:T(8,128)(2,1)}, f32[8,1024]{1,0:T(8,128)}, bf16[1152,1024]{1,0:T(8,128)(2,1)}) custom-call(s32[1]{0:T(128)S(6)} %copy.319.prefix_ref, f32[256,1024]{1,0:T(8,128)} %copy-done.6, bf16[1152,1024]{1,0:T(8,128)(2,1)} %bitcast.175, bf16[256,128]{1,0:T(8,128)(2,1)} %get-tuple-element.134.logit_ref, ...), custom_call_target="tpu_custom_call" | custom-call | flops 6442450944 | bytes 33554432 | tf_op jit(solution)/shard_map/pallas_call | solution.py:387
  566.5 13.6 %add_multiply_fusion = (f32[1572,1024]{1,0:T(8,128)}, f32[1572,1024]{1,0:T(8,128)}, f32[1572,1024]{1,0:T(8,128)}) fusion(f32[1572,1024]{1,0:T(8,128)} %param.51, f32[1572,1024]{1,0:T(8,128)} %param.53, f32[1572,1024]{1,0:T(8,128)} %param.52, bf16[32,8,1024]{2,1,0:T(8,128)(2,1)} %all-to-all-done.1, f32[256,1572]{0,1:T(8,128)S(1)} %copy-done.13, ...), kind=kOutput, calls=%fused_computation.8 | convolution fusion | flops 848729088 | bytes 42379264 | tf_op jit(solution)/shard_map/pv,pd->vd/dot_general | solution.py:1866
  580.7 69.1 %shard_map.434 = (bf16[256,1536]{1,0:T(8,128)(2,1)}, bf16[256,1536]{1,0:T(8,128)(2,1)}, bf16[256,1536]{1,0:T(8,128)(2,1)}, bf16[256,1536]{1,0:T(8,128)(2,1)}, bf...) custom-call(bf16[8,144,1024]{2,1,0:T(8,128)(2,1)} %bitcast.209, ...), custom_call_target="tpu_custom_call" | custom-call | flops 10871635968 | bytes 188743680 | tf_op jit(solution)/shard_map/pallas_call | solution.py:1199
  649.9 20.3 %shard_map.435 = (f32[256,1024]{1,0:T(8,128)}, bf16[1024,4096]{1,0:T(8,128)(2,1)}, f32[8,1024]{1,0:T(8,128)}) custom-call(s32[1]{0:T(128)S(6)} %copy.319.prefix_ref, f32[256,1024]{1,0:T(8,128)} %get-tuple-element.144.grad_ref, bf16[1152,1024]{1,0:T(8,128)(2,1)} %bitcast.173, bf16[256,128]{1,0:T(8,128)(2,1)} %get-tuple-element.160.logit_ref, ...), custom_call_target="tpu_custom_call" | custom-call | flops 6442450944 | bytes 33554432 | tf_op jit(solution)/shard_map/pallas_call | solution.py:387
  684.4 15.4 %all-to-all-start.4 = ((bf16[32,2,4496]{2,1,0:T(2,128)(2,1)}), bf16[32,2,4496]{2,1,0:T(2,128)(2,1)S(1)}, u32[]{:S(2)}, u32[]{:S(2)}) async-start(bf16[32,2,4496]{2,1,0:T(2,128)(2,1)} %reshape.910), calls=%async_computation.4 | async-start | bytes 1179648 | tf_op jit(solution)/shard_map/all_to_all | solution.py:829
  699.8 99.4 %shard_map.436 = f32[2,32,4096]{2,1,0:T(8,128)} custom-call(bf16[4,2,2,2,32,4096]{5,4,3,2,1,0:T(8,128)(2,1)} %bitcast.163, bf16[4,2,2,2,32,4096]{5,4,3,2,1,0:T(8,128)(2,1)} %bitcast.164), custom_call_target="tpu_custom_call" | custom-call | flops 67108864 | bytes 209715200 | tf_op jit(solution)/shard_map/pallas_call | solution.py:1393
  812.4 4.1 collective-permute-start.7
  817.8 55.7 %shard_map.437 = (f32[32,50304]{1,0:T(8,128)}, f32[32,50304]{1,0:T(8,128)}, f32[32,50304]{1,0:T(8,128)}) custom-call(s32[8192]{0:T(1024)S(1)} %get-tuple-element.341.row_ref, s32[100]{0:T(128)S(1)} %get-tuple-element.332.low_ref, s32[100]{0:T(128)S(1)} %get-tuple-element.331.high_ref, bf16[32,8192]{1,0:T(8,128)(2,1)S(1)} %slice.95.arrived_ref, ...), custom_call_target="tpu_custom_call" | custom-call | flops 4294967296 | bytes 52428800 | tf_op jit(solution)/shard_map/pallas_call | solution.py:1536
  880.3 4.0 add_multiply_fusion.2
  885.0 3.8 add_multiply_fusion.1
  (254 shorter events, 93.5 us)
Async XLA Ops:
  7.2 126.3 %all-gather.2.cloned.1.call-start = ((), (), s32[]{:S(2)}) async-start(), calls=%async_computation.5 | async-start | bytes 17301504 | tf_op jit(solution)/shard_map/all_gather | solution.py:1622
  56.2 25.6 %all-to-all-start = ((bf16[32,2,4496]{2,1,0:T(2,128)(2,1)}), bf16[32,2,4496]{2,1,0:T(2,128)(2,1)}, u32[]{:S(2)}, u32[]{:S(2)}) async-start(bf16[32,2,4496]{2,1,0:T(2,128)(2,1)} %reshape.908), calls=%async_computation | async-start | bytes 1179648 | tf_op jit(solution)/shard_map/all_to_all | solution.py:829
  309.1 70.5 %copy-start.1 = (bf16[1152,256]{0,1:T(8,128)(2,1)S(1)}, bf16[1152,256]{0,1:T(8,128)(2,1)}, u32[]{:S(2)}) copy-start(bf16[1152,256]{0,1:T(8,128)(2,1)} %copy-done) | copy-start | bytes 1769476
  309.1 70.5 %copy-start.2 = (bf16[1152,256]{1,0:T(8,128)(2,1)S(1)}, bf16[1152,256]{1,0:T(8,128)(2,1)}, u32[]{:S(2)}) copy-start(bf16[1152,256]{1,0:T(8,128)(2,1)} %copy.285.refs_5_.refs_7_.spread_ref.refs_0_) | copy-start | bytes 1769476
  309.1 70.5 %copy-start.3 = (f32[256,1024]{1,0:T(8,128)S(1)}, f32[256,1024]{1,0:T(8,128)}, u32[]{:S(2)}) copy-start(f32[256,1024]{1,0:T(8,128)} %get-tuple-element.114.middle_ref) | copy-start | bytes 3145732
  309.1 70.5 %copy-start.4 = (f32[16,1024]{1,0:T(8,128)S(1)}, f32[16,1024]{1,0:T(8,128)}, u32[]{:S(2)}) copy-start(f32[16,1024]{1,0:T(8,128)} %pad_convert_fusion.1.refs_1_.refs_3_.gain_ref) | copy-start | bytes 196612
  309.1 70.5 %copy-start.7 = (f32[256,128]{1,0:T(8,128)S(1)}, f32[256,128]{1,0:T(8,128)}, u32[]{:S(2)}) copy-start(f32[256,128]{1,0:T(8,128)} %get-tuple-element.115.gates_ref) | copy-start | bytes 393220
  309.1 70.4 %copy-start.8 = (s32[8]{0:T(128)S(1)}, s32[8]{0:T(128)}, u32[]{:S(2)}) copy-start(s32[8]{0:T(128)} %picked_ref.3) | copy-start | bytes 100
  383.8 25.1 %copy-start.9 = (f32[8,1024]{1,0:T(8,128)}, f32[8,1024]{1,0:T(8,128)S(1)}, u32[]{:S(2)}) copy-start(f32[8,1024]{1,0:T(8,128)S(1)} %get-tuple-element.123.rows_ref) | copy-start | bytes 98308
  384.7 24.3 %all-to-all-start.1 = ((bf16[32,8,1024]{2,1,0:T(8,128)(2,1)}), bf16[32,8,1024]{2,1,0:T(8,128)(2,1)}, u32[]{:S(2)}, u32[]{:S(2)}) async-start(bf16[32,8,1024]{2,1,0:T(8,128)(2,1)} %broadcast_in_dim.36), calls=%async_computation.1 | async-start | bytes 1048576 | tf_op jit(solution)/shard_map/all_to_all | solution.py:829
  418.0 33.6 %copy-start.10 = (f32[8,1024]{1,0:T(8,128)S(1)}, f32[8,1024]{1,0:T(8,128)}, u32[]{:S(2)}) copy-start(f32[8,1024]{1,0:T(8,128)} %copy-done.9) | copy-start | bytes 98308
  419.1 32.6 %all-to-all-start.2 = ((bf16[32,8,2176]{2,1,0:T(8,128)(2,1)}), bf16[32,8,2176]{2,1,0:T(8,128)(2,1)S(1)}, u32[]{:S(2)}, u32[]{:S(2)}) async-start(bf16[32,8,2176]{2,1,0:T(8,128)(2,1)} %pad_maximum_fusion.1), calls=%async_computation.2 | async-start | bytes 2228224 | tf_op jit(solution)/shard_map/all_to_all | solution.py:829
  524.2 41.5 %all-to-all-start.3 = ((f32[32,1,16]{2,1,0:T(1,128)}), f32[32,1,16]{2,1,0:T(1,128)S(1)}, u32[]{:S(2)}, u32[]{:S(2)}) async-start(f32[32,1,16]{2,1,0:T(1,128)} %broadcast_in_dim.39), calls=%async_computation.3 | async-start | bytes 32768 | tf_op jit(solution)/shard_map/all_to_all | solution.py:829
  528.1 52.6 %collective-permute-start = (bf16[256,1536]{1,0:T(8,128)(2,1)}, bf16[256,1536]{1,0:T(8,128)(2,1)S(1)}, u32[]{:S(2)}, u32[]{:S(2)}) collective-permute-start(bf16[256,1536]{1,0:T(8,128)(2,1)} %get-tuple-element.132), channel_id=1, source_target_pairs={{0,0},{16,1},{10,2},{26,3},{11,8},{27,9},{17,10},{1,11},{18,16},{2... | collective-permute-start | bytes 2359304 | tf_op jit(solution)/shard_map/ppermute | solution.py:817
  532.1 117.7 %collective-permute-start.1 = (bf16[256,1536]{1,0:T(8,128)(2,1)}, bf16[256,1536]{1,0:T(8,128)(2,1)}, u32[]{:S(2)}, u32[]{:S(2)}) collective-permute-start(bf16[256,1536]{1,0:T(8,128)(2,1)} %get-tuple-element.155), channel_id=1, source_target_pairs={{16,0},{0,1},{26,2},{10,3},{27,8},{11,9},{1,10},{17,11},{2,16},{18... | collective-permute-start | bytes 2359304 | tf_op jit(solution)/shard_map/ppermute | solution.py:817
  535.9 22.2 %copy-start.31 = (f32[1024,128]{1,0:T(8,128)S(1)}, f32[1024,128]{1,0:T(8,128)}, u32[]{:S(2)}) copy-start(f32[1024,128]{1,0:T(8,128)} %get-tuple-element.172) | copy-start | bytes 1572868
  558.3 91.6 %collective-permute-start.2 = (bf16[256,1536]{1,0:T(8,128)(2,1)}, bf16[256,1536]{1,0:T(8,128)(2,1)}, u32[]{:S(2)}, u32[]{:S(2)}) collective-permute-start(bf16[256,1536]{1,0:T(8,128)(2,1)} %get-tuple-element.156), channel_id=1, source_target_pairs={{10,0},{26,1},{0,2},{16,3},{17,8},{1,9},{11,10},{27,11},{24,16},{8... | collective-permute-start | bytes 2359304 | tf_op jit(solution)/shard_map/ppermute | solution.py:817
  562.0 87.9 %collective-permute-start.3 = (bf16[256,1536]{1,0:T(8,128)(2,1)}, bf16[256,1536]{1,0:T(8,128)(2,1)}, u32[]{:S(2)}, u32[]{:S(2)}) collective-permute-start(bf16[256,1536]{1,0:T(8,128)(2,1)} %get-tuple-element.157), channel_id=1, source_target_pairs={{26,0},{10,1},{16,2},{0,3},{1,8},{17,9},{27,10},{11,11},{8,16},{24... | collective-permute-start | bytes 2359304 | tf_op jit(solution)/shard_map/ppermute | solution.py:817
  684.4 117.0 %all-to-all-start.4 = ((bf16[32,2,4496]{2,1,0:T(2,128)(2,1)}), bf16[32,2,4496]{2,1,0:T(2,128)(2,1)S(1)}, u32[]{:S(2)}, u32[]{:S(2)}) async-start(bf16[32,2,4496]{2,1,0:T(2,128)(2,1)} %reshape.910), calls=%async_computation.4 | async-start | bytes 1179648 | tf_op jit(solution)/shard_map/all_to_all | solution.py:829
  699.8 99.5 %copy-start.18 = (f32[256,1536]{1,0:T(8,128)S(1)}, f32[256,1536]{1,0:T(8,128)}, u32[]{:S(2)}) copy-start(f32[256,1536]{1,0:T(8,128)} %copy-done.17) | copy-start | bytes 4718596
  801.4 15.1 %copy-start.45 = (f32[2,32,8]{1,2,0:T(8,128)S(1)}, f32[2,32,8]{1,2,0:T(8,128)}, u32[]{:S(2)}) copy-start(f32[2,32,8]{1,2,0:T(8,128)} %param.40) | copy-start | bytes 6148
  801.4 15.8 %copy-start.41 = (f32[9,32]{1,0:T(8,128)S(1)}, f32[9,32]{1,0:T(8,128)}, u32[]{:S(2)}) copy-start(f32[9,32]{1,0:T(8,128)} %param.42) | copy-start | bytes 3460
  801.4 15.8 %copy-start.46 = (f32[9,32]{1,0:T(8,128)S(1)}, f32[9,32]{1,0:T(8,128)}, u32[]{:S(2)}) copy-start(f32[9,32]{1,0:T(8,128)} %param.44) | copy-start | bytes 3460
  801.4 15.8 %copy-start.47 = (f32[9,32]{1,0:T(8,128)S(1)}, f32[9,32]{1,0:T(8,128)}, u32[]{:S(2)}) copy-start(f32[9,32]{1,0:T(8,128)} %param.43) | copy-start | bytes 3460
  802.9 72.8 %collective-permute-start.4 = (bf16[256,1536]{1,0:T(8,128)(2,1)}, bf16[256,1536]{1,0:T(8,128)(2,1)S(1)}, u32[]{:S(2)}, u32[]{:S(2)}) collective-permute-start(bf16[256,1536]{1,0:T(8,128)(2,1)} %get-tuple-element.175), channel_id=1, source_target_pairs={{0,0},{16,1},{10,2},{26,3},{11,8},{27,9},{17,10},{1,11},{18,16},{2... | collective-permute-start | bytes 2359304 | tf_op jit(solution)/shard_map/ppermute | solution.py:817
  805.4 70.3 %collective-permute-start.5 = (bf16[256,1536]{1,0:T(8,128)(2,1)}, bf16[256,1536]{1,0:T(8,128)(2,1)S(1)}, u32[]{:S(2)}, u32[]{:S(2)}) collective-permute-start(bf16[256,1536]{1,0:T(8,128)(2,1)} %get-tuple-element.176), channel_id=1, source_target_pairs={{16,0},{0,1},{26,2},{10,3},{27,8},{11,9},{1,10},{17,11},{2,16},{18... | collective-permute-start | bytes 2359304 | tf_op jit(solution)/shard_map/ppermute | solution.py:817
  808.7 67.0 %collective-permute-start.6 = (bf16[256,1536]{1,0:T(8,128)(2,1)}, bf16[256,1536]{1,0:T(8,128)(2,1)S(1)}, u32[]{:S(2)}, u32[]{:S(2)}) collective-permute-start(bf16[256,1536]{1,0:T(8,128)(2,1)} %get-tuple-element.177), channel_id=1, source_target_pairs={{10,0},{26,1},{0,2},{16,3},{17,8},{1,9},{11,10},{27,11},{24,16},{8... | collective-permute-start | bytes 2359304 | tf_op jit(solution)/shard_map/ppermute | solution.py:817
  812.4 63.3 %collective-permute-start.7 = (bf16[256,1536]{1,0:T(8,128)(2,1)}, bf16[256,1536]{1,0:T(8,128)(2,1)S(1)}, u32[]{:S(2)}, u32[]{:S(2)}) collective-permute-start(bf16[256,1536]{1,0:T(8,128)(2,1)} %get-tuple-element.178), channel_id=1, source_target_pairs={{26,0},{10,1},{16,2},{0,3},{1,8},{17,9},{27,10},{11,11},{8,16},{24... | collective-permute-start | bytes 2359304 | tf_op jit(solution)/shard_map/ppermute | solution.py:817
  817.8 55.7 %copy-start.19 = (f32[2,32,4096]{2,1,0:T(8,128)S(1)}, f32[2,32,4096]{2,1,0:T(8,128)}, u32[]{:S(2)}) copy-start(f32[2,32,4096]{2,1,0:T(8,128)} %param.36) | copy-start | bytes 3145732
  817.8 55.7 %copy-start.23 = (f32[32,4096]{1,0:T(8,128)S(1)}, f32[32,4096]{1,0:T(8,128)}, u32[]{:S(2)}) copy-start(f32[32,4096]{1,0:T(8,128)} %get-tuple-element.187) | copy-start | bytes 1572868
  817.8 55.7 %copy-start.26 = (f32[2,32,4096]{2,1,0:T(8,128)S(1)}, f32[2,32,4096]{2,1,0:T(8,128)}, u32[]{:S(2)}) copy-start(f32[2,32,4096]{2,1,0:T(8,128)} %param.38) | copy-start | bytes 3145732
  817.8 55.7 %copy-start.27 = (f32[2,32,4096]{2,1,0:T(8,128)S(1)}, f32[2,32,4096]{2,1,0:T(8,128)}, u32[]{:S(2)}) copy-start(f32[2,32,4096]{2,1,0:T(8,128)} %param.37) | copy-start | bytes 3145732
  (33 other events, 196.0 us)
Sparse Core Ops, SparseCore 0:
  11.6 121.9 all-gather.1

commit v6 on v5

--- a/solution.py
+++ b/solution.py
@@ -1022,7 +1022,7 @@
         swap_start(*swap)
     fetch_expert(part_places(PLANES), part_refs, up_ref, down_ref, copy_sem)
     back = {}
-    for pair in range(4):
+    for pair in (0, 3, 2, 1):
         for turn in (2 * pair, 2 * pair + 1):
             if turn:
                 copies[turn].wait_recv()
@@ -1119,7 +1119,7 @@
     copies = exchange_out(outgoing_ref, pull_ref, send_sem, recv_sem, partners, groups)
     fetch_expert(part_places(part_count), part_refs, up_ref, down_ref, copy_sem)
     back = {}
-    for pair in range(4):
+    for pair in (0, 3, 2, 1):
         rows = slice(pair * 2 * capacity, (pair + 1) * 2 * capacity)
         gate_part, up_part, sigmoid = silu_parts(
             dot_nn(two_blocks(received_ref, pair), up_ref[...])

time: 907 us -> 895 us (0.987)
  Pallas kernels: 584 us -> 566 us
    pallas_call x2, Pallas kernels: 135 us -> 125 us  [backward_exchange(): pl.pallas_call(functools.partial(backward_exchange_kernel, len(parts), ca...]
where the time goes in v6:
time: 895 us; the launch traced here: 884 us
  Pallas kernels  566 us (63%)
  local copies, waits for them, and re-layouts  86.3 us (10%)
  starting transfers between devices  71.9 us (8%)
  waiting for transfers between devices  61.7 us (7%)
  other arithmetic  53.7 us (6%)
  matrix products  26.7 us (3%)
  between operations  18.1 us (2%)
    pallas_call x2, Pallas kernels, forward_exchange(): pl.pallas_call(functools.partial(forward_exchange_kernel, len(pieces)), o...  209 us
    pallas_call x2, Pallas kernels, backward_exchange(): pl.pallas_call(functools.partial(backward_exchange_kernel, len(parts), ca...  125 us
    pallas_call x1, Pallas kernels, owner_sums(): pl.pallas_call(functools.partial(owner_sum_kernel, layers), out_shape=jax...  99.4 us
    pallas_call x1, Pallas kernels, embedding_update_of(): pl.pallas_call(embedding_kernel, grid=(-(-vocabulary // VOCAB_BLOCK),), o...  55.2 us
    all_to_all x5, starting transfers between devices, send_all(): return lax.all_to_all(values, AXES, split_axis=0, concat_axis=0, tiled=True)  43.7 us
    pallas_call x2, Pallas kernels, backward_layer(): pl.pallas_call(functools.partial(backward_kernel, layer_index, capacity),...  41.6 us
    all_gather x1, waiting for transfers between devices, shards(): lax.all_gather(attention.astype(jnp.bfloat16), AXES, axis=1, tiled=True)  36.8 us
    pallas_call x2, Pallas kernels, forward_layer(): pl.pallas_call(functools.partial(forward_kernel, layer_index, capacity, e...  30.5 us
  transfers between devices with their start and end apart: 14, of which 3 were waited for; matrix products, arithmetic and copies ran while one was open for 13% of the time, Pallas kernels for 27%

profile of v6, /device:TPU:9, one launch (start us, length us, event | category | flops | bytes accessed | tf_op | source)
XLA Modules:
  0.0 884.3 jit_solution(7207251896168829240)
XLA Ops:
  12.9 8.8 copy.270
  22.4 28.4 %gather_fusion = bf16[8192,32]{1,0:T(8,128)(2,1)S(1)} fusion(bf16[50304,32]{1,0:T(8,128)(2,1)} %copy.270, s32[8192]{0:T(1024)S(1)} %get-tuple-element.344), kind=kCustom, calls=%fused_computation | custom fusion | bytes 1081344 | tf_op jit(solution)/shard_map/jit(_take)/gather | solution.py:1621
  56.2 6.7 all-to-all-start
  75.4 6.4 all-to-all-done
  81.9 4.0 reshape.909
  96.8 36.8 %all-gather.2.cloned.1.call-done.refs_0_.refs_2_.weight_ref = bf16[2,1024,4096]{2,1,0:T(8,128)(2,1)} async-done(((bf16[2,32,4096]{2,1,0:T(8,128)(2,1)}), bf16[2,1024,4096]{2,1,0:T(8,128)(2,1)}) %all-gather.2.cloned.1.call-update) | async-done | bytes 16777232 | tf_op jit(solution)/shard_map/all_gather | solution.py:1622
  133.5 13.6 %shard_map.426 = (f32[256,1024]{1,0:T(8,128)}, f32[256,2048]{1,0:T(8,128)}, bf16[256,1024]{1,0:T(8,128)(2,1)}, bf16[256,1024]{1,0:T(8,128)(2,1)}, bf16[256,1024]...) custom-call(s32[1]{0:T(128)S(6)} %copy.319.prefix_ref, ...), custom_call_target="tpu_custom_call" | custom-call | flops 3221225472 | bytes 25165824 | tf_op jit(solution)/shard_map/pallas_call | solution.py:223
  147.2 146.5 %shard_map.427 = (bf16[8,144,1024]{2,1,0:T(8,128)(2,1)}, bf16[8,144,1024]{2,1,0:T(8,128)(2,1)}, bf16[256,1536]{1,0:T(8,128)(2,1)}, bf16[256,1536]{1,0:T(8,128)(2...) custom-call(bf16[8,144,1024]{2,1,0:T(8,128)(2,1)} %bitcast.210, ...), custom_call_target="tpu_custom_call" | custom-call | flops 3623878656 | bytes 157286400 | tf_op jit(solution)/shard_map/pallas_call | solution.py:1062
  293.6 16.9 %shard_map.428 = (f32[256,1024]{1,0:T(8,128)}, f32[256,2048]{1,0:T(8,128)}, bf16[256,1024]{1,0:T(8,128)(2,1)}, bf16[256,1024]{1,0:T(8,128)(2,1)}, bf16[256,1024]...) custom-call(s32[1]{0:T(128)S(6)} %copy.319.prefix_ref, ...), custom_call_target="tpu_custom_call" | custom-call | flops 3221225472 | bytes 25165824 | tf_op jit(solution)/shard_map/pallas_call | solution.py:223
  310.6 62.1 %shard_map.429 = (bf16[8,144,1024]{2,1,0:T(8,128)(2,1)}, bf16[8,144,1024]{2,1,0:T(8,128)(2,1)}) custom-call(bf16[8,144,1024]{2,1,0:T(8,128)(2,1)} %bitcast.211, bf16[256,1536]{1,0:T(8,128)(2,1)} %get-tuple-element.117.refs_0_, bf16[256,1536]{1,0:T(8,128)(2,1)} %get-tuple-element.118.refs_1_, bf16[256,1536]{1,0:T(8,128)(2,1)} %get-tuple-element.119.refs_2_, ...), custom_call_target="tpu_custom_call" | custom-call | flops 3623878656 | bytes 157286400 | tf_op jit(solution)/shard_map/pallas_call | solution.py:1062
  377.9 7.3 all-to-all-start.1
  385.2 13.0 %select_reduce_fusion = f32[256,1572]{0,1:T(8,128)S(1)} fusion(f32[256,65]{0,1:T(8,128)S(1)} %concatenate.92, s32[256,65]{0,1:T(8,128)S(1)} %broadcast_subtract_fusion), kind=kLoop, calls=%fused_computation.4 | loop fusion | flops 78071808 | bytes 1742848 | tf_op jit(solution)/shard_map/reduce_sum | solution.py:1727
  398.2 4.6 fusion.5
  402.9 4.1 fusion.76
  407.5 4.1 fusion.4
  413.0 6.2 all-to-all-start.2
  419.5 6.8 sort.14
  427.1 18.4 %all-to-all-done.2.got_ref = bf16[32,8,2176]{2,1,0:T(8,128)(2,1)S(1)} async-done(((bf16[32,8,2176]{2,1,0:T(8,128)(2,1)}), bf16[32,8,2176]{2,1,0:T(8,128)(2,1)S(1)}, u32[]{:S(2)}, u32[]{:S(2)}) %all-to-all-start.2) | async-done | bytes 1114144 | tf_op jit(solution)/shard_map/all_to_all | solution.py:829
  451.0 61.0 %shard_map.432 = (bf16[256,1536]{1,0:T(8,128)(2,1)}, bf16[256,1536]{1,0:T(8,128)(2,1)}, bf16[256,1536]{1,0:T(8,128)(2,1)}, bf16[256,1536]{1,0:T(8,128)(2,1)}, bf...) custom-call(bf16[8,144,1024]{2,1,0:T(8,128)(2,1)} %bitcast.159, ...), custom_call_target="tpu_custom_call" | custom-call | flops 10871635968 | bytes 188743680 | tf_op jit(solution)/shard_map/pallas_call | solution.py:1199
  512.8 4.8 all-to-all-start.3
  517.7 4.0 collective-permute-start
  521.7 3.8 collective-permute-start.1
  525.5 21.3 %shard_map.433 = (f32[256,1024]{1,0:T(8,128)}, bf16[1024,4096]{1,0:T(8,128)(2,1)}, f32[8,1024]{1,0:T(8,128)}, bf16[1152,1024]{1,0:T(8,128)(2,1)}) custom-call(s32[1]{0:T(128)S(6)} %copy.319.prefix_ref, f32[256,1024]{1,0:T(8,128)} %copy-done.6, bf16[1152,1024]{1,0:T(8,128)(2,1)} %bitcast.175, bf16[256,128]{1,0:T(8,128)(2,1)} %get-tuple-element.134.logit_ref, ...), custom_call_target="tpu_custom_call" | custom-call | flops 6442450944 | bytes 33554432 | tf_op jit(solution)/shard_map/pallas_call | solution.py:387
  556.1 13.6 %add_multiply_fusion = (f32[1572,1024]{1,0:T(8,128)}, f32[1572,1024]{1,0:T(8,128)}, f32[1572,1024]{1,0:T(8,128)}) fusion(f32[1572,1024]{1,0:T(8,128)} %param.51, f32[1572,1024]{1,0:T(8,128)} %param.53, f32[1572,1024]{1,0:T(8,128)} %param.52, bf16[32,8,1024]{2,1,0:T(8,128)(2,1)} %all-to-all-done.1, f32[256,1572]{0,1:T(8,128)S(1)} %copy-done.13, ...), kind=kOutput, calls=%fused_computation.8 | convolution fusion | flops 848729088 | bytes 42379264 | tf_op jit(solution)/shard_map/pv,pd->vd/dot_general | solution.py:1866
  570.3 64.0 %shard_map.434 = (bf16[256,1536]{1,0:T(8,128)(2,1)}, bf16[256,1536]{1,0:T(8,128)(2,1)}, bf16[256,1536]{1,0:T(8,128)(2,1)}, bf16[256,1536]{1,0:T(8,128)(2,1)}, bf...) custom-call(bf16[8,144,1024]{2,1,0:T(8,128)(2,1)} %bitcast.209, ...), custom_call_target="tpu_custom_call" | custom-call | flops 10871635968 | bytes 188743680 | tf_op jit(solution)/shard_map/pallas_call | solution.py:1199
  634.3 20.3 %shard_map.435 = (f32[256,1024]{1,0:T(8,128)}, bf16[1024,4096]{1,0:T(8,128)(2,1)}, f32[8,1024]{1,0:T(8,128)}) custom-call(s32[1]{0:T(128)S(6)} %copy.319.prefix_ref, f32[256,1024]{1,0:T(8,128)} %get-tuple-element.144.grad_ref, bf16[1152,1024]{1,0:T(8,128)(2,1)} %bitcast.173, bf16[256,128]{1,0:T(8,128)(2,1)} %get-tuple-element.160.logit_ref, ...), custom_call_target="tpu_custom_call" | custom-call | flops 6442450944 | bytes 33554432 | tf_op jit(solution)/shard_map/pallas_call | solution.py:387
  668.9 18.6 %all-to-all-start.4 = ((bf16[32,2,4496]{2,1,0:T(2,128)(2,1)}), bf16[32,2,4496]{2,1,0:T(2,128)(2,1)S(1)}, u32[]{:S(2)}, u32[]{:S(2)}) async-start(bf16[32,2,4496]{2,1,0:T(2,128)(2,1)} %reshape.910), calls=%async_computation.4 | async-start | bytes 1179648 | tf_op jit(solution)/shard_map/all_to_all | solution.py:829
  687.5 99.4 %shard_map.436 = f32[2,32,4096]{2,1,0:T(8,128)} custom-call(bf16[4,2,2,2,32,4096]{5,4,3,2,1,0:T(8,128)(2,1)} %bitcast.163, bf16[4,2,2,2,32,4096]{5,4,3,2,1,0:T(8,128)(2,1)} %bitcast.164), custom_call_target="tpu_custom_call" | custom-call | flops 67108864 | bytes 209715200 | tf_op jit(solution)/shard_map/pallas_call | solution.py:1393
  800.1 4.1 collective-permute-start.7
  805.5 55.2 %shard_map.437 = (f32[32,50304]{1,0:T(8,128)}, f32[32,50304]{1,0:T(8,128)}, f32[32,50304]{1,0:T(8,128)}) custom-call(s32[8192]{0:T(1024)S(1)} %get-tuple-element.341.row_ref, s32[100]{0:T(128)S(1)} %get-tuple-element.332.low_ref, s32[100]{0:T(128)S(1)} %get-tuple-element.331.high_ref, bf16[32,8192]{1,0:T(8,128)(2,1)S(1)} %slice.95.arrived_ref, ...), custom_call_target="tpu_custom_call" | custom-call | flops 4294967296 | bytes 52428800 | tf_op jit(solution)/shard_map/pallas_call | solution.py:1536
  867.5 4.0 add_multiply_fusion.2
  872.2 3.8 add_multiply_fusion.1
  (254 shorter events, 93.5 us)
Async XLA Ops:
  7.2 126.3 %all-gather.2.cloned.1.call-start = ((), (), s32[]{:S(2)}) async-start(), calls=%async_computation.5 | async-start | bytes 17301504 | tf_op jit(solution)/shard_map/all_gather | solution.py:1622
  56.2 25.6 %all-to-all-start = ((bf16[32,2,4496]{2,1,0:T(2,128)(2,1)}), bf16[32,2,4496]{2,1,0:T(2,128)(2,1)}, u32[]{:S(2)}, u32[]{:S(2)}) async-start(bf16[32,2,4496]{2,1,0:T(2,128)(2,1)} %reshape.908), calls=%async_computation | async-start | bytes 1179648 | tf_op jit(solution)/shard_map/all_to_all | solution.py:829
  310.5 62.2 %copy-start.1 = (bf16[1152,256]{0,1:T(8,128)(2,1)S(1)}, bf16[1152,256]{0,1:T(8,128)(2,1)}, u32[]{:S(2)}) copy-start(bf16[1152,256]{0,1:T(8,128)(2,1)} %copy-done) | copy-start | bytes 1769476
  310.5 62.2 %copy-start.2 = (bf16[1152,256]{1,0:T(8,128)(2,1)S(1)}, bf16[1152,256]{1,0:T(8,128)(2,1)}, u32[]{:S(2)}) copy-start(bf16[1152,256]{1,0:T(8,128)(2,1)} %copy.285.refs_5_.refs_7_.spread_ref.refs_0_) | copy-start | bytes 1769476
  310.5 62.2 %copy-start.3 = (f32[256,1024]{1,0:T(8,128)S(1)}, f32[256,1024]{1,0:T(8,128)}, u32[]{:S(2)}) copy-start(f32[256,1024]{1,0:T(8,128)} %get-tuple-element.114.middle_ref) | copy-start | bytes 3145732
  310.6 62.2 %copy-start.4 = (f32[16,1024]{1,0:T(8,128)S(1)}, f32[16,1024]{1,0:T(8,128)}, u32[]{:S(2)}) copy-start(f32[16,1024]{1,0:T(8,128)} %pad_convert_fusion.1.refs_1_.refs_3_.gain_ref) | copy-start | bytes 196612
  310.6 62.2 %copy-start.7 = (f32[256,128]{1,0:T(8,128)S(1)}, f32[256,128]{1,0:T(8,128)}, u32[]{:S(2)}) copy-start(f32[256,128]{1,0:T(8,128)} %get-tuple-element.115.gates_ref) | copy-start | bytes 393220
  310.6 62.2 %copy-start.8 = (s32[8]{0:T(128)S(1)}, s32[8]{0:T(128)}, u32[]{:S(2)}) copy-start(s32[8]{0:T(128)} %picked_ref.3) | copy-start | bytes 100
  377.0 25.9 %copy-start.9 = (f32[8,1024]{1,0:T(8,128)}, f32[8,1024]{1,0:T(8,128)S(1)}, u32[]{:S(2)}) copy-start(f32[8,1024]{1,0:T(8,128)S(1)} %get-tuple-element.123.rows_ref) | copy-start | bytes 98308
  377.9 25.0 %all-to-all-start.1 = ((bf16[32,8,1024]{2,1,0:T(8,128)(2,1)}), bf16[32,8,1024]{2,1,0:T(8,128)(2,1)}, u32[]{:S(2)}, u32[]{:S(2)}) async-start(bf16[32,8,1024]{2,1,0:T(8,128)(2,1)} %broadcast_in_dim.36), calls=%async_computation.1 | async-start | bytes 1048576 | tf_op jit(solution)/shard_map/all_to_all | solution.py:829
  412.0 33.6 %copy-start.10 = (f32[8,1024]{1,0:T(8,128)S(1)}, f32[8,1024]{1,0:T(8,128)}, u32[]{:S(2)}) copy-start(f32[8,1024]{1,0:T(8,128)} %copy-done.9) | copy-start | bytes 98308
  413.0 32.5 %all-to-all-start.2 = ((bf16[32,8,2176]{2,1,0:T(8,128)(2,1)}), bf16[32,8,2176]{2,1,0:T(8,128)(2,1)S(1)}, u32[]{:S(2)}, u32[]{:S(2)}) async-start(bf16[32,8,2176]{2,1,0:T(8,128)(2,1)} %pad_maximum_fusion.1), calls=%async_computation.2 | async-start | bytes 2228224 | tf_op jit(solution)/shard_map/all_to_all | solution.py:829
  512.8 42.5 %all-to-all-start.3 = ((f32[32,1,16]{2,1,0:T(1,128)}), f32[32,1,16]{2,1,0:T(1,128)S(1)}, u32[]{:S(2)}, u32[]{:S(2)}) async-start(f32[32,1,16]{2,1,0:T(1,128)} %broadcast_in_dim.39), calls=%async_computation.3 | async-start | bytes 32768 | tf_op jit(solution)/shard_map/all_to_all | solution.py:829
  517.7 52.6 %collective-permute-start = (bf16[256,1536]{1,0:T(8,128)(2,1)}, bf16[256,1536]{1,0:T(8,128)(2,1)S(1)}, u32[]{:S(2)}, u32[]{:S(2)}) collective-permute-start(bf16[256,1536]{1,0:T(8,128)(2,1)} %get-tuple-element.132), channel_id=1, source_target_pairs={{0,0},{16,1},{10,2},{26,3},{11,8},{27,9},{17,10},{1,11},{18,16},{2... | collective-permute-start | bytes 2359304 | tf_op jit(solution)/shard_map/ppermute | solution.py:817
  521.7 112.6 %collective-permute-start.1 = (bf16[256,1536]{1,0:T(8,128)(2,1)}, bf16[256,1536]{1,0:T(8,128)(2,1)}, u32[]{:S(2)}, u32[]{:S(2)}) collective-permute-start(bf16[256,1536]{1,0:T(8,128)(2,1)} %get-tuple-element.155), channel_id=1, source_target_pairs={{16,0},{0,1},{26,2},{10,3},{27,8},{11,9},{1,10},{17,11},{2,16},{18... | collective-permute-start | bytes 2359304 | tf_op jit(solution)/shard_map/ppermute | solution.py:817
  525.5 22.2 %copy-start.31 = (f32[1024,128]{1,0:T(8,128)S(1)}, f32[1024,128]{1,0:T(8,128)}, u32[]{:S(2)}) copy-start(f32[1024,128]{1,0:T(8,128)} %get-tuple-element.172) | copy-start | bytes 1572868
  547.9 86.4 %collective-permute-start.2 = (bf16[256,1536]{1,0:T(8,128)(2,1)}, bf16[256,1536]{1,0:T(8,128)(2,1)}, u32[]{:S(2)}, u32[]{:S(2)}) collective-permute-start(bf16[256,1536]{1,0:T(8,128)(2,1)} %get-tuple-element.156), channel_id=1, source_target_pairs={{10,0},{26,1},{0,2},{16,3},{17,8},{1,9},{11,10},{27,11},{24,16},{8... | collective-permute-start | bytes 2359304 | tf_op jit(solution)/shard_map/ppermute | solution.py:817
  551.6 82.7 %collective-permute-start.3 = (bf16[256,1536]{1,0:T(8,128)(2,1)}, bf16[256,1536]{1,0:T(8,128)(2,1)}, u32[]{:S(2)}, u32[]{:S(2)}) collective-permute-start(bf16[256,1536]{1,0:T(8,128)(2,1)} %get-tuple-element.157), channel_id=1, source_target_pairs={{26,0},{10,1},{16,2},{0,3},{1,8},{17,9},{27,10},{11,11},{8,16},{24... | collective-permute-start | bytes 2359304 | tf_op jit(solution)/shard_map/ppermute | solution.py:817
  668.9 120.2 %all-to-all-start.4 = ((bf16[32,2,4496]{2,1,0:T(2,128)(2,1)}), bf16[32,2,4496]{2,1,0:T(2,128)(2,1)S(1)}, u32[]{:S(2)}, u32[]{:S(2)}) async-start(bf16[32,2,4496]{2,1,0:T(2,128)(2,1)} %reshape.910), calls=%async_computation.4 | async-start | bytes 1179648 | tf_op jit(solution)/shard_map/all_to_all | solution.py:829
  687.5 99.5 %copy-start.18 = (f32[256,1536]{1,0:T(8,128)S(1)}, f32[256,1536]{1,0:T(8,128)}, u32[]{:S(2)}) copy-start(f32[256,1536]{1,0:T(8,128)} %copy-done.17) | copy-start | bytes 4718596
  789.1 15.1 %copy-start.45 = (f32[2,32,8]{1,2,0:T(8,128)S(1)}, f32[2,32,8]{1,2,0:T(8,128)}, u32[]{:S(2)}) copy-start(f32[2,32,8]{1,2,0:T(8,128)} %param.40) | copy-start | bytes 6148
  789.1 15.8 %copy-start.41 = (f32[9,32]{1,0:T(8,128)S(1)}, f32[9,32]{1,0:T(8,128)}, u32[]{:S(2)}) copy-start(f32[9,32]{1,0:T(8,128)} %param.42) | copy-start | bytes 3460
  789.1 15.8 %copy-start.46 = (f32[9,32]{1,0:T(8,128)S(1)}, f32[9,32]{1,0:T(8,128)}, u32[]{:S(2)}) copy-start(f32[9,32]{1,0:T(8,128)} %param.44) | copy-start | bytes 3460
  789.1 15.8 %copy-start.47 = (f32[9,32]{1,0:T(8,128)S(1)}, f32[9,32]{1,0:T(8,128)}, u32[]{:S(2)}) copy-start(f32[9,32]{1,0:T(8,128)} %param.43) | copy-start | bytes 3460
  790.6 72.3 %collective-permute-start.4 = (bf16[256,1536]{1,0:T(8,128)(2,1)}, bf16[256,1536]{1,0:T(8,128)(2,1)S(1)}, u32[]{:S(2)}, u32[]{:S(2)}) collective-permute-start(bf16[256,1536]{1,0:T(8,128)(2,1)} %get-tuple-element.175), channel_id=1, source_target_pairs={{0,0},{16,1},{10,2},{26,3},{11,8},{27,9},{17,10},{1,11},{18,16},{2... | collective-permute-start | bytes 2359304 | tf_op jit(solution)/shard_map/ppermute | solution.py:817
  793.1 69.8 %collective-permute-start.5 = (bf16[256,1536]{1,0:T(8,128)(2,1)}, bf16[256,1536]{1,0:T(8,128)(2,1)S(1)}, u32[]{:S(2)}, u32[]{:S(2)}) collective-permute-start(bf16[256,1536]{1,0:T(8,128)(2,1)} %get-tuple-element.176), channel_id=1, source_target_pairs={{16,0},{0,1},{26,2},{10,3},{27,8},{11,9},{1,10},{17,11},{2,16},{18... | collective-permute-start | bytes 2359304 | tf_op jit(solution)/shard_map/ppermute | solution.py:817
  796.4 66.5 %collective-permute-start.6 = (bf16[256,1536]{1,0:T(8,128)(2,1)}, bf16[256,1536]{1,0:T(8,128)(2,1)S(1)}, u32[]{:S(2)}, u32[]{:S(2)}) collective-permute-start(bf16[256,1536]{1,0:T(8,128)(2,1)} %get-tuple-element.177), channel_id=1, source_target_pairs={{10,0},{26,1},{0,2},{16,3},{17,8},{1,9},{11,10},{27,11},{24,16},{8... | collective-permute-start | bytes 2359304 | tf_op jit(solution)/shard_map/ppermute | solution.py:817
  800.1 62.8 %collective-permute-start.7 = (bf16[256,1536]{1,0:T(8,128)(2,1)}, bf16[256,1536]{1,0:T(8,128)(2,1)S(1)}, u32[]{:S(2)}, u32[]{:S(2)}) collective-permute-start(bf16[256,1536]{1,0:T(8,128)(2,1)} %get-tuple-element.178), channel_id=1, source_target_pairs={{26,0},{10,1},{16,2},{0,3},{1,8},{17,9},{27,10},{11,11},{8,16},{24... | collective-permute-start | bytes 2359304 | tf_op jit(solution)/shard_map/ppermute | solution.py:817
  805.5 55.2 %copy-start.19 = (f32[2,32,4096]{2,1,0:T(8,128)S(1)}, f32[2,32,4096]{2,1,0:T(8,128)}, u32[]{:S(2)}) copy-start(f32[2,32,4096]{2,1,0:T(8,128)} %param.36) | copy-start | bytes 3145732
  805.5 55.2 %copy-start.23 = (f32[32,4096]{1,0:T(8,128)S(1)}, f32[32,4096]{1,0:T(8,128)}, u32[]{:S(2)}) copy-start(f32[32,4096]{1,0:T(8,128)} %get-tuple-element.187) | copy-start | bytes 1572868
  805.5 55.2 %copy-start.26 = (f32[2,32,4096]{2,1,0:T(8,128)S(1)}, f32[2,32,4096]{2,1,0:T(8,128)}, u32[]{:S(2)}) copy-start(f32[2,32,4096]{2,1,0:T(8,128)} %param.38) | copy-start | bytes 3145732
  805.5 55.2 %copy-start.27 = (f32[2,32,4096]{2,1,0:T(8,128)S(1)}, f32[2,32,4096]{2,1,0:T(8,128)}, u32[]{:S(2)}) copy-start(f32[2,32,4096]{2,1,0:T(8,128)} %param.37) | copy-start | bytes 3145732
  (33 other events, 195.6 us)
Sparse Core Ops, SparseCore 0:
  11.6 121.9 all-gather.1
